TPU v7x, 512 devices: a whole 4x8x8 slice. The times are simulated.
512 devices in a mesh: blk: 32 (over y_lo, z, core), qgroup: 16 (over x, y_hi).
Axes of the slice: x: 4, y: 8 (y_hi: 4, y_lo: 2; y = y_hi * 2 + y_lo), z: 8, core: 2. Of those that a mesh axis runs over, the one named last changes fastest.
Arguments:
- queries: bfloat16 [16, 256, 4096], P('qgroup', 'blk'), may hold values from -6 to 6
- passages: bfloat16 [8192, 4096], P('blk'), may hold values from -6 to 6
- teacher: float32 [16, 256, 8192], P('qgroup', None, 'blk'), may hold values from -20 to 340
- teacher_rows: int32 [16, 256], P('qgroup', 'blk'), may hold values from 0 to 255, each once within a row
- positives: int32 [16, 256], P('qgroup', 'blk'), may hold values from 0 to 8191
Outputs:
- loss: float32 [16, 256], P('qgroup', 'blk')
- query_grads: bfloat16 [16, 256, 4096], P('qgroup', 'blk')
- passage_grads: bfloat16 [8192, 4096], P('blk', 'qgroup')
Inputs may be any that keep to these rules, and one draw needn't show every extreme that they name: Each group's row of teacher_rows lists all 256 teacher rows once.
All inputs are finite; a program needn't handle non-finite values.
Results may differ from a plain program's by a relative error of at most 0.0051.
Values may be sent and summed in bfloat16 or wider, within the bound.
No kernel may reach another device: no remote copies, remote signals or barrier semaphores. Data moves between devices by JAX's collectives and lax.ppermute only.
A program may use at most 64 MiB of HBM per device.

v0:
```python
import jax
import jax.numpy as jnp
from jax import lax
from jax.sharding import PartitionSpec as P

inv_temp = 50.0


def per_device(queries, passages, teacher, teacher_rows, positives):
    block_rows = passages.shape[0]
    group_query = lax.all_gather(queries[0], "blk", axis=0, tiled=True)
    row_index, positive = (
        lax.all_gather(teacher_rows[0], "blk", axis=0, tiled=True),
        lax.all_gather(positives[0], "blk", axis=0, tiled=True),
    )
    scores = jnp.dot(group_query, passages.T, preferred_element_type=jnp.float32) * inv_temp
    teacher_block = jnp.take(teacher[0], row_index, axis=0)
    local_student = jnp.max(scores, axis=1)
    local_teacher = jnp.max(teacher_block, axis=1)
    top_student, top_teacher = lax.pmax((local_student, local_teacher), "blk")
    sum_student, sum_teacher = lax.psum(
        (
            jnp.sum(jnp.exp(scores - top_student[:, None]), axis=1),
            jnp.sum(jnp.exp(teacher_block - top_teacher[:, None]), axis=1),
        ),
        "blk",
    )
    log_student = scores - top_student[:, None] - jnp.log(sum_student)[:, None]
    log_teacher = teacher_block - top_teacher[:, None] - jnp.log(sum_teacher)[:, None]
    student_prob = jnp.exp(log_student)
    teacher_prob = jnp.exp(log_teacher)
    columns = lax.axis_index("blk") * block_rows + lax.iota(jnp.int32, block_rows)
    onehot = columns[None, :] == positive[:, None]
    loss_terms = jnp.sum(teacher_prob * (log_teacher - log_student), axis=1) - jnp.sum(
        jnp.where(onehot, log_student, 0.0), axis=1
    )
    own_rows = score_grads_rows = group_query.shape[0] // lax.axis_size("blk")
    loss_whole = lax.psum(loss_terms, "blk")
    loss = lax.dynamic_slice_in_dim(loss_whole, lax.axis_index("blk") * own_rows, own_rows)
    score_grads = (
        inv_temp * (2.0 * student_prob - teacher_prob - onehot.astype(jnp.float32))
    ).astype(jnp.bfloat16)
    query_total = lax.psum_scatter(
        jnp.dot(score_grads, passages, preferred_element_type=jnp.float32),
        "blk",
        scatter_dimension=0,
        tiled=True,
    )
    passage_term = lax.dot_general(
        score_grads, group_query, (((0,), (0,)), ((), ())), preferred_element_type=jnp.float32
    )
    received = lax.all_to_all(
        passage_term.astype(jnp.bfloat16), "qgroup", split_axis=1, concat_axis=0, tiled=True
    )
    group_count = lax.axis_size("qgroup")
    stacked = received.reshape(group_count, block_rows, received.shape[1])
    passage_total = jnp.sum(stacked.astype(jnp.float32), axis=0)
    return (loss[None], query_total.astype(jnp.bfloat16)[None], passage_total.astype(jnp.bfloat16))


def solution(mesh):
    in_specs = (
        P("qgroup", "blk", None),
        P("blk", None),
        P("qgroup", None, "blk"),
        P("qgroup", "blk"),
        P("qgroup", "blk"),
    )
    out_specs = (P("qgroup", "blk"), P("qgroup", "blk", None), P("blk", "qgroup"))
    return jax.shard_map(
        per_device, mesh=mesh, in_specs=in_specs, out_specs=out_specs, check_vma=False
    )
```

profile of v0, /device:TPU:1, one launch (start us, length us, event | category | flops | bytes accessed | tf_op | source)
XLA Modules:
  0.0 347.7 jit_solution(5920273415184377773)
XLA Ops:
  7.2 0.0 copy-start
  7.2 0.0 all-gather.5.cloned.1.call-start
  7.2 0.7 all-gather.5.cloned.1.call-update
  7.9 0.0 reduce-scatter.2.cloned.1.call-start
  8.0 1.3 dynamic-slice
  9.9 0.8 bitcast_dynamic-update-slice_fusion
  10.7 0.7 bitcast_dynamic-update-slice_fusion.1
  11.4 20.5 %all-reduce.2 = (s32[256]{0:T(256)S(1)}, s32[256]{0:T(256)S(1)}) all-reduce(s32[256]{0:T(256)S(1)} %bitcast_dynamic-update-slice_fusion, s32[256]{0:T(256)S(1)} %bitcast_dynamic-update-slice_fusion.1), channel_id=4, replica_groups=mesh['blk'=32,'qgroup'=16] {'blk'}, use_global_device_ids=true, to_apply=%add.1 | all-reduce | flops 512 | bytes 4096
  31.9 1.9 gather_fusion
  33.8 0.1 copy.9
  34.0 0.1 select_reduce_fusion
  34.1 49.9 %all-gather.5.cloned.1.call-done = bf16[1,256,4096]{2,1,0:T(8,128)(2,1)} async-done(((bf16[1,8,4096]{2,1,0:T(8,128)(2,1)}), bf16[1,256,4096]{2,1,0:T(8,128)(2,1)}) %all-gather.5.cloned.1.call-update) | async-done | bytes 2097168 | tf_op jit(solution)/shard_map/all_gather | solution.py:11
  83.9 0.0 copy-done
  83.9 2.3 fusion.10
  86.3 52.6 %all-reduce.4 = (f32[256]{0:T(256)S(1)}, f32[256]{0:T(256)S(1)}) all-reduce(f32[256]{0:T(256)S(1)} %get-tuple-element.12, f32[256]{0:T(256)S(1)} %select_reduce_fusion), channel_id=1, replica_groups=mesh['blk'=32,'qgroup'=16] {'blk'}, use_global_device_ids=true, to_apply=%region_5.6 | all-reduce | flops 512 | bytes 4096 | tf_op jit(solution)/shard_map/pmax | solution.py:20
  138.9 0.1 exponential_reduce_fusion
  139.0 54.8 %all-reduce.3 = (f32[256]{0:T(256)S(1)}, f32[256]{0:T(256)S(1)}) all-reduce(f32[256]{0:T(256)S(1)} %get-tuple-element.14, f32[256]{0:T(256)S(1)} %get-tuple-element.15), channel_id=1, replica_groups=mesh['blk'=32,'qgroup'=16] {'blk'}, use_global_device_ids=true, to_apply=%region_7.8 | all-reduce | flops 512 | bytes 4096 | tf_op jit(solution)/shard_map/psum | solution.py:21
  193.8 0.2 fusion.6
  194.0 2.7 fusion.11
  196.6 0.0 reduce-scatter.2.cloned.1.call-update
  196.7 2.3 convolution_convert_fusion
  199.0 1.6 copy.13
  200.5 9.1 %all-to-all-start = ((bf16[256,16,256]{2,0,1:T(8,128)(2,1)}), bf16[256,16,256]{2,0,1:T(8,128)(2,1)}, u32[]{:S(2)}, u32[]{:S(2)}) async-start(bf16[256,16,256]{2,0,1:T(8,128)(2,1)} %bitcast.28), calls=%async_computation.1 | async-start | bytes 4194304 | tf_op jit(solution)/shard_map/all_to_all | solution.py:52
  209.6 94.9 %psum.23 = f32[256]{0:T(256)S(1)} all-reduce(f32[256]{0:T(256)S(1)} %sub.61), channel_id=1, replica_groups=mesh['blk'=32,'qgroup'=16] {'blk'}, use_global_device_ids=true, to_apply=%region_10.11 | all-reduce | flops 256 | bytes 2048 | tf_op jit(solution)/shard_map/psum | solution.py:38
  304.6 0.6 dynamic-slice_bitcast_fusion
  305.1 0.0 all-to-all-done
  305.2 2.6 reduce_sum.52
  307.7 31.6 %reduce-scatter.2.cloned.1.call-done = f32[8,4096]{1,0:T(8,128)} async-done(((f32[256,4096]{1,0:T(8,128)}), f32[8,4096]{1,0:T(8,128)}) %reduce-scatter.2.cloned.1.call-update) | async-done | bytes 131088 | tf_op jit(solution)/shard_map/reduce_scatter | solution.py:43
  339.3 1.5 convert_bitcast_fusion
  (9 shorter events, 0.0 us)
Async XLA Ops:
  7.2 76.8 %copy-start = (bf16[256,4096]{1,0:T(8,128)(2,1)S(1)}, bf16[256,4096]{1,0:T(8,128)(2,1)}, u32[]{:S(2)}) copy-start(bf16[256,4096]{1,0:T(8,128)(2,1)} %param.6) | copy-start | bytes 6291460
  7.2 76.7 %all-gather.5.cloned.1.call-start = ((), (), s32[]{:S(2)}) async-start(), calls=%async_computation.3 | async-start | bytes 2162688 | tf_op jit(solution)/shard_map/all_gather | solution.py:11
  7.9 331.4 %reduce-scatter.2.cloned.1.call-start = ((), (), s32[]{:S(2)}) async-start(), calls=%async_computation.2 | async-start | bytes 4325376 | tf_op jit(solution)/shard_map/reduce_scatter | solution.py:43
  200.5 104.6 %all-to-all-start = ((bf16[256,16,256]{2,0,1:T(8,128)(2,1)}), bf16[256,16,256]{2,0,1:T(8,128)(2,1)}, u32[]{:S(2)}, u32[]{:S(2)}) async-start(bf16[256,16,256]{2,0,1:T(8,128)(2,1)} %bitcast.28), calls=%async_computation.1 | async-start | bytes 4194304 | tf_op jit(solution)/shard_map/all_to_all | solution.py:52
Sparse Core Ops, SparseCore 0:
  10.2 73.7 all-gather.4
  196.8 142.5 reduce-scatter.1
where the time goes:
time: 351 us; the launch traced here: 348 us
  blocking collectives  223 us (64%)
  waiting for transfers between devices  82.2 us (23%)
  between operations  14.8 us (4%)
  starting transfers between devices  9.17 us (3%)
  matrix products  7.31 us (2%)
  local copies, waits for them, and re-layouts  6.97 us (2%)
  other arithmetic  4.51 us (1%)
    psum x1, blocking collectives, per_device(): loss_whole = lax.psum(loss_terms, 'blk')  94.9 us
    psum x1, blocking collectives, per_device(): lax.psum((jnp.sum(jnp.exp(scores - top_student[:, None]), axis=1), jnp.su...  54.8 us
    pmax x1, blocking collectives, per_device(): top_student, top_teacher = lax.pmax((local_student, local_teacher), 'blk')  52.6 us
    all_gather x1, waiting for transfers between devices, per_device(): group_query = lax.all_gather(queries[0], 'blk', axis=0, tiled=True)  49.9 us
    reduce_scatter x1, waiting for transfers between devices, per_device(): lax.psum_scatter(jnp.dot(score_grads, passages, preferred_element_type=jn...  31.6 us
    unnamed x1, blocking collectives  20.5 us
    all_to_all x1, starting transfers between devices, per_device(): lax.all_to_all(passage_term.astype(jnp.bfloat16), 'qgroup', split_axis=1,...  9.09 us
  transfers between devices with their start and end apart: 3, of which 2 were waited for; matrix products, arithmetic and copies ran while one was open for 3% of the time, Pallas kernels for 0%

commit v1 on v0

v1 whole, which is shorter than its diff:
```python
import jax
import jax.numpy as jnp
from jax import lax
from jax.sharding import Mesh, PartitionSpec as P

inv_temp = 50.0
YL, CORES, X = 2, 2, 4
LANES = 128
CHIPS = ("yl", "z")
f32, bf16 = jnp.float32, jnp.bfloat16


def swap_cores(value):
    return lax.ppermute(value, "core", [(0, 1), (1, 0)])


def per_device(queries, passages, teacher, teacher_rows, positives):
    own_rows, depth = queries.shape[1:]
    block_rows = passages.shape[0]
    chips = lax.axis_size("yl") * lax.axis_size("z")
    x_size, yh_size = lax.axis_size("x"), lax.axis_size("yh")
    rows = chips * own_rows
    chip = lax.axis_index("yl") * lax.axis_size("z") + lax.axis_index("z")
    core = lax.axis_index("core")

    indices = jnp.stack(
        [teacher_rows[0], positives[0] // 256, positives[0] % 256], axis=1
    ).astype(bf16)
    sent = jnp.concatenate(
        [queries[0], jnp.pad(indices, ((0, 0), (0, LANES - indices.shape[1])))], axis=1
    )
    passages_other = swap_cores(passages)
    teacher_other = swap_cores(teacher[0])
    gathered = lax.all_to_all(
        jnp.broadcast_to(sent[None], (chips,) + sent.shape), CHIPS, 0, 0, tiled=True
    ).reshape(rows, depth + LANES)
    query = gathered[:, :depth]
    query_other = swap_cores(query)
    codes = gathered[:, depth : depth + LANES].astype(f32).T
    row_index = codes[0:1].astype(jnp.int32)
    positive = codes[1:2].astype(jnp.int32) * 256 + codes[2:3].astype(jnp.int32)

    pick = (lax.broadcasted_iota(jnp.int32, (teacher.shape[1], rows), 0) == row_index).astype(f32)

    def columns(block, logits, which):
        scores = inv_temp * lax.dot_general(
            block, query, (((1,), (1,)), ((), ())), preferred_element_type=f32
        )
        picked = lax.dot_general(
            logits, pick, (((0,), (0,)), ((), ())),
            precision=lax.Precision.HIGHEST, preferred_element_type=f32,
        )
        place = (chip * CORES + which) * block_rows
        onehot = lax.broadcasted_iota(jnp.int32, (block_rows, rows), 0) + place == positive
        return scores, picked, onehot

    parts = [columns(passages, teacher[0], core), columns(passages_other, teacher_other, 1 - core)]
    top_student = jnp.maximum(*[jnp.max(s, axis=0, keepdims=True) for s, _, _ in parts])
    top_teacher = jnp.maximum(*[jnp.max(t, axis=0, keepdims=True) for _, t, _ in parts])
    sums = []
    for s, t, hot in parts:
        below_s, below_t = s - top_student, t - top_teacher
        weight = jnp.exp(below_t)
        sums.append(
            [
                jnp.sum(v, axis=0, keepdims=True)
                for v in (jnp.exp(below_s), weight, weight * (below_t - below_s), jnp.where(hot, s, 0.0))
            ]
        )
    sums = [a + b for a, b in zip(*sums)]
    stats = jnp.concatenate([top_student, top_teacher] + sums + [jnp.zeros((2, rows), f32)], axis=0)
    stats = lax.all_to_all(
        jnp.broadcast_to(stats[None], (chips,) + stats.shape), CHIPS, 0, 0, tiled=True
    )
    tops_s, tops_t, sums_s, sums_t, cross, hits = (stats[:, i] for i in range(6))
    top_s, top_t = jnp.max(tops_s, axis=0, keepdims=True), jnp.max(tops_t, axis=0, keepdims=True)
    lower_s, lower_t = tops_s - top_s, tops_t - top_t
    total_s = jnp.sum(jnp.exp(lower_s) * sums_s, axis=0, keepdims=True)
    weight_t = jnp.exp(lower_t)
    total_t = jnp.sum(weight_t * sums_t, axis=0, keepdims=True)
    cross = jnp.sum(weight_t * (cross + (lower_t - lower_s) * sums_t), axis=0, keepdims=True)
    hit = jnp.sum(hits, axis=0, keepdims=True)
    log_s = jnp.log(total_s)
    losses = cross / total_t - jnp.log(total_t) + log_s - (hit - top_s - log_s)
    loss = lax.dynamic_slice_in_dim(losses[0], chip * own_rows, own_rows)

    scale_s, scale_t = 2.0 * inv_temp / total_s, inv_temp / total_t
    grads, grads_other = (
        (jnp.exp(s - top_s) * scale_s - jnp.exp(t - top_t) * scale_t - jnp.where(hot, inv_temp, 0.0)).astype(bf16)
        for s, t, hot in parts
    )
    grads_back = swap_cores(grads_other)

    query_part = sum(
        lax.dot_general(a, b, (((0,), (0,)), ((), ())), preferred_element_type=f32)
        for a, b in ((grads, passages), (grads_other, passages_other))
    )
    query_parts = lax.all_to_all(
        query_part.astype(bf16).reshape(chips, own_rows, depth), CHIPS, 0, 0, tiled=True
    )
    query_total = jnp.sum(query_parts.astype(f32), axis=0)

    passage_part = jnp.dot(grads, query, preferred_element_type=f32) + jnp.dot(
        grads_back, query_other, preferred_element_type=f32
    )
    passage_part = passage_part.astype(bf16).reshape(block_rows, x_size, depth // x_size).transpose(1, 0, 2)
    passage_part = lax.all_to_all(passage_part, "x", 0, 0, tiled=True)
    passage_part = jnp.sum(passage_part.astype(f32), axis=0).astype(bf16)
    passage_part = passage_part.reshape(block_rows, yh_size, -1).transpose(1, 0, 2)
    passage_part = lax.all_to_all(passage_part, "yh", 0, 0, tiled=True)
    passage_total = jnp.sum(passage_part.astype(f32), axis=0)
    return loss[None], query_total.astype(bf16)[None], passage_total.astype(bf16)


def solution(mesh):
    blk, qgroup = mesh.devices.shape
    split = Mesh(
        mesh.devices.reshape(YL, blk // (YL * CORES), CORES, X, qgroup // X),
        ("yl", "z", "core", "x", "yh"),
    )
    blk, qgroup = ("yl", "z", "core"), ("x", "yh")
    in_specs = (
        P(qgroup, blk, None),
        P(blk, None),
        P(qgroup, None, blk),
        P(qgroup, blk),
        P(qgroup, blk),
    )
    out_specs = (P(qgroup, blk), P(qgroup, blk, None), P(blk, qgroup))
    return jax.shard_map(per_device, mesh=split, in_specs=in_specs, out_specs=out_specs, check_vma=False)
```

time: 351 us -> 159 us (0.45)
  the two profiles are of different devices: /device:TPU:1 before, /device:TPU:8 now
where the time goes in v1:
time: 159 us; the launch traced here: 158 us
  waiting for transfers between devices  86.9 us (55%)
  starting transfers between devices  42.2 us (27%)
  matrix products  13.2 us (8%)
  other arithmetic  7.72 us (5%)
  local copies, waits for them, and re-layouts  6.92 us (4%)
    all_to_all x1, waiting for transfers between devices, per_device(): passage_part = lax.all_to_all(passage_part, 'x', 0, 0, tiled=True)  23.7 us
    all_to_all x1, waiting for transfers between devices, per_device(): lax.all_to_all(query_part.astype(bf16).reshape(chips, own_rows, depth), C...  22.8 us
    all_to_all x1, waiting for transfers between devices, per_device(): lax.all_to_all(jnp.broadcast_to(sent[None], (chips,) + sent.shape), CHIPS...  22.2 us
    all_to_all x1, waiting for transfers between devices, per_device(): passage_part = lax.all_to_all(passage_part, 'yh', 0, 0, tiled=True)  14.1 us
    all_to_all x1, starting transfers between devices, per_device(): lax.all_to_all(jnp.broadcast_to(sent[None], (chips,) + sent.shape), CHIPS...  11.8 us
    ppermute x4, starting transfers between devices, swap_cores(): return lax.ppermute(value, 'core', [(0, 1), (1, 0)])  8.16 us
    all_to_all x1, starting transfers between devices, per_device(): lax.all_to_all(jnp.broadcast_to(stats[None], (chips,) + stats.shape), CHI...  6.53 us
    all_to_all x1, starting transfers between devices, per_device(): passage_part = lax.all_to_all(passage_part, 'yh', 0, 0, tiled=True)  6.2 us
  transfers between devices with their start and end apart: 9, of which 5 were waited for; matrix products, arithmetic and copies ran while one was open for 10% of the time, Pallas kernels for 0%

profile of v1, /device:TPU:8, one launch (start us, length us, event | category | flops | bytes accessed | tf_op | source)
XLA Modules:
  0.0 157.9 jit_solution(3875441892544207678)
XLA Ops:
  0.6 0.0 copy-start
  0.6 0.8 fusion.30
  1.5 0.7 convert_bitcast_fusion.1
  2.1 0.1 copy.62
  2.2 0.8 fusion.22
  3.1 1.1 broadcast_in_dim.17
  4.1 11.8 %all-to-all-start = ((bf16[16,8,4224]{2,1,0:T(8,128)(2,1)}), bf16[16,8,4224]{2,1,0:T(8,128)(2,1)S(1)}, u32[]{:S(2)}, u32[]{:S(2)}) async-start(bf16[16,8,4224]{2,1,0:T(8,128)(2,1)} %broadcast_in_dim.17), calls=%async_computation | async-start | bytes 2162688 | tf_op jit(solution)/shard_map/all_to_all | solution.py:34
  15.9 0.0 copy-done
  15.9 1.9 %collective-permute-start = (bf16[256,4096]{1,0:T(8,128)(2,1)S(1)}, bf16[256,4096]{1,0:T(8,128)(2,1)}, u32[]{:S(2)}, u32[]{:S(2)}) collective-permute-start(bf16[256,4096]{1,0:T(8,128)(2,1)S(1)} %copy-done), channel_id=1, source_target_pairs={{0,16},{16,0},{1,17},{17,1},{2,18},{18,2},{3,19},{19,3},{4,20},{20... | collective-permute-start | bytes 6291464 | tf_op jit(solution)/shard_map/ppermute | solution.py:14
  17.9 2.4 %collective-permute-start.1 = (f32[256,256]{1,0:T(8,128)}, f32[256,256]{1,0:T(8,128)}, u32[]{:S(2)}, u32[]{:S(2)}) collective-permute-start(f32[256,256]{1,0:T(8,128)} %bitcast.6), channel_id=1, source_target_pairs={{0,16},{16,0},{1,17},{17,1},{2,18},{18,2},{3,19},{19,3},{4,20},{20... | collective-permute-start | bytes 786440 | tf_op jit(solution)/shard_map/ppermute | solution.py:14
  20.3 0.0 copy-start.9
  20.3 0.0 copy-start.11
  20.3 22.2 %all-to-all-done = bf16[16,8,4224]{2,1,0:T(8,128)(2,1)S(1)} async-done(((bf16[16,8,4224]{2,1,0:T(8,128)(2,1)}), bf16[16,8,4224]{2,1,0:T(8,128)(2,1)S(1)}, u32[]{:S(2)}, u32[]{:S(2)}) %all-to-all-start) | async-done | bytes 1081376 | tf_op jit(solution)/shard_map/all_to_all | solution.py:34
  42.6 0.2 fusion.24
  42.7 0.0 copy-start.5
  42.8 1.3 fusion.42
  44.1 0.0 collective-permute-done.1
  44.1 1.3 fusion.43
  45.4 0.0 copy-start.1
  45.4 0.9 fusion.40
  46.3 0.0 collective-permute-done
  46.3 2.5 %fusion.41 = (f32[128]{0:T(128)S(1)}, f32[128,256]{1,0:T(8,128)S(1)}) fusion(bf16[256,4096]{1,0:T(8,128)(2,1)} %collective-permute-done, bf16[128,4224]{1,0:T(8,128)(2,1)S(1)} %bitcast.139), kind=kOutput, calls=%fused_computation.87 | convolution fusion | flops 268500864 | bytes 3277312 | tf_op jit(solution)/shard_map/dot_general | solution.py:46
  48.8 0.0 copy-start.2
  48.9 0.0 copy-done.9
  48.9 0.0 copy-done.11
  48.9 0.0 copy-done.5
  48.9 0.0 copy-done.1
  48.9 0.4 fusion.13
  49.3 0.2 copy-done.2
  49.5 0.6 broadcast_in_dim.20
  50.2 6.5 %all-to-all-start.1 = ((f32[16,8,128]{2,1,0:T(8,128)}), f32[16,8,128]{2,1,0:T(8,128)S(1)}, u32[]{:S(2)}, u32[]{:S(2)}) async-start(f32[16,8,128]{2,1,0:T(8,128)} %broadcast_in_dim.20), calls=%async_computation.1 | async-start | bytes 131072 | tf_op jit(solution)/shard_map/all_to_all | solution.py:72
  56.7 1.1 slice.44
  57.8 1.9 %collective-permute-start.3 = (bf16[128,4096]{1,0:T(8,128)(2,1)}, bf16[128,4096]{1,0:T(8,128)(2,1)}, u32[]{:S(2)}, u32[]{:S(2)}) collective-permute-start(bf16[128,4096]{1,0:T(8,128)(2,1)} %slice.44), channel_id=1, source_target_pairs={{0,16},{16,0},{1,17},{17,1},{2,18},{18,2},{3,19},{19,3},{4,20},{20... | collective-permute-start | bytes 3145736 | tf_op jit(solution)/shard_map/ppermute | solution.py:14
  59.7 4.2 %all-to-all-done.1 = f32[16,8,128]{2,1,0:T(8,128)S(1)} async-done(((f32[16,8,128]{2,1,0:T(8,128)}), f32[16,8,128]{2,1,0:T(8,128)S(1)}, u32[]{:S(2)}, u32[]{:S(2)}) %all-to-all-start.1) | async-done | bytes 65568 | tf_op jit(solution)/shard_map/all_to_all | solution.py:72
  64.0 0.0 copy-start.3
  64.0 0.0 copy-start.7
  64.1 0.4 copy-done.3
  64.5 0.0 copy-done.7
  64.5 1.1 fusion.9
  65.7 1.9 %collective-permute-start.2 = (bf16[256,128]{0,1:T(8,128)(2,1)S(1)}, bf16[256,128]{0,1:T(8,128)(2,1)S(1)}, u32[]{:S(2)}, u32[]{:S(2)}) collective-permute-start(bf16[256,128]{0,1:T(8,128)(2,1)S(1)} %fusion.9), channel_id=1, source_target_pairs={{0,16},{16,0},{1,17},{17,1},{2,18},{18,2},{3,19},{19,3},{4,20},{20... | collective-permute-start | bytes 196616 | tf_op jit(solution)/shard_map/ppermute | solution.py:14
  67.6 1.5 fusion.32
  69.1 0.0 collective-permute-done.2
  69.1 0.0 collective-permute-done.3
  69.2 2.0 %fusion = bf16[256,4096]{1,0:T(8,128)(2,1)S(1)} fusion(f32[256,4096]{1,0:T(8,128)S(1)} %fusion.32, bf16[256,128]{0,1:T(8,128)(2,1)S(1)} %collective-permute-done.2, bf16[128,4096]{1,0:T(8,128)(2,1)} %collective-permute-done.3), kind=kOutput, calls=%fused_computation.1 | convolution fusion | flops 270532608 | bytes 7405568 | tf_op jit(solution)/shard_map/dot_general | solution.py:103
  71.1 1.5 copy.65
  72.6 0.0 copy-start.4
  72.6 4.6 %all-to-all-start.3 = ((bf16[4,256,1024]{2,1,0:T(8,128)(2,1)}), bf16[4,256,1024]{2,1,0:T(8,128)(2,1)}, u32[]{:S(2)}, u32[]{:S(2)}) async-start(bf16[4,256,1024]{2,1,0:T(8,128)(2,1)} %bitcast.143), calls=%async_computation.3 | async-start | bytes 4194304 | tf_op jit(solution)/shard_map/all_to_all | solution.py:107
  77.2 0.0 copy-done.4
  77.3 0.0 copy-done.6
  77.3 0.0 copy-done.8
  77.3 0.0 copy-done.10
  77.3 0.5 fusion.34
  77.8 3.1 %fusion.2 = bf16[16,8,4096]{2,1,0:T(8,128)(2,1)} fusion(f32[128,4096]{1,0:T(8,128)S(1)} %fusion.34, bf16[256,128]{0,1:T(8,128)(2,1)S(1)} %fusion.9, bf16[256,4096]{1,0:T(8,128)(2,1)} %collective-permute-done), kind=kOutput, calls=%fused_computation.4 | convolution fusion | flops 269484032 | bytes 5308416 | tf_op jit(solution)/shard_map/dot_general | solution.py:95
  80.9 23.7 %all-to-all-done.3 = bf16[4,256,1024]{2,1,0:T(8,128)(2,1)} async-done(((bf16[4,256,1024]{2,1,0:T(8,128)(2,1)}), bf16[4,256,1024]{2,1,0:T(8,128)(2,1)}, u32[]{:S(2)}, u32[]{:S(2)}) %all-to-all-start.3) | async-done | bytes 2097184 | tf_op jit(solution)/shard_map/all_to_all | solution.py:107
  104.6 4.9 %all-to-all-start.2 = ((bf16[16,8,4096]{2,1,0:T(8,128)(2,1)}), bf16[16,8,4096]{2,1,0:T(8,128)(2,1)S(1)}, u32[]{:S(2)}, u32[]{:S(2)}) async-start(bf16[16,8,4096]{2,1,0:T(8,128)(2,1)} %fusion.2), calls=%async_computation.2 | async-start | bytes 2097152 | tf_op jit(solution)/shard_map/all_to_all | solution.py:98
  109.5 2.0 %reduce_sum.157 = bf16[256,1024]{1,0:T(8,128)(2,1)S(1)} reduce(bf16[4,256,1024]{2,1,0:T(8,128)(2,1)} %all-to-all-done.3, bf16[]{:T(256)} %constant.57.clone.1), dimensions={0}, to_apply=%region_19.20 | reduce | flops 786432 | bytes 2621442 | tf_op jit(solution)/shard_map/reduce_sum | solution.py:108
  111.5 0.2 copy.56
  111.7 1.0 copy.57
  112.7 22.8 %all-to-all-done.2 = bf16[16,8,4096]{2,1,0:T(8,128)(2,1)S(1)} async-done(((bf16[16,8,4096]{2,1,0:T(8,128)(2,1)}), bf16[16,8,4096]{2,1,0:T(8,128)(2,1)S(1)}, u32[]{:S(2)}, u32[]{:S(2)}) %all-to-all-start.2) | async-done | bytes 1048608 | tf_op jit(solution)/shard_map/all_to_all | solution.py:98
  135.5 6.2 %all-to-all-start.4 = ((bf16[4,256,256]{2,1,0:T(8,128)(2,1)}), bf16[4,256,256]{2,1,0:T(8,128)(2,1)S(1)}, u32[]{:S(2)}, u32[]{:S(2)}) async-start(bf16[4,256,256]{2,1,0:T(8,128)(2,1)} %copy.57), calls=%async_computation.4 | async-start | bytes 1048576 | tf_op jit(solution)/shard_map/all_to_all | solution.py:110
  141.7 0.6 dynamic-slice_bitcast_fusion
  142.3 0.8 reduce_sum.156
  143.1 14.1 %all-to-all-done.4 = bf16[4,256,256]{2,1,0:T(8,128)(2,1)S(1)} async-done(((bf16[4,256,256]{2,1,0:T(8,128)(2,1)}), bf16[4,256,256]{2,1,0:T(8,128)(2,1)S(1)}, u32[]{:S(2)}, u32[]{:S(2)}) %all-to-all-start.4) | async-done | bytes 524320 | tf_op jit(solution)/shard_map/all_to_all | solution.py:110
  157.1 0.7 reduce_sum.158
  (19 shorter events, 0.2 us)
Async XLA Ops:
  0.6 15.3 %copy-start = (bf16[256,4096]{1,0:T(8,128)(2,1)S(1)}, bf16[256,4096]{1,0:T(8,128)(2,1)}, u32[]{:S(2)}) copy-start(bf16[256,4096]{1,0:T(8,128)(2,1)} %param.6) | copy-start | bytes 6291460
  4.1 38.4 %all-to-all-start = ((bf16[16,8,4224]{2,1,0:T(8,128)(2,1)}), bf16[16,8,4224]{2,1,0:T(8,128)(2,1)S(1)}, u32[]{:S(2)}, u32[]{:S(2)}) async-start(bf16[16,8,4224]{2,1,0:T(8,128)(2,1)} %broadcast_in_dim.17), calls=%async_computation | async-start | bytes 2162688 | tf_op jit(solution)/shard_map/all_to_all | solution.py:34
  15.9 30.4 %collective-permute-start = (bf16[256,4096]{1,0:T(8,128)(2,1)S(1)}, bf16[256,4096]{1,0:T(8,128)(2,1)}, u32[]{:S(2)}, u32[]{:S(2)}) collective-permute-start(bf16[256,4096]{1,0:T(8,128)(2,1)S(1)} %copy-done), channel_id=1, source_target_pairs={{0,16},{16,0},{1,17},{17,1},{2,18},{18,2},{3,19},{19,3},{4,20},{20... | collective-permute-start | bytes 6291464 | tf_op jit(solution)/shard_map/ppermute | solution.py:14
  17.9 26.2 %collective-permute-start.1 = (f32[256,256]{1,0:T(8,128)}, f32[256,256]{1,0:T(8,128)}, u32[]{:S(2)}, u32[]{:S(2)}) collective-permute-start(f32[256,256]{1,0:T(8,128)} %bitcast.6), channel_id=1, source_target_pairs={{0,16},{16,0},{1,17},{17,1},{2,18},{18,2},{3,19},{19,3},{4,20},{20... | collective-permute-start | bytes 786440 | tf_op jit(solution)/shard_map/ppermute | solution.py:14
  20.3 28.5 %copy-start.9 = (s32[256]{0:T(256)}, s32[256]{0:T(256)S(1)}, u32[]{:S(2)}) copy-start(s32[256]{0:T(256)S(1)} %iota_add_fusion.1) | copy-start | bytes 3076
  20.3 28.5 %copy-start.11 = (s32[256]{0:T(256)}, s32[256]{0:T(256)S(1)}, u32[]{:S(2)}) copy-start(s32[256]{0:T(256)S(1)} %iota_add_fusion) | copy-start | bytes 3076
  42.7 6.1 %copy-start.5 = (s32[128]{0:T(128)}, s32[128]{0:T(128)S(1)}, u32[]{:S(2)}) copy-start(s32[128]{0:T(128)S(1)} %get-tuple-element.11) | copy-start | bytes 1540
  45.4 3.5 %copy-start.1 = (f32[128,256]{1,0:T(8,128)}, f32[128,256]{1,0:T(8,128)S(1)}, u32[]{:S(2)}) copy-start(f32[128,256]{1,0:T(8,128)S(1)} %get-tuple-element.38) | copy-start | bytes 393220
  48.8 0.7 copy-start.2
  50.2 13.7 %all-to-all-start.1 = ((f32[16,8,128]{2,1,0:T(8,128)}), f32[16,8,128]{2,1,0:T(8,128)S(1)}, u32[]{:S(2)}, u32[]{:S(2)}) async-start(f32[16,8,128]{2,1,0:T(8,128)} %broadcast_in_dim.20), calls=%async_computation.1 | async-start | bytes 131072 | tf_op jit(solution)/shard_map/all_to_all | solution.py:72
  57.8 11.3 %collective-permute-start.3 = (bf16[128,4096]{1,0:T(8,128)(2,1)}, bf16[128,4096]{1,0:T(8,128)(2,1)}, u32[]{:S(2)}, u32[]{:S(2)}) collective-permute-start(bf16[128,4096]{1,0:T(8,128)(2,1)} %slice.44), channel_id=1, source_target_pairs={{0,16},{16,0},{1,17},{17,1},{2,18},{18,2},{3,19},{19,3},{4,20},{20... | collective-permute-start | bytes 3145736 | tf_op jit(solution)/shard_map/ppermute | solution.py:14
  64.0 0.5 copy-start.3
  64.0 0.5 copy-start.7
  65.7 3.5 %collective-permute-start.2 = (bf16[256,128]{0,1:T(8,128)(2,1)S(1)}, bf16[256,128]{0,1:T(8,128)(2,1)S(1)}, u32[]{:S(2)}, u32[]{:S(2)}) collective-permute-start(bf16[256,128]{0,1:T(8,128)(2,1)S(1)} %fusion.9), channel_id=1, source_target_pairs={{0,16},{16,0},{1,17},{17,1},{2,18},{18,2},{3,19},{19,3},{4,20},{20... | collective-permute-start | bytes 196616 | tf_op jit(solution)/shard_map/ppermute | solution.py:14
  72.6 4.6 %copy-start.4 = (f32[128]{0:T(128)S(1)}, f32[128]{0:T(128)}, u32[]{:S(2)}) copy-start(f32[128]{0:T(128)} %copy-done.3) | copy-start | bytes 1540
  72.6 4.6 %copy-start.6 = (s32[128]{0:T(128)S(1)}, s32[128]{0:T(128)}, u32[]{:S(2)}) copy-start(s32[128]{0:T(128)} %copy-done.5) | copy-start | bytes 1540
  72.6 4.6 %copy-start.8 = (f32[128]{0:T(128)S(1)}, f32[128]{0:T(128)}, u32[]{:S(2)}) copy-start(f32[128]{0:T(128)} %copy-done.7) | copy-start | bytes 1540
  72.6 4.6 %copy-start.10 = (s32[256]{0:T(256)S(1)}, s32[256]{0:T(256)}, u32[]{:S(2)}) copy-start(s32[256]{0:T(256)} %copy-done.9) | copy-start | bytes 3076
  72.6 31.9 %all-to-all-start.3 = ((bf16[4,256,1024]{2,1,0:T(8,128)(2,1)}), bf16[4,256,1024]{2,1,0:T(8,128)(2,1)}, u32[]{:S(2)}, u32[]{:S(2)}) async-start(bf16[4,256,1024]{2,1,0:T(8,128)(2,1)} %bitcast.143), calls=%async_computation.3 | async-start | bytes 4194304 | tf_op jit(solution)/shard_map/all_to_all | solution.py:107
  104.6 30.9 %all-to-all-start.2 = ((bf16[16,8,4096]{2,1,0:T(8,128)(2,1)}), bf16[16,8,4096]{2,1,0:T(8,128)(2,1)S(1)}, u32[]{:S(2)}, u32[]{:S(2)}) async-start(bf16[16,8,4096]{2,1,0:T(8,128)(2,1)} %fusion.2), calls=%async_computation.2 | async-start | bytes 2097152 | tf_op jit(solution)/shard_map/all_to_all | solution.py:98
  135.5 21.6 %all-to-all-start.4 = ((bf16[4,256,256]{2,1,0:T(8,128)(2,1)}), bf16[4,256,256]{2,1,0:T(8,128)(2,1)S(1)}, u32[]{:S(2)}, u32[]{:S(2)}) async-start(bf16[4,256,256]{2,1,0:T(8,128)(2,1)} %copy.57), calls=%async_computation.4 | async-start | bytes 1048576 | tf_op jit(solution)/shard_map/all_to_all | solution.py:110

commit v2 on v1

--- a/solution.py
+++ b/solution.py
@@ -14,6 +14,18 @@
     return lax.ppermute(value, "core", [(0, 1), (1, 0)])
 
 
+def shift(value, axis, by):
+    if by == 0:
+        return value
+    size = lax.axis_size(axis)
+    return lax.ppermute(value, axis, [(i, (i + by) % size) for i in range(size)])
+
+
+def column_slice(value, axis, which, count):
+    width = value.shape[axis] // count
+    return lax.dynamic_slice_in_dim(value, which % count * width, width, axis)
+
+
 def per_device(queries, passages, teacher, teacher_rows, positives):
     own_rows, depth = queries.shape[1:]
     block_rows = passages.shape[0]
@@ -21,7 +33,7 @@
     x_size, yh_size = lax.axis_size("x"), lax.axis_size("yh")
     rows = chips * own_rows
     chip = lax.axis_index("yl") * lax.axis_size("z") + lax.axis_index("z")
-    core = lax.axis_index("core")
+    core, x, yh = lax.axis_index("core"), lax.axis_index("x"), lax.axis_index("yh")
 
     indices = jnp.stack(
         [teacher_rows[0], positives[0] // 256, positives[0] % 256], axis=1
@@ -35,7 +47,8 @@
         jnp.broadcast_to(sent[None], (chips,) + sent.shape), CHIPS, 0, 0, tiled=True
     ).reshape(rows, depth + LANES)
     query = gathered[:, :depth]
-    query_other = swap_cores(query)
+    queries_x = [column_slice(query, 1, x + d, x_size) for d in range(x_size)]
+    queries_x = [shift(v, "x", d) for d, v in enumerate(queries_x)]
     codes = gathered[:, depth : depth + LANES].astype(f32).T
     row_index = codes[0:1].astype(jnp.int32)
     positive = codes[1:2].astype(jnp.int32) * 256 + codes[2:3].astype(jnp.int32)
@@ -89,7 +102,7 @@
         (jnp.exp(s - top_s) * scale_s - jnp.exp(t - top_t) * scale_t - jnp.where(hot, inv_temp, 0.0)).astype(bf16)
         for s, t, hot in parts
     )
-    grads_back = swap_cores(grads_other)
+    grads_x = [shift(jnp.concatenate([grads, grads_other]), "x", d) for d in range(x_size)]
 
     query_part = sum(
         lax.dot_general(a, b, (((0,), (0,)), ((), ())), preferred_element_type=f32)
@@ -100,15 +113,12 @@
     )
     query_total = jnp.sum(query_parts.astype(f32), axis=0)
 
-    passage_part = jnp.dot(grads, query, preferred_element_type=f32) + jnp.dot(
-        grads_back, query_other, preferred_element_type=f32
-    )
-    passage_part = passage_part.astype(bf16).reshape(block_rows, x_size, depth // x_size).transpose(1, 0, 2)
-    passage_part = lax.all_to_all(passage_part, "x", 0, 0, tiled=True)
-    passage_part = jnp.sum(passage_part.astype(f32), axis=0).astype(bf16)
-    passage_part = passage_part.reshape(block_rows, yh_size, -1).transpose(1, 0, 2)
-    passage_part = lax.all_to_all(passage_part, "yh", 0, 0, tiled=True)
-    passage_total = jnp.sum(passage_part.astype(f32), axis=0)
+    grads_x, queries_x = jnp.concatenate(grads_x, axis=1), jnp.concatenate(queries_x)
+    part_other = jnp.dot(grads_x[block_rows:], queries_x, preferred_element_type=f32).astype(bf16)
+    part = jnp.dot(grads_x[:block_rows], queries_x, preferred_element_type=f32)
+    part = (part + swap_cores(part_other).astype(f32)).astype(bf16)
+    parts = [shift(column_slice(part, 1, yh + d, yh_size), "yh", d) for d in range(yh_size)]
+    passage_total = sum(v.astype(f32) for v in parts)
     return loss[None], query_total.astype(bf16)[None], passage_total.astype(bf16)
 
 

time: 159 us -> 133 us (0.84)
  the two profiles are of different devices: /device:TPU:8 before, /device:TPU:1 now
where the time goes in v2:
time: 133 us; the launch traced here: 131 us
  starting transfers between devices  64.9 us (49%)
  waiting for transfers between devices  43.2 us (32%)
  matrix products  11.6 us (9%)
  other arithmetic  5.75 us (4%)
  local copies, waits for them, and re-layouts  4.64 us (3%)
    ppermute x9, starting transfers between devices, shift(): lax.ppermute(value, axis, [(i, (i + by) % size) for i in range(size)])  33.5 us
    all_to_all x1, waiting for transfers between devices, per_device(): lax.all_to_all(jnp.broadcast_to(sent[None], (chips,) + sent.shape), CHIPS...  21.2 us
    ppermute x9, waiting for transfers between devices, shift(): lax.ppermute(value, axis, [(i, (i + by) % size) for i in range(size)])  14.3 us
    all_to_all x1, starting transfers between devices, per_device(): lax.all_to_all(jnp.broadcast_to(sent[None], (chips,) + sent.shape), CHIPS...  12 us
    ppermute x3, starting transfers between devices, swap_cores(): return lax.ppermute(value, 'core', [(0, 1), (1, 0)])  8.34 us
    all_to_all x1, starting transfers between devices, per_device(): lax.all_to_all(jnp.broadcast_to(stats[None], (chips,) + stats.shape), CHI...  7.26 us
    all_to_all x1, waiting for transfers between devices, per_device(): lax.all_to_all(jnp.broadcast_to(stats[None], (chips,) + stats.shape), CHI...  6.23 us
    all_to_all x1, starting transfers between devices, per_device(): lax.all_to_all(query_part.astype(bf16).reshape(chips, own_rows, depth), C...  3.78 us
  transfers between devices with their start and end apart: 15, of which 6 were waited for; matrix products, arithmetic and copies ran while one was open for 6% of the time, Pallas kernels for 0%

profile of v2, /device:TPU:1, one launch (start us, length us, event | category | flops | bytes accessed | tf_op | source)
XLA Modules:
  0.0 131.2 jit_solution(5290278528871112040)
XLA Ops:
  0.6 0.0 copy-start
  0.6 0.8 convert_bitcast_fusion.1
  1.4 0.7 fusion.32
  2.1 0.1 copy.35
  2.2 0.8 fusion.24
  3.1 1.1 broadcast_in_dim.17
  4.1 12.0 %all-to-all-start = ((bf16[16,8,4224]{2,1,0:T(8,128)(2,1)}), bf16[16,8,4224]{2,1,0:T(8,128)(2,1)S(1)}, u32[]{:S(2)}, u32[]{:S(2)}) async-start(bf16[16,8,4224]{2,1,0:T(8,128)(2,1)} %broadcast_in_dim.17), calls=%async_computation | async-start | bytes 2162688 | tf_op jit(solution)/shard_map/all_to_all | solution.py:46
  16.1 0.0 copy-done
  16.1 2.9 %collective-permute-start = (bf16[256,4096]{1,0:T(8,128)(2,1)S(1)}, bf16[256,4096]{1,0:T(8,128)(2,1)}, u32[]{:S(2)}, u32[]{:S(2)}) collective-permute-start(bf16[256,4096]{1,0:T(8,128)(2,1)S(1)} %copy-done), channel_id=1, source_target_pairs={{0,16},{16,0},{1,17},{17,1},{2,18},{18,2},{3,19},{19,3},{4,20},{20... | collective-permute-start | bytes 6291464 | tf_op jit(solution)/shard_map/ppermute | solution.py:14
  19.0 1.9 %collective-permute-start.1 = (f32[256,256]{1,0:T(8,128)}, f32[256,256]{1,0:T(8,128)}, u32[]{:S(2)}, u32[]{:S(2)}) collective-permute-start(f32[256,256]{1,0:T(8,128)} %bitcast.6), channel_id=1, source_target_pairs={{0,16},{16,0},{1,17},{17,1},{2,18},{18,2},{3,19},{19,3},{4,20},{20... | collective-permute-start | bytes 786440 | tf_op jit(solution)/shard_map/ppermute | solution.py:14
  21.0 21.2 %all-to-all-done = bf16[16,8,4224]{2,1,0:T(8,128)(2,1)S(1)} async-done(((bf16[16,8,4224]{2,1,0:T(8,128)(2,1)}), bf16[16,8,4224]{2,1,0:T(8,128)(2,1)S(1)}, u32[]{:S(2)}, u32[]{:S(2)}) %all-to-all-start) | async-done | bytes 1081376 | tf_op jit(solution)/shard_map/all_to_all | solution.py:46
  42.2 0.2 fusion.26
  42.4 1.3 %fusion.41 = (f32[128]{0:T(128)S(1)}, f32[128,256]{1,0:T(8,128)S(1)}) fusion(f32[1,256,256]{2,1,0:T(8,128)} %param.7, s32[128]{0:T(128)S(1)} %get-tuple-element.12), kind=kOutput, calls=%fused_computation.100 | convolution fusion | flops 100728704 | bytes 394240 | tf_op jit(solution)/shard_map/dot_general | solution.py:62
  43.7 0.0 collective-permute-done.1
  43.7 1.3 %fusion.42 = (f32[128]{0:T(128)S(1)}, f32[128,256]{1,0:T(8,128)S(1)}) fusion(f32[256,256]{1,0:T(8,128)} %collective-permute-done.1, s32[128]{0:T(128)S(1)} %get-tuple-element.12), kind=kOutput, calls=%fused_computation.101 | convolution fusion | flops 100728704 | bytes 394240 | tf_op jit(solution)/shard_map/dot_general | solution.py:62
  45.1 0.9 fusion.39
  46.0 0.0 copy-start.2
  46.0 0.0 collective-permute-done
  46.0 2.6 %fusion.40 = (f32[128]{0:T(128)S(1)}, f32[128,256]{1,0:T(8,128)S(1)}) fusion(bf16[256,4096]{1,0:T(8,128)(2,1)} %collective-permute-done, bf16[128,4224]{1,0:T(8,128)(2,1)S(1)} %bitcast.124), kind=kOutput, calls=%fused_computation.99 | convolution fusion | flops 268500864 | bytes 3277312 | tf_op jit(solution)/shard_map/dot_general | solution.py:59
  48.6 0.0 copy-start.3
  48.6 0.0 copy-done.2
  48.6 0.4 fusion.15
  49.0 0.2 copy-done.3
  49.3 0.6 broadcast_in_dim.20
  49.9 7.3 %all-to-all-start.1 = ((f32[16,8,128]{2,1,0:T(8,128)}), f32[16,8,128]{2,1,0:T(8,128)S(1)}, u32[]{:S(2)}, u32[]{:S(2)}) async-start(f32[16,8,128]{2,1,0:T(8,128)} %broadcast_in_dim.20), calls=%async_computation.1 | async-start | bytes 131072 | tf_op jit(solution)/shard_map/all_to_all | solution.py:85
  57.2 1.1 slice.52
  58.3 6.2 %all-to-all-done.1 = f32[16,8,128]{2,1,0:T(8,128)S(1)} async-done(((f32[16,8,128]{2,1,0:T(8,128)}), f32[16,8,128]{2,1,0:T(8,128)S(1)}, u32[]{:S(2)}, u32[]{:S(2)}) %all-to-all-start.1) | async-done | bytes 65568 | tf_op jit(solution)/shard_map/all_to_all | solution.py:85
  64.7 1.2 fusion.11
  65.9 0.5 fusion.43
  66.3 3.1 %fusion.1 = bf16[16,8,4096]{2,1,0:T(8,128)(2,1)} fusion(f32[128,4096]{1,0:T(8,128)S(1)} %fusion.43, bf16[256,128]{0,1:T(8,128)(2,1)S(1)} %get-tuple-element.33, bf16[256,4096]{1,0:T(8,128)(2,1)} %collective-permute-done), kind=kOutput, calls=%fused_computation.2 | convolution fusion | flops 269484032 | bytes 5308416 | tf_op jit(solution)/shard_map/dot_general | solution.py:108
  69.4 0.0 copy-start.1
  69.4 3.8 %all-to-all-start.2 = ((bf16[16,8,4096]{2,1,0:T(8,128)(2,1)}), bf16[16,8,4096]{2,1,0:T(8,128)(2,1)S(1)}, u32[]{:S(2)}, u32[]{:S(2)}) async-start(bf16[16,8,4096]{2,1,0:T(8,128)(2,1)} %fusion.1), calls=%async_computation.2 | async-start | bytes 2097152 | tf_op jit(solution)/shard_map/all_to_all | solution.py:111
  73.2 4.4 %collective-permute-start.4 = (bf16[512,128]{0,1:T(8,128)(2,1)S(1)}, bf16[512,128]{0,1:T(8,128)(2,1)S(1)}, u32[]{:S(2)}, u32[]{:S(2)}) collective-permute-start(bf16[512,128]{0,1:T(8,128)(2,1)S(1)} %pad_maximum_fusion.4), channel_id=1, source_target_pairs={{0,12},{4,0},{8,4},{12,8},{1,13},{5,1},{9,5},{13,9},{2,14},{6,2},{... | collective-permute-start | bytes 393224 | tf_op jit(solution)/shard_map/ppermute | solution.py:21
  77.6 0.0 copy-done.1
  77.6 0.1 constant_dynamic-slice_fusion.6
  77.7 1.9 %collective-permute-start.5 = (bf16[128,1024]{1,0:T(8,128)(2,1)S(1)}, bf16[128,1024]{1,0:T(8,128)(2,1)S(1)}, u32[]{:S(2)}, u32[]{:S(2)}) collective-permute-start(bf16[128,1024]{1,0:T(8,128)(2,1)S(1)} %get-tuple-element.21), channel_id=1, source_target_pairs={{0,4},{4,8},{8,12},{12,0},{1,5},{5,9},{9,13},{13,1},{2,6},{6,10},{... | collective-permute-start | bytes 786440 | tf_op jit(solution)/shard_map/ppermute | solution.py:21
  79.7 4.6 %collective-permute-start.7 = (bf16[128,1024]{1,0:T(8,128)(2,1)S(1)}, bf16[128,1024]{1,0:T(8,128)(2,1)S(1)}, u32[]{:S(2)}, u32[]{:S(2)}) collective-permute-start(bf16[128,1024]{1,0:T(8,128)(2,1)S(1)} %get-tuple-element.22), channel_id=1, source_target_pairs={{0,12},{4,0},{8,4},{12,8},{1,13},{5,1},{9,5},{13,9},{2,14},{6,2},{... | collective-permute-start | bytes 786440 | tf_op jit(solution)/shard_map/ppermute | solution.py:21
  84.2 1.9 %collective-permute-start.6 = (bf16[128,1024]{1,0:T(8,128)(2,1)S(1)}, bf16[128,1024]{1,0:T(8,128)(2,1)S(1)}, u32[]{:S(2)}, u32[]{:S(2)}) collective-permute-start(bf16[128,1024]{1,0:T(8,128)(2,1)S(1)} %get-tuple-element.23), channel_id=1, source_target_pairs={{0,8},{4,12},{8,0},{12,4},{1,9},{5,13},{9,1},{13,5},{2,10},{6,14},... | collective-permute-start | bytes 786440 | tf_op jit(solution)/shard_map/ppermute | solution.py:21
  86.2 4.9 %collective-permute-start.3 = (bf16[512,128]{0,1:T(8,128)(2,1)S(1)}, bf16[512,128]{0,1:T(8,128)(2,1)S(1)}, u32[]{:S(2)}, u32[]{:S(2)}) collective-permute-start(bf16[512,128]{0,1:T(8,128)(2,1)S(1)} %pad_maximum_fusion.4), channel_id=1, source_target_pairs={{0,8},{4,12},{8,0},{12,4},{1,9},{5,13},{9,1},{13,5},{2,10},{6,14},... | collective-permute-start | bytes 393224 | tf_op jit(solution)/shard_map/ppermute | solution.py:21
  91.0 0.0 collective-permute-done.4
  91.0 1.9 %collective-permute-start.2 = (bf16[512,128]{0,1:T(8,128)(2,1)S(1)}, bf16[512,128]{0,1:T(8,128)(2,1)S(1)}, u32[]{:S(2)}, u32[]{:S(2)}) collective-permute-start(bf16[512,128]{0,1:T(8,128)(2,1)S(1)} %pad_maximum_fusion.4), channel_id=1, source_target_pairs={{0,4},{4,8},{8,12},{12,0},{1,5},{5,9},{9,13},{13,1},{2,6},{6,10},{... | collective-permute-start | bytes 393224 | tf_op jit(solution)/shard_map/ppermute | solution.py:21
  93.0 2.5 %collective-permute-done.3 = bf16[512,128]{0,1:T(8,128)(2,1)S(1)} collective-permute-done((bf16[512,128]{0,1:T(8,128)(2,1)S(1)}, bf16[512,128]{0,1:T(8,128)(2,1)S(1)}, u32[]{:S(2)}, u32[]{:S(2)}) %collective-permute-start.3) | collective-permute-done | bytes 131104 | tf_op jit(solution)/shard_map/ppermute | solution.py:21
  95.5 5.5 %collective-permute-done.2 = bf16[512,128]{0,1:T(8,128)(2,1)S(1)} collective-permute-done((bf16[512,128]{0,1:T(8,128)(2,1)S(1)}, bf16[512,128]{0,1:T(8,128)(2,1)S(1)}, u32[]{:S(2)}, u32[]{:S(2)}) %collective-permute-start.2) | collective-permute-done | bytes 131104 | tf_op jit(solution)/shard_map/ppermute | solution.py:21
  101.1 0.0 collective-permute-done.5
  101.1 0.0 collective-permute-done.7
  101.1 0.0 collective-permute-done.6
  101.1 0.0 copy-start.4
  101.1 0.7 copy-done.4
  101.8 0.5 convolution_convert_fusion
  102.2 3.6 %collective-permute-start.8 = (bf16[256,1024]{1,0:T(8,128)(2,1)S(1)}, bf16[256,1024]{1,0:T(8,128)(2,1)S(1)}, u32[]{:S(2)}, u32[]{:S(2)}) collective-permute-start(bf16[256,1024]{1,0:T(8,128)(2,1)S(1)} %convolution_convert_fusion), channel_id=1, source_target_pairs={{0,16},{16,0},{1,17},{17,1},{2,18},{18,2},{3,19},{19,3},{4,20},{20... | collective-permute-start | bytes 1572872 | tf_op jit(solution)/shard_map/ppermute | solution.py:14
  105.8 1.5 %collective-permute-done.8 = bf16[256,1024]{1,0:T(8,128)(2,1)S(1)} collective-permute-done((bf16[256,1024]{1,0:T(8,128)(2,1)S(1)}, bf16[256,1024]{1,0:T(8,128)(2,1)S(1)}, u32[]{:S(2)}, u32[]{:S(2)}) %collective-permute-start.8) | collective-permute-done | bytes 524320 | tf_op jit(solution)/shard_map/ppermute | solution.py:14
  107.3 1.4 %fusion.2 = bf16[256,1024]{1,0:T(8,128)(2,1)S(1)} fusion(bf16[256,1024]{1,0:T(8,128)(2,1)S(1)} %collective-permute-done.8, bf16[512,512]{0,1:T(8,128)(2,1)S(1)} %pad_maximum_fusion.1, bf16[128,1024]{1,0:T(8,128)(2,1)S(1)} %collective-permute-done.7, bf16[128,1024]{1,0:T(8,128)(2,1)} %copy-done.4, bf16[128,1024]{1,0:T(8,128)(2,1)S(1)} %collective-permute-done.5, ...), kind=kOutput, calls=%fused_computation.5 | convolution fusion | flops 273416192 | bytes 2359296 | tf_op jit(solution)/shard_map/dot_general | solution.py:118
  108.7 0.1 constant_dynamic-slice_fusion.2
  108.8 4.2 %collective-permute-start.9 = (bf16[256,256]{1,0:T(8,128)(2,1)S(1)}, bf16[256,256]{1,0:T(8,128)(2,1)S(1)}, u32[]{:S(2)}, u32[]{:S(2)}) collective-permute-start(bf16[256,256]{1,0:T(8,128)(2,1)S(1)} %get-tuple-element.24), channel_id=1, source_target_pairs={{0,1},{1,2},{2,3},{3,0},{4,5},{5,6},{6,7},{7,4},{8,9},{9,10},{10,1... | collective-permute-start | bytes 393224 | tf_op jit(solution)/shard_map/ppermute | solution.py:21
  113.0 3.2 %collective-permute-start.11 = (bf16[256,256]{1,0:T(8,128)(2,1)S(1)}, bf16[256,256]{1,0:T(8,128)(2,1)S(1)}, u32[]{:S(2)}, u32[]{:S(2)}) collective-permute-start(bf16[256,256]{1,0:T(8,128)(2,1)S(1)} %get-tuple-element.25), channel_id=1, source_target_pairs={{0,3},{1,0},{2,1},{3,2},{4,7},{5,4},{6,5},{7,6},{8,11},{9,8},{10,9... | collective-permute-start | bytes 393224 | tf_op jit(solution)/shard_map/ppermute | solution.py:21
  116.2 6.6 %collective-permute-start.10 = (bf16[256,256]{1,0:T(8,128)(2,1)S(1)}, bf16[256,256]{1,0:T(8,128)(2,1)S(1)}, u32[]{:S(2)}, u32[]{:S(2)}) collective-permute-start(bf16[256,256]{1,0:T(8,128)(2,1)S(1)} %get-tuple-element.26), channel_id=1, source_target_pairs={{0,2},{1,3},{2,0},{3,1},{4,6},{5,7},{6,4},{7,5},{8,10},{9,11},{10,... | collective-permute-start | bytes 393224 | tf_op jit(solution)/shard_map/ppermute | solution.py:21
  122.8 0.6 dynamic-slice_bitcast_fusion
  123.4 0.0 collective-permute-done.9
  123.4 0.0 collective-permute-done.11
  123.4 6.3 %collective-permute-done.10 = bf16[256,256]{1,0:T(8,128)(2,1)S(1)} collective-permute-done((bf16[256,256]{1,0:T(8,128)(2,1)S(1)}, bf16[256,256]{1,0:T(8,128)(2,1)S(1)}, u32[]{:S(2)}, u32[]{:S(2)}) %collective-permute-start.10) | collective-permute-done | bytes 131104 | tf_op jit(solution)/shard_map/ppermute | solution.py:21
  129.7 0.7 add_convert_fusion
  130.4 0.0 all-to-all-done.2
  130.4 0.8 reduce_sum.132
  (18 shorter events, 0.2 us)
Async XLA Ops:
  0.6 15.5 %copy-start = (bf16[256,4096]{1,0:T(8,128)(2,1)S(1)}, bf16[256,4096]{1,0:T(8,128)(2,1)}, u32[]{:S(2)}) copy-start(bf16[256,4096]{1,0:T(8,128)(2,1)} %param.6) | copy-start | bytes 6291460
  4.1 38.0 %all-to-all-start = ((bf16[16,8,4224]{2,1,0:T(8,128)(2,1)}), bf16[16,8,4224]{2,1,0:T(8,128)(2,1)S(1)}, u32[]{:S(2)}, u32[]{:S(2)}) async-start(bf16[16,8,4224]{2,1,0:T(8,128)(2,1)} %broadcast_in_dim.17), calls=%async_computation | async-start | bytes 2162688 | tf_op jit(solution)/shard_map/all_to_all | solution.py:46
  16.1 29.8 %collective-permute-start = (bf16[256,4096]{1,0:T(8,128)(2,1)S(1)}, bf16[256,4096]{1,0:T(8,128)(2,1)}, u32[]{:S(2)}, u32[]{:S(2)}) collective-permute-start(bf16[256,4096]{1,0:T(8,128)(2,1)S(1)} %copy-done), channel_id=1, source_target_pairs={{0,16},{16,0},{1,17},{17,1},{2,18},{18,2},{3,19},{19,3},{4,20},{20... | collective-permute-start | bytes 6291464 | tf_op jit(solution)/shard_map/ppermute | solution.py:14
  19.0 24.7 %collective-permute-start.1 = (f32[256,256]{1,0:T(8,128)}, f32[256,256]{1,0:T(8,128)}, u32[]{:S(2)}, u32[]{:S(2)}) collective-permute-start(f32[256,256]{1,0:T(8,128)} %bitcast.6), channel_id=1, source_target_pairs={{0,16},{16,0},{1,17},{17,1},{2,18},{18,2},{3,19},{19,3},{4,20},{20... | collective-permute-start | bytes 786440 | tf_op jit(solution)/shard_map/ppermute | solution.py:14
  46.0 2.6 %copy-start.2 = (f32[128,256]{1,0:T(8,128)}, f32[128,256]{1,0:T(8,128)S(1)}, u32[]{:S(2)}) copy-start(f32[128,256]{1,0:T(8,128)S(1)} %get-tuple-element.41) | copy-start | bytes 393220
  48.6 0.7 copy-start.3
  49.9 14.6 %all-to-all-start.1 = ((f32[16,8,128]{2,1,0:T(8,128)}), f32[16,8,128]{2,1,0:T(8,128)S(1)}, u32[]{:S(2)}, u32[]{:S(2)}) async-start(f32[16,8,128]{2,1,0:T(8,128)} %broadcast_in_dim.20), calls=%async_computation.1 | async-start | bytes 131072 | tf_op jit(solution)/shard_map/all_to_all | solution.py:85
  69.4 8.2 %copy-start.1 = (bf16[128,4096]{1,0:T(8,128)(2,1)S(1)}, bf16[128,4096]{1,0:T(8,128)(2,1)}, u32[]{:S(2)}) copy-start(bf16[128,4096]{1,0:T(8,128)(2,1)} %slice.52) | copy-start | bytes 3145732
  69.4 61.0 %all-to-all-start.2 = ((bf16[16,8,4096]{2,1,0:T(8,128)(2,1)}), bf16[16,8,4096]{2,1,0:T(8,128)(2,1)S(1)}, u32[]{:S(2)}, u32[]{:S(2)}) async-start(bf16[16,8,4096]{2,1,0:T(8,128)(2,1)} %fusion.1), calls=%async_computation.2 | async-start | bytes 2097152 | tf_op jit(solution)/shard_map/all_to_all | solution.py:111
  73.2 17.8 %collective-permute-start.4 = (bf16[512,128]{0,1:T(8,128)(2,1)S(1)}, bf16[512,128]{0,1:T(8,128)(2,1)S(1)}, u32[]{:S(2)}, u32[]{:S(2)}) collective-permute-start(bf16[512,128]{0,1:T(8,128)(2,1)S(1)} %pad_maximum_fusion.4), channel_id=1, source_target_pairs={{0,12},{4,0},{8,4},{12,8},{1,13},{5,1},{9,5},{13,9},{2,14},{6,2},{... | collective-permute-start | bytes 393224 | tf_op jit(solution)/shard_map/ppermute | solution.py:21
  77.7 23.3 %collective-permute-start.5 = (bf16[128,1024]{1,0:T(8,128)(2,1)S(1)}, bf16[128,1024]{1,0:T(8,128)(2,1)S(1)}, u32[]{:S(2)}, u32[]{:S(2)}) collective-permute-start(bf16[128,1024]{1,0:T(8,128)(2,1)S(1)} %get-tuple-element.21), channel_id=1, source_target_pairs={{0,4},{4,8},{8,12},{12,0},{1,5},{5,9},{9,13},{13,1},{2,6},{6,10},{... | collective-permute-start | bytes 786440 | tf_op jit(solution)/shard_map/ppermute | solution.py:21
  79.7 21.4 %collective-permute-start.7 = (bf16[128,1024]{1,0:T(8,128)(2,1)S(1)}, bf16[128,1024]{1,0:T(8,128)(2,1)S(1)}, u32[]{:S(2)}, u32[]{:S(2)}) collective-permute-start(bf16[128,1024]{1,0:T(8,128)(2,1)S(1)} %get-tuple-element.22), channel_id=1, source_target_pairs={{0,12},{4,0},{8,4},{12,8},{1,13},{5,1},{9,5},{13,9},{2,14},{6,2},{... | collective-permute-start | bytes 786440 | tf_op jit(solution)/shard_map/ppermute | solution.py:21
  84.2 16.8 %collective-permute-start.6 = (bf16[128,1024]{1,0:T(8,128)(2,1)S(1)}, bf16[128,1024]{1,0:T(8,128)(2,1)S(1)}, u32[]{:S(2)}, u32[]{:S(2)}) collective-permute-start(bf16[128,1024]{1,0:T(8,128)(2,1)S(1)} %get-tuple-element.23), channel_id=1, source_target_pairs={{0,8},{4,12},{8,0},{12,4},{1,9},{5,13},{9,1},{13,5},{2,10},{6,14},... | collective-permute-start | bytes 786440 | tf_op jit(solution)/shard_map/ppermute | solution.py:21
  86.2 9.3 %collective-permute-start.3 = (bf16[512,128]{0,1:T(8,128)(2,1)S(1)}, bf16[512,128]{0,1:T(8,128)(2,1)S(1)}, u32[]{:S(2)}, u32[]{:S(2)}) collective-permute-start(bf16[512,128]{0,1:T(8,128)(2,1)S(1)} %pad_maximum_fusion.4), channel_id=1, source_target_pairs={{0,8},{4,12},{8,0},{12,4},{1,9},{5,13},{9,1},{13,5},{2,10},{6,14},... | collective-permute-start | bytes 393224 | tf_op jit(solution)/shard_map/ppermute | solution.py:21
  91.0 10.0 %collective-permute-start.2 = (bf16[512,128]{0,1:T(8,128)(2,1)S(1)}, bf16[512,128]{0,1:T(8,128)(2,1)S(1)}, u32[]{:S(2)}, u32[]{:S(2)}) collective-permute-start(bf16[512,128]{0,1:T(8,128)(2,1)S(1)} %pad_maximum_fusion.4), channel_id=1, source_target_pairs={{0,4},{4,8},{8,12},{12,0},{1,5},{5,9},{9,13},{13,1},{2,6},{6,10},{... | collective-permute-start | bytes 393224 | tf_op jit(solution)/shard_map/ppermute | solution.py:21
  101.1 0.7 copy-start.4
  102.2 5.1 %collective-permute-start.8 = (bf16[256,1024]{1,0:T(8,128)(2,1)S(1)}, bf16[256,1024]{1,0:T(8,128)(2,1)S(1)}, u32[]{:S(2)}, u32[]{:S(2)}) collective-permute-start(bf16[256,1024]{1,0:T(8,128)(2,1)S(1)} %convolution_convert_fusion), channel_id=1, source_target_pairs={{0,16},{16,0},{1,17},{17,1},{2,18},{18,2},{3,19},{19,3},{4,20},{20... | collective-permute-start | bytes 1572872 | tf_op jit(solution)/shard_map/ppermute | solution.py:14
  108.8 14.6 %collective-permute-start.9 = (bf16[256,256]{1,0:T(8,128)(2,1)S(1)}, bf16[256,256]{1,0:T(8,128)(2,1)S(1)}, u32[]{:S(2)}, u32[]{:S(2)}) collective-permute-start(bf16[256,256]{1,0:T(8,128)(2,1)S(1)} %get-tuple-element.24), channel_id=1, source_target_pairs={{0,1},{1,2},{2,3},{3,0},{4,5},{5,6},{6,7},{7,4},{8,9},{9,10},{10,1... | collective-permute-start | bytes 393224 | tf_op jit(solution)/shard_map/ppermute | solution.py:21
  113.0 10.4 %collective-permute-start.11 = (bf16[256,256]{1,0:T(8,128)(2,1)S(1)}, bf16[256,256]{1,0:T(8,128)(2,1)S(1)}, u32[]{:S(2)}, u32[]{:S(2)}) collective-permute-start(bf16[256,256]{1,0:T(8,128)(2,1)S(1)} %get-tuple-element.25), channel_id=1, source_target_pairs={{0,3},{1,0},{2,1},{3,2},{4,7},{5,4},{6,5},{7,6},{8,11},{9,8},{10,9... | collective-permute-start | bytes 393224 | tf_op jit(solution)/shard_map/ppermute | solution.py:21
  116.2 13.5 %collective-permute-start.10 = (bf16[256,256]{1,0:T(8,128)(2,1)S(1)}, bf16[256,256]{1,0:T(8,128)(2,1)S(1)}, u32[]{:S(2)}, u32[]{:S(2)}) collective-permute-start(bf16[256,256]{1,0:T(8,128)(2,1)S(1)} %get-tuple-element.26), channel_id=1, source_target_pairs={{0,2},{1,3},{2,0},{3,1},{4,6},{5,7},{6,4},{7,5},{8,10},{9,11},{10,... | collective-permute-start | bytes 393224 | tf_op jit(solution)/shard_map/ppermute | solution.py:21

commit v3 on v2

v3 whole, which is shorter than its diff:
```python
import jax
import jax.numpy as jnp
from jax import lax
from jax.experimental import pallas as pl
from jax.experimental.pallas import tpu as pltpu
from jax.sharding import Mesh, PartitionSpec as P

inv_temp = 50.0
YL, CORES, X = 2, 2, 4
LANES = 128
STATS = 8
CHIPS = ("yl", "z")
f32, bf16, i32 = jnp.float32, jnp.bfloat16, jnp.int32
VMEM = pl.BlockSpec(memory_space=pltpu.VMEM)
SMEM = pl.BlockSpec(memory_space=pltpu.SMEM)
PARAMS = pltpu.CompilerParams(vmem_limit_bytes=40 * 1024 * 1024)


def shift(value, axis, by):
    if by == 0:
        return value
    size = lax.axis_size(axis)
    return lax.ppermute(value, axis, [(i, (i + by) % size) for i in range(size)])


def column_slice(value, which, count):
    width = value.shape[1] // count
    return lax.dynamic_slice_in_dim(value, which % count * width, width, 1)


def in_core_order(own, other, axis):
    first, second = jnp.concatenate([own, other], axis), jnp.concatenate([other, own], axis)
    return jnp.where(lax.axis_index("core") == 0, first, second)


def hits(positive, place, shape):
    return lax.broadcasted_iota(i32, shape, 0) + place == positive


def score_kernel(place, query, passages, teacher, scores, logits, positives, stats):
    depth = passages.shape[1]
    rows = query.shape[0]
    codes = query[:, depth:].astype(f32).T
    row_index = codes[0:1].astype(i32)
    positive = codes[1:2].astype(i32) * 256 + codes[2:3].astype(i32)
    positives[...] = positive
    s = inv_temp * lax.dot_general(
        passages[...], query[:, :depth], (((1,), (1,)), ((), ())), preferred_element_type=f32
    )
    pick = (lax.broadcasted_iota(i32, (teacher.shape[0], rows), 0) == row_index).astype(f32)
    t = lax.dot_general(
        teacher[...], pick, (((0,), (0,)), ((), ())),
        precision=lax.Precision.HIGHEST, preferred_element_type=f32,
    )
    scores[...] = s
    logits[...] = t
    top_s, top_t = jnp.max(s, axis=0, keepdims=True), jnp.max(t, axis=0, keepdims=True)
    below_s, below_t = s - top_s, t - top_t
    weight = jnp.exp(below_t)
    hot = hits(positive, place[0], s.shape)
    sums = [
        jnp.sum(v, axis=0, keepdims=True)
        for v in (jnp.exp(below_s), weight, weight * (below_t - below_s), jnp.where(hot, s, 0.0))
    ]
    whole = jnp.concatenate([top_s, top_t] + sums + [jnp.zeros((STATS - 6, rows), f32)], axis=0)
    stats[...] = jnp.broadcast_to(whole[None], stats.shape)


def grad_kernel(place, scores, logits, positives, stats, grads, sent, losses):
    tops_s, tops_t, sums_s, sums_t, cross, hit = (stats[:, i, :] for i in range(6))
    top_s, top_t = jnp.max(tops_s, axis=0, keepdims=True), jnp.max(tops_t, axis=0, keepdims=True)
    lower_s, lower_t = tops_s - top_s, tops_t - top_t
    total_s = jnp.sum(jnp.exp(lower_s) * sums_s, axis=0, keepdims=True)
    weight_t = jnp.exp(lower_t)
    total_t = jnp.sum(weight_t * sums_t, axis=0, keepdims=True)
    cross = jnp.sum(weight_t * (cross + (lower_t - lower_s) * sums_t), axis=0, keepdims=True)
    log_s = jnp.log(total_s)
    own = jnp.sum(hit, axis=0, keepdims=True)
    losses[...] = cross / total_t - jnp.log(total_t) + log_s - (own - top_s - log_s)
    s, t = scores[...], logits[...]
    hot = hits(positives[...], place[0], s.shape)
    values = (
        jnp.exp(s - top_s) * (2.0 * inv_temp / total_s)
        - jnp.exp(t - top_t) * (inv_temp / total_t)
        - jnp.where(hot, inv_temp, 0.0)
    ).astype(bf16)
    grads[...] = values
    half = values.shape[0] // CORES
    for slot in range(sent.shape[0]):
        sent[slot] = values[slot % CORES * half : (slot % CORES + 1) * half]


def passage_kernel(position, grads, query, query_other, out):
    x, core = position[0], position[1]
    groups = query.shape[0]
    total = jnp.zeros(out.shape[1:], f32)
    for d in range(groups):
        group = lax.rem(x + groups - d, groups) * CORES
        for which, columns in ((core, query), (1 - core, query_other)):
            total += jnp.dot(grads[group + which], columns[d], preferred_element_type=f32)
    out[0] = total.astype(bf16)


def per_device(queries, passages, teacher, teacher_rows, positives):
    own_rows, depth = queries.shape[1:]
    block_rows = passages.shape[0]
    chips = lax.axis_size("yl") * lax.axis_size("z")
    x_size, yh_size = lax.axis_size("x"), lax.axis_size("yh")
    rows, wide = chips * own_rows, CORES * block_rows
    chip = lax.axis_index("yl") * lax.axis_size("z") + lax.axis_index("z")
    core, x, yh = lax.axis_index("core"), lax.axis_index("x"), lax.axis_index("yh")
    place = (chip * wide).astype(i32)[None]

    indices = jnp.stack(
        [teacher_rows[0], positives[0] // 256, positives[0] % 256], axis=1
    ).astype(bf16)
    sent = jnp.concatenate(
        [queries[0], jnp.pad(indices, ((0, 0), (0, LANES - indices.shape[1])))], axis=1
    )
    passages = in_core_order(passages, shift(passages, "core", 1), 0)
    teacher = in_core_order(teacher[0], shift(teacher[0], "core", 1), 1)
    query = lax.all_to_all(
        jnp.broadcast_to(sent[None], (chips,) + sent.shape), CHIPS, 0, 0, tiled=True
    ).reshape(rows, depth + LANES)

    scores, logits, positive, stats = pl.pallas_call(
        score_kernel,
        out_shape=(
            jax.ShapeDtypeStruct((wide, rows), f32),
            jax.ShapeDtypeStruct((wide, rows), f32),
            jax.ShapeDtypeStruct((1, rows), i32),
            jax.ShapeDtypeStruct((chips, STATS, rows), f32),
        ),
        in_specs=[SMEM] + [VMEM] * 3,
        out_specs=(VMEM,) * 4,
        compiler_params=PARAMS,
    )(place, query, passages, teacher)
    columns = [shift(column_slice(query[:, :depth], x + d, x_size), "x", d) for d in range(x_size)]
    stats = lax.all_to_all(stats, CHIPS, 0, 0, tiled=True)
    stats, columns = lax.optimization_barrier((stats, columns))
    columns = jnp.stack(columns)
    columns_other = shift(columns, "core", 1)

    grads, sent, losses = pl.pallas_call(
        grad_kernel,
        out_shape=(
            jax.ShapeDtypeStruct((wide, rows), bf16),
            jax.ShapeDtypeStruct((x_size * CORES, block_rows, rows), bf16),
            jax.ShapeDtypeStruct((1, rows), f32),
        ),
        in_specs=[SMEM] + [VMEM] * 4,
        out_specs=(VMEM,) * 3,
        compiler_params=PARAMS,
    )(place, scores, logits, positive, stats)
    loss = lax.dynamic_slice_in_dim(losses[0], chip * own_rows, own_rows)
    grads_x = lax.all_to_all(sent, ("x", "core"), 0, 0, tiled=True)

    query_part = lax.dot_general(
        grads, passages, (((0,), (0,)), ((), ())), preferred_element_type=f32
    ).astype(bf16)
    grads_x, query_part = lax.optimization_barrier((grads_x, query_part))
    query_parts = lax.all_to_all(query_part.reshape(chips, own_rows, depth), CHIPS, 0, 0, tiled=True)
    query_total = jnp.sum(query_parts.astype(f32), axis=0)

    width = depth // (x_size * yh_size)
    part = pl.pallas_call(
        passage_kernel,
        grid=(yh_size,),
        out_shape=jax.ShapeDtypeStruct((yh_size, block_rows, width), bf16),
        in_specs=[
            SMEM,
            pl.BlockSpec((x_size * CORES, block_rows, rows), lambda i: (0, 0, 0)),
            pl.BlockSpec((x_size, rows, width), lambda i: (0, 0, i)),
            pl.BlockSpec((x_size, rows, width), lambda i: (0, 0, i)),
        ],
        out_specs=pl.BlockSpec((1, block_rows, width), lambda i: (i, 0, 0)),
        compiler_params=PARAMS,
    )(jnp.stack([x, core]).astype(i32), grads_x, columns, columns_other)
    parts = [
        shift(lax.dynamic_index_in_dim(part, (yh + d) % yh_size, 0, False), "yh", d) for d in range(yh_size)
    ]
    passage_total = sum(v.astype(f32) for v in parts)
    return loss[None], query_total.astype(bf16)[None], passage_total.astype(bf16)


def solution(mesh):
    blk, qgroup = mesh.devices.shape
    split = Mesh(
        mesh.devices.reshape(YL, blk // (YL * CORES), CORES, X, qgroup // X),
        ("yl", "z", "core", "x", "yh"),
    )
    blk, qgroup = ("yl", "z", "core"), ("x", "yh")
    in_specs = (
        P(qgroup, blk, None),
        P(blk, None),
        P(qgroup, None, blk),
        P(qgroup, blk),
        P(qgroup, blk),
    )
    out_specs = (P(qgroup, blk), P(qgroup, blk, None), P(blk, qgroup))
    return jax.shard_map(per_device, mesh=split, in_specs=in_specs, out_specs=out_specs, check_vma=False)
```

time: 133 us -> 129 us (0.970)
  the two profiles are of different devices: /device:TPU:1 before, /device:TPU:9 now
where the time goes in v3:
time: 129 us; the launch traced here: 128 us
  starting transfers between devices  54.2 us (42%)
  waiting for transfers between devices  37 us (29%)
  blocking collectives  13 us (10%)
  other arithmetic  9.6 us (7%)
  Pallas kernels  5.28 us (4%)
  local copies, waits for them, and re-layouts  3.92 us (3%)
  matrix products  3.91 us (3%)
    ppermute x9, starting transfers between devices, shift(): lax.ppermute(value, axis, [(i, (i + by) % size) for i in range(size)])  31.5 us
    all_to_all x1, waiting for transfers between devices, per_device(): lax.all_to_all(jnp.broadcast_to(sent[None], (chips,) + sent.shape), CHIPS...  17.8 us
    ppermute x9, waiting for transfers between devices, shift(): lax.ppermute(value, axis, [(i, (i + by) % size) for i in range(size)])  13.6 us
    all_to_all x1, blocking collectives, per_device(): stats = lax.all_to_all(stats, CHIPS, 0, 0, tiled=True)  13 us
    all_to_all x1, starting transfers between devices, per_device(): lax.all_to_all(jnp.broadcast_to(sent[None], (chips,) + sent.shape), CHIPS...  11.2 us
    all_to_all x1, starting transfers between devices, per_device(): grads_x = lax.all_to_all(sent, ('x', 'core'), 0, 0, tiled=True)  6.16 us
    all_to_all x1, waiting for transfers between devices, per_device(): grads_x = lax.all_to_all(sent, ('x', 'core'), 0, 0, tiled=True)  5.59 us
    all_to_all x1, starting transfers between devices, per_device(): lax.all_to_all(query_part.reshape(chips, own_rows, depth), CHIPS, 0, 0, t...  5.26 us
  transfers between devices with their start and end apart: 12, of which 6 were waited for; matrix products, arithmetic and copies ran while one was open for 8% of the time, Pallas kernels for 3%

profile of v3, /device:TPU:9, one launch (start us, length us, event | category | flops | bytes accessed | tf_op | source)
XLA Modules:
  0.0 127.9 jit_solution(17496286974137659233)
XLA Ops:
  0.6 0.7 fusion.6
  1.3 0.7 convert_bitcast_fusion
  2.0 0.1 copy.9
  2.1 0.8 fusion.4
  2.9 1.1 broadcast_in_dim.14
  4.0 11.2 %all-to-all-start = ((bf16[16,8,4224]{2,1,0:T(8,128)(2,1)}), bf16[16,8,4224]{2,1,0:T(8,128)(2,1)S(1)}, u32[]{:S(2)}, u32[]{:S(2)}) async-start(bf16[16,8,4224]{2,1,0:T(8,128)(2,1)} %broadcast_in_dim.14), calls=%async_computation | async-start | bytes 2162688 | tf_op jit(solution)/shard_map/all_to_all | solution.py:122
  15.2 3.1 %collective-permute-start = (bf16[256,4096]{1,0:T(8,128)(2,1)}, bf16[256,4096]{1,0:T(8,128)(2,1)}, u32[]{:S(2)}, u32[]{:S(2)}) collective-permute-start(bf16[256,4096]{1,0:T(8,128)(2,1)} %param.6), channel_id=1, source_target_pairs={{0,16},{16,0},{1,17},{17,1},{2,18},{18,2},{3,19},{19,3},{4,20},{20... | collective-permute-start | bytes 6291464 | tf_op jit(solution)/shard_map/ppermute | solution.py:23
  18.3 1.9 %collective-permute-start.1 = (f32[256,256]{1,0:T(8,128)}, f32[256,256]{1,0:T(8,128)S(1)}, u32[]{:S(2)}, u32[]{:S(2)}) collective-permute-start(f32[256,256]{1,0:T(8,128)} %bitcast.45), channel_id=1, source_target_pairs={{0,16},{16,0},{1,17},{17,1},{2,18},{18,2},{3,19},{19,3},{4,20},{20... | collective-permute-start | bytes 786440 | tf_op jit(solution)/shard_map/ppermute | solution.py:23
  20.3 2.4 %collective-permute-done.1 = f32[256,256]{1,0:T(8,128)S(1)} collective-permute-done((f32[256,256]{1,0:T(8,128)}, f32[256,256]{1,0:T(8,128)S(1)}, u32[]{:S(2)}, u32[]{:S(2)}) %collective-permute-start.1) | collective-permute-done | bytes 262176 | tf_op jit(solution)/shard_map/ppermute | solution.py:23
  22.7 1.1 maximum_select_fusion.1.teacher
  23.8 17.8 %all-to-all-done = bf16[16,8,4224]{2,1,0:T(8,128)(2,1)S(1)} async-done(((bf16[16,8,4224]{2,1,0:T(8,128)(2,1)}), bf16[16,8,4224]{2,1,0:T(8,128)(2,1)S(1)}, u32[]{:S(2)}, u32[]{:S(2)}) %all-to-all-start) | async-done | bytes 1081376 | tf_op jit(solution)/shard_map/all_to_all | solution.py:122
  41.6 0.0 copy-start.1
  41.6 0.1 slice.3
  41.7 0.1 constant_dynamic-slice_fusion.1
  41.8 3.3 %collective-permute-start.2 = (bf16[128,1024]{1,0:T(8,128)(2,1)S(1)}, bf16[128,1024]{1,0:T(8,128)(2,1)S(1)}, u32[]{:S(2)}, u32[]{:S(2)}) collective-permute-start(bf16[128,1024]{1,0:T(8,128)(2,1)S(1)} %get-tuple-element.33), channel_id=1, source_target_pairs={{0,4},{4,8},{8,12},{12,0},{1,5},{5,9},{9,13},{13,1},{2,6},{6,10},{... | collective-permute-start | bytes 786440 | tf_op jit(solution)/shard_map/ppermute | solution.py:23
  45.1 4.4 %collective-permute-start.3 = (bf16[128,1024]{1,0:T(8,128)(2,1)S(1)}, bf16[128,1024]{1,0:T(8,128)(2,1)S(1)}, u32[]{:S(2)}, u32[]{:S(2)}) collective-permute-start(bf16[128,1024]{1,0:T(8,128)(2,1)S(1)} %get-tuple-element.32), channel_id=1, source_target_pairs={{0,8},{4,12},{8,0},{12,4},{1,9},{5,13},{9,1},{13,5},{2,10},{6,14},... | collective-permute-start | bytes 786440 | tf_op jit(solution)/shard_map/ppermute | solution.py:23
  49.4 3.1 %collective-permute-start.4 = (bf16[128,1024]{1,0:T(8,128)(2,1)S(1)}, bf16[128,1024]{1,0:T(8,128)(2,1)S(1)}, u32[]{:S(2)}, u32[]{:S(2)}) collective-permute-start(bf16[128,1024]{1,0:T(8,128)(2,1)S(1)} %get-tuple-element.31), channel_id=1, source_target_pairs={{0,12},{4,0},{8,4},{12,8},{1,13},{5,1},{9,5},{13,9},{2,14},{6,2},{... | collective-permute-start | bytes 786440 | tf_op jit(solution)/shard_map/ppermute | solution.py:23
  52.5 0.0 collective-permute-done
  52.5 0.0 copy-done.1
  52.5 3.4 %maximum_select_fusion.passages = bf16[512,4096]{1,0:T(8,128)(2,1)S(1)} fusion(bf16[256,4096]{1,0:T(8,128)(2,1)} %collective-permute-done, bf16[256,4096]{1,0:T(8,128)(2,1)S(1)} %copy-done.1, pred[]{:T(512)S(6)} %eq.15), kind=kLoop, calls=%fused_computation.1 | loop fusion | flops 18874368 | bytes 8388609 | tf_op jit(solution)/shard_map/jit(_where)/select_n | solution.py:33
  55.9 1.8 %shard_map.76 = (f32[512,128]{1,0:T(8,128)S(1)}, f32[512,128]{1,0:T(8,128)S(1)}, s32[1,128]{1,0:T(1,128)S(1)}, f32[16,8,128]{2,1,0:T(8,128)S(1)}) custom-call(s32[1]{0:T(128)} %bitcast.place, bf16[128,4224]{1,0:T(8,128)(2,1)S(1)} %bitcast.43, bf16[512,4096]{1,0:T(8,128)(2,1)S(1)} %maximum_select_fusion.passages, f32[256,512]{1,0:T(8,128)S(1)} %maximum_select_fusion.1.teacher), custom_call_target="tpu_custom_call" | custom-call | tf_op jit(solution)/shard_map/pallas_call | solution.py:126
  57.7 0.0 copy-start
  57.7 1.9 %copy-done = bf16[512,4096]{1,0:T(8,128)(2,1)} copy-done((bf16[512,4096]{1,0:T(8,128)(2,1)}, bf16[512,4096]{1,0:T(8,128)(2,1)S(1)}, u32[]{:S(2)}) %copy-start) | copy-done | bytes 4194328
  59.6 13.0 %all_to_all.20.stats = f32[16,8,128]{2,1,0:T(8,128)S(1)} all-to-all(f32[16,8,128]{2,1,0:T(8,128)S(1)} %get-tuple-element.20), channel_id=1, replica_groups=mesh['yl'=2,'z'=8,'core'=2,'x'=4,'yh'=4] {'yl','z'}, dimensions={0} | all-to-all | bytes 131072 | tf_op jit(solution)/shard_map/all_to_all | solution.py:139
  72.7 0.0 collective-permute-done.2
  72.7 0.0 collective-permute-done.3
  72.7 0.0 collective-permute-done.4
  72.7 1.0 shard_map.77
  73.7 6.2 %all-to-all-start.2 = ((bf16[8,256,128]{2,1,0:T(8,128)(2,1)}), bf16[8,256,128]{2,1,0:T(8,128)(2,1)S(1)}, u32[]{:S(2)}, u32[]{:S(2)}) async-start(bf16[8,256,128]{2,1,0:T(8,128)(2,1)} %get-tuple-element.23), calls=%async_computation.2 | async-start | bytes 1048576 | tf_op jit(solution)/shard_map/all_to_all | solution.py:156
  79.9 3.9 %convolution_convert_fusion = bf16[128,4096]{1,0:T(8,128)(2,1)} fusion(bf16[512,128]{1,0:T(8,128)(2,1)S(1)} %get-tuple-element.24, bf16[512,4096]{1,0:T(8,128)(2,1)} %copy-done), kind=kOutput, calls=%fused_computation | convolution fusion | flops 537395200 | bytes 5373952 | tf_op jit(solution)/shard_map/dot_general | solution.py:158
  83.8 5.6 %all-to-all-done.2.grads = bf16[8,256,128]{2,1,0:T(8,128)(2,1)S(1)} async-done(((bf16[8,256,128]{2,1,0:T(8,128)(2,1)}), bf16[8,256,128]{2,1,0:T(8,128)(2,1)S(1)}, u32[]{:S(2)}, u32[]{:S(2)}) %all-to-all-start.2) | async-done | bytes 524320 | tf_op jit(solution)/shard_map/all_to_all | solution.py:156
  89.4 5.3 %all-to-all-start.3 = ((bf16[16,8,4096]{2,1,0:T(8,128)(2,1)}), bf16[16,8,4096]{2,1,0:T(8,128)(2,1)}, u32[]{:S(2)}, u32[]{:S(2)}) async-start(bf16[16,8,4096]{2,1,0:T(8,128)(2,1)} %bitcast.6), calls=%async_computation.3 | async-start | bytes 2097152 | tf_op jit(solution)/shard_map/all_to_all | solution.py:162
  94.6 0.1 pad_maximum_fusion.query
  94.8 3.1 %collective-permute-start.5 = (bf16[4,128,1024]{2,1,0:T(8,128)(2,1)S(1)}, bf16[4,128,1024]{2,1,0:T(8,128)(2,1)S(1)}, u32[]{:S(2)}, u32[]{:S(2)}) collective-permute-start(bf16[4,128,1024]{2,1,0:T(8,128)(2,1)S(1)} %pad_maximum_fusion.query), channel_id=1, source_target_pairs={{0,16},{16,0},{1,17},{17,1},{2,18},{18,2},{3,19},{19,3},{4,20},{20... | collective-permute-start | bytes 3145736 | tf_op jit(solution)/shard_map/ppermute | solution.py:23
  97.9 0.1 pad_add_fusion.position
  97.9 2.1 %collective-permute-done.5.query_other = bf16[4,128,1024]{2,1,0:T(8,128)(2,1)S(1)} collective-permute-done((bf16[4,128,1024]{2,1,0:T(8,128)(2,1)S(1)}, bf16[4,128,1024]{2,1,0:T(8,128)(2,1)S(1)}, u32[]{:S(2)}, u32[]{:S(2)}) %collective-permute-start.5) | collective-permute-done | bytes 1048608 | tf_op jit(solution)/shard_map/ppermute | solution.py:23
  100.1 2.5 %shard_map.78 = bf16[4,256,256]{2,1,0:T(8,128)(2,1)S(1)} custom-call(s32[2]{0:T(128)S(1)} %pad_add_fusion.position, bf16[8,256,128]{2,1,0:T(8,128)(2,1)S(1)} %all-to-all-done.2.grads, bf16[4,128,1024]{2,1,0:T(8,128)(2,1)S(1)} %pad_maximum_fusion.query, bf16[4,128,1024]{2,1,0:T(8,128)(2,1)S(1)} %collective-permute-done.5.query_other), custom_call_target="tpu_custom_call" | custom-call | tf_op jit(solution)/shard_map/pallas_call | solution.py:166
  102.6 5.0 %collective-permute-start.8 = (bf16[256,256]{1,0:T(8,128)(2,1)S(1)}, bf16[256,256]{1,0:T(8,128)(2,1)S(1)}, u32[]{:S(2)}, u32[]{:S(2)}) collective-permute-start(bf16[256,256]{1,0:T(8,128)(2,1)S(1)} %get-tuple-element.36), channel_id=1, source_target_pairs={{0,3},{1,0},{2,1},{3,2},{4,7},{5,4},{6,5},{7,6},{8,11},{9,8},{10,9... | collective-permute-start | bytes 393224 | tf_op jit(solution)/shard_map/ppermute | solution.py:23
  107.6 4.4 %collective-permute-start.7 = (bf16[256,256]{1,0:T(8,128)(2,1)S(1)}, bf16[256,256]{1,0:T(8,128)(2,1)S(1)}, u32[]{:S(2)}, u32[]{:S(2)}) collective-permute-start(bf16[256,256]{1,0:T(8,128)(2,1)S(1)} %get-tuple-element.37), channel_id=1, source_target_pairs={{0,2},{1,3},{2,0},{3,1},{4,6},{5,7},{6,4},{7,5},{8,10},{9,11},{10,... | collective-permute-start | bytes 393224 | tf_op jit(solution)/shard_map/ppermute | solution.py:23
  112.1 3.3 %collective-permute-start.6 = (bf16[256,256]{1,0:T(8,128)(2,1)S(1)}, bf16[256,256]{1,0:T(8,128)(2,1)S(1)}, u32[]{:S(2)}, u32[]{:S(2)}) collective-permute-start(bf16[256,256]{1,0:T(8,128)(2,1)S(1)} %get-tuple-element.35), channel_id=1, source_target_pairs={{0,1},{1,2},{2,3},{3,0},{4,5},{5,6},{6,7},{7,4},{8,9},{9,10},{10,1... | collective-permute-start | bytes 393224 | tf_op jit(solution)/shard_map/ppermute | solution.py:23
  115.4 0.6 constant_dynamic-slice_fusion
  116.0 0.0 collective-permute-done.8
  116.0 4.5 %collective-permute-done.7 = bf16[256,256]{1,0:T(8,128)(2,1)S(1)} collective-permute-done((bf16[256,256]{1,0:T(8,128)(2,1)S(1)}, bf16[256,256]{1,0:T(8,128)(2,1)S(1)}, u32[]{:S(2)}, u32[]{:S(2)}) %collective-permute-start.7) | collective-permute-done | bytes 131104 | tf_op jit(solution)/shard_map/ppermute | solution.py:23
  120.5 4.7 %collective-permute-done.6 = bf16[256,256]{1,0:T(8,128)(2,1)S(1)} collective-permute-done((bf16[256,256]{1,0:T(8,128)(2,1)S(1)}, bf16[256,256]{1,0:T(8,128)(2,1)S(1)}, u32[]{:S(2)}, u32[]{:S(2)}) %collective-permute-start.6) | collective-permute-done | bytes 131104 | tf_op jit(solution)/shard_map/ppermute | solution.py:23
  125.1 0.7 fusion.2
  125.9 0.0 all-to-all-done.3
  125.9 2.0 %reduce_sum.12 = bf16[8,4096]{1,0:T(8,128)(2,1)} reduce(bf16[16,8,4096]{2,1,0:T(8,128)(2,1)} %all-to-all-done.3, bf16[]{:T(256)} %constant.110.clone.1), dimensions={0}, to_apply=%region_0.1 | reduce | flops 491520 | bytes 1114114 | tf_op jit(solution)/shard_map/reduce_sum | solution.py:163
  (2 shorter events, 0.0 us)
Async XLA Ops:
  4.0 37.6 %all-to-all-start = ((bf16[16,8,4224]{2,1,0:T(8,128)(2,1)}), bf16[16,8,4224]{2,1,0:T(8,128)(2,1)S(1)}, u32[]{:S(2)}, u32[]{:S(2)}) async-start(bf16[16,8,4224]{2,1,0:T(8,128)(2,1)} %broadcast_in_dim.14), calls=%async_computation | async-start | bytes 2162688 | tf_op jit(solution)/shard_map/all_to_all | solution.py:122
  15.2 37.3 %collective-permute-start = (bf16[256,4096]{1,0:T(8,128)(2,1)}, bf16[256,4096]{1,0:T(8,128)(2,1)}, u32[]{:S(2)}, u32[]{:S(2)}) collective-permute-start(bf16[256,4096]{1,0:T(8,128)(2,1)} %param.6), channel_id=1, source_target_pairs={{0,16},{16,0},{1,17},{17,1},{2,18},{18,2},{3,19},{19,3},{4,20},{20... | collective-permute-start | bytes 6291464 | tf_op jit(solution)/shard_map/ppermute | solution.py:23
  18.3 4.3 %collective-permute-start.1 = (f32[256,256]{1,0:T(8,128)}, f32[256,256]{1,0:T(8,128)S(1)}, u32[]{:S(2)}, u32[]{:S(2)}) collective-permute-start(f32[256,256]{1,0:T(8,128)} %bitcast.45), channel_id=1, source_target_pairs={{0,16},{16,0},{1,17},{17,1},{2,18},{18,2},{3,19},{19,3},{4,20},{20... | collective-permute-start | bytes 786440 | tf_op jit(solution)/shard_map/ppermute | solution.py:23
  41.6 10.9 %copy-start.1 = (bf16[256,4096]{1,0:T(8,128)(2,1)S(1)}, bf16[256,4096]{1,0:T(8,128)(2,1)}, u32[]{:S(2)}) copy-start(bf16[256,4096]{1,0:T(8,128)(2,1)} %param.6) | copy-start | bytes 6291460
  41.8 30.9 %collective-permute-start.2 = (bf16[128,1024]{1,0:T(8,128)(2,1)S(1)}, bf16[128,1024]{1,0:T(8,128)(2,1)S(1)}, u32[]{:S(2)}, u32[]{:S(2)}) collective-permute-start(bf16[128,1024]{1,0:T(8,128)(2,1)S(1)} %get-tuple-element.33), channel_id=1, source_target_pairs={{0,4},{4,8},{8,12},{12,0},{1,5},{5,9},{9,13},{13,1},{2,6},{6,10},{... | collective-permute-start | bytes 786440 | tf_op jit(solution)/shard_map/ppermute | solution.py:23
  45.1 27.6 %collective-permute-start.3 = (bf16[128,1024]{1,0:T(8,128)(2,1)S(1)}, bf16[128,1024]{1,0:T(8,128)(2,1)S(1)}, u32[]{:S(2)}, u32[]{:S(2)}) collective-permute-start(bf16[128,1024]{1,0:T(8,128)(2,1)S(1)} %get-tuple-element.32), channel_id=1, source_target_pairs={{0,8},{4,12},{8,0},{12,4},{1,9},{5,13},{9,1},{13,5},{2,10},{6,14},... | collective-permute-start | bytes 786440 | tf_op jit(solution)/shard_map/ppermute | solution.py:23
  49.4 23.2 %collective-permute-start.4 = (bf16[128,1024]{1,0:T(8,128)(2,1)S(1)}, bf16[128,1024]{1,0:T(8,128)(2,1)S(1)}, u32[]{:S(2)}, u32[]{:S(2)}) collective-permute-start(bf16[128,1024]{1,0:T(8,128)(2,1)S(1)} %get-tuple-element.31), channel_id=1, source_target_pairs={{0,12},{4,0},{8,4},{12,8},{1,13},{5,1},{9,5},{13,9},{2,14},{6,2},{... | collective-permute-start | bytes 786440 | tf_op jit(solution)/shard_map/ppermute | solution.py:23
  57.7 2.0 %copy-start = (bf16[512,4096]{1,0:T(8,128)(2,1)}, bf16[512,4096]{1,0:T(8,128)(2,1)S(1)}, u32[]{:S(2)}) copy-start(bf16[512,4096]{1,0:T(8,128)(2,1)S(1)} %maximum_select_fusion.passages) | copy-start | bytes 12582916
  73.7 15.7 %all-to-all-start.2 = ((bf16[8,256,128]{2,1,0:T(8,128)(2,1)}), bf16[8,256,128]{2,1,0:T(8,128)(2,1)S(1)}, u32[]{:S(2)}, u32[]{:S(2)}) async-start(bf16[8,256,128]{2,1,0:T(8,128)(2,1)} %get-tuple-element.23), calls=%async_computation.2 | async-start | bytes 1048576 | tf_op jit(solution)/shard_map/all_to_all | solution.py:156
  89.4 36.5 %all-to-all-start.3 = ((bf16[16,8,4096]{2,1,0:T(8,128)(2,1)}), bf16[16,8,4096]{2,1,0:T(8,128)(2,1)}, u32[]{:S(2)}, u32[]{:S(2)}) async-start(bf16[16,8,4096]{2,1,0:T(8,128)(2,1)} %bitcast.6), calls=%async_computation.3 | async-start | bytes 2097152 | tf_op jit(solution)/shard_map/all_to_all | solution.py:162
  94.8 5.3 %collective-permute-start.5 = (bf16[4,128,1024]{2,1,0:T(8,128)(2,1)S(1)}, bf16[4,128,1024]{2,1,0:T(8,128)(2,1)S(1)}, u32[]{:S(2)}, u32[]{:S(2)}) collective-permute-start(bf16[4,128,1024]{2,1,0:T(8,128)(2,1)S(1)} %pad_maximum_fusion.query), channel_id=1, source_target_pairs={{0,16},{16,0},{1,17},{17,1},{2,18},{18,2},{3,19},{19,3},{4,20},{20... | collective-permute-start | bytes 3145736 | tf_op jit(solution)/shard_map/ppermute | solution.py:23
  102.6 13.4 %collective-permute-start.8 = (bf16[256,256]{1,0:T(8,128)(2,1)S(1)}, bf16[256,256]{1,0:T(8,128)(2,1)S(1)}, u32[]{:S(2)}, u32[]{:S(2)}) collective-permute-start(bf16[256,256]{1,0:T(8,128)(2,1)S(1)} %get-tuple-element.36), channel_id=1, source_target_pairs={{0,3},{1,0},{2,1},{3,2},{4,7},{5,4},{6,5},{7,6},{8,11},{9,8},{10,9... | collective-permute-start | bytes 393224 | tf_op jit(solution)/shard_map/ppermute | solution.py:23
  107.6 12.8 %collective-permute-start.7 = (bf16[256,256]{1,0:T(8,128)(2,1)S(1)}, bf16[256,256]{1,0:T(8,128)(2,1)S(1)}, u32[]{:S(2)}, u32[]{:S(2)}) collective-permute-start(bf16[256,256]{1,0:T(8,128)(2,1)S(1)} %get-tuple-element.37), channel_id=1, source_target_pairs={{0,2},{1,3},{2,0},{3,1},{4,6},{5,7},{6,4},{7,5},{8,10},{9,11},{10,... | collective-permute-start | bytes 393224 | tf_op jit(solution)/shard_map/ppermute | solution.py:23
  112.1 13.1 %collective-permute-start.6 = (bf16[256,256]{1,0:T(8,128)(2,1)S(1)}, bf16[256,256]{1,0:T(8,128)(2,1)S(1)}, u32[]{:S(2)}, u32[]{:S(2)}) collective-permute-start(bf16[256,256]{1,0:T(8,128)(2,1)S(1)} %get-tuple-element.35), channel_id=1, source_target_pairs={{0,1},{1,2},{2,3},{3,0},{4,5},{5,6},{6,7},{7,4},{8,9},{9,10},{10,1... | collective-permute-start | bytes 393224 | tf_op jit(solution)/shard_map/ppermute | solution.py:23

commit v4 on v3

v4 whole, which is shorter than its diff:
```python
import functools

import jax
import jax.numpy as jnp
from jax import lax
from jax.experimental import pallas as pl
from jax.experimental.pallas import tpu as pltpu
from jax.sharding import Mesh, PartitionSpec as P

inv_temp = 50.0
YL, CORES, X = 2, 2, 4
LANES = 128
STATS = 8
CHIPS = ("yl", "z")
f32, bf16, i32 = jnp.float32, jnp.bfloat16, jnp.int32
VMEM = pl.BlockSpec(memory_space=pltpu.VMEM)
SMEM = pl.BlockSpec(memory_space=pltpu.SMEM)
PARAMS = pltpu.CompilerParams(vmem_limit_bytes=16 * 1024 * 1024)


def shift(value, axis, by):
    if by == 0:
        return value
    size = lax.axis_size(axis)
    return lax.ppermute(value, axis, [(i, (i + by) % size) for i in range(size)])


def column_slice(value, which, count):
    width = value.shape[1] // count
    return lax.dynamic_slice_in_dim(value, which % count * width, width, 1)


def hits(positive, place, shape):
    return lax.broadcasted_iota(i32, shape, 0) + place == positive


def send_kernel(teacher_rows, positives, queries, out):
    own_rows, depth = queries.shape
    shape = (own_rows, out.shape[2] - depth)
    row, column = lax.broadcasted_iota(i32, shape, 0), lax.broadcasted_iota(i32, shape, 1)
    codes = jnp.zeros(shape, i32)
    for r in range(own_rows):
        positive = positives[0, r]
        for c, code in enumerate((teacher_rows[0, r], lax.shift_right_logical(positive, 8), positive & 255)):
            codes = jnp.where((row == r) & (column == c), code, codes)
    codes = codes.astype(f32).astype(bf16)
    for chip in range(out.shape[0]):
        out[chip, :, :depth] = queries[...]
        out[chip, :, depth:] = codes


def score_kernel(places, query, passages, passages_other, teacher, teacher_other, scores, logits, positives, stats):
    depth = passages.shape[1]
    rows = query.shape[0]
    codes = query[:, depth:].astype(f32).T
    row_index = codes[0:1].astype(i32)
    positive = codes[1:2].astype(i32) * 256 + codes[2:3].astype(i32)
    positives[...] = positive
    pick = (lax.broadcasted_iota(i32, (teacher.shape[0], rows), 0) == row_index).astype(f32)
    parts = []
    for half, (block, table) in enumerate(((passages, teacher), (passages_other, teacher_other))):
        s = inv_temp * lax.dot_general(
            block[...], query[:, :depth], (((1,), (1,)), ((), ())), preferred_element_type=f32
        )
        t = lax.dot_general(
            table[...], pick, (((0,), (0,)), ((), ())),
            precision=lax.Precision.HIGHEST, preferred_element_type=f32,
        )
        scores[half] = s
        logits[half] = t
        parts.append((s, t, hits(positive, places[half], s.shape)))
    top_s, top_t = (jnp.maximum(*[jnp.max(p[i], axis=0, keepdims=True) for p in parts]) for i in (0, 1))
    sums = []
    for s, t, hot in parts:
        below_s, below_t = s - top_s, t - top_t
        weight = jnp.exp(below_t)
        values = (jnp.exp(below_s), weight, weight * (below_t - below_s), jnp.where(hot, s, 0.0))
        sums.append([jnp.sum(v, axis=0, keepdims=True) for v in values])
    sums = [a + b for a, b in zip(*sums)]
    whole = jnp.concatenate([top_s, top_t] + sums + [jnp.zeros((STATS - 6, rows), f32)], axis=0)
    stats[...] = jnp.broadcast_to(whole[None], stats.shape)


def grad_kernel(places, scores, logits, positives, stats, grads, grads_other, losses):
    tops_s, tops_t, sums_s, sums_t, cross, hit = (stats[:, i, :] for i in range(6))
    top_s, top_t = jnp.max(tops_s, axis=0, keepdims=True), jnp.max(tops_t, axis=0, keepdims=True)
    lower_s, lower_t = tops_s - top_s, tops_t - top_t
    total_s = jnp.sum(jnp.exp(lower_s) * sums_s, axis=0, keepdims=True)
    weight_t = jnp.exp(lower_t)
    total_t = jnp.sum(weight_t * sums_t, axis=0, keepdims=True)
    cross = jnp.sum(weight_t * (cross + (lower_t - lower_s) * sums_t), axis=0, keepdims=True)
    log_s = jnp.log(total_s)
    own = jnp.sum(hit, axis=0, keepdims=True)
    losses[...] = cross / total_t - jnp.log(total_t) + log_s - (own - top_s - log_s)
    scale_s, scale_t = 2.0 * inv_temp / total_s, inv_temp / total_t
    for half, out in enumerate((grads, grads_other)):
        hot = hits(positives[...], places[half], out.shape)
        out[...] = (
            jnp.exp(scores[half] - top_s) * scale_s
            - jnp.exp(logits[half] - top_t) * scale_t
            - jnp.where(hot, inv_temp, 0.0)
        ).astype(bf16)


def query_kernel(grads, grads_other, passages, passages_other, out):
    total = 0.0
    for g, p in ((grads, passages), (grads_other, passages_other)):
        total += lax.dot_general(g[...], p[...], (((0,), (0,)), ((), ())), preferred_element_type=f32)
    out[...] = total.astype(bf16)


def passage_kernel(groups, yh, *refs):
    grads, query, query_other = (refs[k * groups : (k + 1) * groups] for k in range(3))
    outs = refs[3 * groups :]
    width = outs[0].shape[1]
    for i, out in enumerate(outs):
        columns = pl.ds(pl.multiple_of(lax.rem(yh[0] + i, len(outs)) * width, width), width)
        total = jnp.zeros(out.shape, f32)
        for g, own, other in zip(grads, query, query_other):
            total += jnp.dot(g[0], own[:, columns], preferred_element_type=f32)
            total += jnp.dot(g[1], other[:, columns], preferred_element_type=f32)
        out[...] = total.astype(bf16)


def per_device(queries, passages, teacher, teacher_rows, positives):
    own_rows, depth = queries.shape[1:]
    block_rows = passages.shape[0]
    chips = lax.axis_size("yl") * lax.axis_size("z")
    x_size, yh_size = lax.axis_size("x"), lax.axis_size("yh")
    rows = chips * own_rows
    chip = lax.axis_index("yl") * lax.axis_size("z") + lax.axis_index("z")
    core, x, yh = lax.axis_index("core"), lax.axis_index("x"), lax.axis_index("yh")
    places = ((chip * CORES + jnp.stack([core, 1 - core])) * block_rows).astype(i32)

    sent = pl.pallas_call(
        send_kernel,
        out_shape=jax.ShapeDtypeStruct((chips, own_rows, depth + LANES), bf16),
        in_specs=[SMEM, SMEM, VMEM],
        out_specs=VMEM,
        compiler_params=PARAMS,
    )(teacher_rows, positives, queries[0])
    passages_other, teacher_other = shift(passages, "core", 1), shift(teacher[0], "core", 1)
    query = lax.all_to_all(sent, CHIPS, 0, 0, tiled=True).reshape(rows, depth + LANES)

    scores, logits, positive, stats = pl.pallas_call(
        score_kernel,
        out_shape=(
            jax.ShapeDtypeStruct((CORES, block_rows, rows), f32),
            jax.ShapeDtypeStruct((CORES, block_rows, rows), f32),
            jax.ShapeDtypeStruct((1, rows), i32),
            jax.ShapeDtypeStruct((chips, STATS, rows), f32),
        ),
        in_specs=[SMEM] + [VMEM] * 5,
        out_specs=(VMEM,) * 4,
        compiler_params=PARAMS,
    )(places, query, passages, passages_other, teacher[0], teacher_other)
    query, stats = lax.optimization_barrier((query, stats))
    columns = [shift(column_slice(query[:, :depth], x + d, x_size), "x", d) for d in range(x_size)]
    stats = lax.all_to_all(stats, CHIPS, 0, 0, tiled=True)
    stats, columns = lax.optimization_barrier((stats, columns))

    grads, grads_other, losses = pl.pallas_call(
        grad_kernel,
        out_shape=(
            jax.ShapeDtypeStruct((block_rows, rows), bf16),
            jax.ShapeDtypeStruct((block_rows, rows), bf16),
            jax.ShapeDtypeStruct((1, rows), f32),
        ),
        in_specs=[SMEM] + [VMEM] * 4,
        out_specs=(VMEM,) * 3,
        compiler_params=PARAMS,
    )(places, scores, logits, positive, stats)
    loss = lax.dynamic_slice_in_dim(losses[0], chip * own_rows, own_rows)

    grads_back = shift(grads_other, "core", 1)
    columns_other = shift(jnp.stack(columns), "core", 1)
    query_part = pl.pallas_call(
        query_kernel,
        out_shape=jax.ShapeDtypeStruct((rows, depth), bf16),
        in_specs=[VMEM] * 4,
        out_specs=VMEM,
        compiler_params=PARAMS,
    )(grads, grads_other, passages, passages_other)
    query_parts = lax.all_to_all(query_part.reshape(chips, own_rows, depth), CHIPS, 0, 0, tiled=True)
    query_total = jnp.sum(query_parts.astype(f32), axis=0)

    block_grads = jnp.stack([grads, grads_back])
    block_grads = [shift(block_grads, "x", d) for d in range(x_size)]
    width = depth // (x_size * yh_size)
    parts = pl.pallas_call(
        functools.partial(passage_kernel, x_size),
        out_shape=(jax.ShapeDtypeStruct((block_rows, width), bf16),) * yh_size,
        in_specs=[SMEM] + [VMEM] * (3 * x_size),
        out_specs=(VMEM,) * yh_size,
        compiler_params=PARAMS,
    )(yh.astype(i32)[None], *block_grads, *columns, *columns_other)
    parts = [shift(part, "yh", d) for d, part in enumerate(parts)]
    passage_total = sum(v.astype(f32) for v in parts)
    return loss[None], query_total.astype(bf16)[None], passage_total.astype(bf16)


def solution(mesh):
    blk, qgroup = mesh.devices.shape
    split = Mesh(
        mesh.devices.reshape(YL, blk // (YL * CORES), CORES, X, qgroup // X),
        ("yl", "z", "core", "x", "yh"),
    )
    blk, qgroup = ("yl", "z", "core"), ("x", "yh")
    in_specs = (
        P(qgroup, blk, None),
        P(blk, None),
        P(qgroup, None, blk),
        P(qgroup, blk),
        P(qgroup, blk),
    )
    out_specs = (P(qgroup, blk), P(qgroup, blk, None), P(blk, qgroup))
    return jax.shard_map(per_device, mesh=split, in_specs=in_specs, out_specs=out_specs, check_vma=False)
```

time: 129 us -> 131 us (1.016)
  the two profiles are of different devices: /device:TPU:9 before, /device:TPU:15 now
where the time goes in v4:
time: 131 us; the launch traced here: 130 us
  starting transfers between devices  58.6 us (45%)
  waiting for transfers between devices  40.5 us (31%)
  blocking collectives  12.6 us (10%)
  Pallas kernels  9.33 us (7%)
  local copies, waits for them, and re-layouts  5.19 us (4%)
  other arithmetic  2.96 us (2%)
    ppermute x13, starting transfers between devices, shift(): lax.ppermute(value, axis, [(i, (i + by) % size) for i in range(size)])  42 us
    all_to_all x1, waiting for transfers between devices, per_device(): lax.all_to_all(sent, CHIPS, 0, 0, tiled=True).reshape(rows, depth + LANES)  23.5 us
    ppermute x13, waiting for transfers between devices, shift(): lax.ppermute(value, axis, [(i, (i + by) % size) for i in range(size)])  17 us
    all_to_all x1, blocking collectives, per_device(): stats = lax.all_to_all(stats, CHIPS, 0, 0, tiled=True)  12.6 us
    all_to_all x1, starting transfers between devices, per_device(): lax.all_to_all(sent, CHIPS, 0, 0, tiled=True).reshape(rows, depth + LANES)  11.2 us
    all_to_all x1, starting transfers between devices, per_device(): lax.all_to_all(query_part.reshape(chips, own_rows, depth), CHIPS, 0, 0, t...  5.33 us
    pallas_call x1, Pallas kernels, per_device(): pl.pallas_call(score_kernel, out_shape=(jax.ShapeDtypeStruct((CORES, bloc...  3.43 us
    pallas_call x1, Pallas kernels, per_device(): pl.pallas_call(query_kernel, out_shape=jax.ShapeDtypeStruct((rows, depth)...  3.33 us
  transfers between devices with their start and end apart: 15, of which 7 were waited for; matrix products, arithmetic and copies ran while one was open for 2% of the time, Pallas kernels for 1%

profile of v4, /device:TPU:15, one launch (start us, length us, event | category | flops | bytes accessed | tf_op | source)
XLA Modules:
  0.0 130.1 jit_solution(4355802786486419678)
XLA Ops:
  0.6 0.0 copy-start
  0.6 0.0 copy-start.2
  0.7 2.7 %collective-permute-start = (bf16[256,4096]{1,0:T(8,128)(2,1)}, bf16[256,4096]{1,0:T(8,128)(2,1)}, u32[]{:S(2)}, u32[]{:S(2)}) collective-permute-start(bf16[256,4096]{1,0:T(8,128)(2,1)} %passages.3), channel_id=1, source_target_pairs={{0,16},{16,0},{1,17},{17,1},{2,18},{18,2},{3,19},{19,3},{4,20},{20... | collective-permute-start | bytes 6291464 | tf_op jit(solution)/shard_map/ppermute | solution.py:25
  3.4 0.0 copy-start.3
  3.4 0.8 copy-done.3
  4.2 0.0 copy-start.4
  4.2 0.7 copy-done.4
  4.9 0.0 copy-start.5
  4.9 0.7 copy-done.5
  5.5 0.6 shard_map.76
  6.2 0.0 copy-start.1
  6.2 1.0 copy-done.1
  7.2 11.2 %all-to-all-start = ((bf16[16,8,4224]{2,1,0:T(8,128)(2,1)}), bf16[16,8,4224]{2,1,0:T(8,128)(2,1)S(1)}, u32[]{:S(2)}, u32[]{:S(2)}) async-start(bf16[16,8,4224]{2,1,0:T(8,128)(2,1)} %copy-done.1), calls=%async_computation | async-start | bytes 2162688 | tf_op jit(solution)/shard_map/all_to_all | solution.py:143
  18.4 0.0 copy-done.2
  18.4 2.5 %collective-permute-start.1 = (f32[256,256]{1,0:T(8,128)S(1)}, f32[256,256]{1,0:T(8,128)}, u32[]{:S(2)}, u32[]{:S(2)}) collective-permute-start(f32[256,256]{1,0:T(8,128)S(1)} %bitcast.29), channel_id=1, source_target_pairs={{0,16},{16,0},{1,17},{17,1},{2,18},{18,2},{3,19},{19,3},{4,20},{20... | collective-permute-start | bytes 786440 | tf_op jit(solution)/shard_map/ppermute | solution.py:25
  21.0 0.1 fusion.places
  21.0 1.1 collective-permute-done.1.teacher_other
  22.2 23.5 %all-to-all-done = bf16[16,8,4224]{2,1,0:T(8,128)(2,1)S(1)} async-done(((bf16[16,8,4224]{2,1,0:T(8,128)(2,1)}), bf16[16,8,4224]{2,1,0:T(8,128)(2,1)S(1)}, u32[]{:S(2)}, u32[]{:S(2)}) %all-to-all-start) | async-done | bytes 1081376 | tf_op jit(solution)/shard_map/all_to_all | solution.py:143
  45.7 0.0 collective-permute-done.passages_other
  45.7 0.0 copy-done
  45.7 3.4 %shard_map.77 = (f32[2,256,128]{2,1,0:T(8,128)S(1)}, f32[2,256,128]{2,1,0:T(8,128)S(1)}, s32[1,128]{1,0:T(1,128)S(1)}, f32[16,8,128]{2,1,0:T(8,128)S(1)}) custom-call(s32[2]{0:T(128)S(1)} %fusion.places, bf16[128,4224]{1,0:T(8,128)(2,1)S(1)} %bitcast.22, bf16[256,4096]{1,0:T(8,128)(2,1)S(1)} %copy-done, ...), custom_call_target="tpu_custom_call" | custom-call | tf_op jit(solution)/shard_map/pallas_call | solution.py:145
  49.1 0.1 slice.2
  49.2 0.1 constant_dynamic-slice_fusion.1
  49.3 2.1 %collective-permute-start.2 = (bf16[128,1024]{1,0:T(8,128)(2,1)S(1)}, bf16[128,1024]{1,0:T(8,128)(2,1)S(1)}, u32[]{:S(2)}, u32[]{:S(2)}) collective-permute-start(bf16[128,1024]{1,0:T(8,128)(2,1)S(1)} %get-tuple-element.45), channel_id=1, source_target_pairs={{0,4},{4,8},{8,12},{12,0},{1,5},{5,9},{9,13},{13,1},{2,6},{6,10},{... | collective-permute-start | bytes 786440 | tf_op jit(solution)/shard_map/ppermute | solution.py:25
  51.5 4.0 %collective-permute-start.3 = (bf16[128,1024]{1,0:T(8,128)(2,1)S(1)}, bf16[128,1024]{1,0:T(8,128)(2,1)S(1)}, u32[]{:S(2)}, u32[]{:S(2)}) collective-permute-start(bf16[128,1024]{1,0:T(8,128)(2,1)S(1)} %get-tuple-element.44), channel_id=1, source_target_pairs={{0,8},{4,12},{8,0},{12,4},{1,9},{5,13},{9,1},{13,5},{2,10},{6,14},... | collective-permute-start | bytes 786440 | tf_op jit(solution)/shard_map/ppermute | solution.py:25
  55.5 1.9 %collective-permute-start.4 = (bf16[128,1024]{1,0:T(8,128)(2,1)S(1)}, bf16[128,1024]{1,0:T(8,128)(2,1)S(1)}, u32[]{:S(2)}, u32[]{:S(2)}) collective-permute-start(bf16[128,1024]{1,0:T(8,128)(2,1)S(1)} %get-tuple-element.43), channel_id=1, source_target_pairs={{0,12},{4,0},{8,4},{12,8},{1,13},{5,1},{9,5},{13,9},{2,14},{6,2},{... | collective-permute-start | bytes 786440 | tf_op jit(solution)/shard_map/ppermute | solution.py:25
  57.4 12.6 %all_to_all.15.stats = f32[16,8,128]{2,1,0:T(8,128)S(1)} all-to-all(f32[16,8,128]{2,1,0:T(8,128)S(1)} %get-tuple-element.25), channel_id=1, replica_groups=mesh['yl'=2,'z'=8,'core'=2,'x'=4,'yh'=4] {'yl','z'}, dimensions={0} | all-to-all | bytes 131072 | tf_op jit(solution)/shard_map/all_to_all | solution.py:159
  70.0 0.0 collective-permute-done.2.refs_5_
  70.0 0.0 collective-permute-done.3.refs_6_
  70.0 0.0 collective-permute-done.4.refs_7_
  70.0 0.7 shard_map.78
  70.8 3.3 %shard_map.79 = bf16[128,4096]{1,0:T(8,128)(2,1)} custom-call(bf16[256,128]{1,0:T(8,128)(2,1)S(1)} %get-tuple-element.29.grads, bf16[256,128]{1,0:T(8,128)(2,1)S(1)} %get-tuple-element.30.grads_other, bf16[256,4096]{1,0:T(8,128)(2,1)S(1)} %copy-done, bf16[256,4096]{1,0:T(8,128)(2,1)} %collective-permute-done.passages_other), custom_call_target="tpu_custom_call" | custom-call | tf_op jit(solution)/shard_map/pallas_call | solution.py:177
  74.1 5.3 %all-to-all-start.2 = ((bf16[16,8,4096]{2,1,0:T(8,128)(2,1)}), bf16[16,8,4096]{2,1,0:T(8,128)(2,1)}, u32[]{:S(2)}, u32[]{:S(2)}) async-start(bf16[16,8,4096]{2,1,0:T(8,128)(2,1)} %bitcast.5), calls=%async_computation.2 | async-start | bytes 2097152 | tf_op jit(solution)/shard_map/all_to_all | solution.py:184
  79.4 0.1 pad_maximum_fusion
  79.6 4.5 %collective-permute-start.9 = (bf16[4,128,1024]{2,1,0:T(8,128)(2,1)S(1)}, bf16[4,128,1024]{2,1,0:T(8,128)(2,1)}, u32[]{:S(2)}, u32[]{:S(2)}) collective-permute-start(bf16[4,128,1024]{2,1,0:T(8,128)(2,1)S(1)} %pad_maximum_fusion), channel_id=1, source_target_pairs={{0,16},{16,0},{1,17},{17,1},{2,18},{18,2},{3,19},{19,3},{4,20},{20... | collective-permute-start | bytes 3145736 | tf_op jit(solution)/shard_map/ppermute | solution.py:25
  84.1 1.9 %collective-permute-start.5 = (bf16[256,128]{1,0:T(8,128)(2,1)S(1)}, bf16[256,128]{1,0:T(8,128)(2,1)S(1)}, u32[]{:S(2)}, u32[]{:S(2)}) collective-permute-start(bf16[256,128]{1,0:T(8,128)(2,1)S(1)} %get-tuple-element.30.grads_other), channel_id=1, source_target_pairs={{0,16},{16,0},{1,17},{17,1},{2,18},{18,2},{3,19},{19,3},{4,20},{20... | collective-permute-start | bytes 196616 | tf_op jit(solution)/shard_map/ppermute | solution.py:25
  86.0 1.2 collective-permute-done.5
  87.3 4.8 %collective-permute-start.6 = (bf16[2,256,128]{2,1,0:T(8,128)(2,1)S(1)}, bf16[2,256,128]{2,1,0:T(8,128)(2,1)S(1)}, u32[]{:S(2)}, u32[]{:S(2)}) collective-permute-start(bf16[2,256,128]{2,1,0:T(8,128)(2,1)S(1)} %pad_maximum_fusion.1.refs_0_), channel_id=1, source_target_pairs={{0,4},{4,8},{8,12},{12,0},{1,5},{5,9},{9,13},{13,1},{2,6},{6,10},{... | collective-permute-start | bytes 393224 | tf_op jit(solution)/shard_map/ppermute | solution.py:25
  92.1 1.9 %collective-permute-start.7 = (bf16[2,256,128]{2,1,0:T(8,128)(2,1)S(1)}, bf16[2,256,128]{2,1,0:T(8,128)(2,1)S(1)}, u32[]{:S(2)}, u32[]{:S(2)}) collective-permute-start(bf16[2,256,128]{2,1,0:T(8,128)(2,1)S(1)} %pad_maximum_fusion.1.refs_0_), channel_id=1, source_target_pairs={{0,8},{4,12},{8,0},{12,4},{1,9},{5,13},{9,1},{13,5},{2,10},{6,14},... | collective-permute-start | bytes 393224 | tf_op jit(solution)/shard_map/ppermute | solution.py:25
  94.1 2.8 %collective-permute-start.8 = (bf16[2,256,128]{2,1,0:T(8,128)(2,1)S(1)}, bf16[2,256,128]{2,1,0:T(8,128)(2,1)S(1)}, u32[]{:S(2)}, u32[]{:S(2)}) collective-permute-start(bf16[2,256,128]{2,1,0:T(8,128)(2,1)S(1)} %pad_maximum_fusion.1.refs_0_), channel_id=1, source_target_pairs={{0,12},{4,0},{8,4},{12,8},{1,13},{5,1},{9,5},{13,9},{2,14},{6,2},{... | collective-permute-start | bytes 393224 | tf_op jit(solution)/shard_map/ppermute | solution.py:25
  96.8 0.0 collective-permute-done.9
  96.9 1.3 slice_bitcast_fusion
  98.1 0.0 collective-permute-done.6.refs_1_
  98.1 2.1 %collective-permute-done.7.refs_2_ = bf16[2,256,128]{2,1,0:T(8,128)(2,1)S(1)} collective-permute-done((bf16[2,256,128]{2,1,0:T(8,128)(2,1)S(1)}, bf16[2,256,128]{2,1,0:T(8,128)(2,1)S(1)}, u32[]{:S(2)}, u32[]{:S(2)}) %collective-permute-start.7) | collective-permute-done | bytes 131104 | tf_op jit(solution)/shard_map/ppermute | solution.py:25
  100.2 3.3 %collective-permute-done.8.refs_3_ = bf16[2,256,128]{2,1,0:T(8,128)(2,1)S(1)} collective-permute-done((bf16[2,256,128]{2,1,0:T(8,128)(2,1)S(1)}, bf16[2,256,128]{2,1,0:T(8,128)(2,1)S(1)}, u32[]{:S(2)}, u32[]{:S(2)}) %collective-permute-start.8) | collective-permute-done | bytes 131104 | tf_op jit(solution)/shard_map/ppermute | solution.py:25
  103.6 1.2 shard_map.80
  104.8 5.0 %collective-permute-start.12 = (bf16[256,256]{1,0:T(8,128)(2,1)S(1)}, bf16[256,256]{1,0:T(8,128)(2,1)S(1)}, u32[]{:S(2)}, u32[]{:S(2)}) collective-permute-start(bf16[256,256]{1,0:T(8,128)(2,1)S(1)} %get-tuple-element.38), channel_id=1, source_target_pairs={{0,3},{1,0},{2,1},{3,2},{4,7},{5,4},{6,5},{7,6},{8,11},{9,8},{10,9... | collective-permute-start | bytes 393224 | tf_op jit(solution)/shard_map/ppermute | solution.py:25
  109.8 4.4 %collective-permute-start.11 = (bf16[256,256]{1,0:T(8,128)(2,1)S(1)}, bf16[256,256]{1,0:T(8,128)(2,1)S(1)}, u32[]{:S(2)}, u32[]{:S(2)}) collective-permute-start(bf16[256,256]{1,0:T(8,128)(2,1)S(1)} %get-tuple-element.37), channel_id=1, source_target_pairs={{0,2},{1,3},{2,0},{3,1},{4,6},{5,7},{6,4},{7,5},{8,10},{9,11},{10,... | collective-permute-start | bytes 393224 | tf_op jit(solution)/shard_map/ppermute | solution.py:25
  114.3 3.3 %collective-permute-start.10 = (bf16[256,256]{1,0:T(8,128)(2,1)S(1)}, bf16[256,256]{1,0:T(8,128)(2,1)S(1)}, u32[]{:S(2)}, u32[]{:S(2)}) collective-permute-start(bf16[256,256]{1,0:T(8,128)(2,1)S(1)} %get-tuple-element.36), channel_id=1, source_target_pairs={{0,1},{1,2},{2,3},{3,0},{4,5},{5,6},{6,7},{7,4},{8,9},{9,10},{10,1... | collective-permute-start | bytes 393224 | tf_op jit(solution)/shard_map/ppermute | solution.py:25
  117.6 0.6 constant_dynamic-slice_fusion
  118.2 0.0 collective-permute-done.12
  118.2 3.5 %collective-permute-done.11 = bf16[256,256]{1,0:T(8,128)(2,1)S(1)} collective-permute-done((bf16[256,256]{1,0:T(8,128)(2,1)S(1)}, bf16[256,256]{1,0:T(8,128)(2,1)S(1)}, u32[]{:S(2)}, u32[]{:S(2)}) %collective-permute-start.11) | collective-permute-done | bytes 131104 | tf_op jit(solution)/shard_map/ppermute | solution.py:25
  121.7 5.6 %collective-permute-done.10 = bf16[256,256]{1,0:T(8,128)(2,1)S(1)} collective-permute-done((bf16[256,256]{1,0:T(8,128)(2,1)S(1)}, bf16[256,256]{1,0:T(8,128)(2,1)S(1)}, u32[]{:S(2)}, u32[]{:S(2)}) %collective-permute-start.10) | collective-permute-done | bytes 131104 | tf_op jit(solution)/shard_map/ppermute | solution.py:25
  127.3 0.7 add_convert_fusion
  128.0 0.0 all-to-all-done.2
  128.0 2.0 %reduce_sum.12 = bf16[8,4096]{1,0:T(8,128)(2,1)} reduce(bf16[16,8,4096]{2,1,0:T(8,128)(2,1)} %all-to-all-done.2, bf16[]{:T(256)} %constant.67.clone.1), dimensions={0}, to_apply=%region_0.1 | reduce | flops 491520 | bytes 1114114 | tf_op jit(solution)/shard_map/reduce_sum | solution.py:185
  (1 shorter events, 0.0 us)
Async XLA Ops:
  0.6 45.1 %copy-start = (bf16[256,4096]{1,0:T(8,128)(2,1)S(1)}, bf16[256,4096]{1,0:T(8,128)(2,1)}, u32[]{:S(2)}) copy-start(bf16[256,4096]{1,0:T(8,128)(2,1)} %passages.3) | copy-start | bytes 6291460
  0.6 17.8 %copy-start.2 = (f32[1,256,256]{2,1,0:T(8,128)S(1)}, f32[1,256,256]{2,1,0:T(8,128)}, u32[]{:S(2)}) copy-start(f32[1,256,256]{2,1,0:T(8,128)} %param.7) | copy-start | bytes 786436
  0.7 45.0 %collective-permute-start = (bf16[256,4096]{1,0:T(8,128)(2,1)}, bf16[256,4096]{1,0:T(8,128)(2,1)}, u32[]{:S(2)}, u32[]{:S(2)}) collective-permute-start(bf16[256,4096]{1,0:T(8,128)(2,1)} %passages.3), channel_id=1, source_target_pairs={{0,16},{16,0},{1,17},{17,1},{2,18},{18,2},{3,19},{19,3},{4,20},{20... | collective-permute-start | bytes 6291464 | tf_op jit(solution)/shard_map/ppermute | solution.py:25
  3.4 0.8 copy-start.3
  4.2 0.7 copy-start.4
  4.9 0.7 copy-start.5
  6.2 1.0 copy-start.1
  7.2 38.5 %all-to-all-start = ((bf16[16,8,4224]{2,1,0:T(8,128)(2,1)}), bf16[16,8,4224]{2,1,0:T(8,128)(2,1)S(1)}, u32[]{:S(2)}, u32[]{:S(2)}) async-start(bf16[16,8,4224]{2,1,0:T(8,128)(2,1)} %copy-done.1), calls=%async_computation | async-start | bytes 2162688 | tf_op jit(solution)/shard_map/all_to_all | solution.py:143
  18.4 3.8 %collective-permute-start.1 = (f32[256,256]{1,0:T(8,128)S(1)}, f32[256,256]{1,0:T(8,128)}, u32[]{:S(2)}, u32[]{:S(2)}) collective-permute-start(f32[256,256]{1,0:T(8,128)S(1)} %bitcast.29), channel_id=1, source_target_pairs={{0,16},{16,0},{1,17},{17,1},{2,18},{18,2},{3,19},{19,3},{4,20},{20... | collective-permute-start | bytes 786440 | tf_op jit(solution)/shard_map/ppermute | solution.py:25
  49.3 20.7 %collective-permute-start.2 = (bf16[128,1024]{1,0:T(8,128)(2,1)S(1)}, bf16[128,1024]{1,0:T(8,128)(2,1)S(1)}, u32[]{:S(2)}, u32[]{:S(2)}) collective-permute-start(bf16[128,1024]{1,0:T(8,128)(2,1)S(1)} %get-tuple-element.45), channel_id=1, source_target_pairs={{0,4},{4,8},{8,12},{12,0},{1,5},{5,9},{9,13},{13,1},{2,6},{6,10},{... | collective-permute-start | bytes 786440 | tf_op jit(solution)/shard_map/ppermute | solution.py:25
  51.5 18.6 %collective-permute-start.3 = (bf16[128,1024]{1,0:T(8,128)(2,1)S(1)}, bf16[128,1024]{1,0:T(8,128)(2,1)S(1)}, u32[]{:S(2)}, u32[]{:S(2)}) collective-permute-start(bf16[128,1024]{1,0:T(8,128)(2,1)S(1)} %get-tuple-element.44), channel_id=1, source_target_pairs={{0,8},{4,12},{8,0},{12,4},{1,9},{5,13},{9,1},{13,5},{2,10},{6,14},... | collective-permute-start | bytes 786440 | tf_op jit(solution)/shard_map/ppermute | solution.py:25
  55.5 14.5 %collective-permute-start.4 = (bf16[128,1024]{1,0:T(8,128)(2,1)S(1)}, bf16[128,1024]{1,0:T(8,128)(2,1)S(1)}, u32[]{:S(2)}, u32[]{:S(2)}) collective-permute-start(bf16[128,1024]{1,0:T(8,128)(2,1)S(1)} %get-tuple-element.43), channel_id=1, source_target_pairs={{0,12},{4,0},{8,4},{12,8},{1,13},{5,1},{9,5},{13,9},{2,14},{6,2},{... | collective-permute-start | bytes 786440 | tf_op jit(solution)/shard_map/ppermute | solution.py:25
  74.1 54.0 %all-to-all-start.2 = ((bf16[16,8,4096]{2,1,0:T(8,128)(2,1)}), bf16[16,8,4096]{2,1,0:T(8,128)(2,1)}, u32[]{:S(2)}, u32[]{:S(2)}) async-start(bf16[16,8,4096]{2,1,0:T(8,128)(2,1)} %bitcast.5), calls=%async_computation.2 | async-start | bytes 2097152 | tf_op jit(solution)/shard_map/all_to_all | solution.py:184
  79.6 17.3 %collective-permute-start.9 = (bf16[4,128,1024]{2,1,0:T(8,128)(2,1)S(1)}, bf16[4,128,1024]{2,1,0:T(8,128)(2,1)}, u32[]{:S(2)}, u32[]{:S(2)}) collective-permute-start(bf16[4,128,1024]{2,1,0:T(8,128)(2,1)S(1)} %pad_maximum_fusion), channel_id=1, source_target_pairs={{0,16},{16,0},{1,17},{17,1},{2,18},{18,2},{3,19},{19,3},{4,20},{20... | collective-permute-start | bytes 3145736 | tf_op jit(solution)/shard_map/ppermute | solution.py:25
  84.1 3.1 %collective-permute-start.5 = (bf16[256,128]{1,0:T(8,128)(2,1)S(1)}, bf16[256,128]{1,0:T(8,128)(2,1)S(1)}, u32[]{:S(2)}, u32[]{:S(2)}) collective-permute-start(bf16[256,128]{1,0:T(8,128)(2,1)S(1)} %get-tuple-element.30.grads_other), channel_id=1, source_target_pairs={{0,16},{16,0},{1,17},{17,1},{2,18},{18,2},{3,19},{19,3},{4,20},{20... | collective-permute-start | bytes 196616 | tf_op jit(solution)/shard_map/ppermute | solution.py:25
  87.3 10.9 %collective-permute-start.6 = (bf16[2,256,128]{2,1,0:T(8,128)(2,1)S(1)}, bf16[2,256,128]{2,1,0:T(8,128)(2,1)S(1)}, u32[]{:S(2)}, u32[]{:S(2)}) collective-permute-start(bf16[2,256,128]{2,1,0:T(8,128)(2,1)S(1)} %pad_maximum_fusion.1.refs_0_), channel_id=1, source_target_pairs={{0,4},{4,8},{8,12},{12,0},{1,5},{5,9},{9,13},{13,1},{2,6},{6,10},{... | collective-permute-start | bytes 393224 | tf_op jit(solution)/shard_map/ppermute | solution.py:25
  92.1 8.1 %collective-permute-start.7 = (bf16[2,256,128]{2,1,0:T(8,128)(2,1)S(1)}, bf16[2,256,128]{2,1,0:T(8,128)(2,1)S(1)}, u32[]{:S(2)}, u32[]{:S(2)}) collective-permute-start(bf16[2,256,128]{2,1,0:T(8,128)(2,1)S(1)} %pad_maximum_fusion.1.refs_0_), channel_id=1, source_target_pairs={{0,8},{4,12},{8,0},{12,4},{1,9},{5,13},{9,1},{13,5},{2,10},{6,14},... | collective-permute-start | bytes 393224 | tf_op jit(solution)/shard_map/ppermute | solution.py:25
  94.1 9.5 %collective-permute-start.8 = (bf16[2,256,128]{2,1,0:T(8,128)(2,1)S(1)}, bf16[2,256,128]{2,1,0:T(8,128)(2,1)S(1)}, u32[]{:S(2)}, u32[]{:S(2)}) collective-permute-start(bf16[2,256,128]{2,1,0:T(8,128)(2,1)S(1)} %pad_maximum_fusion.1.refs_0_), channel_id=1, source_target_pairs={{0,12},{4,0},{8,4},{12,8},{1,13},{5,1},{9,5},{13,9},{2,14},{6,2},{... | collective-permute-start | bytes 393224 | tf_op jit(solution)/shard_map/ppermute | solution.py:25
  104.8 13.3 %collective-permute-start.12 = (bf16[256,256]{1,0:T(8,128)(2,1)S(1)}, bf16[256,256]{1,0:T(8,128)(2,1)S(1)}, u32[]{:S(2)}, u32[]{:S(2)}) collective-permute-start(bf16[256,256]{1,0:T(8,128)(2,1)S(1)} %get-tuple-element.38), channel_id=1, source_target_pairs={{0,3},{1,0},{2,1},{3,2},{4,7},{5,4},{6,5},{7,6},{8,11},{9,8},{10,9... | collective-permute-start | bytes 393224 | tf_op jit(solution)/shard_map/ppermute | solution.py:25
  109.8 11.8 %collective-permute-start.11 = (bf16[256,256]{1,0:T(8,128)(2,1)S(1)}, bf16[256,256]{1,0:T(8,128)(2,1)S(1)}, u32[]{:S(2)}, u32[]{:S(2)}) collective-permute-start(bf16[256,256]{1,0:T(8,128)(2,1)S(1)} %get-tuple-element.37), channel_id=1, source_target_pairs={{0,2},{1,3},{2,0},{3,1},{4,6},{5,7},{6,4},{7,5},{8,10},{9,11},{10,... | collective-permute-start | bytes 393224 | tf_op jit(solution)/shard_map/ppermute | solution.py:25
  114.3 13.1 %collective-permute-start.10 = (bf16[256,256]{1,0:T(8,128)(2,1)S(1)}, bf16[256,256]{1,0:T(8,128)(2,1)S(1)}, u32[]{:S(2)}, u32[]{:S(2)}) collective-permute-start(bf16[256,256]{1,0:T(8,128)(2,1)S(1)} %get-tuple-element.36), channel_id=1, source_target_pairs={{0,1},{1,2},{2,3},{3,0},{4,5},{5,6},{6,7},{7,4},{8,9},{9,10},{10,1... | collective-permute-start | bytes 393224 | tf_op jit(solution)/shard_map/ppermute | solution.py:25

commit v5 on v4

--- a/solution.py
+++ b/solution.py
@@ -14,6 +14,7 @@
 CHIPS = ("yl", "z")
 f32, bf16, i32 = jnp.float32, jnp.bfloat16, jnp.int32
 VMEM = pl.BlockSpec(memory_space=pltpu.VMEM)
+ANY = pl.BlockSpec(memory_space=pl.ANY)
 SMEM = pl.BlockSpec(memory_space=pltpu.SMEM)
 PARAMS = pltpu.CompilerParams(vmem_limit_bytes=16 * 1024 * 1024)
 
@@ -34,19 +35,30 @@
     return lax.broadcasted_iota(i32, shape, 0) + place == positive
 
 
-def send_kernel(teacher_rows, positives, queries, out):
+def send_kernel(teacher_rows, positives, queries, out, rows_smem, positives_smem, buffer, sems):
     own_rows, depth = queries.shape
     shape = (own_rows, out.shape[2] - depth)
+    loads = [
+        pltpu.make_async_copy(teacher_rows, rows_smem, sems.at[0]),
+        pltpu.make_async_copy(positives, positives_smem, sems.at[1]),
+        pltpu.make_async_copy(queries, buffer.at[:, pl.ds(0, depth)], sems.at[2]),
+    ]
+    for load in loads:
+        load.start()
+    for load in loads:
+        load.wait()
     row, column = lax.broadcasted_iota(i32, shape, 0), lax.broadcasted_iota(i32, shape, 1)
     codes = jnp.zeros(shape, i32)
     for r in range(own_rows):
-        positive = positives[0, r]
-        for c, code in enumerate((teacher_rows[0, r], lax.shift_right_logical(positive, 8), positive & 255)):
+        positive = positives_smem[0, r]
+        for c, code in enumerate((rows_smem[0, r], lax.shift_right_logical(positive, 8), positive & 255)):
             codes = jnp.where((row == r) & (column == c), code, codes)
-    codes = codes.astype(f32).astype(bf16)
-    for chip in range(out.shape[0]):
-        out[chip, :, :depth] = queries[...]
-        out[chip, :, depth:] = codes
+    buffer[:, depth:] = codes.astype(f32).astype(bf16)
+    stores = [pltpu.make_async_copy(buffer, out.at[chip], sems.at[3 + chip]) for chip in range(out.shape[0])]
+    for store in stores:
+        store.start()
+    for store in stores:
+        store.wait()
 
 
 def score_kernel(places, query, passages, passages_other, teacher, teacher_other, scores, logits, positives, stats):
@@ -81,7 +93,7 @@
     stats[...] = jnp.broadcast_to(whole[None], stats.shape)
 
 
-def grad_kernel(places, scores, logits, positives, stats, grads, grads_other, losses):
+def grad_kernel(places, scores, logits, positives, stats, grads, grads_other, sent, losses):
     tops_s, tops_t, sums_s, sums_t, cross, hit = (stats[:, i, :] for i in range(6))
     top_s, top_t = jnp.max(tops_s, axis=0, keepdims=True), jnp.max(tops_t, axis=0, keepdims=True)
     lower_s, lower_t = tops_s - top_s, tops_t - top_t
@@ -95,11 +107,15 @@
     scale_s, scale_t = 2.0 * inv_temp / total_s, inv_temp / total_t
     for half, out in enumerate((grads, grads_other)):
         hot = hits(positives[...], places[half], out.shape)
-        out[...] = (
+        values = (
             jnp.exp(scores[half] - top_s) * scale_s
             - jnp.exp(logits[half] - top_t) * scale_t
             - jnp.where(hot, inv_temp, 0.0)
         ).astype(bf16)
+        out[...] = values
+        which = places[CORES + half]
+        for group in range(sent.shape[0] // CORES):
+            sent[group * CORES + which] = values
 
 
 def query_kernel(grads, grads_other, passages, passages_other, out):
@@ -109,17 +125,25 @@
     out[...] = total.astype(bf16)
 
 
-def passage_kernel(groups, yh, *refs):
-    grads, query, query_other = (refs[k * groups : (k + 1) * groups] for k in range(3))
-    outs = refs[3 * groups :]
+def passage_kernel(groups, position, grads, *refs):
+    x, core, yh = position[0], position[1], position[2]
+    query, query_other, outs = refs[:groups], refs[groups], refs[groups + 1 :]
     width = outs[0].shape[1]
     for i, out in enumerate(outs):
-        columns = pl.ds(pl.multiple_of(lax.rem(yh[0] + i, len(outs)) * width, width), width)
+        columns = pl.ds(pl.multiple_of(lax.rem(yh + i, len(outs)) * width, width), width)
         total = jnp.zeros(out.shape, f32)
-        for g, own, other in zip(grads, query, query_other):
-            total += jnp.dot(g[0], own[:, columns], preferred_element_type=f32)
-            total += jnp.dot(g[1], other[:, columns], preferred_element_type=f32)
+        for d in range(groups):
+            group = lax.rem(x + groups - d, groups) * CORES
+            total += jnp.dot(grads[group + core], query[d][:, columns], preferred_element_type=f32)
+            total += jnp.dot(grads[group + 1 - core], query_other[d, :, columns], preferred_element_type=f32)
         out[...] = total.astype(bf16)
+
+
+def sum_kernel(parts, out):
+    total = parts[0].astype(f32)
+    for i in range(1, parts.shape[0]):
+        total += parts[i].astype(f32)
+    out[...] = total.astype(bf16)
 
 
 def per_device(queries, passages, teacher, teacher_rows, positives):
@@ -130,15 +154,23 @@
     rows = chips * own_rows
     chip = lax.axis_index("yl") * lax.axis_size("z") + lax.axis_index("z")
     core, x, yh = lax.axis_index("core"), lax.axis_index("x"), lax.axis_index("yh")
-    places = ((chip * CORES + jnp.stack([core, 1 - core])) * block_rows).astype(i32)
+    cores = jnp.stack([core, 1 - core])
+    places = jnp.concatenate([(chip * CORES + cores) * block_rows, cores]).astype(i32)
 
     sent = pl.pallas_call(
         send_kernel,
         out_shape=jax.ShapeDtypeStruct((chips, own_rows, depth + LANES), bf16),
-        in_specs=[SMEM, SMEM, VMEM],
-        out_specs=VMEM,
+        in_specs=[ANY] * 3,
+        out_specs=ANY,
+        scratch_shapes=[
+            pltpu.SMEM((1, own_rows), i32),
+            pltpu.SMEM((1, own_rows), i32),
+            pltpu.VMEM((own_rows, depth + LANES), bf16),
+            pltpu.SemaphoreType.DMA((3 + chips,)),
+        ],
         compiler_params=PARAMS,
     )(teacher_rows, positives, queries[0])
+    sent, passages, teacher = lax.optimization_barrier((sent, passages, teacher))
     passages_other, teacher_other = shift(passages, "core", 1), shift(teacher[0], "core", 1)
     query = lax.all_to_all(sent, CHIPS, 0, 0, tiled=True).reshape(rows, depth + LANES)
 
@@ -157,46 +189,54 @@
     query, stats = lax.optimization_barrier((query, stats))
     columns = [shift(column_slice(query[:, :depth], x + d, x_size), "x", d) for d in range(x_size)]
     stats = lax.all_to_all(stats, CHIPS, 0, 0, tiled=True)
-    stats, columns = lax.optimization_barrier((stats, columns))
-
-    grads, grads_other, losses = pl.pallas_call(
+    columns_other = shift(jnp.stack(columns), "core", 1)
+    stats, columns, columns_other = lax.optimization_barrier((stats, columns, columns_other))
+
+    grads, grads_other, sent, losses = pl.pallas_call(
         grad_kernel,
         out_shape=(
             jax.ShapeDtypeStruct((block_rows, rows), bf16),
             jax.ShapeDtypeStruct((block_rows, rows), bf16),
+            jax.ShapeDtypeStruct((x_size * CORES, block_rows, rows), bf16),
             jax.ShapeDtypeStruct((1, rows), f32),
         ),
         in_specs=[SMEM] + [VMEM] * 4,
-        out_specs=(VMEM,) * 3,
+        out_specs=(VMEM,) * 4,
         compiler_params=PARAMS,
     )(places, scores, logits, positive, stats)
     loss = lax.dynamic_slice_in_dim(losses[0], chip * own_rows, own_rows)
 
-    grads_back = shift(grads_other, "core", 1)
-    columns_other = shift(jnp.stack(columns), "core", 1)
+    block_grads = lax.all_to_all(sent, ("x", "core"), 0, 0, tiled=True)
+    width = depth // x_size
     query_part = pl.pallas_call(
         query_kernel,
+        grid=(x_size,),
         out_shape=jax.ShapeDtypeStruct((rows, depth), bf16),
-        in_specs=[VMEM] * 4,
+        in_specs=[pl.BlockSpec((block_rows, rows), lambda i: (0, 0))] * 2
+        + [pl.BlockSpec((block_rows, width), lambda i: (0, i))] * 2,
+        out_specs=pl.BlockSpec((rows, width), lambda i: (0, i)),
+        compiler_params=PARAMS,
+    )(grads, grads_other, passages, passages_other)
+    query_part, block_grads = lax.optimization_barrier((query_part, block_grads))
+    query_parts = lax.all_to_all(query_part.reshape(chips, own_rows, depth), CHIPS, 0, 0, tiled=True)
+    query_total = pl.pallas_call(
+        sum_kernel,
+        out_shape=jax.ShapeDtypeStruct((own_rows, depth), bf16),
+        in_specs=[VMEM],
         out_specs=VMEM,
         compiler_params=PARAMS,
-    )(grads, grads_other, passages, passages_other)
-    query_parts = lax.all_to_all(query_part.reshape(chips, own_rows, depth), CHIPS, 0, 0, tiled=True)
-    query_total = jnp.sum(query_parts.astype(f32), axis=0)
-
-    block_grads = jnp.stack([grads, grads_back])
-    block_grads = [shift(block_grads, "x", d) for d in range(x_size)]
-    width = depth // (x_size * yh_size)
+    )(query_parts)
+
     parts = pl.pallas_call(
         functools.partial(passage_kernel, x_size),
-        out_shape=(jax.ShapeDtypeStruct((block_rows, width), bf16),) * yh_size,
-        in_specs=[SMEM] + [VMEM] * (3 * x_size),
+        out_shape=(jax.ShapeDtypeStruct((block_rows, width // yh_size), bf16),) * yh_size,
+        in_specs=[SMEM] + [VMEM] * (2 + x_size),
         out_specs=(VMEM,) * yh_size,
         compiler_params=PARAMS,
-    )(yh.astype(i32)[None], *block_grads, *columns, *columns_other)
+    )(jnp.stack([x, core, yh]).astype(i32), block_grads, *columns, columns_other)
     parts = [shift(part, "yh", d) for d, part in enumerate(parts)]
     passage_total = sum(v.astype(f32) for v in parts)
-    return loss[None], query_total.astype(bf16)[None], passage_total.astype(bf16)
+    return loss[None], query_total[None], passage_total.astype(bf16)
 
 
 def solution(mesh):

time: 131 us -> 145 us (1.11)
  the two profiles are of different devices: /device:TPU:15 before, /device:TPU:1 now
where the time goes in v5:
time: 145 us; the launch traced here: 143 us
  starting transfers between devices  52.4 us (36%)
  waiting for transfers between devices  50.7 us (35%)
  Pallas kernels  15.7 us (11%)
  blocking collectives  13.5 us (9%)
  local copies, waits for them, and re-layouts  8.66 us (6%)
    ppermute x9, starting transfers between devices, shift(): lax.ppermute(value, axis, [(i, (i + by) % size) for i in range(size)])  36.8 us
    all_to_all x1, waiting for transfers between devices, per_device(): lax.all_to_all(sent, CHIPS, 0, 0, tiled=True).reshape(rows, depth + LANES)  23.9 us
    ppermute x9, waiting for transfers between devices, shift(): lax.ppermute(value, axis, [(i, (i + by) % size) for i in range(size)])  22.3 us
    all_to_all x1, blocking collectives, per_device(): stats = lax.all_to_all(stats, CHIPS, 0, 0, tiled=True)  13.5 us
    unnamed x32, local copies, waits for them, and re-layouts  7.89 us
    all_to_all x1, starting transfers between devices, per_device(): lax.all_to_all(sent, CHIPS, 0, 0, tiled=True).reshape(rows, depth + LANES)  5.79 us
    all_to_all x1, starting transfers between devices, per_device(): block_grads = lax.all_to_all(sent, ('x', 'core'), 0, 0, tiled=True)  5.42 us
    all_to_all x1, waiting for transfers between devices, per_device(): block_grads = lax.all_to_all(sent, ('x', 'core'), 0, 0, tiled=True)  4.47 us
  transfers between devices with their start and end apart: 12, of which 8 were waited for; matrix products, arithmetic and copies ran while one was open for 1% of the time, Pallas kernels for 5%

profile of v5, /device:TPU:1, one launch (start us, length us, event | category | flops | bytes accessed | tf_op | source)
XLA Modules:
  0.0 142.9 jit_solution(9228396855860472584)
XLA Ops:
  0.6 0.0 copy-start.10
  0.6 0.0 copy-start
  0.7 0.0 copy-start.13
  0.7 1.0 copy-done.13
  1.6 0.0 copy-start.14
  1.6 0.7 copy-done.14
  2.3 0.0 copy-start.15
  2.3 0.7 copy-done.15
  3.0 2.1 %shard_map.76 = bf16[16,8,4224]{2,1,0:T(8,128)(2,1)S(1)} custom-call(s32[1,8]{1,0:T(1,128)S(1)} %copy-done.14, s32[1,8]{1,0:T(1,128)S(1)} %copy-done.15, bf16[8,4096]{1,0:T(8,128)(2,1)S(1)} %bitcast.21), custom_call_target="tpu_custom_call" | custom-call | tf_op jit(solution)/shard_map/pallas_call | solution.py:160
  5.1 0.0 copy-start.1
  5.1 1.0 copy-done.1
  6.1 8.8 %collective-permute-start = (bf16[256,4096]{1,0:T(8,128)(2,1)}, bf16[256,4096]{1,0:T(8,128)(2,1)}, u32[]{:S(2)}, u32[]{:S(2)}) collective-permute-start(bf16[256,4096]{1,0:T(8,128)(2,1)} %passages.1), channel_id=1, source_target_pairs={{0,16},{16,0},{1,17},{17,1},{2,18},{18,2},{3,19},{19,3},{4,20},{20... | collective-permute-start | bytes 6291464 | tf_op jit(solution)/shard_map/ppermute | solution.py:26
  14.9 5.8 %all-to-all-start = ((bf16[16,8,4224]{2,1,0:T(8,128)(2,1)}), bf16[16,8,4224]{2,1,0:T(8,128)(2,1)S(1)}, u32[]{:S(2)}, u32[]{:S(2)}) async-start(bf16[16,8,4224]{2,1,0:T(8,128)(2,1)} %copy-done.1), calls=%async_computation | async-start | bytes 2162688 | tf_op jit(solution)/shard_map/all_to_all | solution.py:175
  20.7 0.0 copy-done.10
  20.7 2.2 %collective-permute-start.1 = (f32[256,256]{1,0:T(8,128)S(1)}, f32[256,256]{1,0:T(8,128)}, u32[]{:S(2)}, u32[]{:S(2)}) collective-permute-start(f32[256,256]{1,0:T(8,128)S(1)} %bitcast.19), channel_id=1, source_target_pairs={{0,16},{16,0},{1,17},{17,1},{2,18},{18,2},{3,19},{19,3},{4,20},{20... | collective-permute-start | bytes 786440 | tf_op jit(solution)/shard_map/ppermute | solution.py:26
  23.0 0.1 fusion
  23.0 0.1 pad_add_fusion.places
  23.1 1.1 collective-permute-done.1.teacher_other
  24.3 23.9 %all-to-all-done = bf16[16,8,4224]{2,1,0:T(8,128)(2,1)S(1)} async-done(((bf16[16,8,4224]{2,1,0:T(8,128)(2,1)}), bf16[16,8,4224]{2,1,0:T(8,128)(2,1)S(1)}, u32[]{:S(2)}, u32[]{:S(2)}) %all-to-all-start) | async-done | bytes 1081376 | tf_op jit(solution)/shard_map/all_to_all | solution.py:175
  48.1 0.0 collective-permute-done.passages_other
  48.1 0.0 copy-done
  48.1 3.4 %shard_map.77 = (f32[2,256,128]{2,1,0:T(8,128)S(1)}, f32[2,256,128]{2,1,0:T(8,128)S(1)}, s32[1,128]{1,0:T(1,128)S(1)}, f32[16,8,128]{2,1,0:T(8,128)S(1)}) custom-call(s32[4]{0:T(128)S(1)} %pad_add_fusion.places, bf16[128,4224]{1,0:T(8,128)(2,1)S(1)} %bitcast.13, bf16[256,4096]{1,0:T(8,128)(2,1)S(1)} %copy-done, ...), custom_call_target="tpu_custom_call" | custom-call | tf_op jit(solution)/shard_map/pallas_call | solution.py:177
  51.6 0.1 slice.2
  51.7 0.1 constant_dynamic-slice_fusion.1
  51.8 4.4 %collective-permute-start.4 = (bf16[128,1024]{1,0:T(8,128)(2,1)S(1)}, bf16[128,1024]{1,0:T(8,128)(2,1)S(1)}, u32[]{:S(2)}, u32[]{:S(2)}) collective-permute-start(bf16[128,1024]{1,0:T(8,128)(2,1)S(1)} %get-tuple-element.53), channel_id=1, source_target_pairs={{0,12},{4,0},{8,4},{12,8},{1,13},{5,1},{9,5},{13,9},{2,14},{6,2},{... | collective-permute-start | bytes 786440 | tf_op jit(solution)/shard_map/ppermute | solution.py:26
  56.2 2.4 %collective-permute-start.3 = (bf16[128,1024]{1,0:T(8,128)(2,1)S(1)}, bf16[128,1024]{1,0:T(8,128)(2,1)S(1)}, u32[]{:S(2)}, u32[]{:S(2)}) collective-permute-start(bf16[128,1024]{1,0:T(8,128)(2,1)S(1)} %get-tuple-element.54), channel_id=1, source_target_pairs={{0,8},{4,12},{8,0},{12,4},{1,9},{5,13},{9,1},{13,5},{2,10},{6,14},... | collective-permute-start | bytes 786440 | tf_op jit(solution)/shard_map/ppermute | solution.py:26
  58.6 2.5 %collective-permute-start.2 = (bf16[128,1024]{1,0:T(8,128)(2,1)S(1)}, bf16[128,1024]{1,0:T(8,128)(2,1)S(1)}, u32[]{:S(2)}, u32[]{:S(2)}) collective-permute-start(bf16[128,1024]{1,0:T(8,128)(2,1)S(1)} %get-tuple-element.55), channel_id=1, source_target_pairs={{0,4},{4,8},{8,12},{12,0},{1,5},{5,9},{9,13},{13,1},{2,6},{6,10},{... | collective-permute-start | bytes 786440 | tf_op jit(solution)/shard_map/ppermute | solution.py:26
  61.1 0.2 collective-permute-done.4.refs_3_
  61.3 4.7 %collective-permute-done.3.refs_2_ = bf16[128,1024]{1,0:T(8,128)(2,1)S(1)} collective-permute-done((bf16[128,1024]{1,0:T(8,128)(2,1)S(1)}, bf16[128,1024]{1,0:T(8,128)(2,1)S(1)}, u32[]{:S(2)}, u32[]{:S(2)}) %collective-permute-start.3) | collective-permute-done | bytes 262176 | tf_op jit(solution)/shard_map/ppermute | solution.py:26
  66.0 7.2 %collective-permute-done.2.refs_1_ = bf16[128,1024]{1,0:T(8,128)(2,1)S(1)} collective-permute-done((bf16[128,1024]{1,0:T(8,128)(2,1)S(1)}, bf16[128,1024]{1,0:T(8,128)(2,1)S(1)}, u32[]{:S(2)}, u32[]{:S(2)}) %collective-permute-start.2) | collective-permute-done | bytes 262176 | tf_op jit(solution)/shard_map/ppermute | solution.py:26
  73.2 0.1 pad_maximum_fusion
  73.3 0.0 copy-start.4
  73.4 0.7 copy-done.4
  74.1 0.0 copy-start.6
  74.1 0.7 copy-done.6
  74.8 0.0 copy-start.8
  74.8 0.7 copy-done.8
  75.5 2.6 %collective-permute-start.5 = (bf16[4,128,1024]{2,1,0:T(8,128)(2,1)S(1)}, bf16[4,128,1024]{2,1,0:T(8,128)(2,1)S(1)}, u32[]{:S(2)}, u32[]{:S(2)}) collective-permute-start(bf16[4,128,1024]{2,1,0:T(8,128)(2,1)S(1)} %pad_maximum_fusion), channel_id=1, source_target_pairs={{0,16},{16,0},{1,17},{17,1},{2,18},{18,2},{3,19},{19,3},{4,20},{20... | collective-permute-start | bytes 3145736 | tf_op jit(solution)/shard_map/ppermute | solution.py:26
  78.1 13.5 %all_to_all.20.stats = f32[16,8,128]{2,1,0:T(8,128)S(1)} all-to-all(f32[16,8,128]{2,1,0:T(8,128)S(1)} %get-tuple-element.35), channel_id=1, replica_groups=mesh['yl'=2,'z'=8,'core'=2,'x'=4,'yh'=4] {'yl','z'}, dimensions={0} | all-to-all | bytes 131072 | tf_op jit(solution)/shard_map/all_to_all | solution.py:191
  91.6 0.0 collective-permute-done.5.refs_4_
  91.6 1.0 copy-done.2
  92.6 1.5 %shard_map.78 = (bf16[256,128]{1,0:T(8,128)(2,1)S(1)}, bf16[256,128]{1,0:T(8,128)(2,1)S(1)}, bf16[8,256,128]{2,1,0:T(8,128)(2,1)}, f32[1,128]{1,0:T(1,128)S(1)}) custom-call(s32[4]{0:T(128)S(1)} %pad_add_fusion.places, f32[2,256,128]{2,1,0:T(8,128)S(1)} %get-tuple-element.31.scores, f32[2,256,128]{2,1,0:T(8,128)S(1)} %get-tuple-element.32.logits, ...), custom_call_target="tpu_custom_call" | custom-call | tf_op jit(solution)/shard_map/pallas_call | solution.py:195
  94.1 0.6 copy-done.11
  94.7 5.4 %all-to-all-start.2 = ((bf16[8,256,128]{2,1,0:T(8,128)(2,1)}), bf16[8,256,128]{2,1,0:T(8,128)(2,1)}, u32[]{:S(2)}, u32[]{:S(2)}) async-start(bf16[8,256,128]{2,1,0:T(8,128)(2,1)} %get-tuple-element.41), calls=%async_computation.2 | async-start | bytes 1048576 | tf_op jit(solution)/shard_map/all_to_all | solution.py:209
  100.2 0.8 copy-done.12
  101.0 4.3 %shard_map.79 = bf16[128,4096]{1,0:T(8,128)(2,1)} custom-call(bf16[256,128]{1,0:T(8,128)(2,1)S(1)} %get-tuple-element.39.grads, bf16[256,128]{1,0:T(8,128)(2,1)S(1)} %copy-done.12, bf16[256,4096]{1,0:T(8,128)(2,1)S(1)} %copy-done, bf16[256,4096]{1,0:T(8,128)(2,1)} %collective-permute-done.passages_other), custom_call_target="tpu_custom_call" | custom-call | tf_op jit(solution)/shard_map/pallas_call | solution.py:211
  105.3 4.5 %all-to-all-done.2.grads = bf16[8,256,128]{2,1,0:T(8,128)(2,1)} async-done(((bf16[8,256,128]{2,1,0:T(8,128)(2,1)}), bf16[8,256,128]{2,1,0:T(8,128)(2,1)}, u32[]{:S(2)}, u32[]{:S(2)}) %all-to-all-start.2) | async-done | bytes 524320 | tf_op jit(solution)/shard_map/all_to_all | solution.py:209
  109.8 4.3 %all-to-all-start.3 = ((bf16[16,8,4096]{2,1,0:T(8,128)(2,1)}), bf16[16,8,4096]{2,1,0:T(8,128)(2,1)}, u32[]{:S(2)}, u32[]{:S(2)}) async-start(bf16[16,8,4096]{2,1,0:T(8,128)(2,1)} %bitcast.9), calls=%async_computation.3 | async-start | bytes 2097152 | tf_op jit(solution)/shard_map/all_to_all | solution.py:221
  114.1 0.1 pad_add_fusion.1.position
  114.2 0.0 copy-done.3
  114.2 0.0 copy-done.5
  114.2 0.0 copy-done.7
  114.2 0.0 copy-done.9
  114.2 2.3 %shard_map.81 = (bf16[256,256]{1,0:T(8,128)(2,1)S(1)}, bf16[256,256]{1,0:T(8,128)(2,1)S(1)}, bf16[256,256]{1,0:T(8,128)(2,1)S(1)}, bf16[256,256]{1,0:T(8,128)(2,1)S(1)}) custom-call(s32[3]{0:T(128)S(1)} %pad_add_fusion.1.position, bf16[8,256,128]{2,1,0:T(8,128)(2,1)} %all-to-all-done.2.grads, bf16[128,1024]{1,0:T(8,128)(2,1)S(1)} %get-tuple-element.44.refs_0_, ...), custom_call_target="tpu_custom_call" | custom-call | tf_op jit(solution)/shard_map/pallas_call | solution.py:230
  116.5 4.2 %collective-permute-start.6 = (bf16[256,256]{1,0:T(8,128)(2,1)S(1)}, bf16[256,256]{1,0:T(8,128)(2,1)S(1)}, u32[]{:S(2)}, u32[]{:S(2)}) collective-permute-start(bf16[256,256]{1,0:T(8,128)(2,1)S(1)} %get-tuple-element.50), channel_id=1, source_target_pairs={{0,1},{1,2},{2,3},{3,0},{4,5},{5,6},{6,7},{7,4},{8,9},{9,10},{10,1... | collective-permute-start | bytes 393224 | tf_op jit(solution)/shard_map/ppermute | solution.py:26
  120.8 4.8 %collective-permute-start.7 = (bf16[256,256]{1,0:T(8,128)(2,1)S(1)}, bf16[256,256]{1,0:T(8,128)(2,1)S(1)}, u32[]{:S(2)}, u32[]{:S(2)}) collective-permute-start(bf16[256,256]{1,0:T(8,128)(2,1)S(1)} %get-tuple-element.51), channel_id=1, source_target_pairs={{0,2},{1,3},{2,0},{3,1},{4,6},{5,7},{6,4},{7,5},{8,10},{9,11},{10,... | collective-permute-start | bytes 393224 | tf_op jit(solution)/shard_map/ppermute | solution.py:26
  125.5 5.0 %collective-permute-start.8 = (bf16[256,256]{1,0:T(8,128)(2,1)S(1)}, bf16[256,256]{1,0:T(8,128)(2,1)S(1)}, u32[]{:S(2)}, u32[]{:S(2)}) collective-permute-start(bf16[256,256]{1,0:T(8,128)(2,1)S(1)} %get-tuple-element.52), channel_id=1, source_target_pairs={{0,3},{1,0},{2,1},{3,2},{4,7},{5,4},{6,5},{7,6},{8,11},{9,8},{10,9... | collective-permute-start | bytes 393224 | tf_op jit(solution)/shard_map/ppermute | solution.py:26
  130.5 0.6 constant_dynamic-slice_fusion
  131.1 4.3 %collective-permute-done.6 = bf16[256,256]{1,0:T(8,128)(2,1)S(1)} collective-permute-done((bf16[256,256]{1,0:T(8,128)(2,1)S(1)}, bf16[256,256]{1,0:T(8,128)(2,1)S(1)}, u32[]{:S(2)}, u32[]{:S(2)}) %collective-permute-start.6) | collective-permute-done | bytes 131104 | tf_op jit(solution)/shard_map/ppermute | solution.py:26
  135.4 4.8 %collective-permute-done.7 = bf16[256,256]{1,0:T(8,128)(2,1)S(1)} collective-permute-done((bf16[256,256]{1,0:T(8,128)(2,1)S(1)}, bf16[256,256]{1,0:T(8,128)(2,1)S(1)}, u32[]{:S(2)}, u32[]{:S(2)}) %collective-permute-start.7) | collective-permute-done | bytes 131104 | tf_op jit(solution)/shard_map/ppermute | solution.py:26
  140.2 0.0 collective-permute-done.8
  140.2 0.7 add_convert_fusion
  140.9 0.0 all-to-all-done.3.parts
  140.9 2.0 %shard_map.80 = bf16[8,4096]{1,0:T(8,128)(2,1)} custom-call(bf16[16,8,4096]{2,1,0:T(8,128)(2,1)} %all-to-all-done.3.parts), custom_call_target="tpu_custom_call" | custom-call | tf_op jit(solution)/shard_map/pallas_call | solution.py:222
  (7 shorter events, 0.0 us)
Async XLA Ops:
  0.6 20.1 %copy-start.10 = (f32[1,256,256]{2,1,0:T(8,128)S(1)}, f32[1,256,256]{2,1,0:T(8,128)}, u32[]{:S(2)}) copy-start(f32[1,256,256]{2,1,0:T(8,128)} %param.7) | copy-start | bytes 786436
  0.6 47.5 %copy-start = (bf16[256,4096]{1,0:T(8,128)(2,1)S(1)}, bf16[256,4096]{1,0:T(8,128)(2,1)}, u32[]{:S(2)}) copy-start(bf16[256,4096]{1,0:T(8,128)(2,1)} %passages.1) | copy-start | bytes 6291460
  0.7 1.0 copy-start.13
  1.6 0.7 copy-start.14
  2.3 0.7 copy-start.15
  5.1 1.0 copy-start.1
  6.1 42.0 %collective-permute-start = (bf16[256,4096]{1,0:T(8,128)(2,1)}, bf16[256,4096]{1,0:T(8,128)(2,1)}, u32[]{:S(2)}, u32[]{:S(2)}) collective-permute-start(bf16[256,4096]{1,0:T(8,128)(2,1)} %passages.1), channel_id=1, source_target_pairs={{0,16},{16,0},{1,17},{17,1},{2,18},{18,2},{3,19},{19,3},{4,20},{20... | collective-permute-start | bytes 6291464 | tf_op jit(solution)/shard_map/ppermute | solution.py:26
  14.9 33.2 %all-to-all-start = ((bf16[16,8,4224]{2,1,0:T(8,128)(2,1)}), bf16[16,8,4224]{2,1,0:T(8,128)(2,1)S(1)}, u32[]{:S(2)}, u32[]{:S(2)}) async-start(bf16[16,8,4224]{2,1,0:T(8,128)(2,1)} %copy-done.1), calls=%async_computation | async-start | bytes 2162688 | tf_op jit(solution)/shard_map/all_to_all | solution.py:175
  20.7 3.6 %collective-permute-start.1 = (f32[256,256]{1,0:T(8,128)S(1)}, f32[256,256]{1,0:T(8,128)}, u32[]{:S(2)}, u32[]{:S(2)}) collective-permute-start(f32[256,256]{1,0:T(8,128)S(1)} %bitcast.19), channel_id=1, source_target_pairs={{0,16},{16,0},{1,17},{17,1},{2,18},{18,2},{3,19},{19,3},{4,20},{20... | collective-permute-start | bytes 786440 | tf_op jit(solution)/shard_map/ppermute | solution.py:26
  51.8 9.5 %collective-permute-start.4 = (bf16[128,1024]{1,0:T(8,128)(2,1)S(1)}, bf16[128,1024]{1,0:T(8,128)(2,1)S(1)}, u32[]{:S(2)}, u32[]{:S(2)}) collective-permute-start(bf16[128,1024]{1,0:T(8,128)(2,1)S(1)} %get-tuple-element.53), channel_id=1, source_target_pairs={{0,12},{4,0},{8,4},{12,8},{1,13},{5,1},{9,5},{13,9},{2,14},{6,2},{... | collective-permute-start | bytes 786440 | tf_op jit(solution)/shard_map/ppermute | solution.py:26
  56.2 9.8 %collective-permute-start.3 = (bf16[128,1024]{1,0:T(8,128)(2,1)S(1)}, bf16[128,1024]{1,0:T(8,128)(2,1)S(1)}, u32[]{:S(2)}, u32[]{:S(2)}) collective-permute-start(bf16[128,1024]{1,0:T(8,128)(2,1)S(1)} %get-tuple-element.54), channel_id=1, source_target_pairs={{0,8},{4,12},{8,0},{12,4},{1,9},{5,13},{9,1},{13,5},{2,10},{6,14},... | collective-permute-start | bytes 786440 | tf_op jit(solution)/shard_map/ppermute | solution.py:26
  58.6 14.6 %collective-permute-start.2 = (bf16[128,1024]{1,0:T(8,128)(2,1)S(1)}, bf16[128,1024]{1,0:T(8,128)(2,1)S(1)}, u32[]{:S(2)}, u32[]{:S(2)}) collective-permute-start(bf16[128,1024]{1,0:T(8,128)(2,1)S(1)} %get-tuple-element.55), channel_id=1, source_target_pairs={{0,4},{4,8},{8,12},{12,0},{1,5},{5,9},{9,13},{13,1},{2,6},{6,10},{... | collective-permute-start | bytes 786440 | tf_op jit(solution)/shard_map/ppermute | solution.py:26
  73.3 0.7 copy-start.4
  74.1 0.7 copy-start.6
  74.8 0.7 copy-start.8
  75.5 16.1 %collective-permute-start.5 = (bf16[4,128,1024]{2,1,0:T(8,128)(2,1)S(1)}, bf16[4,128,1024]{2,1,0:T(8,128)(2,1)S(1)}, u32[]{:S(2)}, u32[]{:S(2)}) collective-permute-start(bf16[4,128,1024]{2,1,0:T(8,128)(2,1)S(1)} %pad_maximum_fusion), channel_id=1, source_target_pairs={{0,16},{16,0},{1,17},{17,1},{2,18},{18,2},{3,19},{19,3},{4,20},{20... | collective-permute-start | bytes 3145736 | tf_op jit(solution)/shard_map/ppermute | solution.py:26
  91.6 1.0 copy-start.2
  94.1 0.6 copy-start.11
  94.7 15.0 %all-to-all-start.2 = ((bf16[8,256,128]{2,1,0:T(8,128)(2,1)}), bf16[8,256,128]{2,1,0:T(8,128)(2,1)}, u32[]{:S(2)}, u32[]{:S(2)}) async-start(bf16[8,256,128]{2,1,0:T(8,128)(2,1)} %get-tuple-element.41), calls=%async_computation.2 | async-start | bytes 1048576 | tf_op jit(solution)/shard_map/all_to_all | solution.py:209
  100.2 0.8 copy-start.12
  105.3 8.9 %copy-start.3 = (bf16[4,128,1024]{2,1,0:T(8,128)(2,1)S(1)}, bf16[4,128,1024]{2,1,0:T(8,128)(2,1)}, u32[]{:S(2)}) copy-start(bf16[4,128,1024]{2,1,0:T(8,128)(2,1)} %copy-done.2) | copy-start | bytes 3145732
  105.3 8.9 %copy-start.5 = (bf16[128,1024]{1,0:T(8,128)(2,1)S(1)}, bf16[128,1024]{1,0:T(8,128)(2,1)}, u32[]{:S(2)}) copy-start(bf16[128,1024]{1,0:T(8,128)(2,1)} %copy-done.4) | copy-start | bytes 786436
  105.3 8.9 %copy-start.7 = (bf16[128,1024]{1,0:T(8,128)(2,1)S(1)}, bf16[128,1024]{1,0:T(8,128)(2,1)}, u32[]{:S(2)}) copy-start(bf16[128,1024]{1,0:T(8,128)(2,1)} %copy-done.6) | copy-start | bytes 786436
  105.3 8.9 %copy-start.9 = (bf16[128,1024]{1,0:T(8,128)(2,1)S(1)}, bf16[128,1024]{1,0:T(8,128)(2,1)}, u32[]{:S(2)}) copy-start(bf16[128,1024]{1,0:T(8,128)(2,1)} %copy-done.8) | copy-start | bytes 786436
  109.8 31.2 %all-to-all-start.3 = ((bf16[16,8,4096]{2,1,0:T(8,128)(2,1)}), bf16[16,8,4096]{2,1,0:T(8,128)(2,1)}, u32[]{:S(2)}, u32[]{:S(2)}) async-start(bf16[16,8,4096]{2,1,0:T(8,128)(2,1)} %bitcast.9), calls=%async_computation.3 | async-start | bytes 2097152 | tf_op jit(solution)/shard_map/all_to_all | solution.py:221
  116.5 18.8 %collective-permute-start.6 = (bf16[256,256]{1,0:T(8,128)(2,1)S(1)}, bf16[256,256]{1,0:T(8,128)(2,1)S(1)}, u32[]{:S(2)}, u32[]{:S(2)}) collective-permute-start(bf16[256,256]{1,0:T(8,128)(2,1)S(1)} %get-tuple-element.50), channel_id=1, source_target_pairs={{0,1},{1,2},{2,3},{3,0},{4,5},{5,6},{6,7},{7,4},{8,9},{9,10},{10,1... | collective-permute-start | bytes 393224 | tf_op jit(solution)/shard_map/ppermute | solution.py:26
  120.8 19.5 %collective-permute-start.7 = (bf16[256,256]{1,0:T(8,128)(2,1)S(1)}, bf16[256,256]{1,0:T(8,128)(2,1)S(1)}, u32[]{:S(2)}, u32[]{:S(2)}) collective-permute-start(bf16[256,256]{1,0:T(8,128)(2,1)S(1)} %get-tuple-element.51), channel_id=1, source_target_pairs={{0,2},{1,3},{2,0},{3,1},{4,6},{5,7},{6,4},{7,5},{8,10},{9,11},{10,... | collective-permute-start | bytes 393224 | tf_op jit(solution)/shard_map/ppermute | solution.py:26
  125.5 14.7 %collective-permute-start.8 = (bf16[256,256]{1,0:T(8,128)(2,1)S(1)}, bf16[256,256]{1,0:T(8,128)(2,1)S(1)}, u32[]{:S(2)}, u32[]{:S(2)}) collective-permute-start(bf16[256,256]{1,0:T(8,128)(2,1)S(1)} %get-tuple-element.52), channel_id=1, source_target_pairs={{0,3},{1,0},{2,1},{3,2},{4,7},{5,4},{6,5},{7,6},{8,11},{9,8},{10,9... | collective-permute-start | bytes 393224 | tf_op jit(solution)/shard_map/ppermute | solution.py:26

commit v6 on v5

v6 whole, which is shorter than its diff:
```python
import functools

import jax
import jax.numpy as jnp
from jax import lax
from jax.experimental import pallas as pl
from jax.experimental.pallas import tpu as pltpu
from jax.sharding import Mesh, PartitionSpec as P

inv_temp = 50.0
YL, CORES, X = 2, 2, 4
LANES = 128
STATS = 24
CHIPS = ("yl", "z")
f32, bf16, i32 = jnp.float32, jnp.bfloat16, jnp.int32
VMEM = pl.BlockSpec(memory_space=pltpu.VMEM)
ANY = pl.BlockSpec(memory_space=pl.ANY)
HBM = pl.BlockSpec(memory_space=pltpu.HBM)
SMEM = pl.BlockSpec(memory_space=pltpu.SMEM)
PARAMS = pltpu.CompilerParams(vmem_limit_bytes=16 * 1024 * 1024)


def shift(value, axis, by):
    if by == 0:
        return value
    size = lax.axis_size(axis)
    return lax.ppermute(value, axis, [(i, (i + by) % size) for i in range(size)])


def hits(positive, place, shape):
    return lax.broadcasted_iota(i32, shape, 0) + place == positive


def send_kernel(indices, queries, out, numbers, buffer, sems):
    own_rows, depth = queries.shape
    shape = (own_rows, out.shape[2] - depth)
    loads = [
        pltpu.make_async_copy(indices, numbers, sems.at[0]),
        pltpu.make_async_copy(queries, buffer.at[:, pl.ds(0, depth)], sems.at[1]),
    ]
    for load in loads:
        load.start()
    for load in loads:
        load.wait()
    row, column = lax.broadcasted_iota(i32, shape, 0), lax.broadcasted_iota(i32, shape, 1)
    codes = jnp.zeros(shape, i32)
    for r in range(own_rows):
        for c in range(3):
            code = lax.shift_right_logical(numbers[0, r], 8 * c) & 255
            codes = jnp.where((row == r) & (column == c), code, codes)
    buffer[:, depth:] = codes.astype(f32).astype(bf16)
    stores = [pltpu.make_async_copy(buffer, out.at[chip], sems.at[2 + chip]) for chip in range(out.shape[0])]
    for store in stores:
        store.start()
    for store in stores:
        store.wait()


def score_kernel(
    places, query, passages, teacher, teacher_other, passages_other, values, positives, stats, block, sem
):
    fetch = pltpu.make_async_copy(passages_other, block, sem)
    fetch.start()
    depth = passages.shape[1]
    rows = query.shape[0]
    codes = query[:, depth:].astype(f32).T
    row_index = codes[0:1].astype(i32)
    positive = codes[1:2].astype(i32) + 256 * codes[2:3].astype(i32)
    positives[...] = positive
    pick = (lax.broadcasted_iota(i32, (teacher.shape[0], rows), 0) == row_index).astype(f32)
    parts = []
    for half, table in enumerate((teacher, teacher_other)):
        if half:
            fetch.wait()
        s = inv_temp * lax.dot_general(
            (block if half else passages)[...], query[:, :depth], (((1,), (1,)), ((), ())), preferred_element_type=f32
        )
        t = lax.dot_general(
            table[...], pick, (((0,), (0,)), ((), ())),
            precision=lax.Precision.HIGHEST, preferred_element_type=f32,
        )
        values[half] = s
        values[CORES + half] = t
        parts.append((s, t, hits(positive, places[half], s.shape)))
    top_s, top_t = (jnp.maximum(*[jnp.max(p[i], axis=0, keepdims=True) for p in parts]) for i in (0, 1))
    sums = []
    for s, t, hot in parts:
        below_s, below_t = s - top_s, t - top_t
        weight = jnp.exp(below_t)
        terms = (jnp.exp(below_s), weight, weight * (below_t - below_s), jnp.where(hot, s, 0.0))
        sums.append([jnp.sum(v, axis=0, keepdims=True) for v in terms])
    sums = [a + b for a, b in zip(*sums)]
    whole = jnp.concatenate([top_s, top_t] + sums + [jnp.zeros((STATS - 6, rows), f32)], axis=0)
    stats[...] = jnp.broadcast_to(whole[None], stats.shape)


def slice_kernel(x, query, after, *outs):
    del after
    width = outs[0].shape[1]
    for d, out in enumerate(outs):
        out[...] = query[:, pl.ds(pl.multiple_of(lax.rem(x[0] + d, len(outs)) * width, width), width)]


def grad_kernel(places, logits, positives, stats, grads, sent, losses, buffer, sems):
    tops_s, tops_t, sums_s, sums_t, cross, hit = (stats[:, i, :] for i in range(6))
    top_s, top_t = jnp.max(tops_s, axis=0, keepdims=True), jnp.max(tops_t, axis=0, keepdims=True)
    lower_s, lower_t = tops_s - top_s, tops_t - top_t
    total_s = jnp.sum(jnp.exp(lower_s) * sums_s, axis=0, keepdims=True)
    weight_t = jnp.exp(lower_t)
    total_t = jnp.sum(weight_t * sums_t, axis=0, keepdims=True)
    cross = jnp.sum(weight_t * (cross + (lower_t - lower_s) * sums_t), axis=0, keepdims=True)
    log_s = jnp.log(total_s)
    own = jnp.sum(hit, axis=0, keepdims=True)
    losses[...] = cross / total_t - jnp.log(total_t) + log_s - (own - top_s - log_s)
    scale_s, scale_t = 2.0 * inv_temp / total_s, inv_temp / total_t
    for half in range(CORES):
        hot = hits(positives[...], places[half], logits.shape[1:])
        values = (
            jnp.exp(logits[half] - top_s) * scale_s
            - jnp.exp(logits[CORES + half] - top_t) * scale_t
            - jnp.where(hot, inv_temp, 0.0)
        )
        grads[half] = values.T.astype(bf16)
        buffer[places[CORES + half]] = values.astype(bf16)
    stores = [
        pltpu.make_async_copy(buffer, sent.at[pl.ds(group * CORES, CORES)], sems.at[group])
        for group in range(sent.shape[0] // CORES)
    ]
    for store in stores:
        store.start()
    for store in stores:
        store.wait()


def query_kernel(grads, passages, passages_other, out):
    total = jnp.dot(grads[0], passages[...], preferred_element_type=f32)
    total += jnp.dot(grads[1], passages_other[...], preferred_element_type=f32)
    out[...] = total.astype(bf16)


def passage_kernel(groups, position, grads, *refs):
    x, core, yh = position[0], position[1], position[2]
    query, query_other, outs = refs[:groups], refs[groups], refs[groups + 1 :]
    width = outs[0].shape[1]
    for i, out in enumerate(outs):
        columns = pl.ds(pl.multiple_of(lax.rem(yh + i, len(outs)) * width, width), width)
        total = jnp.zeros(out.shape, f32)
        for d in range(groups):
            group = lax.rem(x + groups - d, groups) * CORES
            total += jnp.dot(grads[group + core], query[d][:, columns], preferred_element_type=f32)
            total += jnp.dot(grads[group + 1 - core], query_other[d, :, columns], preferred_element_type=f32)
        out[...] = total.astype(bf16)


def sum_kernel(parts, out):
    total = parts[0].astype(f32)
    for i in range(1, parts.shape[0]):
        total += parts[i].astype(f32)
    out[...] = total.astype(bf16)


def per_device(queries, passages, teacher, teacher_rows, positives):
    own_rows, depth = queries.shape[1:]
    block_rows = passages.shape[0]
    chips = lax.axis_size("yl") * lax.axis_size("z")
    x_size, yh_size = lax.axis_size("x"), lax.axis_size("yh")
    rows = chips * own_rows
    chip = lax.axis_index("yl") * lax.axis_size("z") + lax.axis_index("z")
    core, x, yh = lax.axis_index("core"), lax.axis_index("x"), lax.axis_index("yh")
    cores = jnp.stack([core, 1 - core])
    places = jnp.concatenate([(chip * CORES + cores) * block_rows, cores]).astype(i32)

    sent = pl.pallas_call(
        send_kernel,
        out_shape=jax.ShapeDtypeStruct((chips, own_rows, depth + LANES), bf16),
        in_specs=[HBM] * 2,
        out_specs=HBM,
        scratch_shapes=[
            pltpu.SMEM((1, own_rows), i32),
            pltpu.VMEM((own_rows, depth + LANES), bf16),
            pltpu.SemaphoreType.DMA((2 + chips,)),
        ],
        compiler_params=PARAMS,
    )(teacher_rows + 256 * positives, queries[0])
    passages_other, teacher_other = shift(passages, "core", 1), shift(teacher[0], "core", 1)
    query = lax.all_to_all(sent, CHIPS, 0, 0, tiled=True).reshape(rows, depth + LANES)

    logits, positive, stats = pl.pallas_call(
        score_kernel,
        out_shape=(
            jax.ShapeDtypeStruct((2 * CORES, block_rows, rows), f32),
            jax.ShapeDtypeStruct((1, rows), i32),
            jax.ShapeDtypeStruct((chips, STATS, rows), f32),
        ),
        in_specs=[SMEM] + [VMEM] * 4 + [ANY],
        out_specs=(VMEM,) * 3,
        scratch_shapes=[pltpu.VMEM((block_rows, depth), bf16), pltpu.SemaphoreType.DMA],
        compiler_params=PARAMS,
    )(places, query, passages, teacher[0], teacher_other, passages_other)
    slices = pl.pallas_call(
        slice_kernel,
        out_shape=(jax.ShapeDtypeStruct((rows, depth // x_size), bf16),) * x_size,
        in_specs=[SMEM, VMEM, VMEM],
        out_specs=(VMEM,) * x_size,
        compiler_params=PARAMS,
    )(x.astype(i32)[None], query, positive)
    columns = [shift(value, "x", d) for d, value in enumerate(slices)]
    stats = lax.all_to_all(stats, CHIPS, 0, 0, tiled=True)
    stats, columns = lax.optimization_barrier((stats, columns))
    columns_other = shift(jnp.stack(columns), "core", 1)

    grads, sent, losses = pl.pallas_call(
        grad_kernel,
        out_shape=(
            jax.ShapeDtypeStruct((CORES, rows, block_rows), bf16),
            jax.ShapeDtypeStruct((x_size * CORES, block_rows, rows), bf16),
            jax.ShapeDtypeStruct((1, rows), f32),
        ),
        in_specs=[SMEM] + [VMEM] * 3,
        out_specs=(VMEM, HBM, VMEM),
        scratch_shapes=[pltpu.VMEM((CORES, block_rows, rows), bf16), pltpu.SemaphoreType.DMA((x_size,))],
        compiler_params=PARAMS,
    )(places, logits, positive, stats)
    loss = lax.dynamic_slice_in_dim(losses[0], chip * own_rows, own_rows)

    block_grads = lax.all_to_all(sent, ("x", "core"), 0, 0, tiled=True)
    width = depth // x_size
    query_part = pl.pallas_call(
        query_kernel,
        grid=(x_size,),
        out_shape=jax.ShapeDtypeStruct((rows, depth), bf16),
        in_specs=[pl.BlockSpec((CORES, rows, block_rows), lambda i: (0, 0, 0))]
        + [pl.BlockSpec((block_rows, width), lambda i: (0, i))] * 2,
        out_specs=pl.BlockSpec((rows, width), lambda i: (0, i)),
        compiler_params=PARAMS,
    )(grads, passages, passages_other)
    query_part, block_grads, columns_other = lax.optimization_barrier((query_part, block_grads, columns_other))
    query_parts = lax.all_to_all(query_part.reshape(chips, own_rows, depth), CHIPS, 0, 0, tiled=True)
    query_total = pl.pallas_call(
        sum_kernel,
        out_shape=jax.ShapeDtypeStruct((own_rows, depth), bf16),
        in_specs=[VMEM],
        out_specs=VMEM,
        compiler_params=PARAMS,
    )(query_parts)

    parts = pl.pallas_call(
        functools.partial(passage_kernel, x_size),
        out_shape=(jax.ShapeDtypeStruct((block_rows, width // yh_size), bf16),) * yh_size,
        in_specs=[SMEM] + [VMEM] * (2 + x_size),
        out_specs=(VMEM,) * yh_size,
        compiler_params=PARAMS,
    )(jnp.stack([x, core, yh]).astype(i32), block_grads, *columns, columns_other)
    parts = [shift(part, "yh", d) for d, part in enumerate(parts)]
    passage_total = sum(v.astype(f32) for v in parts)
    return loss[None], query_total[None], passage_total.astype(bf16)


def solution(mesh):
    blk, qgroup = mesh.devices.shape
    split = Mesh(
        mesh.devices.reshape(YL, blk // (YL * CORES), CORES, X, qgroup // X),
        ("yl", "z", "core", "x", "yh"),
    )
    blk, qgroup = ("yl", "z", "core"), ("x", "yh")
    in_specs = (
        P(qgroup, blk, None),
        P(blk, None),
        P(qgroup, None, blk),
        P(qgroup, blk),
        P(qgroup, blk),
    )
    out_specs = (P(qgroup, blk), P(qgroup, blk, None), P(blk, qgroup))
    return jax.shard_map(per_device, mesh=split, in_specs=in_specs, out_specs=out_specs, check_vma=False)
```

time: 145 us -> 137 us (0.945)
  blocking collectives: 13.5 us -> 0 us
  starting transfers between devices: 52.4 us -> 63.5 us
  waiting for transfers between devices: 50.7 us -> 47.3 us
  local copies, waits for them, and re-layouts: 8.66 us -> 5.65 us
  other arithmetic: 1.09 us -> 2.77 us
    all_to_all x1 -> x0, blocking collectives: 13.5 us -> none  [per_device(): stats = lax.all_to_all(stats, CHIPS, 0, 0, tiled=True)]
    all_to_all x0 -> x1, starting transfers between devices: none -> 6.33 us  [per_device(): stats = lax.all_to_all(stats, CHIPS, 0, 0, tiled=True)]
    ppermute x9, waiting for transfers between devices: 22.3 us -> 18.2 us  [shift(): lax.ppermute(value, axis, [(i, (i + by) % size) for i in range(size)])]
    all_to_all x1, starting transfers between devices: 4.34 us -> 7.5 us  [per_device(): lax.all_to_all(query_part.reshape(chips, own_rows, depth), CHIPS, 0, 0, t...]
    unnamed x32 -> x20, local copies, waits for them, and re-layouts: 7.89 us -> 5.07 us
    ppermute x9, starting transfers between devices: 36.8 us -> 39.5 us  [shift(): lax.ppermute(value, axis, [(i, (i + by) % size) for i in range(size)])]
    pallas_call x2 -> x3, Pallas kernels: 4.97 us -> 5.89 us  [the longest x1 3.93 us: per_device(): pl.pallas_call(score_kernel, out_shape=(jax.ShapeDtypeStruct((2 * CORES,...]
  transfers between devices with their start and end apart: 12 -> 13, of which waited for: 8 -> 8; matrix products, arithmetic and copies ran while one was open for 1% -> 2% of each run, Pallas kernels for 5% -> 8%
where the time goes in v6:
time: 137 us; the launch traced here: 136 us
  starting transfers between devices  63.5 us (46%)
  waiting for transfers between devices  47.3 us (35%)
  Pallas kernels  16.2 us (12%)
  local copies, waits for them, and re-layouts  5.65 us (4%)
  other arithmetic  2.77 us (2%)
    ppermute x9, starting transfers between devices, shift(): lax.ppermute(value, axis, [(i, (i + by) % size) for i in range(size)])  39.5 us
    all_to_all x1, waiting for transfers between devices, per_device(): lax.all_to_all(sent, CHIPS, 0, 0, tiled=True).reshape(rows, depth + LANES)  23.9 us
    ppermute x9, waiting for transfers between devices, shift(): lax.ppermute(value, axis, [(i, (i + by) % size) for i in range(size)])  18.2 us
    all_to_all x1, starting transfers between devices, per_device(): lax.all_to_all(query_part.reshape(chips, own_rows, depth), CHIPS, 0, 0, t...  7.5 us
    all_to_all x1, starting transfers between devices, per_device(): stats = lax.all_to_all(stats, CHIPS, 0, 0, tiled=True)  6.33 us
    all_to_all x1, starting transfers between devices, per_device(): lax.all_to_all(sent, CHIPS, 0, 0, tiled=True).reshape(rows, depth + LANES)  5.78 us
    all_to_all x1, waiting for transfers between devices, per_device(): block_grads = lax.all_to_all(sent, ('x', 'core'), 0, 0, tiled=True)  5.22 us
    unnamed x20, local copies, waits for them, and re-layouts  5.07 us
  transfers between devices with their start and end apart: 13, of which 8 were waited for; matrix products, arithmetic and copies ran while one was open for 2% of the time, Pallas kernels for 8%

profile of v6, /device:TPU:1, one launch (start us, length us, event | category | flops | bytes accessed | tf_op | source)
XLA Modules:
  0.0 136.3 jit_solution(404725592429574453)
XLA Ops:
  0.6 0.0 copy-start
  0.6 0.0 copy-start.7
  0.7 8.9 %collective-permute-start.1 = (bf16[256,4096]{1,0:T(8,128)(2,1)}, bf16[256,4096]{1,0:T(8,128)(2,1)}, u32[]{:S(2)}, u32[]{:S(2)}) collective-permute-start(bf16[256,4096]{1,0:T(8,128)(2,1)} %passages.3), channel_id=1, source_target_pairs={{0,16},{16,0},{1,17},{17,1},{2,18},{18,2},{3,19},{19,3},{4,20},{20... | collective-permute-start | bytes 6291464 | tf_op jit(solution)/shard_map/ppermute | solution.py:27
  9.6 0.7 multiply_add_fusion.indices
  10.3 0.0 copy-start.9
  10.3 0.8 copy-done.9
  11.1 2.1 %shard_map.76 = bf16[16,8,4224]{2,1,0:T(8,128)(2,1)S(1)} custom-call(s32[1,8]{1,0:T(1,128)S(1)} %multiply_add_fusion.indices, bf16[8,4096]{1,0:T(8,128)(2,1)S(1)} %bitcast.21), custom_call_target="tpu_custom_call" | custom-call | tf_op jit(solution)/shard_map/pallas_call | solution.py:173
  13.2 0.0 copy-start.1
  13.2 1.0 copy-done.1
  14.2 5.8 %all-to-all-start = ((bf16[16,8,4224]{2,1,0:T(8,128)(2,1)}), bf16[16,8,4224]{2,1,0:T(8,128)(2,1)S(1)}, u32[]{:S(2)}, u32[]{:S(2)}) async-start(bf16[16,8,4224]{2,1,0:T(8,128)(2,1)} %copy-done.1), calls=%async_computation | async-start | bytes 2162688 | tf_op jit(solution)/shard_map/all_to_all | solution.py:186
  20.0 0.0 copy-done.7
  20.0 2.2 %collective-permute-start = (f32[256,256]{1,0:T(8,128)S(1)}, f32[256,256]{1,0:T(8,128)}, u32[]{:S(2)}, u32[]{:S(2)}) collective-permute-start(f32[256,256]{1,0:T(8,128)S(1)} %bitcast.19), channel_id=1, source_target_pairs={{0,16},{16,0},{1,17},{17,1},{2,18},{18,2},{3,19},{19,3},{4,20},{20... | collective-permute-start | bytes 786440 | tf_op jit(solution)/shard_map/ppermute | solution.py:27
  22.2 0.1 fusion
  22.3 0.1 pad_add_fusion.places
  22.4 1.2 collective-permute-done.teacher_other
  23.6 23.9 %all-to-all-done = bf16[16,8,4224]{2,1,0:T(8,128)(2,1)S(1)} async-done(((bf16[16,8,4224]{2,1,0:T(8,128)(2,1)}), bf16[16,8,4224]{2,1,0:T(8,128)(2,1)S(1)}, u32[]{:S(2)}, u32[]{:S(2)}) %all-to-all-start) | async-done | bytes 1081376 | tf_op jit(solution)/shard_map/all_to_all | solution.py:186
  47.4 0.0 collective-permute-done.1.passages_other
  47.4 0.0 copy-done
  47.4 3.9 %shard_map.77 = (f32[4,256,128]{2,1,0:T(8,128)S(1)}, s32[1,128]{1,0:T(1,128)S(1)}, f32[16,24,128]{2,1,0:T(8,128)S(1)}) custom-call(s32[4]{0:T(128)S(1)} %pad_add_fusion.places, bf16[128,4224]{1,0:T(8,128)(2,1)S(1)} %bitcast.13, bf16[256,4096]{1,0:T(8,128)(2,1)S(1)} %copy-done, f32[256,256]{1,0:T(8,128)S(1)} %bitcast.20, ...), custom_call_target="tpu_custom_call" | custom-call | tf_op jit(solution)/shard_map/pallas_call | solution.py:188
  51.4 0.0 copy-start.4
  51.4 0.8 copy-done.4
  52.2 0.0 copy-start.8
  52.2 0.7 copy-done.8
  52.9 6.3 %all-to-all-start.1 = ((f32[16,24,128]{2,1,0:T(8,128)}), f32[16,24,128]{2,1,0:T(8,128)}, u32[]{:S(2)}, u32[]{:S(2)}) async-start(f32[16,24,128]{2,1,0:T(8,128)} %copy-done.8), calls=%async_computation.1 | async-start | bytes 393216 | tf_op jit(solution)/shard_map/all_to_all | solution.py:208
  59.2 0.1 shard_map.78
  59.3 3.1 %collective-permute-start.2 = (bf16[128,1024]{1,0:T(8,128)(2,1)S(1)}, bf16[128,1024]{1,0:T(8,128)(2,1)S(1)}, u32[]{:S(2)}, u32[]{:S(2)}) collective-permute-start(bf16[128,1024]{1,0:T(8,128)(2,1)S(1)} %get-tuple-element.29), channel_id=1, source_target_pairs={{0,4},{4,8},{8,12},{12,0},{1,5},{5,9},{9,13},{13,1},{2,6},{6,10},{... | collective-permute-start | bytes 786440 | tf_op jit(solution)/shard_map/ppermute | solution.py:27
  62.4 4.4 %collective-permute-start.3 = (bf16[128,1024]{1,0:T(8,128)(2,1)S(1)}, bf16[128,1024]{1,0:T(8,128)(2,1)S(1)}, u32[]{:S(2)}, u32[]{:S(2)}) collective-permute-start(bf16[128,1024]{1,0:T(8,128)(2,1)S(1)} %get-tuple-element.30), channel_id=1, source_target_pairs={{0,8},{4,12},{8,0},{12,4},{1,9},{5,13},{9,1},{13,5},{2,10},{6,14},... | collective-permute-start | bytes 786440 | tf_op jit(solution)/shard_map/ppermute | solution.py:27
  66.8 3.1 %collective-permute-start.4 = (bf16[128,1024]{1,0:T(8,128)(2,1)S(1)}, bf16[128,1024]{1,0:T(8,128)(2,1)S(1)}, u32[]{:S(2)}, u32[]{:S(2)}) collective-permute-start(bf16[128,1024]{1,0:T(8,128)(2,1)S(1)} %get-tuple-element.31), channel_id=1, source_target_pairs={{0,12},{4,0},{8,4},{12,8},{1,13},{5,1},{9,5},{13,9},{2,14},{6,2},{... | collective-permute-start | bytes 786440 | tf_op jit(solution)/shard_map/ppermute | solution.py:27
  69.9 0.0 collective-permute-done.2.refs_1_
  69.9 6.2 %collective-permute-done.3.refs_2_ = bf16[128,1024]{1,0:T(8,128)(2,1)S(1)} collective-permute-done((bf16[128,1024]{1,0:T(8,128)(2,1)S(1)}, bf16[128,1024]{1,0:T(8,128)(2,1)S(1)}, u32[]{:S(2)}, u32[]{:S(2)}) %collective-permute-start.3) | collective-permute-done | bytes 262176 | tf_op jit(solution)/shard_map/ppermute | solution.py:27
  76.1 1.2 collective-permute-done.4.refs_3_
  77.3 0.0 copy-start.2
  77.3 0.0 all-to-all-done.1.stats
  77.3 0.0 copy-start.5
  77.3 1.1 pad_maximum_fusion
  78.4 3.9 %collective-permute-start.5 = (bf16[4,128,1024]{2,1,0:T(8,128)(2,1)}, bf16[4,128,1024]{2,1,0:T(8,128)(2,1)}, u32[]{:S(2)}, u32[]{:S(2)}) collective-permute-start(bf16[4,128,1024]{2,1,0:T(8,128)(2,1)} %pad_maximum_fusion), channel_id=1, source_target_pairs={{0,16},{16,0},{1,17},{17,1},{2,18},{18,2},{3,19},{19,3},{4,20},{20... | collective-permute-start | bytes 3145736 | tf_op jit(solution)/shard_map/ppermute | solution.py:27
  82.3 0.0 copy-done.5
  82.3 1.9 %shard_map.79 = (bf16[2,128,256]{2,1,0:T(8,128)(2,1)S(1)}, bf16[8,256,128]{2,1,0:T(8,128)(2,1)S(1)}, f32[1,128]{1,0:T(1,128)S(1)}) custom-call(s32[4]{0:T(128)S(1)} %pad_add_fusion.places, f32[4,256,128]{2,1,0:T(8,128)S(1)} %copy-done.5, s32[1,128]{1,0:T(1,128)S(1)} %get-tuple-element.26.after.positives, f32[16,24,128]{2,1,0:T(8,128)} %all-to-all-done.1.stats), custom_call_target="tpu_custom_call" | custom-call | tf_op jit(solution)/shard_map/pallas_call | solution.py:212
  84.2 0.0 copy-start.6
  84.2 0.8 copy-done.6
  85.0 0.0 copy-done.2
  85.0 4.5 %all-to-all-start.2 = ((bf16[8,256,128]{2,1,0:T(8,128)(2,1)}), bf16[8,256,128]{2,1,0:T(8,128)(2,1)S(1)}, u32[]{:S(2)}, u32[]{:S(2)}) async-start(bf16[8,256,128]{2,1,0:T(8,128)(2,1)} %copy-done.6), calls=%async_computation.2 | async-start | bytes 1048576 | tf_op jit(solution)/shard_map/all_to_all | solution.py:226
  89.5 4.3 %shard_map.80 = bf16[128,4096]{1,0:T(8,128)(2,1)} custom-call(bf16[2,128,256]{2,1,0:T(8,128)(2,1)S(1)} %get-tuple-element.34.grads, bf16[256,4096]{1,0:T(8,128)(2,1)S(1)} %copy-done, bf16[256,4096]{1,0:T(8,128)(2,1)} %collective-permute-done.1.passages_other), custom_call_target="tpu_custom_call" | custom-call | tf_op jit(solution)/shard_map/pallas_call | solution.py:228
  93.7 5.2 %all-to-all-done.2.grads = bf16[8,256,128]{2,1,0:T(8,128)(2,1)S(1)} async-done(((bf16[8,256,128]{2,1,0:T(8,128)(2,1)}), bf16[8,256,128]{2,1,0:T(8,128)(2,1)S(1)}, u32[]{:S(2)}, u32[]{:S(2)}) %all-to-all-start.2) | async-done | bytes 524320 | tf_op jit(solution)/shard_map/all_to_all | solution.py:226
  98.9 0.0 collective-permute-done.5.refs_4_
  98.9 7.5 %all-to-all-start.3 = ((bf16[16,8,4096]{2,1,0:T(8,128)(2,1)}), bf16[16,8,4096]{2,1,0:T(8,128)(2,1)S(1)}, u32[]{:S(2)}, u32[]{:S(2)}) async-start(bf16[16,8,4096]{2,1,0:T(8,128)(2,1)} %bitcast.10), calls=%async_computation.3 | async-start | bytes 2097152 | tf_op jit(solution)/shard_map/all_to_all | solution.py:238
  106.4 0.1 pad_add_fusion.1.position
  106.5 0.0 copy-start.3
  106.5 0.9 copy-done.3
  107.5 3.2 %shard_map.82 = (bf16[256,256]{1,0:T(8,128)(2,1)S(1)}, bf16[256,256]{1,0:T(8,128)(2,1)}, bf16[256,256]{1,0:T(8,128)(2,1)}, bf16[256,256]{1,0:T(8,128)(2,1)}) custom-call(s32[3]{0:T(128)S(1)} %pad_add_fusion.1.position, bf16[8,256,128]{2,1,0:T(8,128)(2,1)S(1)} %all-to-all-done.2.grads, bf16[128,1024]{1,0:T(8,128)(2,1)S(1)} %get-tuple-element.36.refs_0_, ...), custom_call_target="tpu_custom_call" | custom-call | tf_op jit(solution)/shard_map/pallas_call | solution.py:247
  110.6 4.2 %collective-permute-start.6 = (bf16[256,256]{1,0:T(8,128)(2,1)}, bf16[256,256]{1,0:T(8,128)(2,1)S(1)}, u32[]{:S(2)}, u32[]{:S(2)}) collective-permute-start(bf16[256,256]{1,0:T(8,128)(2,1)} %get-tuple-element.44), channel_id=1, source_target_pairs={{0,1},{1,2},{2,3},{3,0},{4,5},{5,6},{6,7},{7,4},{8,9},{9,10},{10,1... | collective-permute-start | bytes 393224 | tf_op jit(solution)/shard_map/ppermute | solution.py:27
  114.9 4.8 %collective-permute-start.7 = (bf16[256,256]{1,0:T(8,128)(2,1)}, bf16[256,256]{1,0:T(8,128)(2,1)S(1)}, u32[]{:S(2)}, u32[]{:S(2)}) collective-permute-start(bf16[256,256]{1,0:T(8,128)(2,1)} %get-tuple-element.45), channel_id=1, source_target_pairs={{0,2},{1,3},{2,0},{3,1},{4,6},{5,7},{6,4},{7,5},{8,10},{9,11},{10,... | collective-permute-start | bytes 393224 | tf_op jit(solution)/shard_map/ppermute | solution.py:27
  119.6 5.0 %collective-permute-start.8 = (bf16[256,256]{1,0:T(8,128)(2,1)}, bf16[256,256]{1,0:T(8,128)(2,1)S(1)}, u32[]{:S(2)}, u32[]{:S(2)}) collective-permute-start(bf16[256,256]{1,0:T(8,128)(2,1)} %get-tuple-element.46), channel_id=1, source_target_pairs={{0,3},{1,0},{2,1},{3,2},{4,7},{5,4},{6,5},{7,6},{8,11},{9,8},{10,9... | collective-permute-start | bytes 393224 | tf_op jit(solution)/shard_map/ppermute | solution.py:27
  124.6 0.6 constant_dynamic-slice_fusion
  125.2 1.6 %collective-permute-done.6 = bf16[256,256]{1,0:T(8,128)(2,1)S(1)} collective-permute-done((bf16[256,256]{1,0:T(8,128)(2,1)}, bf16[256,256]{1,0:T(8,128)(2,1)S(1)}, u32[]{:S(2)}, u32[]{:S(2)}) %collective-permute-start.6) | collective-permute-done | bytes 131104 | tf_op jit(solution)/shard_map/ppermute | solution.py:27
  126.8 5.1 %collective-permute-done.7 = bf16[256,256]{1,0:T(8,128)(2,1)S(1)} collective-permute-done((bf16[256,256]{1,0:T(8,128)(2,1)}, bf16[256,256]{1,0:T(8,128)(2,1)S(1)}, u32[]{:S(2)}, u32[]{:S(2)}) %collective-permute-start.7) | collective-permute-done | bytes 131104 | tf_op jit(solution)/shard_map/ppermute | solution.py:27
  131.9 2.9 %collective-permute-done.8 = bf16[256,256]{1,0:T(8,128)(2,1)S(1)} collective-permute-done((bf16[256,256]{1,0:T(8,128)(2,1)}, bf16[256,256]{1,0:T(8,128)(2,1)S(1)}, u32[]{:S(2)}, u32[]{:S(2)}) %collective-permute-start.8) | collective-permute-done | bytes 131104 | tf_op jit(solution)/shard_map/ppermute | solution.py:27
  134.8 0.7 add_convert_fusion
  135.5 0.0 all-to-all-done.3.parts
  135.5 0.8 shard_map.81
Async XLA Ops:
  0.6 46.8 %copy-start = (bf16[256,4096]{1,0:T(8,128)(2,1)S(1)}, bf16[256,4096]{1,0:T(8,128)(2,1)}, u32[]{:S(2)}) copy-start(bf16[256,4096]{1,0:T(8,128)(2,1)} %passages.3) | copy-start | bytes 6291460
  0.6 19.4 %copy-start.7 = (f32[1,256,256]{2,1,0:T(8,128)S(1)}, f32[1,256,256]{2,1,0:T(8,128)}, u32[]{:S(2)}) copy-start(f32[1,256,256]{2,1,0:T(8,128)} %param.7) | copy-start | bytes 786436
  0.7 46.8 %collective-permute-start.1 = (bf16[256,4096]{1,0:T(8,128)(2,1)}, bf16[256,4096]{1,0:T(8,128)(2,1)}, u32[]{:S(2)}, u32[]{:S(2)}) collective-permute-start(bf16[256,4096]{1,0:T(8,128)(2,1)} %passages.3), channel_id=1, source_target_pairs={{0,16},{16,0},{1,17},{17,1},{2,18},{18,2},{3,19},{19,3},{4,20},{20... | collective-permute-start | bytes 6291464 | tf_op jit(solution)/shard_map/ppermute | solution.py:27
  10.3 0.8 copy-start.9
  13.2 1.0 copy-start.1
  14.2 33.2 %all-to-all-start = ((bf16[16,8,4224]{2,1,0:T(8,128)(2,1)}), bf16[16,8,4224]{2,1,0:T(8,128)(2,1)S(1)}, u32[]{:S(2)}, u32[]{:S(2)}) async-start(bf16[16,8,4224]{2,1,0:T(8,128)(2,1)} %copy-done.1), calls=%async_computation | async-start | bytes 2162688 | tf_op jit(solution)/shard_map/all_to_all | solution.py:186
  20.0 3.6 %collective-permute-start = (f32[256,256]{1,0:T(8,128)S(1)}, f32[256,256]{1,0:T(8,128)}, u32[]{:S(2)}, u32[]{:S(2)}) collective-permute-start(f32[256,256]{1,0:T(8,128)S(1)} %bitcast.19), channel_id=1, source_target_pairs={{0,16},{16,0},{1,17},{17,1},{2,18},{18,2},{3,19},{19,3},{4,20},{20... | collective-permute-start | bytes 786440 | tf_op jit(solution)/shard_map/ppermute | solution.py:27
  51.4 0.8 copy-start.4
  52.2 0.7 copy-start.8
  52.9 24.4 %all-to-all-start.1 = ((f32[16,24,128]{2,1,0:T(8,128)}), f32[16,24,128]{2,1,0:T(8,128)}, u32[]{:S(2)}, u32[]{:S(2)}) async-start(f32[16,24,128]{2,1,0:T(8,128)} %copy-done.8), calls=%async_computation.1 | async-start | bytes 393216 | tf_op jit(solution)/shard_map/all_to_all | solution.py:208
  59.3 10.6 %collective-permute-start.2 = (bf16[128,1024]{1,0:T(8,128)(2,1)S(1)}, bf16[128,1024]{1,0:T(8,128)(2,1)S(1)}, u32[]{:S(2)}, u32[]{:S(2)}) collective-permute-start(bf16[128,1024]{1,0:T(8,128)(2,1)S(1)} %get-tuple-element.29), channel_id=1, source_target_pairs={{0,4},{4,8},{8,12},{12,0},{1,5},{5,9},{9,13},{13,1},{2,6},{6,10},{... | collective-permute-start | bytes 786440 | tf_op jit(solution)/shard_map/ppermute | solution.py:27
  62.4 13.7 %collective-permute-start.3 = (bf16[128,1024]{1,0:T(8,128)(2,1)S(1)}, bf16[128,1024]{1,0:T(8,128)(2,1)S(1)}, u32[]{:S(2)}, u32[]{:S(2)}) collective-permute-start(bf16[128,1024]{1,0:T(8,128)(2,1)S(1)} %get-tuple-element.30), channel_id=1, source_target_pairs={{0,8},{4,12},{8,0},{12,4},{1,9},{5,13},{9,1},{13,5},{2,10},{6,14},... | collective-permute-start | bytes 786440 | tf_op jit(solution)/shard_map/ppermute | solution.py:27
  66.8 10.5 %collective-permute-start.4 = (bf16[128,1024]{1,0:T(8,128)(2,1)S(1)}, bf16[128,1024]{1,0:T(8,128)(2,1)S(1)}, u32[]{:S(2)}, u32[]{:S(2)}) collective-permute-start(bf16[128,1024]{1,0:T(8,128)(2,1)S(1)} %get-tuple-element.31), channel_id=1, source_target_pairs={{0,12},{4,0},{8,4},{12,8},{1,13},{5,1},{9,5},{13,9},{2,14},{6,2},{... | collective-permute-start | bytes 786440 | tf_op jit(solution)/shard_map/ppermute | solution.py:27
  77.3 7.7 %copy-start.2 = (bf16[128,1024]{1,0:T(8,128)(2,1)}, bf16[128,1024]{1,0:T(8,128)(2,1)S(1)}, u32[]{:S(2)}) copy-start(bf16[128,1024]{1,0:T(8,128)(2,1)S(1)} %collective-permute-done.4.refs_3_) | copy-start | bytes 786436
  77.3 5.0 %copy-start.5 = (f32[4,256,128]{2,1,0:T(8,128)S(1)}, f32[4,256,128]{2,1,0:T(8,128)}, u32[]{:S(2)}) copy-start(f32[4,256,128]{2,1,0:T(8,128)} %copy-done.4) | copy-start | bytes 1572868
  78.4 20.5 %collective-permute-start.5 = (bf16[4,128,1024]{2,1,0:T(8,128)(2,1)}, bf16[4,128,1024]{2,1,0:T(8,128)(2,1)}, u32[]{:S(2)}, u32[]{:S(2)}) collective-permute-start(bf16[4,128,1024]{2,1,0:T(8,128)(2,1)} %pad_maximum_fusion), channel_id=1, source_target_pairs={{0,16},{16,0},{1,17},{17,1},{2,18},{18,2},{3,19},{19,3},{4,20},{20... | collective-permute-start | bytes 3145736 | tf_op jit(solution)/shard_map/ppermute | solution.py:27
  84.2 0.8 copy-start.6
  85.0 13.9 %all-to-all-start.2 = ((bf16[8,256,128]{2,1,0:T(8,128)(2,1)}), bf16[8,256,128]{2,1,0:T(8,128)(2,1)S(1)}, u32[]{:S(2)}, u32[]{:S(2)}) async-start(bf16[8,256,128]{2,1,0:T(8,128)(2,1)} %copy-done.6), calls=%async_computation.2 | async-start | bytes 1048576 | tf_op jit(solution)/shard_map/all_to_all | solution.py:226
  98.9 36.6 %all-to-all-start.3 = ((bf16[16,8,4096]{2,1,0:T(8,128)(2,1)}), bf16[16,8,4096]{2,1,0:T(8,128)(2,1)S(1)}, u32[]{:S(2)}, u32[]{:S(2)}) async-start(bf16[16,8,4096]{2,1,0:T(8,128)(2,1)} %bitcast.10), calls=%async_computation.3 | async-start | bytes 2097152 | tf_op jit(solution)/shard_map/all_to_all | solution.py:238
  106.5 1.0 copy-start.3
  110.6 16.2 %collective-permute-start.6 = (bf16[256,256]{1,0:T(8,128)(2,1)}, bf16[256,256]{1,0:T(8,128)(2,1)S(1)}, u32[]{:S(2)}, u32[]{:S(2)}) collective-permute-start(bf16[256,256]{1,0:T(8,128)(2,1)} %get-tuple-element.44), channel_id=1, source_target_pairs={{0,1},{1,2},{2,3},{3,0},{4,5},{5,6},{6,7},{7,4},{8,9},{9,10},{10,1... | collective-permute-start | bytes 393224 | tf_op jit(solution)/shard_map/ppermute | solution.py:27
  114.9 17.1 %collective-permute-start.7 = (bf16[256,256]{1,0:T(8,128)(2,1)}, bf16[256,256]{1,0:T(8,128)(2,1)S(1)}, u32[]{:S(2)}, u32[]{:S(2)}) collective-permute-start(bf16[256,256]{1,0:T(8,128)(2,1)} %get-tuple-element.45), channel_id=1, source_target_pairs={{0,2},{1,3},{2,0},{3,1},{4,6},{5,7},{6,4},{7,5},{8,10},{9,11},{10,... | collective-permute-start | bytes 393224 | tf_op jit(solution)/shard_map/ppermute | solution.py:27
  119.6 15.1 %collective-permute-start.8 = (bf16[256,256]{1,0:T(8,128)(2,1)}, bf16[256,256]{1,0:T(8,128)(2,1)S(1)}, u32[]{:S(2)}, u32[]{:S(2)}) collective-permute-start(bf16[256,256]{1,0:T(8,128)(2,1)} %get-tuple-element.46), channel_id=1, source_target_pairs={{0,3},{1,0},{2,1},{3,2},{4,7},{5,4},{6,5},{7,6},{8,11},{9,8},{10,9... | collective-permute-start | bytes 393224 | tf_op jit(solution)/shard_map/ppermute | solution.py:27

commit v7 on v6

v7 whole, which is shorter than its diff:
```python
import functools

import jax
import jax.numpy as jnp
from jax import lax
from jax.experimental import pallas as pl
from jax.experimental.pallas import tpu as pltpu
from jax.sharding import Mesh, PartitionSpec as P

inv_temp = 50.0
YL, CORES, X = 2, 2, 4
LANES = 128
STATS = 8
CHIPS = ("yl", "z")
f32, bf16, i32 = jnp.float32, jnp.bfloat16, jnp.int32
VMEM = pl.BlockSpec(memory_space=pltpu.VMEM)
ANY = pl.BlockSpec(memory_space=pl.ANY)
SMEM = pl.BlockSpec(memory_space=pltpu.SMEM)
PARAMS = pltpu.CompilerParams(vmem_limit_bytes=16 * 1024 * 1024)


def shift(value, axis, by):
    if by == 0:
        return value
    size = lax.axis_size(axis)
    return lax.ppermute(value, axis, [(i, (i + by) % size) for i in range(size)])


def hits(positive, place, shape):
    return lax.broadcasted_iota(i32, shape, 0) + place == positive


def score_kernel(places, query, passages, passages_other, teacher, teacher_other, values, positives, stats):
    depth = passages.shape[1]
    rows = query.shape[0]
    codes = query[:, depth:].astype(f32).T
    row_index = codes[0:1].astype(i32)
    positive = codes[1:2].astype(i32) + 256 * codes[2:3].astype(i32)
    positives[...] = positive
    pick = (lax.broadcasted_iota(i32, (teacher.shape[0], rows), 0) == row_index).astype(f32)
    parts = []
    for half, (block, table) in enumerate(((passages, teacher), (passages_other, teacher_other))):
        s = inv_temp * lax.dot_general(
            block[...], query[:, :depth], (((1,), (1,)), ((), ())), preferred_element_type=f32
        )
        t = lax.dot_general(
            table[...], pick, (((0,), (0,)), ((), ())),
            precision=lax.Precision.HIGHEST, preferred_element_type=f32,
        )
        values[half] = s
        values[CORES + half] = t
        parts.append((s, t, hits(positive, places[half], s.shape)))
    top_s, top_t = (jnp.maximum(*[jnp.max(p[i], axis=0, keepdims=True) for p in parts]) for i in (0, 1))
    sums = []
    for s, t, hot in parts:
        below_s, below_t = s - top_s, t - top_t
        weight = jnp.exp(below_t)
        terms = (jnp.exp(below_s), weight, weight * (below_t - below_s), jnp.where(hot, s, 0.0))
        sums.append([jnp.sum(v, axis=0, keepdims=True) for v in terms])
    sums = [a + b for a, b in zip(*sums)]
    whole = jnp.concatenate([top_s, top_t] + sums + [jnp.zeros((STATS - 6, rows), f32)], axis=0)
    stats[...] = jnp.broadcast_to(whole[None], stats.shape)


def slice_kernel(x, query, after, *outs):
    del after
    width = outs[0].shape[1]
    for d, out in enumerate(outs):
        out[...] = query[:, pl.ds(pl.multiple_of(lax.rem(x[0] + d, len(outs)) * width, width), width)]


def grad_kernel(places, logits, positives, stats, rows_first, grads, grads_other, losses):
    tops_s, tops_t, sums_s, sums_t, cross, hit = (stats[:, i, :] for i in range(6))
    top_s, top_t = jnp.max(tops_s, axis=0, keepdims=True), jnp.max(tops_t, axis=0, keepdims=True)
    lower_s, lower_t = tops_s - top_s, tops_t - top_t
    total_s = jnp.sum(jnp.exp(lower_s) * sums_s, axis=0, keepdims=True)
    weight_t = jnp.exp(lower_t)
    total_t = jnp.sum(weight_t * sums_t, axis=0, keepdims=True)
    cross = jnp.sum(weight_t * (cross + (lower_t - lower_s) * sums_t), axis=0, keepdims=True)
    log_s = jnp.log(total_s)
    own = jnp.sum(hit, axis=0, keepdims=True)
    losses[...] = cross / total_t - jnp.log(total_t) + log_s - (own - top_s - log_s)
    scale_s, scale_t = 2.0 * inv_temp / total_s, inv_temp / total_t
    for half, out in enumerate((grads, grads_other)):
        hot = hits(positives[...], places[half], out.shape)
        values = (
            jnp.exp(logits[half] - top_s) * scale_s
            - jnp.exp(logits[CORES + half] - top_t) * scale_t
            - jnp.where(hot, inv_temp, 0.0)
        )
        rows_first[half] = values.T.astype(bf16)
        out[...] = values.astype(bf16)


def query_kernel(grads, passages, passages_other, out):
    total = jnp.dot(grads[0], passages[...], preferred_element_type=f32)
    total += jnp.dot(grads[1], passages_other[...], preferred_element_type=f32)
    out[...] = total.astype(bf16)


def passage_kernel(groups, *refs):
    grads, query, query_other, out = refs[:groups], refs[groups : 2 * groups], refs[2 * groups], refs[-1]
    width = out.shape[2]
    for yh in range(out.shape[0]):
        columns = slice(yh * width, (yh + 1) * width)
        total = jnp.zeros(out.shape[1:], f32)
        for d in range(groups):
            total += jnp.dot(grads[d][0], query[d][:, columns], preferred_element_type=f32)
            total += jnp.dot(grads[d][1], query_other[d, :, columns], preferred_element_type=f32)
        out[yh] = total.astype(bf16)


def sum_kernel(parts, out):
    total = parts[0].astype(f32)
    for i in range(1, parts.shape[0]):
        total += parts[i].astype(f32)
    out[...] = total.astype(bf16)


def per_device(queries, passages, teacher, teacher_rows, positives):
    own_rows, depth = queries.shape[1:]
    block_rows = passages.shape[0]
    chips = lax.axis_size("yl") * lax.axis_size("z")
    x_size, yh_size = lax.axis_size("x"), lax.axis_size("yh")
    rows = chips * own_rows
    chip = lax.axis_index("yl") * lax.axis_size("z") + lax.axis_index("z")
    core, x, yh = lax.axis_index("core"), lax.axis_index("x"), lax.axis_index("yh")
    cores = jnp.stack([core, 1 - core])
    places = jnp.concatenate([(chip * CORES + cores) * block_rows, cores]).astype(i32)

    indices = jnp.stack(
        [teacher_rows[0], positives[0] % 256, positives[0] // 256], axis=1
    ).astype(bf16)
    sent = jnp.concatenate(
        [queries[0], jnp.pad(indices, ((0, 0), (0, LANES - indices.shape[1])))], axis=1
    )
    passages_other, teacher_other = shift(passages, "core", 1), shift(teacher[0], "core", 1)
    query = lax.all_to_all(
        jnp.broadcast_to(sent[None], (chips,) + sent.shape), CHIPS, 0, 0, tiled=True
    ).reshape(rows, depth + LANES)

    logits, positive, stats = pl.pallas_call(
        score_kernel,
        out_shape=(
            jax.ShapeDtypeStruct((2 * CORES, block_rows, rows), f32),
            jax.ShapeDtypeStruct((1, rows), i32),
            jax.ShapeDtypeStruct((chips, STATS, rows), f32),
        ),
        in_specs=[SMEM] + [VMEM] * 5,
        out_specs=(VMEM,) * 3,
        compiler_params=PARAMS,
    )(places, query, passages, passages_other, teacher[0], teacher_other)
    stats = lax.all_to_all(stats, CHIPS, 0, 0, tiled=True)
    rows_first, grads, grads_other, losses = pl.pallas_call(
        grad_kernel,
        out_shape=(
            jax.ShapeDtypeStruct((CORES, rows, block_rows), bf16),
            jax.ShapeDtypeStruct((block_rows, rows), bf16),
            jax.ShapeDtypeStruct((block_rows, rows), bf16),
            jax.ShapeDtypeStruct((1, rows), f32),
        ),
        in_specs=[SMEM] + [VMEM] * 3,
        out_specs=(VMEM,) * 4,
        compiler_params=PARAMS,
    )(places, logits, positive, stats)
    loss = lax.dynamic_slice_in_dim(losses[0], chip * own_rows, own_rows)

    width = depth // x_size
    query_part = pl.pallas_call(
        query_kernel,
        grid=(x_size,),
        out_shape=jax.ShapeDtypeStruct((rows, depth), bf16),
        in_specs=[pl.BlockSpec((CORES, rows, block_rows), lambda i: (0, 0, 0))]
        + [pl.BlockSpec((block_rows, width), lambda i: (0, i))] * 2,
        out_specs=pl.BlockSpec((rows, width), lambda i: (0, i)),
        compiler_params=PARAMS,
    )(rows_first, passages, passages_other)
    query_part, grads_back = lax.optimization_barrier((query_part, shift(grads_other, "core", 1)))
    query_parts = lax.all_to_all(query_part.reshape(chips, own_rows, depth), CHIPS, 0, 0, tiled=True)

    slices = pl.pallas_call(
        slice_kernel,
        out_shape=(jax.ShapeDtypeStruct((rows, width), bf16),) * x_size,
        in_specs=[SMEM, VMEM, ANY],
        out_specs=(VMEM,) * x_size,
        compiler_params=PARAMS,
    )(x.astype(i32)[None], query, query_part)
    columns = [shift(value, "x", d) for d, value in enumerate(slices)]
    block_grads = jnp.stack([grads, grads_back])
    block_grads = [shift(block_grads, "x", d) for d in range(x_size)]
    columns, block_grads = lax.optimization_barrier((columns, block_grads))
    columns_other = shift(jnp.stack(columns), "core", 1)
    part = pl.pallas_call(
        functools.partial(passage_kernel, x_size),
        out_shape=jax.ShapeDtypeStruct((yh_size, block_rows, width // yh_size), bf16),
        in_specs=[VMEM] * (2 * x_size + 1),
        out_specs=VMEM,
        compiler_params=PARAMS,
    )(*block_grads, *columns, columns_other)
    query_parts, part = lax.optimization_barrier((query_parts, part))
    part = lax.all_to_all(part, "yh", 0, 0, tiled=True)
    query_total, passage_total = (
        pl.pallas_call(
            sum_kernel,
            out_shape=jax.ShapeDtypeStruct(value.shape[1:], bf16),
            in_specs=[VMEM],
            out_specs=VMEM,
            compiler_params=PARAMS,
        )(value)
        for value in (query_parts, part)
    )
    return loss[None], query_total[None], passage_total


def solution(mesh):
    blk, qgroup = mesh.devices.shape
    split = Mesh(
        mesh.devices.reshape(YL, blk // (YL * CORES), CORES, X, qgroup // X),
        ("yl", "z", "core", "x", "yh"),
    )
    blk, qgroup = ("yl", "z", "core"), ("x", "yh")
    in_specs = (
        P(qgroup, blk, None),
        P(blk, None),
        P(qgroup, None, blk),
        P(qgroup, blk),
        P(qgroup, blk),
    )
    out_specs = (P(qgroup, blk), P(qgroup, blk, None), P(blk, qgroup))
    return jax.shard_map(per_device, mesh=split, in_specs=in_specs, out_specs=out_specs, check_vma=False)
```

time: 137 us -> 133 us (0.971)
  the two profiles are of different devices: /device:TPU:1 before, /device:TPU:8 now
where the time goes in v7:
time: 133 us; the launch traced here: 132 us
  starting transfers between devices  51.1 us (38%)
  waiting for transfers between devices  50.6 us (38%)
  blocking collectives  13.3 us (10%)
  Pallas kernels  12.2 us (9%)
  other arithmetic  2.49 us (2%)
  local copies, waits for them, and re-layouts  1.75 us (1%)
    ppermute x10, starting transfers between devices, shift(): lax.ppermute(value, axis, [(i, (i + by) % size) for i in range(size)])  28.2 us
    all_to_all x1, waiting for transfers between devices, per_device(): lax.all_to_all(jnp.broadcast_to(sent[None], (chips,) + sent.shape), CHIPS...  24.3 us
    all_to_all x1, waiting for transfers between devices, per_device(): part = lax.all_to_all(part, 'yh', 0, 0, tiled=True)  15.5 us
    all_to_all x1, blocking collectives, per_device(): stats = lax.all_to_all(stats, CHIPS, 0, 0, tiled=True)  13.3 us
    all_to_all x1, starting transfers between devices, per_device(): lax.all_to_all(jnp.broadcast_to(sent[None], (chips,) + sent.shape), CHIPS...  11.8 us
    ppermute x10, waiting for transfers between devices, shift(): lax.ppermute(value, axis, [(i, (i + by) % size) for i in range(size)])  10.8 us
    all_to_all x1, starting transfers between devices, per_device(): part = lax.all_to_all(part, 'yh', 0, 0, tiled=True)  6.2 us
    all_to_all x1, starting transfers between devices, per_device(): lax.all_to_all(query_part.reshape(chips, own_rows, depth), CHIPS, 0, 0, t...  4.91 us
  transfers between devices with their start and end apart: 13, of which 6 were waited for; matrix products, arithmetic and copies ran while one was open for 3% of the time, Pallas kernels for 5%

profile of v7, /device:TPU:8, one launch (start us, length us, event | category | flops | bytes accessed | tf_op | source)
XLA Modules:
  0.0 132.2 jit_solution(9658087890689260515)
XLA Ops:
  0.6 0.0 copy-start
  0.6 0.0 copy-start.1
  0.7 2.1 %collective-permute-start = (bf16[256,4096]{1,0:T(8,128)(2,1)}, bf16[256,4096]{1,0:T(8,128)(2,1)}, u32[]{:S(2)}, u32[]{:S(2)}) collective-permute-start(bf16[256,4096]{1,0:T(8,128)(2,1)} %passages.3), channel_id=1, source_target_pairs={{0,16},{16,0},{1,17},{17,1},{2,18},{18,2},{3,19},{19,3},{4,20},{20... | collective-permute-start | bytes 6291464 | tf_op jit(solution)/shard_map/ppermute | solution.py:26
  2.7 0.7 convert_bitcast_fusion
  3.4 0.7 fusion.2
  4.1 0.1 copy.9
  4.1 0.8 fusion.1
  5.0 1.1 broadcast_in_dim.6
  6.1 11.8 %all-to-all-start = ((bf16[16,8,4224]{2,1,0:T(8,128)(2,1)}), bf16[16,8,4224]{2,1,0:T(8,128)(2,1)S(1)}, u32[]{:S(2)}, u32[]{:S(2)}) async-start(bf16[16,8,4224]{2,1,0:T(8,128)(2,1)} %broadcast_in_dim.6), calls=%async_computation | async-start | bytes 2162688 | tf_op jit(solution)/shard_map/all_to_all | solution.py:138
  17.8 0.0 copy-done.1
  17.9 1.9 %collective-permute-start.1 = (f32[256,256]{1,0:T(8,128)S(1)}, f32[256,256]{1,0:T(8,128)}, u32[]{:S(2)}, u32[]{:S(2)}) collective-permute-start(f32[256,256]{1,0:T(8,128)S(1)} %bitcast.39), channel_id=1, source_target_pairs={{0,16},{16,0},{1,17},{17,1},{2,18},{18,2},{3,19},{19,3},{4,20},{20... | collective-permute-start | bytes 786440 | tf_op jit(solution)/shard_map/ppermute | solution.py:26
  19.8 0.1 fusion.3
  19.9 0.1 pad_add_fusion.places
  20.0 1.5 %collective-permute-done.1.teacher_other = f32[256,256]{1,0:T(8,128)} collective-permute-done((f32[256,256]{1,0:T(8,128)S(1)}, f32[256,256]{1,0:T(8,128)}, u32[]{:S(2)}, u32[]{:S(2)}) %collective-permute-start.1) | collective-permute-done | bytes 262176 | tf_op jit(solution)/shard_map/ppermute | solution.py:26
  21.4 24.3 %all-to-all-done = bf16[16,8,4224]{2,1,0:T(8,128)(2,1)S(1)} async-done(((bf16[16,8,4224]{2,1,0:T(8,128)(2,1)}), bf16[16,8,4224]{2,1,0:T(8,128)(2,1)S(1)}, u32[]{:S(2)}, u32[]{:S(2)}) %all-to-all-start) | async-done | bytes 1081376 | tf_op jit(solution)/shard_map/all_to_all | solution.py:138
  45.7 0.0 collective-permute-done.passages_other
  45.7 0.0 copy-done
  45.7 3.5 %shard_map.76 = (f32[4,256,128]{2,1,0:T(8,128)S(1)}, s32[1,128]{1,0:T(1,128)S(1)}, f32[16,8,128]{2,1,0:T(8,128)S(1)}) custom-call(s32[4]{0:T(128)S(1)} %pad_add_fusion.places, bf16[128,4224]{1,0:T(8,128)(2,1)S(1)} %bitcast.33, bf16[256,4096]{1,0:T(8,128)(2,1)S(1)} %copy-done, bf16[256,4096]{1,0:T(8,128)(2,1)} %collective-permute-done.passages_other, ...), custom_call_target="tpu_custom_call" | custom-call | tf_op jit(solution)/shard_map/pallas_call | solution.py:142
  49.2 13.3 %all_to_all.20.stats = f32[16,8,128]{2,1,0:T(8,128)S(1)} all-to-all(f32[16,8,128]{2,1,0:T(8,128)S(1)} %get-tuple-element.28), channel_id=1, replica_groups=mesh['yl'=2,'z'=8,'core'=2,'x'=4,'yh'=4] {'yl','z'}, dimensions={0} | all-to-all | bytes 131072 | tf_op jit(solution)/shard_map/all_to_all | solution.py:153
  62.5 0.8 shard_map.77
  63.3 1.9 %collective-permute-start.2 = (bf16[256,128]{1,0:T(8,128)(2,1)S(1)}, bf16[256,128]{1,0:T(8,128)(2,1)S(1)}, u32[]{:S(2)}, u32[]{:S(2)}) collective-permute-start(bf16[256,128]{1,0:T(8,128)(2,1)S(1)} %get-tuple-element.31), channel_id=1, source_target_pairs={{0,16},{16,0},{1,17},{17,1},{2,18},{18,2},{3,19},{19,3},{4,20},{20... | collective-permute-start | bytes 196616 | tf_op jit(solution)/shard_map/ppermute | solution.py:26
  65.2 4.3 %shard_map.78.after = bf16[128,4096]{1,0:T(8,128)(2,1)} custom-call(bf16[2,128,256]{2,1,0:T(8,128)(2,1)S(1)} %get-tuple-element.30.grads, bf16[256,4096]{1,0:T(8,128)(2,1)S(1)} %copy-done, bf16[256,4096]{1,0:T(8,128)(2,1)} %collective-permute-done.passages_other), custom_call_target="tpu_custom_call" | custom-call | tf_op jit(solution)/shard_map/pallas_call | solution.py:169
  69.5 0.0 collective-permute-done.2
  69.5 4.9 %all-to-all-start.2 = ((bf16[16,8,4096]{2,1,0:T(8,128)(2,1)}), bf16[16,8,4096]{2,1,0:T(8,128)(2,1)S(1)}, u32[]{:S(2)}, u32[]{:S(2)}) async-start(bf16[16,8,4096]{2,1,0:T(8,128)(2,1)} %bitcast.7), calls=%async_computation.2 | async-start | bytes 2097152 | tf_op jit(solution)/shard_map/all_to_all | solution.py:179
  74.5 0.1 shard_map.79
  74.5 4.7 %collective-permute-start.8 = (bf16[2,256,128]{2,1,0:T(8,128)(2,1)S(1)}, bf16[2,256,128]{2,1,0:T(8,128)(2,1)S(1)}, u32[]{:S(2)}, u32[]{:S(2)}) collective-permute-start(bf16[2,256,128]{2,1,0:T(8,128)(2,1)S(1)} %pad_maximum_fusion.1.refs_0_), channel_id=1, source_target_pairs={{0,12},{4,0},{8,4},{12,8},{1,13},{5,1},{9,5},{13,9},{2,14},{6,2},{... | collective-permute-start | bytes 393224 | tf_op jit(solution)/shard_map/ppermute | solution.py:26
  79.2 1.9 %collective-permute-start.3 = (bf16[128,1024]{1,0:T(8,128)(2,1)S(1)}, bf16[128,1024]{1,0:T(8,128)(2,1)S(1)}, u32[]{:S(2)}, u32[]{:S(2)}) collective-permute-start(bf16[128,1024]{1,0:T(8,128)(2,1)S(1)} %get-tuple-element.34), channel_id=1, source_target_pairs={{0,4},{4,8},{8,12},{12,0},{1,5},{5,9},{9,13},{13,1},{2,6},{6,10},{... | collective-permute-start | bytes 786440 | tf_op jit(solution)/shard_map/ppermute | solution.py:26
  81.1 4.2 %collective-permute-start.4 = (bf16[128,1024]{1,0:T(8,128)(2,1)S(1)}, bf16[128,1024]{1,0:T(8,128)(2,1)S(1)}, u32[]{:S(2)}, u32[]{:S(2)}) collective-permute-start(bf16[128,1024]{1,0:T(8,128)(2,1)S(1)} %get-tuple-element.35), channel_id=1, source_target_pairs={{0,8},{4,12},{8,0},{12,4},{1,9},{5,13},{9,1},{13,5},{2,10},{6,14},... | collective-permute-start | bytes 786440 | tf_op jit(solution)/shard_map/ppermute | solution.py:26
  85.3 3.1 %collective-permute-start.5 = (bf16[128,1024]{1,0:T(8,128)(2,1)S(1)}, bf16[128,1024]{1,0:T(8,128)(2,1)S(1)}, u32[]{:S(2)}, u32[]{:S(2)}) collective-permute-start(bf16[128,1024]{1,0:T(8,128)(2,1)S(1)} %get-tuple-element.36), channel_id=1, source_target_pairs={{0,12},{4,0},{8,4},{12,8},{1,13},{5,1},{9,5},{13,9},{2,14},{6,2},{... | collective-permute-start | bytes 786440 | tf_op jit(solution)/shard_map/ppermute | solution.py:26
  88.4 4.6 %collective-permute-start.7 = (bf16[2,256,128]{2,1,0:T(8,128)(2,1)S(1)}, bf16[2,256,128]{2,1,0:T(8,128)(2,1)S(1)}, u32[]{:S(2)}, u32[]{:S(2)}) collective-permute-start(bf16[2,256,128]{2,1,0:T(8,128)(2,1)S(1)} %pad_maximum_fusion.1.refs_0_), channel_id=1, source_target_pairs={{0,8},{4,12},{8,0},{12,4},{1,9},{5,13},{9,1},{13,5},{2,10},{6,14},... | collective-permute-start | bytes 393224 | tf_op jit(solution)/shard_map/ppermute | solution.py:26
  93.0 0.0 collective-permute-done.8.refs_3_
  93.1 1.9 %collective-permute-start.6 = (bf16[2,256,128]{2,1,0:T(8,128)(2,1)S(1)}, bf16[2,256,128]{2,1,0:T(8,128)(2,1)S(1)}, u32[]{:S(2)}, u32[]{:S(2)}) collective-permute-start(bf16[2,256,128]{2,1,0:T(8,128)(2,1)S(1)} %pad_maximum_fusion.1.refs_0_), channel_id=1, source_target_pairs={{0,4},{4,8},{8,12},{12,0},{1,5},{5,9},{9,13},{13,1},{2,6},{6,10},{... | collective-permute-start | bytes 393224 | tf_op jit(solution)/shard_map/ppermute | solution.py:26
  95.0 4.0 %collective-permute-done.7.refs_2_ = bf16[2,256,128]{2,1,0:T(8,128)(2,1)S(1)} collective-permute-done((bf16[2,256,128]{2,1,0:T(8,128)(2,1)S(1)}, bf16[2,256,128]{2,1,0:T(8,128)(2,1)S(1)}, u32[]{:S(2)}, u32[]{:S(2)}) %collective-permute-start.7) | collective-permute-done | bytes 131104 | tf_op jit(solution)/shard_map/ppermute | solution.py:26
  99.0 2.7 %collective-permute-done.6.refs_1_ = bf16[2,256,128]{2,1,0:T(8,128)(2,1)S(1)} collective-permute-done((bf16[2,256,128]{2,1,0:T(8,128)(2,1)S(1)}, bf16[2,256,128]{2,1,0:T(8,128)(2,1)S(1)}, u32[]{:S(2)}, u32[]{:S(2)}) %collective-permute-start.6) | collective-permute-done | bytes 131104 | tf_op jit(solution)/shard_map/ppermute | solution.py:26
  101.7 0.0 collective-permute-done.3.refs_5_
  101.7 0.0 collective-permute-done.4.refs_6_
  101.7 0.0 collective-permute-done.5.refs_7_
  101.7 0.1 pad_maximum_fusion
  101.9 1.9 %collective-permute-start.9 = (bf16[4,128,1024]{2,1,0:T(8,128)(2,1)S(1)}, bf16[4,128,1024]{2,1,0:T(8,128)(2,1)S(1)}, u32[]{:S(2)}, u32[]{:S(2)}) collective-permute-start(bf16[4,128,1024]{2,1,0:T(8,128)(2,1)S(1)} %pad_maximum_fusion), channel_id=1, source_target_pairs={{0,16},{16,0},{1,17},{17,1},{2,18},{18,2},{3,19},{19,3},{4,20},{20... | collective-permute-start | bytes 3145736 | tf_op jit(solution)/shard_map/ppermute | solution.py:26
  103.8 2.6 %collective-permute-done.9.refs_8_ = bf16[4,128,1024]{2,1,0:T(8,128)(2,1)S(1)} collective-permute-done((bf16[4,128,1024]{2,1,0:T(8,128)(2,1)S(1)}, bf16[4,128,1024]{2,1,0:T(8,128)(2,1)S(1)}, u32[]{:S(2)}, u32[]{:S(2)}) %collective-permute-start.9) | collective-permute-done | bytes 1048608 | tf_op jit(solution)/shard_map/ppermute | solution.py:26
  106.4 2.0 %shard_map.80 = bf16[4,256,256]{2,1,0:T(8,128)(2,1)} custom-call(bf16[2,256,128]{2,1,0:T(8,128)(2,1)S(1)} %pad_maximum_fusion.1.refs_0_, bf16[2,256,128]{2,1,0:T(8,128)(2,1)S(1)} %collective-permute-done.6.refs_1_, bf16[2,256,128]{2,1,0:T(8,128)(2,1)S(1)} %collective-permute-done.7.refs_2_, bf16[2,256,128]{2,1,0:T(8,128)(2,1)S(1)} %collective-permute-done.8.refs_3_, ...), custom_call_target="tpu_custom_call" | custom-call | tf_op jit(solution)/shard_map/pallas_call | solution.py:193
  108.4 0.0 all-to-all-done.2.parts
  108.5 6.2 %all-to-all-start.3 = ((bf16[4,256,256]{2,1,0:T(8,128)(2,1)}), bf16[4,256,256]{2,1,0:T(8,128)(2,1)S(1)}, u32[]{:S(2)}, u32[]{:S(2)}) async-start(bf16[4,256,256]{2,1,0:T(8,128)(2,1)} %shard_map.80), calls=%async_computation.3 | async-start | bytes 1048576 | tf_op jit(solution)/shard_map/all_to_all | solution.py:201
  114.7 0.6 constant_dynamic-slice_fusion
  115.2 0.8 shard_map.81
  116.0 15.5 %all-to-all-done.3.parts = bf16[4,256,256]{2,1,0:T(8,128)(2,1)S(1)} async-done(((bf16[4,256,256]{2,1,0:T(8,128)(2,1)}), bf16[4,256,256]{2,1,0:T(8,128)(2,1)S(1)}, u32[]{:S(2)}, u32[]{:S(2)}) %all-to-all-start.3) | async-done | bytes 524320 | tf_op jit(solution)/shard_map/all_to_all | solution.py:201
  131.5 0.7 shard_map.82
  (2 shorter events, 0.0 us)
Async XLA Ops:
  0.6 45.1 %copy-start = (bf16[256,4096]{1,0:T(8,128)(2,1)S(1)}, bf16[256,4096]{1,0:T(8,128)(2,1)}, u32[]{:S(2)}) copy-start(bf16[256,4096]{1,0:T(8,128)(2,1)} %passages.3) | copy-start | bytes 6291460
  0.6 17.2 %copy-start.1 = (f32[1,256,256]{2,1,0:T(8,128)S(1)}, f32[1,256,256]{2,1,0:T(8,128)}, u32[]{:S(2)}) copy-start(f32[1,256,256]{2,1,0:T(8,128)} %param.7) | copy-start | bytes 786436
  0.7 45.0 %collective-permute-start = (bf16[256,4096]{1,0:T(8,128)(2,1)}, bf16[256,4096]{1,0:T(8,128)(2,1)}, u32[]{:S(2)}, u32[]{:S(2)}) collective-permute-start(bf16[256,4096]{1,0:T(8,128)(2,1)} %passages.3), channel_id=1, source_target_pairs={{0,16},{16,0},{1,17},{17,1},{2,18},{18,2},{3,19},{19,3},{4,20},{20... | collective-permute-start | bytes 6291464 | tf_op jit(solution)/shard_map/ppermute | solution.py:26
  6.1 39.6 %all-to-all-start = ((bf16[16,8,4224]{2,1,0:T(8,128)(2,1)}), bf16[16,8,4224]{2,1,0:T(8,128)(2,1)S(1)}, u32[]{:S(2)}, u32[]{:S(2)}) async-start(bf16[16,8,4224]{2,1,0:T(8,128)(2,1)} %broadcast_in_dim.6), calls=%async_computation | async-start | bytes 2162688 | tf_op jit(solution)/shard_map/all_to_all | solution.py:138
  17.9 3.6 %collective-permute-start.1 = (f32[256,256]{1,0:T(8,128)S(1)}, f32[256,256]{1,0:T(8,128)}, u32[]{:S(2)}, u32[]{:S(2)}) collective-permute-start(f32[256,256]{1,0:T(8,128)S(1)} %bitcast.39), channel_id=1, source_target_pairs={{0,16},{16,0},{1,17},{17,1},{2,18},{18,2},{3,19},{19,3},{4,20},{20... | collective-permute-start | bytes 786440 | tf_op jit(solution)/shard_map/ppermute | solution.py:26
  63.3 6.2 %collective-permute-start.2 = (bf16[256,128]{1,0:T(8,128)(2,1)S(1)}, bf16[256,128]{1,0:T(8,128)(2,1)S(1)}, u32[]{:S(2)}, u32[]{:S(2)}) collective-permute-start(bf16[256,128]{1,0:T(8,128)(2,1)S(1)} %get-tuple-element.31), channel_id=1, source_target_pairs={{0,16},{16,0},{1,17},{17,1},{2,18},{18,2},{3,19},{19,3},{4,20},{20... | collective-permute-start | bytes 196616 | tf_op jit(solution)/shard_map/ppermute | solution.py:26
  69.5 38.9 %all-to-all-start.2 = ((bf16[16,8,4096]{2,1,0:T(8,128)(2,1)}), bf16[16,8,4096]{2,1,0:T(8,128)(2,1)S(1)}, u32[]{:S(2)}, u32[]{:S(2)}) async-start(bf16[16,8,4096]{2,1,0:T(8,128)(2,1)} %bitcast.7), calls=%async_computation.2 | async-start | bytes 2097152 | tf_op jit(solution)/shard_map/all_to_all | solution.py:179
  74.5 18.5 %collective-permute-start.8 = (bf16[2,256,128]{2,1,0:T(8,128)(2,1)S(1)}, bf16[2,256,128]{2,1,0:T(8,128)(2,1)S(1)}, u32[]{:S(2)}, u32[]{:S(2)}) collective-permute-start(bf16[2,256,128]{2,1,0:T(8,128)(2,1)S(1)} %pad_maximum_fusion.1.refs_0_), channel_id=1, source_target_pairs={{0,12},{4,0},{8,4},{12,8},{1,13},{5,1},{9,5},{13,9},{2,14},{6,2},{... | collective-permute-start | bytes 393224 | tf_op jit(solution)/shard_map/ppermute | solution.py:26
  79.2 22.5 %collective-permute-start.3 = (bf16[128,1024]{1,0:T(8,128)(2,1)S(1)}, bf16[128,1024]{1,0:T(8,128)(2,1)S(1)}, u32[]{:S(2)}, u32[]{:S(2)}) collective-permute-start(bf16[128,1024]{1,0:T(8,128)(2,1)S(1)} %get-tuple-element.34), channel_id=1, source_target_pairs={{0,4},{4,8},{8,12},{12,0},{1,5},{5,9},{9,13},{13,1},{2,6},{6,10},{... | collective-permute-start | bytes 786440 | tf_op jit(solution)/shard_map/ppermute | solution.py:26
  81.1 20.6 %collective-permute-start.4 = (bf16[128,1024]{1,0:T(8,128)(2,1)S(1)}, bf16[128,1024]{1,0:T(8,128)(2,1)S(1)}, u32[]{:S(2)}, u32[]{:S(2)}) collective-permute-start(bf16[128,1024]{1,0:T(8,128)(2,1)S(1)} %get-tuple-element.35), channel_id=1, source_target_pairs={{0,8},{4,12},{8,0},{12,4},{1,9},{5,13},{9,1},{13,5},{2,10},{6,14},... | collective-permute-start | bytes 786440 | tf_op jit(solution)/shard_map/ppermute | solution.py:26
  85.3 16.4 %collective-permute-start.5 = (bf16[128,1024]{1,0:T(8,128)(2,1)S(1)}, bf16[128,1024]{1,0:T(8,128)(2,1)S(1)}, u32[]{:S(2)}, u32[]{:S(2)}) collective-permute-start(bf16[128,1024]{1,0:T(8,128)(2,1)S(1)} %get-tuple-element.36), channel_id=1, source_target_pairs={{0,12},{4,0},{8,4},{12,8},{1,13},{5,1},{9,5},{13,9},{2,14},{6,2},{... | collective-permute-start | bytes 786440 | tf_op jit(solution)/shard_map/ppermute | solution.py:26
  88.4 10.6 %collective-permute-start.7 = (bf16[2,256,128]{2,1,0:T(8,128)(2,1)S(1)}, bf16[2,256,128]{2,1,0:T(8,128)(2,1)S(1)}, u32[]{:S(2)}, u32[]{:S(2)}) collective-permute-start(bf16[2,256,128]{2,1,0:T(8,128)(2,1)S(1)} %pad_maximum_fusion.1.refs_0_), channel_id=1, source_target_pairs={{0,8},{4,12},{8,0},{12,4},{1,9},{5,13},{9,1},{13,5},{2,10},{6,14},... | collective-permute-start | bytes 393224 | tf_op jit(solution)/shard_map/ppermute | solution.py:26
  93.1 8.6 %collective-permute-start.6 = (bf16[2,256,128]{2,1,0:T(8,128)(2,1)S(1)}, bf16[2,256,128]{2,1,0:T(8,128)(2,1)S(1)}, u32[]{:S(2)}, u32[]{:S(2)}) collective-permute-start(bf16[2,256,128]{2,1,0:T(8,128)(2,1)S(1)} %pad_maximum_fusion.1.refs_0_), channel_id=1, source_target_pairs={{0,4},{4,8},{8,12},{12,0},{1,5},{5,9},{9,13},{13,1},{2,6},{6,10},{... | collective-permute-start | bytes 393224 | tf_op jit(solution)/shard_map/ppermute | solution.py:26
  101.9 4.6 %collective-permute-start.9 = (bf16[4,128,1024]{2,1,0:T(8,128)(2,1)S(1)}, bf16[4,128,1024]{2,1,0:T(8,128)(2,1)S(1)}, u32[]{:S(2)}, u32[]{:S(2)}) collective-permute-start(bf16[4,128,1024]{2,1,0:T(8,128)(2,1)S(1)} %pad_maximum_fusion), channel_id=1, source_target_pairs={{0,16},{16,0},{1,17},{17,1},{2,18},{18,2},{3,19},{19,3},{4,20},{20... | collective-permute-start | bytes 3145736 | tf_op jit(solution)/shard_map/ppermute | solution.py:26
  108.5 23.0 %all-to-all-start.3 = ((bf16[4,256,256]{2,1,0:T(8,128)(2,1)}), bf16[4,256,256]{2,1,0:T(8,128)(2,1)S(1)}, u32[]{:S(2)}, u32[]{:S(2)}) async-start(bf16[4,256,256]{2,1,0:T(8,128)(2,1)} %shard_map.80), calls=%async_computation.3 | async-start | bytes 1048576 | tf_op jit(solution)/shard_map/all_to_all | solution.py:201

commit v8 on v7

--- a/solution.py
+++ b/solution.py
@@ -62,14 +62,18 @@
     stats[...] = jnp.broadcast_to(whole[None], stats.shape)
 
 
-def slice_kernel(x, query, after, *outs):
+def pack_kernel(x, query, grads, after, *outs):
     del after
+    rows = query.shape[0]
     width = outs[0].shape[1]
+    tall = outs[0].shape[0] - rows
     for d, out in enumerate(outs):
-        out[...] = query[:, pl.ds(pl.multiple_of(lax.rem(x[0] + d, len(outs)) * width, width), width)]
-
-
-def grad_kernel(places, logits, positives, stats, rows_first, grads, grads_other, losses):
+        out[:rows] = query[:, pl.ds(pl.multiple_of(lax.rem(x[0] + d, len(outs)) * width, width), width)]
+        for k in range(width // rows):
+            out[rows:, k * rows : (k + 1) * rows] = grads[k * tall : (k + 1) * tall]
+
+
+def grad_kernel(places, logits, positives, stats, rows_first, grads, losses):
     tops_s, tops_t, sums_s, sums_t, cross, hit = (stats[:, i, :] for i in range(6))
     top_s, top_t = jnp.max(tops_s, axis=0, keepdims=True), jnp.max(tops_t, axis=0, keepdims=True)
     lower_s, lower_t = tops_s - top_s, tops_t - top_t
@@ -81,15 +85,16 @@
     own = jnp.sum(hit, axis=0, keepdims=True)
     losses[...] = cross / total_t - jnp.log(total_t) + log_s - (own - top_s - log_s)
     scale_s, scale_t = 2.0 * inv_temp / total_s, inv_temp / total_t
-    for half, out in enumerate((grads, grads_other)):
-        hot = hits(positives[...], places[half], out.shape)
+    block_rows = logits.shape[1]
+    for half in range(CORES):
+        hot = hits(positives[...], places[half], logits.shape[1:])
         values = (
             jnp.exp(logits[half] - top_s) * scale_s
             - jnp.exp(logits[CORES + half] - top_t) * scale_t
             - jnp.where(hot, inv_temp, 0.0)
         )
         rows_first[half] = values.T.astype(bf16)
-        out[...] = values.astype(bf16)
+        grads[half * block_rows : (half + 1) * block_rows] = values.astype(bf16)
 
 
 def query_kernel(grads, passages, passages_other, out):
@@ -98,16 +103,29 @@
     out[...] = total.astype(bf16)
 
 
-def passage_kernel(groups, *refs):
-    grads, query, query_other, out = refs[:groups], refs[groups : 2 * groups], refs[2 * groups], refs[-1]
+def products(packed, half, block_rows, rows):
+    tall = packed[0].shape[0] - rows
+    total = 0.0
+    for ref in packed:
+        steps = block_rows // tall
+        grads = jnp.concatenate(
+            [ref[rows:, k * rows : (k + 1) * rows] for k in range(half * steps, (half + 1) * steps)], axis=0
+        )
+        total += jnp.dot(grads, ref[:rows], preferred_element_type=f32)
+    return total
+
+
+def other_kernel(rows, *refs):
+    out = refs[-1]
+    out[...] = products(refs[:-1], 1, out.shape[0], rows).astype(bf16)
+
+
+def own_kernel(rows, *refs):
+    back, out = refs[-2], refs[-1]
     width = out.shape[2]
+    total = (products(refs[:-2], 0, back.shape[0], rows) + back[...].astype(f32)).astype(bf16)
     for yh in range(out.shape[0]):
-        columns = slice(yh * width, (yh + 1) * width)
-        total = jnp.zeros(out.shape[1:], f32)
-        for d in range(groups):
-            total += jnp.dot(grads[d][0], query[d][:, columns], preferred_element_type=f32)
-            total += jnp.dot(grads[d][1], query_other[d, :, columns], preferred_element_type=f32)
-        out[yh] = total.astype(bf16)
+        out[yh] = total[:, yh * width : (yh + 1) * width]
 
 
 def sum_kernel(parts, out):
@@ -122,7 +140,7 @@
     block_rows = passages.shape[0]
     chips = lax.axis_size("yl") * lax.axis_size("z")
     x_size, yh_size = lax.axis_size("x"), lax.axis_size("yh")
-    rows = chips * own_rows
+    rows, wide = chips * own_rows, CORES * block_rows
     chip = lax.axis_index("yl") * lax.axis_size("z") + lax.axis_index("z")
     core, x, yh = lax.axis_index("core"), lax.axis_index("x"), lax.axis_index("yh")
     cores = jnp.stack([core, 1 - core])
@@ -151,16 +169,15 @@
         compiler_params=PARAMS,
     )(places, query, passages, passages_other, teacher[0], teacher_other)
     stats = lax.all_to_all(stats, CHIPS, 0, 0, tiled=True)
-    rows_first, grads, grads_other, losses = pl.pallas_call(
+    rows_first, grads, losses = pl.pallas_call(
         grad_kernel,
         out_shape=(
             jax.ShapeDtypeStruct((CORES, rows, block_rows), bf16),
-            jax.ShapeDtypeStruct((block_rows, rows), bf16),
-            jax.ShapeDtypeStruct((block_rows, rows), bf16),
+            jax.ShapeDtypeStruct((wide, rows), bf16),
             jax.ShapeDtypeStruct((1, rows), f32),
         ),
         in_specs=[SMEM] + [VMEM] * 3,
-        out_specs=(VMEM,) * 4,
+        out_specs=(VMEM,) * 3,
         compiler_params=PARAMS,
     )(places, logits, positive, stats)
     loss = lax.dynamic_slice_in_dim(losses[0], chip * own_rows, own_rows)
@@ -168,35 +185,36 @@
     width = depth // x_size
     query_part = pl.pallas_call(
         query_kernel,
-        grid=(x_size,),
         out_shape=jax.ShapeDtypeStruct((rows, depth), bf16),
-        in_specs=[pl.BlockSpec((CORES, rows, block_rows), lambda i: (0, 0, 0))]
-        + [pl.BlockSpec((block_rows, width), lambda i: (0, i))] * 2,
-        out_specs=pl.BlockSpec((rows, width), lambda i: (0, i)),
+        in_specs=[VMEM] * 3,
+        out_specs=VMEM,
         compiler_params=PARAMS,
     )(rows_first, passages, passages_other)
-    query_part, grads_back = lax.optimization_barrier((query_part, shift(grads_other, "core", 1)))
     query_parts = lax.all_to_all(query_part.reshape(chips, own_rows, depth), CHIPS, 0, 0, tiled=True)
 
-    slices = pl.pallas_call(
-        slice_kernel,
-        out_shape=(jax.ShapeDtypeStruct((rows, width), bf16),) * x_size,
-        in_specs=[SMEM, VMEM, ANY],
+    packed_shape = jax.ShapeDtypeStruct((rows + wide * rows // width, width), bf16)
+    packed = pl.pallas_call(
+        pack_kernel,
+        out_shape=(packed_shape,) * x_size,
+        in_specs=[SMEM, VMEM, VMEM, ANY],
         out_specs=(VMEM,) * x_size,
         compiler_params=PARAMS,
-    )(x.astype(i32)[None], query, query_part)
-    columns = [shift(value, "x", d) for d, value in enumerate(slices)]
-    block_grads = jnp.stack([grads, grads_back])
-    block_grads = [shift(block_grads, "x", d) for d in range(x_size)]
-    columns, block_grads = lax.optimization_barrier((columns, block_grads))
-    columns_other = shift(jnp.stack(columns), "core", 1)
+    )(x.astype(i32)[None], query, grads, query_part)
+    packed = [shift(value, "x", d) for d, value in enumerate(packed)]
+    part_other = pl.pallas_call(
+        functools.partial(other_kernel, rows),
+        out_shape=jax.ShapeDtypeStruct((block_rows, width), bf16),
+        in_specs=[VMEM] * x_size,
+        out_specs=VMEM,
+        compiler_params=PARAMS,
+    )(*packed)
     part = pl.pallas_call(
-        functools.partial(passage_kernel, x_size),
+        functools.partial(own_kernel, rows),
         out_shape=jax.ShapeDtypeStruct((yh_size, block_rows, width // yh_size), bf16),
-        in_specs=[VMEM] * (2 * x_size + 1),
+        in_specs=[VMEM] * (x_size + 1),
         out_specs=VMEM,
         compiler_params=PARAMS,
-    )(*block_grads, *columns, columns_other)
+    )(*packed, shift(part_other, "core", 1))
     query_parts, part = lax.optimization_barrier((query_parts, part))
     part = lax.all_to_all(part, "yh", 0, 0, tiled=True)
     query_total, passage_total = (

time: 133 us -> 126 us (0.947)
  the two profiles are of different devices: /device:TPU:8 before, /device:TPU:10 now
where the time goes in v8:
time: 126 us
  waiting for transfers between devices  56.9 us (45%)
  starting transfers between devices  39.3 us (31%)
  blocking collectives  13.3 us (11%)
  Pallas kernels  11.3 us (9%)
  other arithmetic  2.34 us (2%)
  local copies, waits for them, and re-layouts  1.74 us (1%)
    all_to_all x1, waiting for transfers between devices, per_device(): lax.all_to_all(jnp.broadcast_to(sent[None], (chips,) + sent.shape), CHIPS...  24.3 us
    ppermute x6, waiting for transfers between devices, shift(): lax.ppermute(value, axis, [(i, (i + by) % size) for i in range(size)])  17.2 us
    ppermute x6, starting transfers between devices, shift(): lax.ppermute(value, axis, [(i, (i + by) % size) for i in range(size)])  16.4 us
    all_to_all x1, waiting for transfers between devices, per_device(): part = lax.all_to_all(part, 'yh', 0, 0, tiled=True)  15.4 us
    all_to_all x1, blocking collectives, per_device(): stats = lax.all_to_all(stats, CHIPS, 0, 0, tiled=True)  13.3 us
    all_to_all x1, starting transfers between devices, per_device(): lax.all_to_all(jnp.broadcast_to(sent[None], (chips,) + sent.shape), CHIPS...  11.8 us
    all_to_all x1, starting transfers between devices, per_device(): part = lax.all_to_all(part, 'yh', 0, 0, tiled=True)  6.19 us
    all_to_all x1, starting transfers between devices, per_device(): lax.all_to_all(query_part.reshape(chips, own_rows, depth), CHIPS, 0, 0, t...  4.91 us
  transfers between devices with their start and end apart: 9, of which 7 were waited for; matrix products, arithmetic and copies ran while one was open for 3% of the time, Pallas kernels for 2%

profile of v8, /device:TPU:10, one launch (start us, length us, event | category | flops | bytes accessed | tf_op | source)
XLA Modules:
  0.0 125.6 jit_solution(15636578824697745055)
XLA Ops:
  0.6 0.0 copy-start
  0.6 0.0 copy-start.1
  0.7 2.1 %collective-permute-start = (bf16[256,4096]{1,0:T(8,128)(2,1)}, bf16[256,4096]{1,0:T(8,128)(2,1)}, u32[]{:S(2)}, u32[]{:S(2)}) collective-permute-start(bf16[256,4096]{1,0:T(8,128)(2,1)} %passages.3), channel_id=1, source_target_pairs={{0,16},{16,0},{1,17},{17,1},{2,18},{18,2},{3,19},{19,3},{4,20},{20... | collective-permute-start | bytes 6291464 | tf_op jit(solution)/shard_map/ppermute | solution.py:26
  2.7 0.7 fusion.2
  3.4 0.7 convert_bitcast_fusion
  4.1 0.1 copy.9
  4.2 0.8 fusion.1
  5.0 1.0 broadcast_in_dim.6
  6.0 11.8 %all-to-all-start = ((bf16[16,8,4224]{2,1,0:T(8,128)(2,1)}), bf16[16,8,4224]{2,1,0:T(8,128)(2,1)S(1)}, u32[]{:S(2)}, u32[]{:S(2)}) async-start(bf16[16,8,4224]{2,1,0:T(8,128)(2,1)} %broadcast_in_dim.6), calls=%async_computation | async-start | bytes 2162688 | tf_op jit(solution)/shard_map/all_to_all | solution.py:156
  17.8 0.0 copy-done.1
  17.8 1.9 %collective-permute-start.1 = (f32[256,256]{1,0:T(8,128)S(1)}, f32[256,256]{1,0:T(8,128)}, u32[]{:S(2)}, u32[]{:S(2)}) collective-permute-start(f32[256,256]{1,0:T(8,128)S(1)} %bitcast.29), channel_id=1, source_target_pairs={{0,16},{16,0},{1,17},{17,1},{2,18},{18,2},{3,19},{19,3},{4,20},{20... | collective-permute-start | bytes 786440 | tf_op jit(solution)/shard_map/ppermute | solution.py:26
  19.8 0.1 fusion.3
  19.9 0.1 pad_add_fusion.places
  19.9 1.5 %collective-permute-done.1.teacher_other = f32[256,256]{1,0:T(8,128)} collective-permute-done((f32[256,256]{1,0:T(8,128)S(1)}, f32[256,256]{1,0:T(8,128)}, u32[]{:S(2)}, u32[]{:S(2)}) %collective-permute-start.1) | collective-permute-done | bytes 262176 | tf_op jit(solution)/shard_map/ppermute | solution.py:26
  21.4 24.3 %all-to-all-done = bf16[16,8,4224]{2,1,0:T(8,128)(2,1)S(1)} async-done(((bf16[16,8,4224]{2,1,0:T(8,128)(2,1)}), bf16[16,8,4224]{2,1,0:T(8,128)(2,1)S(1)}, u32[]{:S(2)}, u32[]{:S(2)}) %all-to-all-start) | async-done | bytes 1081376 | tf_op jit(solution)/shard_map/all_to_all | solution.py:156
  45.7 0.0 collective-permute-done.passages_other
  45.7 0.0 copy-done
  45.7 3.4 %shard_map.76 = (f32[4,256,128]{2,1,0:T(8,128)S(1)}, s32[1,128]{1,0:T(1,128)S(1)}, f32[16,8,128]{2,1,0:T(8,128)S(1)}) custom-call(s32[4]{0:T(128)S(1)} %pad_add_fusion.places, bf16[128,4224]{1,0:T(8,128)(2,1)S(1)} %bitcast.27, bf16[256,4096]{1,0:T(8,128)(2,1)S(1)} %copy-done, bf16[256,4096]{1,0:T(8,128)(2,1)} %collective-permute-done.passages_other, ...), custom_call_target="tpu_custom_call" | custom-call | tf_op jit(solution)/shard_map/pallas_call | solution.py:160
  49.1 13.3 %all_to_all.20.stats = f32[16,8,128]{2,1,0:T(8,128)S(1)} all-to-all(f32[16,8,128]{2,1,0:T(8,128)S(1)} %get-tuple-element.17), channel_id=1, replica_groups=mesh['yl'=2,'z'=8,'core'=2,'x'=4,'yh'=4] {'yl','z'}, dimensions={0} | all-to-all | bytes 131072 | tf_op jit(solution)/shard_map/all_to_all | solution.py:171
  62.5 0.8 shard_map.77
  63.3 3.3 %shard_map.78.after = bf16[128,4096]{1,0:T(8,128)(2,1)} custom-call(bf16[2,128,256]{2,1,0:T(8,128)(2,1)S(1)} %get-tuple-element.19.grads, bf16[256,4096]{1,0:T(8,128)(2,1)S(1)} %copy-done, bf16[256,4096]{1,0:T(8,128)(2,1)} %collective-permute-done.passages_other), custom_call_target="tpu_custom_call" | custom-call | tf_op jit(solution)/shard_map/pallas_call | solution.py:186
  66.6 4.9 %all-to-all-start.2 = ((bf16[16,8,4096]{2,1,0:T(8,128)(2,1)}), bf16[16,8,4096]{2,1,0:T(8,128)(2,1)S(1)}, u32[]{:S(2)}, u32[]{:S(2)}) async-start(bf16[16,8,4096]{2,1,0:T(8,128)(2,1)} %bitcast.7), calls=%async_computation.2 | async-start | bytes 2097152 | tf_op jit(solution)/shard_map/all_to_all | solution.py:193
  71.5 0.2 shard_map.79
  71.6 3.4 %collective-permute-start.2 = (bf16[192,1024]{1,0:T(8,128)(2,1)S(1)}, bf16[192,1024]{1,0:T(8,128)(2,1)S(1)}, u32[]{:S(2)}, u32[]{:S(2)}) collective-permute-start(bf16[192,1024]{1,0:T(8,128)(2,1)S(1)} %get-tuple-element.22), channel_id=1, source_target_pairs={{0,4},{4,8},{8,12},{12,0},{1,5},{5,9},{9,13},{13,1},{2,6},{6,10},{... | collective-permute-start | bytes 1179656 | tf_op jit(solution)/shard_map/ppermute | solution.py:26
  75.0 3.0 %collective-permute-start.3 = (bf16[192,1024]{1,0:T(8,128)(2,1)S(1)}, bf16[192,1024]{1,0:T(8,128)(2,1)S(1)}, u32[]{:S(2)}, u32[]{:S(2)}) collective-permute-start(bf16[192,1024]{1,0:T(8,128)(2,1)S(1)} %get-tuple-element.23), channel_id=1, source_target_pairs={{0,8},{4,12},{8,0},{12,4},{1,9},{5,13},{9,1},{13,5},{2,10},{6,14},... | collective-permute-start | bytes 1179656 | tf_op jit(solution)/shard_map/ppermute | solution.py:26
  78.1 4.1 %collective-permute-start.4 = (bf16[192,1024]{1,0:T(8,128)(2,1)S(1)}, bf16[192,1024]{1,0:T(8,128)(2,1)S(1)}, u32[]{:S(2)}, u32[]{:S(2)}) collective-permute-start(bf16[192,1024]{1,0:T(8,128)(2,1)S(1)} %get-tuple-element.24), channel_id=1, source_target_pairs={{0,12},{4,0},{8,4},{12,8},{1,13},{5,1},{9,5},{13,9},{2,14},{6,2},{... | collective-permute-start | bytes 1179656 | tf_op jit(solution)/shard_map/ppermute | solution.py:26
  82.1 3.5 %collective-permute-done.2.refs_1_ = bf16[192,1024]{1,0:T(8,128)(2,1)S(1)} collective-permute-done((bf16[192,1024]{1,0:T(8,128)(2,1)S(1)}, bf16[192,1024]{1,0:T(8,128)(2,1)S(1)}, u32[]{:S(2)}, u32[]{:S(2)}) %collective-permute-start.2) | collective-permute-done | bytes 393248 | tf_op jit(solution)/shard_map/ppermute | solution.py:26
  85.6 4.9 %collective-permute-done.3.refs_2_ = bf16[192,1024]{1,0:T(8,128)(2,1)S(1)} collective-permute-done((bf16[192,1024]{1,0:T(8,128)(2,1)S(1)}, bf16[192,1024]{1,0:T(8,128)(2,1)S(1)}, u32[]{:S(2)}, u32[]{:S(2)}) %collective-permute-start.3) | collective-permute-done | bytes 393248 | tf_op jit(solution)/shard_map/ppermute | solution.py:26
  90.5 5.4 %collective-permute-done.4.refs_3_ = bf16[192,1024]{1,0:T(8,128)(2,1)S(1)} collective-permute-done((bf16[192,1024]{1,0:T(8,128)(2,1)S(1)}, bf16[192,1024]{1,0:T(8,128)(2,1)S(1)}, u32[]{:S(2)}, u32[]{:S(2)}) %collective-permute-start.4) | collective-permute-done | bytes 393248 | tf_op jit(solution)/shard_map/ppermute | solution.py:26
  95.9 0.7 shard_map.80
  96.6 1.9 %collective-permute-start.5 = (bf16[256,1024]{1,0:T(8,128)(2,1)S(1)}, bf16[256,1024]{1,0:T(8,128)(2,1)S(1)}, u32[]{:S(2)}, u32[]{:S(2)}) collective-permute-start(bf16[256,1024]{1,0:T(8,128)(2,1)S(1)} %shard_map.80), channel_id=1, source_target_pairs={{0,16},{16,0},{1,17},{17,1},{2,18},{18,2},{3,19},{19,3},{4,20},{20... | collective-permute-start | bytes 1572872 | tf_op jit(solution)/shard_map/ppermute | solution.py:26
  98.6 1.9 %collective-permute-done.5.refs_4_ = bf16[256,1024]{1,0:T(8,128)(2,1)S(1)} collective-permute-done((bf16[256,1024]{1,0:T(8,128)(2,1)S(1)}, bf16[256,1024]{1,0:T(8,128)(2,1)S(1)}, u32[]{:S(2)}, u32[]{:S(2)}) %collective-permute-start.5) | collective-permute-done | bytes 524320 | tf_op jit(solution)/shard_map/ppermute | solution.py:26
  100.4 1.5 %shard_map.81 = bf16[4,256,256]{2,1,0:T(8,128)(2,1)} custom-call(bf16[192,1024]{1,0:T(8,128)(2,1)S(1)} %get-tuple-element.21.refs_0_, bf16[192,1024]{1,0:T(8,128)(2,1)S(1)} %collective-permute-done.2.refs_1_, bf16[192,1024]{1,0:T(8,128)(2,1)S(1)} %collective-permute-done.3.refs_2_, bf16[192,1024]{1,0:T(8,128)(2,1)S(1)} %collective-permute-done.4.refs_3_, ...), custom_call_target="tpu_custom_call" | custom-call | tf_op jit(solution)/shard_map/pallas_call | solution.py:211
  101.9 0.0 all-to-all-done.2.parts
  101.9 6.2 %all-to-all-start.3 = ((bf16[4,256,256]{2,1,0:T(8,128)(2,1)}), bf16[4,256,256]{2,1,0:T(8,128)(2,1)S(1)}, u32[]{:S(2)}, u32[]{:S(2)}) async-start(bf16[4,256,256]{2,1,0:T(8,128)(2,1)} %shard_map.81), calls=%async_computation.3 | async-start | bytes 1048576 | tf_op jit(solution)/shard_map/all_to_all | solution.py:219
  108.1 0.6 constant_dynamic-slice_fusion
  108.7 0.8 shard_map.82
  109.5 15.4 %all-to-all-done.3.parts = bf16[4,256,256]{2,1,0:T(8,128)(2,1)S(1)} async-done(((bf16[4,256,256]{2,1,0:T(8,128)(2,1)}), bf16[4,256,256]{2,1,0:T(8,128)(2,1)S(1)}, u32[]{:S(2)}, u32[]{:S(2)}) %all-to-all-start.3) | async-done | bytes 524320 | tf_op jit(solution)/shard_map/all_to_all | solution.py:219
  124.9 0.7 shard_map.83
  (1 shorter events, 0.0 us)
Async XLA Ops:
  0.6 45.1 %copy-start = (bf16[256,4096]{1,0:T(8,128)(2,1)S(1)}, bf16[256,4096]{1,0:T(8,128)(2,1)}, u32[]{:S(2)}) copy-start(bf16[256,4096]{1,0:T(8,128)(2,1)} %passages.3) | copy-start | bytes 6291460
  0.6 17.2 %copy-start.1 = (f32[1,256,256]{2,1,0:T(8,128)S(1)}, f32[1,256,256]{2,1,0:T(8,128)}, u32[]{:S(2)}) copy-start(f32[1,256,256]{2,1,0:T(8,128)} %param.7) | copy-start | bytes 786436
  0.7 45.0 %collective-permute-start = (bf16[256,4096]{1,0:T(8,128)(2,1)}, bf16[256,4096]{1,0:T(8,128)(2,1)}, u32[]{:S(2)}, u32[]{:S(2)}) collective-permute-start(bf16[256,4096]{1,0:T(8,128)(2,1)} %passages.3), channel_id=1, source_target_pairs={{0,16},{16,0},{1,17},{17,1},{2,18},{18,2},{3,19},{19,3},{4,20},{20... | collective-permute-start | bytes 6291464 | tf_op jit(solution)/shard_map/ppermute | solution.py:26
  6.0 39.6 %all-to-all-start = ((bf16[16,8,4224]{2,1,0:T(8,128)(2,1)}), bf16[16,8,4224]{2,1,0:T(8,128)(2,1)S(1)}, u32[]{:S(2)}, u32[]{:S(2)}) async-start(bf16[16,8,4224]{2,1,0:T(8,128)(2,1)} %broadcast_in_dim.6), calls=%async_computation | async-start | bytes 2162688 | tf_op jit(solution)/shard_map/all_to_all | solution.py:156
  17.8 3.6 %collective-permute-start.1 = (f32[256,256]{1,0:T(8,128)S(1)}, f32[256,256]{1,0:T(8,128)}, u32[]{:S(2)}, u32[]{:S(2)}) collective-permute-start(f32[256,256]{1,0:T(8,128)S(1)} %bitcast.29), channel_id=1, source_target_pairs={{0,16},{16,0},{1,17},{17,1},{2,18},{18,2},{3,19},{19,3},{4,20},{20... | collective-permute-start | bytes 786440 | tf_op jit(solution)/shard_map/ppermute | solution.py:26
  66.6 35.4 %all-to-all-start.2 = ((bf16[16,8,4096]{2,1,0:T(8,128)(2,1)}), bf16[16,8,4096]{2,1,0:T(8,128)(2,1)S(1)}, u32[]{:S(2)}, u32[]{:S(2)}) async-start(bf16[16,8,4096]{2,1,0:T(8,128)(2,1)} %bitcast.7), calls=%async_computation.2 | async-start | bytes 2097152 | tf_op jit(solution)/shard_map/all_to_all | solution.py:193
  71.6 13.9 %collective-permute-start.2 = (bf16[192,1024]{1,0:T(8,128)(2,1)S(1)}, bf16[192,1024]{1,0:T(8,128)(2,1)S(1)}, u32[]{:S(2)}, u32[]{:S(2)}) collective-permute-start(bf16[192,1024]{1,0:T(8,128)(2,1)S(1)} %get-tuple-element.22), channel_id=1, source_target_pairs={{0,4},{4,8},{8,12},{12,0},{1,5},{5,9},{9,13},{13,1},{2,6},{6,10},{... | collective-permute-start | bytes 1179656 | tf_op jit(solution)/shard_map/ppermute | solution.py:26
  75.0 15.5 %collective-permute-start.3 = (bf16[192,1024]{1,0:T(8,128)(2,1)S(1)}, bf16[192,1024]{1,0:T(8,128)(2,1)S(1)}, u32[]{:S(2)}, u32[]{:S(2)}) collective-permute-start(bf16[192,1024]{1,0:T(8,128)(2,1)S(1)} %get-tuple-element.23), channel_id=1, source_target_pairs={{0,8},{4,12},{8,0},{12,4},{1,9},{5,13},{9,1},{13,5},{2,10},{6,14},... | collective-permute-start | bytes 1179656 | tf_op jit(solution)/shard_map/ppermute | solution.py:26
  78.1 17.9 %collective-permute-start.4 = (bf16[192,1024]{1,0:T(8,128)(2,1)S(1)}, bf16[192,1024]{1,0:T(8,128)(2,1)S(1)}, u32[]{:S(2)}, u32[]{:S(2)}) collective-permute-start(bf16[192,1024]{1,0:T(8,128)(2,1)S(1)} %get-tuple-element.24), channel_id=1, source_target_pairs={{0,12},{4,0},{8,4},{12,8},{1,13},{5,1},{9,5},{13,9},{2,14},{6,2},{... | collective-permute-start | bytes 1179656 | tf_op jit(solution)/shard_map/ppermute | solution.py:26
  96.6 3.8 %collective-permute-start.5 = (bf16[256,1024]{1,0:T(8,128)(2,1)S(1)}, bf16[256,1024]{1,0:T(8,128)(2,1)S(1)}, u32[]{:S(2)}, u32[]{:S(2)}) collective-permute-start(bf16[256,1024]{1,0:T(8,128)(2,1)S(1)} %shard_map.80), channel_id=1, source_target_pairs={{0,16},{16,0},{1,17},{17,1},{2,18},{18,2},{3,19},{19,3},{4,20},{20... | collective-permute-start | bytes 1572872 | tf_op jit(solution)/shard_map/ppermute | solution.py:26
  101.9 23.0 %all-to-all-start.3 = ((bf16[4,256,256]{2,1,0:T(8,128)(2,1)}), bf16[4,256,256]{2,1,0:T(8,128)(2,1)S(1)}, u32[]{:S(2)}, u32[]{:S(2)}) async-start(bf16[4,256,256]{2,1,0:T(8,128)(2,1)} %shard_map.81), calls=%async_computation.3 | async-start | bytes 1048576 | tf_op jit(solution)/shard_map/all_to_all | solution.py:219

commit v9 on v8

--- a/solution.py
+++ b/solution.py
@@ -11,6 +11,7 @@
 YL, CORES, X = 2, 2, 4
 LANES = 128
 STATS = 8
+PIECES = 3
 CHIPS = ("yl", "z")
 f32, bf16, i32 = jnp.float32, jnp.bfloat16, jnp.int32
 VMEM = pl.BlockSpec(memory_space=pltpu.VMEM)
@@ -28,6 +29,14 @@
 
 def hits(positive, place, shape):
     return lax.broadcasted_iota(i32, shape, 0) + place == positive
+
+
+def teacher_kernel(teacher, out):
+    rest = teacher[...].T
+    for i in range(PIECES):
+        piece = rest.astype(bf16)
+        out[i] = piece
+        rest = rest - piece.astype(f32)
 
 
 def score_kernel(places, query, passages, passages_other, teacher, teacher_other, values, positives, stats):
@@ -37,16 +46,13 @@
     row_index = codes[0:1].astype(i32)
     positive = codes[1:2].astype(i32) + 256 * codes[2:3].astype(i32)
     positives[...] = positive
-    pick = (lax.broadcasted_iota(i32, (teacher.shape[0], rows), 0) == row_index).astype(f32)
+    pick = (lax.broadcasted_iota(i32, (teacher.shape[2], rows), 0) == row_index).astype(f32).astype(bf16)
     parts = []
     for half, (block, table) in enumerate(((passages, teacher), (passages_other, teacher_other))):
         s = inv_temp * lax.dot_general(
             block[...], query[:, :depth], (((1,), (1,)), ((), ())), preferred_element_type=f32
         )
-        t = lax.dot_general(
-            table[...], pick, (((0,), (0,)), ((), ())),
-            precision=lax.Precision.HIGHEST, preferred_element_type=f32,
-        )
+        t = sum(jnp.dot(table[i], pick, preferred_element_type=f32) for i in range(PIECES))
         values[half] = s
         values[CORES + half] = t
         parts.append((s, t, hits(positive, places[half], s.shape)))
@@ -62,13 +68,12 @@
     stats[...] = jnp.broadcast_to(whole[None], stats.shape)
 
 
-def pack_kernel(x, query, grads, after, *outs):
-    del after
+def pack_kernel(places, query, grads, *outs):
     rows = query.shape[0]
     width = outs[0].shape[1]
     tall = outs[0].shape[0] - rows
     for d, out in enumerate(outs):
-        out[:rows] = query[:, pl.ds(pl.multiple_of(lax.rem(x[0] + d, len(outs)) * width, width), width)]
+        out[:rows] = query[:, pl.ds(pl.multiple_of(lax.rem(places[2] + d, len(outs)) * width, width), width)]
         for k in range(width // rows):
             out[rows:, k * rows : (k + 1) * rows] = grads[k * tall : (k + 1) * tall]
 
@@ -97,7 +102,8 @@
         grads[half * block_rows : (half + 1) * block_rows] = values.astype(bf16)
 
 
-def query_kernel(grads, passages, passages_other, out):
+def query_kernel(grads, passages, passages_other, after, out):
+    del after
     total = jnp.dot(grads[0], passages[...], preferred_element_type=f32)
     total += jnp.dot(grads[1], passages_other[...], preferred_element_type=f32)
     out[...] = total.astype(bf16)
@@ -120,19 +126,18 @@
     out[...] = products(refs[:-1], 1, out.shape[0], rows).astype(bf16)
 
 
-def own_kernel(rows, *refs):
-    back, out = refs[-2], refs[-1]
-    width = out.shape[2]
-    total = (products(refs[:-2], 0, back.shape[0], rows) + back[...].astype(f32)).astype(bf16)
-    for yh in range(out.shape[0]):
-        out[yh] = total[:, yh * width : (yh + 1) * width]
-
-
-def sum_kernel(parts, out):
-    total = parts[0].astype(f32)
-    for i in range(1, parts.shape[0]):
-        total += parts[i].astype(f32)
-    out[...] = total.astype(bf16)
+def own_kernel(groups, rows, places, *refs):
+    packed, back, outs, total = refs[:groups], refs[groups], refs[groups + 1 : -1], refs[-1]
+    width = outs[0].shape[1]
+    total[...] = (products(packed, 0, back.shape[0], rows) + back[...].astype(f32)).astype(bf16)
+    for d, out in enumerate(outs):
+        out[...] = total[:, pl.ds(pl.multiple_of(lax.rem(places[3] + d, len(outs)) * width, width), width)]
+
+
+def sum_kernel(query_parts, *refs):
+    parts, query_total, total = refs[:-2], refs[-2], refs[-1]
+    query_total[...] = sum(query_parts[i].astype(f32) for i in range(query_parts.shape[0])).astype(bf16)
+    total[...] = sum(part[...].astype(f32) for part in parts).astype(bf16)
 
 
 def per_device(queries, passages, teacher, teacher_rows, positives):
@@ -143,8 +148,9 @@
     rows, wide = chips * own_rows, CORES * block_rows
     chip = lax.axis_index("yl") * lax.axis_size("z") + lax.axis_index("z")
     core, x, yh = lax.axis_index("core"), lax.axis_index("x"), lax.axis_index("yh")
-    cores = jnp.stack([core, 1 - core])
-    places = jnp.concatenate([(chip * CORES + cores) * block_rows, cores]).astype(i32)
+    places = jnp.stack(
+        [(chip * CORES + core) * block_rows, (chip * CORES + 1 - core) * block_rows, x, yh]
+    ).astype(i32)
 
     indices = jnp.stack(
         [teacher_rows[0], positives[0] % 256, positives[0] // 256], axis=1
@@ -152,11 +158,20 @@
     sent = jnp.concatenate(
         [queries[0], jnp.pad(indices, ((0, 0), (0, LANES - indices.shape[1])))], axis=1
     )
-    passages_other, teacher_other = shift(passages, "core", 1), shift(teacher[0], "core", 1)
+    passages_other = shift(passages, "core", 1)
     query = lax.all_to_all(
         jnp.broadcast_to(sent[None], (chips,) + sent.shape), CHIPS, 0, 0, tiled=True
     ).reshape(rows, depth + LANES)
 
+    table = pl.pallas_call(
+        teacher_kernel,
+        out_shape=jax.ShapeDtypeStruct((PIECES, block_rows, teacher.shape[1]), bf16),
+        in_specs=[VMEM],
+        out_specs=VMEM,
+        compiler_params=PARAMS,
+        cost_estimate=pl.CostEstimate(flops=10**11, bytes_accessed=2**21, transcendentals=0),
+    )(teacher[0])
+    table_other = shift(table, "core", 1)
     logits, positive, stats = pl.pallas_call(
         score_kernel,
         out_shape=(
@@ -167,7 +182,7 @@
         in_specs=[SMEM] + [VMEM] * 5,
         out_specs=(VMEM,) * 3,
         compiler_params=PARAMS,
-    )(places, query, passages, passages_other, teacher[0], teacher_other)
+    )(places, query, passages, passages_other, table, table_other)
     stats = lax.all_to_all(stats, CHIPS, 0, 0, tiled=True)
     rows_first, grads, losses = pl.pallas_call(
         grad_kernel,
@@ -183,23 +198,22 @@
     loss = lax.dynamic_slice_in_dim(losses[0], chip * own_rows, own_rows)
 
     width = depth // x_size
-    query_part = pl.pallas_call(
-        query_kernel,
-        out_shape=jax.ShapeDtypeStruct((rows, depth), bf16),
-        in_specs=[VMEM] * 3,
-        out_specs=VMEM,
-        compiler_params=PARAMS,
-    )(rows_first, passages, passages_other)
-    query_parts = lax.all_to_all(query_part.reshape(chips, own_rows, depth), CHIPS, 0, 0, tiled=True)
-
     packed_shape = jax.ShapeDtypeStruct((rows + wide * rows // width, width), bf16)
     packed = pl.pallas_call(
         pack_kernel,
         out_shape=(packed_shape,) * x_size,
-        in_specs=[SMEM, VMEM, VMEM, ANY],
+        in_specs=[SMEM, VMEM, VMEM],
         out_specs=(VMEM,) * x_size,
         compiler_params=PARAMS,
-    )(x.astype(i32)[None], query, grads, query_part)
+    )(places, query, grads)
+    query_part = pl.pallas_call(
+        query_kernel,
+        out_shape=jax.ShapeDtypeStruct((rows, depth), bf16),
+        in_specs=[VMEM] * 3 + [ANY],
+        out_specs=VMEM,
+        compiler_params=PARAMS,
+    )(rows_first, passages, passages_other, packed[0])
+    query_parts = lax.all_to_all(query_part.reshape(chips, own_rows, depth), CHIPS, 0, 0, tiled=True)
     packed = [shift(value, "x", d) for d, value in enumerate(packed)]
     part_other = pl.pallas_call(
         functools.partial(other_kernel, rows),
@@ -207,26 +221,27 @@
         in_specs=[VMEM] * x_size,
         out_specs=VMEM,
         compiler_params=PARAMS,
+        cost_estimate=pl.CostEstimate(flops=10**11, bytes_accessed=2**21, transcendentals=0),
     )(*packed)
-    part = pl.pallas_call(
-        functools.partial(own_kernel, rows),
-        out_shape=jax.ShapeDtypeStruct((yh_size, block_rows, width // yh_size), bf16),
-        in_specs=[VMEM] * (x_size + 1),
-        out_specs=VMEM,
-        compiler_params=PARAMS,
-    )(*packed, shift(part_other, "core", 1))
-    query_parts, part = lax.optimization_barrier((query_parts, part))
-    part = lax.all_to_all(part, "yh", 0, 0, tiled=True)
-    query_total, passage_total = (
-        pl.pallas_call(
-            sum_kernel,
-            out_shape=jax.ShapeDtypeStruct(value.shape[1:], bf16),
-            in_specs=[VMEM],
-            out_specs=VMEM,
-            compiler_params=PARAMS,
-        )(value)
-        for value in (query_parts, part)
-    )
+    parts = pl.pallas_call(
+        functools.partial(own_kernel, x_size, rows),
+        out_shape=(jax.ShapeDtypeStruct((block_rows, width // yh_size), bf16),) * yh_size,
+        in_specs=[SMEM] + [VMEM] * (x_size + 1),
+        out_specs=(VMEM,) * yh_size,
+        scratch_shapes=[pltpu.VMEM((block_rows, width), bf16)],
+        compiler_params=PARAMS,
+    )(places, *packed, shift(part_other, "core", 1))
+    parts = [shift(part, "yh", d) for d, part in enumerate(parts)]
+    query_total, passage_total = pl.pallas_call(
+        sum_kernel,
+        out_shape=(
+            jax.ShapeDtypeStruct((own_rows, depth), bf16),
+            jax.ShapeDtypeStruct(parts[0].shape, bf16),
+        ),
+        in_specs=[VMEM] * (1 + yh_size),
+        out_specs=(VMEM,) * 2,
+        compiler_params=PARAMS,
+    )(query_parts, *parts)
     return loss[None], query_total[None], passage_total
 
 

time: 126 us -> 117 us (0.929)
  the two profiles are of different devices: /device:TPU:10 before, /device:TPU:1 now
where the time goes in v9:
time: 117 us
  starting transfers between devices  48.9 us (42%)
  waiting for transfers between devices  35.4 us (30%)
  blocking collectives  14.4 us (12%)
  Pallas kernels  12.9 us (11%)
  other arithmetic  2.41 us (2%)
  local copies, waits for them, and re-layouts  1.77 us (2%)
    ppermute x9, starting transfers between devices, shift(): lax.ppermute(value, axis, [(i, (i + by) % size) for i in range(size)])  33.1 us
    all_to_all x1, waiting for transfers between devices, per_device(): lax.all_to_all(jnp.broadcast_to(sent[None], (chips,) + sent.shape), CHIPS...  18.3 us
    ppermute x9, waiting for transfers between devices, shift(): lax.ppermute(value, axis, [(i, (i + by) % size) for i in range(size)])  17 us
    all_to_all x1, blocking collectives, per_device(): stats = lax.all_to_all(stats, CHIPS, 0, 0, tiled=True)  14.4 us
    all_to_all x1, starting transfers between devices, per_device(): lax.all_to_all(jnp.broadcast_to(sent[None], (chips,) + sent.shape), CHIPS...  12 us
    all_to_all x1, starting transfers between devices, per_device(): lax.all_to_all(query_part.reshape(chips, own_rows, depth), CHIPS, 0, 0, t...  3.78 us
    pallas_call x1, Pallas kernels, per_device(): pl.pallas_call(score_kernel, out_shape=(jax.ShapeDtypeStruct((2 * CORES,...  3.38 us
    pallas_call x1, Pallas kernels, per_device(): pl.pallas_call(query_kernel, out_shape=jax.ShapeDtypeStruct((rows, depth)...  3.3 us
  transfers between devices with their start and end apart: 11, of which 7 were waited for; matrix products, arithmetic and copies ran while one was open for 1% of the time, Pallas kernels for 5%

profile of v9, /device:TPU:1, one launch (start us, length us, event | category | flops | bytes accessed | tf_op | source)
XLA Modules:
  0.0 116.6 jit_solution(3059548855291553532)
XLA Ops:
  0.6 0.0 copy-start
  0.6 0.0 copy-start.3
  0.7 0.8 convert_bitcast_fusion
  1.5 0.7 fusion.2
  2.1 0.1 copy.9
  2.2 0.8 fusion.1
  3.1 1.1 broadcast_in_dim.4
  4.2 12.0 %all-to-all-start = ((bf16[16,8,4224]{2,1,0:T(8,128)(2,1)}), bf16[16,8,4224]{2,1,0:T(8,128)(2,1)S(1)}, u32[]{:S(2)}, u32[]{:S(2)}) async-start(bf16[16,8,4224]{2,1,0:T(8,128)(2,1)} %broadcast_in_dim.4), calls=%async_computation | async-start | bytes 2162688 | tf_op jit(solution)/shard_map/all_to_all | solution.py:162
  16.1 0.0 copy-done
  16.2 2.9 %collective-permute-start = (bf16[256,4096]{1,0:T(8,128)(2,1)S(1)}, bf16[256,4096]{1,0:T(8,128)(2,1)}, u32[]{:S(2)}, u32[]{:S(2)}) collective-permute-start(bf16[256,4096]{1,0:T(8,128)(2,1)S(1)} %copy-done), channel_id=1, source_target_pairs={{0,16},{16,0},{1,17},{17,1},{2,18},{18,2},{3,19},{19,3},{4,20},{20... | collective-permute-start | bytes 6291464 | tf_op jit(solution)/shard_map/ppermute | solution.py:27
  19.0 0.0 copy-done.3
  19.0 0.9 shard_map.76.teacher
  19.9 1.9 %collective-permute-start.1 = (bf16[3,256,256]{2,1,0:T(8,128)(2,1)}, bf16[3,256,256]{2,1,0:T(8,128)(2,1)}, u32[]{:S(2)}, u32[]{:S(2)}) collective-permute-start(bf16[3,256,256]{2,1,0:T(8,128)(2,1)} %shard_map.76.teacher), channel_id=1, source_target_pairs={{0,16},{16,0},{1,17},{17,1},{2,18},{18,2},{3,19},{19,3},{4,20},{20... | collective-permute-start | bytes 1179656 | tf_op jit(solution)/shard_map/ppermute | solution.py:27
  21.9 0.1 pad_add_fusion.places
  21.9 1.9 %collective-permute-done.1.teacher_other = bf16[3,256,256]{2,1,0:T(8,128)(2,1)} collective-permute-done((bf16[3,256,256]{2,1,0:T(8,128)(2,1)}, bf16[3,256,256]{2,1,0:T(8,128)(2,1)}, u32[]{:S(2)}, u32[]{:S(2)}) %collective-permute-start.1) | collective-permute-done | bytes 393248 | tf_op jit(solution)/shard_map/ppermute | solution.py:27
  23.9 18.3 %all-to-all-done = bf16[16,8,4224]{2,1,0:T(8,128)(2,1)S(1)} async-done(((bf16[16,8,4224]{2,1,0:T(8,128)(2,1)}), bf16[16,8,4224]{2,1,0:T(8,128)(2,1)S(1)}, u32[]{:S(2)}, u32[]{:S(2)}) %all-to-all-start) | async-done | bytes 1081376 | tf_op jit(solution)/shard_map/all_to_all | solution.py:162
  42.2 0.0 collective-permute-done.passages_other
  42.2 3.4 %shard_map.77 = (f32[4,256,128]{2,1,0:T(8,128)S(1)}, s32[1,128]{1,0:T(1,128)S(1)}, f32[16,8,128]{2,1,0:T(8,128)S(1)}) custom-call(s32[4]{0:T(128)S(1)} %pad_add_fusion.places, bf16[128,4224]{1,0:T(8,128)(2,1)S(1)} %bitcast.28, bf16[256,4096]{1,0:T(8,128)(2,1)S(1)} %copy-done, bf16[256,4096]{1,0:T(8,128)(2,1)} %collective-permute-done.passages_other, ...), custom_call_target="tpu_custom_call" | custom-call | tf_op jit(solution)/shard_map/pallas_call | solution.py:175
  45.6 14.4 %all_to_all.15.stats = f32[16,8,128]{2,1,0:T(8,128)S(1)} all-to-all(f32[16,8,128]{2,1,0:T(8,128)S(1)} %get-tuple-element.21), channel_id=1, replica_groups=mesh['yl'=2,'z'=8,'core'=2,'x'=4,'yh'=4] {'yl','z'}, dimensions={0} | all-to-all | bytes 131072 | tf_op jit(solution)/shard_map/all_to_all | solution.py:186
  60.0 0.8 shard_map.78
  60.8 1.7 %shard_map.79 = (bf16[192,1024]{1,0:T(8,128)(2,1)S(1)}, bf16[192,1024]{1,0:T(8,128)(2,1)}, bf16[192,1024]{1,0:T(8,128)(2,1)}, bf16[192,1024]{1,0:T(8,128)(2,1)}) custom-call(s32[4]{0:T(128)S(1)} %pad_add_fusion.places, bf16[128,4224]{1,0:T(8,128)(2,1)S(1)} %bitcast.29, bf16[512,128]{1,0:T(8,128)(2,1)S(1)} %get-tuple-element.24.grads), custom_call_target="tpu_custom_call" | custom-call | tf_op jit(solution)/shard_map/pallas_call | solution.py:202
  62.5 0.0 copy-start.1
  62.5 3.1 %collective-permute-start.2 = (bf16[192,1024]{1,0:T(8,128)(2,1)}, bf16[192,1024]{1,0:T(8,128)(2,1)S(1)}, u32[]{:S(2)}, u32[]{:S(2)}) collective-permute-start(bf16[192,1024]{1,0:T(8,128)(2,1)} %get-tuple-element.26), channel_id=1, source_target_pairs={{0,4},{4,8},{8,12},{12,0},{1,5},{5,9},{9,13},{13,1},{2,6},{6,10},{... | collective-permute-start | bytes 1179656 | tf_op jit(solution)/shard_map/ppermute | solution.py:27
  65.7 4.4 %collective-permute-start.3 = (bf16[192,1024]{1,0:T(8,128)(2,1)}, bf16[192,1024]{1,0:T(8,128)(2,1)S(1)}, u32[]{:S(2)}, u32[]{:S(2)}) collective-permute-start(bf16[192,1024]{1,0:T(8,128)(2,1)} %get-tuple-element.27), channel_id=1, source_target_pairs={{0,8},{4,12},{8,0},{12,4},{1,9},{5,13},{9,1},{13,5},{2,10},{6,14},... | collective-permute-start | bytes 1179656 | tf_op jit(solution)/shard_map/ppermute | solution.py:27
  70.0 3.1 %collective-permute-start.4 = (bf16[192,1024]{1,0:T(8,128)(2,1)}, bf16[192,1024]{1,0:T(8,128)(2,1)S(1)}, u32[]{:S(2)}, u32[]{:S(2)}) collective-permute-start(bf16[192,1024]{1,0:T(8,128)(2,1)} %get-tuple-element.28), channel_id=1, source_target_pairs={{0,12},{4,0},{8,4},{12,8},{1,13},{5,1},{9,5},{13,9},{2,14},{6,2},{... | collective-permute-start | bytes 1179656 | tf_op jit(solution)/shard_map/ppermute | solution.py:27
  73.1 3.3 %shard_map.80 = bf16[128,4096]{1,0:T(8,128)(2,1)} custom-call(bf16[2,128,256]{2,1,0:T(8,128)(2,1)S(1)} %get-tuple-element.23.grads, bf16[256,4096]{1,0:T(8,128)(2,1)S(1)} %copy-done, bf16[256,4096]{1,0:T(8,128)(2,1)} %collective-permute-done.passages_other, bf16[192,1024]{1,0:T(8,128)(2,1)S(1)} %get-tuple-element.25.after.refs_0_), custom_call_target="tpu_custom_call" | custom-call | tf_op jit(solution)/shard_map/pallas_call | solution.py:209
  76.4 0.0 copy-done.1
  76.4 0.0 copy-start.2
  76.4 3.8 %all-to-all-start.2 = ((bf16[16,8,4096]{2,1,0:T(8,128)(2,1)}), bf16[16,8,4096]{2,1,0:T(8,128)(2,1)S(1)}, u32[]{:S(2)}, u32[]{:S(2)}) async-start(bf16[16,8,4096]{2,1,0:T(8,128)(2,1)} %bitcast.9), calls=%async_computation.2 | async-start | bytes 2097152 | tf_op jit(solution)/shard_map/all_to_all | solution.py:216
  80.2 0.0 collective-permute-done.2.refs_1_
  80.2 3.7 %collective-permute-done.3.refs_2_ = bf16[192,1024]{1,0:T(8,128)(2,1)S(1)} collective-permute-done((bf16[192,1024]{1,0:T(8,128)(2,1)}, bf16[192,1024]{1,0:T(8,128)(2,1)S(1)}, u32[]{:S(2)}, u32[]{:S(2)}) %collective-permute-start.3) | collective-permute-done | bytes 393248 | tf_op jit(solution)/shard_map/ppermute | solution.py:27
  83.9 2.5 %collective-permute-done.4.refs_3_ = bf16[192,1024]{1,0:T(8,128)(2,1)S(1)} collective-permute-done((bf16[192,1024]{1,0:T(8,128)(2,1)}, bf16[192,1024]{1,0:T(8,128)(2,1)S(1)}, u32[]{:S(2)}, u32[]{:S(2)}) %collective-permute-start.4) | collective-permute-done | bytes 393248 | tf_op jit(solution)/shard_map/ppermute | solution.py:27
  86.4 0.0 copy-done.2
  86.4 0.7 shard_map.81
  87.1 3.8 %collective-permute-start.5 = (bf16[256,1024]{1,0:T(8,128)(2,1)S(1)}, bf16[256,1024]{1,0:T(8,128)(2,1)S(1)}, u32[]{:S(2)}, u32[]{:S(2)}) collective-permute-start(bf16[256,1024]{1,0:T(8,128)(2,1)S(1)} %shard_map.81), channel_id=1, source_target_pairs={{0,16},{16,0},{1,17},{17,1},{2,18},{18,2},{3,19},{19,3},{4,20},{20... | collective-permute-start | bytes 1572872 | tf_op jit(solution)/shard_map/ppermute | solution.py:27
  90.9 1.5 %collective-permute-done.5.refs_4_ = bf16[256,1024]{1,0:T(8,128)(2,1)S(1)} collective-permute-done((bf16[256,1024]{1,0:T(8,128)(2,1)S(1)}, bf16[256,1024]{1,0:T(8,128)(2,1)S(1)}, u32[]{:S(2)}, u32[]{:S(2)}) %collective-permute-start.5) | collective-permute-done | bytes 524320 | tf_op jit(solution)/shard_map/ppermute | solution.py:27
  92.5 1.3 %shard_map.82 = (bf16[256,256]{1,0:T(8,128)(2,1)S(1)}, bf16[256,256]{1,0:T(8,128)(2,1)S(1)}, bf16[256,256]{1,0:T(8,128)(2,1)S(1)}, bf16[256,256]{1,0:T(8,128)(2,1)S(1)}) custom-call(s32[4]{0:T(128)S(1)} %pad_add_fusion.places, bf16[192,1024]{1,0:T(8,128)(2,1)S(1)} %copy-done.2, bf16[192,1024]{1,0:T(8,128)(2,1)S(1)} %collective-permute-done.2.refs_1_, ...), custom_call_target="tpu_custom_call" | custom-call | tf_op jit(solution)/shard_map/pallas_call | solution.py:226
  93.8 4.2 %collective-permute-start.6 = (bf16[256,256]{1,0:T(8,128)(2,1)S(1)}, bf16[256,256]{1,0:T(8,128)(2,1)S(1)}, u32[]{:S(2)}, u32[]{:S(2)}) collective-permute-start(bf16[256,256]{1,0:T(8,128)(2,1)S(1)} %get-tuple-element.30), channel_id=1, source_target_pairs={{0,1},{1,2},{2,3},{3,0},{4,5},{5,6},{6,7},{7,4},{8,9},{9,10},{10,1... | collective-permute-start | bytes 393224 | tf_op jit(solution)/shard_map/ppermute | solution.py:27
  98.0 4.7 %collective-permute-start.7 = (bf16[256,256]{1,0:T(8,128)(2,1)S(1)}, bf16[256,256]{1,0:T(8,128)(2,1)S(1)}, u32[]{:S(2)}, u32[]{:S(2)}) collective-permute-start(bf16[256,256]{1,0:T(8,128)(2,1)S(1)} %get-tuple-element.31), channel_id=1, source_target_pairs={{0,2},{1,3},{2,0},{3,1},{4,6},{5,7},{6,4},{7,5},{8,10},{9,11},{10,... | collective-permute-start | bytes 393224 | tf_op jit(solution)/shard_map/ppermute | solution.py:27
  102.8 5.0 %collective-permute-start.8 = (bf16[256,256]{1,0:T(8,128)(2,1)S(1)}, bf16[256,256]{1,0:T(8,128)(2,1)S(1)}, u32[]{:S(2)}, u32[]{:S(2)}) collective-permute-start(bf16[256,256]{1,0:T(8,128)(2,1)S(1)} %get-tuple-element.32), channel_id=1, source_target_pairs={{0,3},{1,0},{2,1},{3,2},{4,7},{5,4},{6,5},{7,6},{8,11},{9,8},{10,9... | collective-permute-start | bytes 393224 | tf_op jit(solution)/shard_map/ppermute | solution.py:27
  107.7 0.6 constant_dynamic-slice_fusion
  108.3 0.0 collective-permute-done.6.refs_1_
  108.3 2.4 %collective-permute-done.7.refs_2_ = bf16[256,256]{1,0:T(8,128)(2,1)S(1)} collective-permute-done((bf16[256,256]{1,0:T(8,128)(2,1)S(1)}, bf16[256,256]{1,0:T(8,128)(2,1)S(1)}, u32[]{:S(2)}, u32[]{:S(2)}) %collective-permute-start.7) | collective-permute-done | bytes 131104 | tf_op jit(solution)/shard_map/ppermute | solution.py:27
  110.7 5.0 %collective-permute-done.8.refs_3_ = bf16[256,256]{1,0:T(8,128)(2,1)S(1)} collective-permute-done((bf16[256,256]{1,0:T(8,128)(2,1)S(1)}, bf16[256,256]{1,0:T(8,128)(2,1)S(1)}, u32[]{:S(2)}, u32[]{:S(2)}) %collective-permute-start.8) | collective-permute-done | bytes 131104 | tf_op jit(solution)/shard_map/ppermute | solution.py:27
  115.7 0.0 all-to-all-done.2.query_parts
  115.7 0.9 shard_map.83
  (1 shorter events, 0.0 us)
Async XLA Ops:
  0.6 15.5 %copy-start = (bf16[256,4096]{1,0:T(8,128)(2,1)S(1)}, bf16[256,4096]{1,0:T(8,128)(2,1)}, u32[]{:S(2)}) copy-start(bf16[256,4096]{1,0:T(8,128)(2,1)} %passages.3) | copy-start | bytes 6291460
  0.6 18.4 %copy-start.3 = (f32[1,256,256]{2,1,0:T(8,128)S(1)}, f32[1,256,256]{2,1,0:T(8,128)}, u32[]{:S(2)}) copy-start(f32[1,256,256]{2,1,0:T(8,128)} %param.7) | copy-start | bytes 786436
  4.2 38.0 %all-to-all-start = ((bf16[16,8,4224]{2,1,0:T(8,128)(2,1)}), bf16[16,8,4224]{2,1,0:T(8,128)(2,1)S(1)}, u32[]{:S(2)}, u32[]{:S(2)}) async-start(bf16[16,8,4224]{2,1,0:T(8,128)(2,1)} %broadcast_in_dim.4), calls=%async_computation | async-start | bytes 2162688 | tf_op jit(solution)/shard_map/all_to_all | solution.py:162
  16.2 26.0 %collective-permute-start = (bf16[256,4096]{1,0:T(8,128)(2,1)S(1)}, bf16[256,4096]{1,0:T(8,128)(2,1)}, u32[]{:S(2)}, u32[]{:S(2)}) collective-permute-start(bf16[256,4096]{1,0:T(8,128)(2,1)S(1)} %copy-done), channel_id=1, source_target_pairs={{0,16},{16,0},{1,17},{17,1},{2,18},{18,2},{3,19},{19,3},{4,20},{20... | collective-permute-start | bytes 6291464 | tf_op jit(solution)/shard_map/ppermute | solution.py:27
  19.9 3.9 %collective-permute-start.1 = (bf16[3,256,256]{2,1,0:T(8,128)(2,1)}, bf16[3,256,256]{2,1,0:T(8,128)(2,1)}, u32[]{:S(2)}, u32[]{:S(2)}) collective-permute-start(bf16[3,256,256]{2,1,0:T(8,128)(2,1)} %shard_map.76.teacher), channel_id=1, source_target_pairs={{0,16},{16,0},{1,17},{17,1},{2,18},{18,2},{3,19},{19,3},{4,20},{20... | collective-permute-start | bytes 1179656 | tf_op jit(solution)/shard_map/ppermute | solution.py:27
  62.5 13.9 %copy-start.1 = (bf16[192,1024]{1,0:T(8,128)(2,1)}, bf16[192,1024]{1,0:T(8,128)(2,1)S(1)}, u32[]{:S(2)}) copy-start(bf16[192,1024]{1,0:T(8,128)(2,1)S(1)} %get-tuple-element.25.after.refs_0_) | copy-start | bytes 1179652
  62.5 17.7 %collective-permute-start.2 = (bf16[192,1024]{1,0:T(8,128)(2,1)}, bf16[192,1024]{1,0:T(8,128)(2,1)S(1)}, u32[]{:S(2)}, u32[]{:S(2)}) collective-permute-start(bf16[192,1024]{1,0:T(8,128)(2,1)} %get-tuple-element.26), channel_id=1, source_target_pairs={{0,4},{4,8},{8,12},{12,0},{1,5},{5,9},{9,13},{13,1},{2,6},{6,10},{... | collective-permute-start | bytes 1179656 | tf_op jit(solution)/shard_map/ppermute | solution.py:27
  65.7 18.3 %collective-permute-start.3 = (bf16[192,1024]{1,0:T(8,128)(2,1)}, bf16[192,1024]{1,0:T(8,128)(2,1)S(1)}, u32[]{:S(2)}, u32[]{:S(2)}) collective-permute-start(bf16[192,1024]{1,0:T(8,128)(2,1)} %get-tuple-element.27), channel_id=1, source_target_pairs={{0,8},{4,12},{8,0},{12,4},{1,9},{5,13},{9,1},{13,5},{2,10},{6,14},... | collective-permute-start | bytes 1179656 | tf_op jit(solution)/shard_map/ppermute | solution.py:27
  70.0 16.4 %collective-permute-start.4 = (bf16[192,1024]{1,0:T(8,128)(2,1)}, bf16[192,1024]{1,0:T(8,128)(2,1)S(1)}, u32[]{:S(2)}, u32[]{:S(2)}) collective-permute-start(bf16[192,1024]{1,0:T(8,128)(2,1)} %get-tuple-element.28), channel_id=1, source_target_pairs={{0,12},{4,0},{8,4},{12,8},{1,13},{5,1},{9,5},{13,9},{2,14},{6,2},{... | collective-permute-start | bytes 1179656 | tf_op jit(solution)/shard_map/ppermute | solution.py:27
  76.4 10.0 %copy-start.2 = (bf16[192,1024]{1,0:T(8,128)(2,1)S(1)}, bf16[192,1024]{1,0:T(8,128)(2,1)}, u32[]{:S(2)}) copy-start(bf16[192,1024]{1,0:T(8,128)(2,1)} %copy-done.1) | copy-start | bytes 1179652
  76.4 39.3 %all-to-all-start.2 = ((bf16[16,8,4096]{2,1,0:T(8,128)(2,1)}), bf16[16,8,4096]{2,1,0:T(8,128)(2,1)S(1)}, u32[]{:S(2)}, u32[]{:S(2)}) async-start(bf16[16,8,4096]{2,1,0:T(8,128)(2,1)} %bitcast.9), calls=%async_computation.2 | async-start | bytes 2097152 | tf_op jit(solution)/shard_map/all_to_all | solution.py:216
  87.1 5.4 %collective-permute-start.5 = (bf16[256,1024]{1,0:T(8,128)(2,1)S(1)}, bf16[256,1024]{1,0:T(8,128)(2,1)S(1)}, u32[]{:S(2)}, u32[]{:S(2)}) collective-permute-start(bf16[256,1024]{1,0:T(8,128)(2,1)S(1)} %shard_map.81), channel_id=1, source_target_pairs={{0,16},{16,0},{1,17},{17,1},{2,18},{18,2},{3,19},{19,3},{4,20},{20... | collective-permute-start | bytes 1572872 | tf_op jit(solution)/shard_map/ppermute | solution.py:27
  93.8 14.6 %collective-permute-start.6 = (bf16[256,256]{1,0:T(8,128)(2,1)S(1)}, bf16[256,256]{1,0:T(8,128)(2,1)S(1)}, u32[]{:S(2)}, u32[]{:S(2)}) collective-permute-start(bf16[256,256]{1,0:T(8,128)(2,1)S(1)} %get-tuple-element.30), channel_id=1, source_target_pairs={{0,1},{1,2},{2,3},{3,0},{4,5},{5,6},{6,7},{7,4},{8,9},{9,10},{10,1... | collective-permute-start | bytes 393224 | tf_op jit(solution)/shard_map/ppermute | solution.py:27
  98.0 12.7 %collective-permute-start.7 = (bf16[256,256]{1,0:T(8,128)(2,1)S(1)}, bf16[256,256]{1,0:T(8,128)(2,1)S(1)}, u32[]{:S(2)}, u32[]{:S(2)}) collective-permute-start(bf16[256,256]{1,0:T(8,128)(2,1)S(1)} %get-tuple-element.31), channel_id=1, source_target_pairs={{0,2},{1,3},{2,0},{3,1},{4,6},{5,7},{6,4},{7,5},{8,10},{9,11},{10,... | collective-permute-start | bytes 393224 | tf_op jit(solution)/shard_map/ppermute | solution.py:27
  102.8 12.9 %collective-permute-start.8 = (bf16[256,256]{1,0:T(8,128)(2,1)S(1)}, bf16[256,256]{1,0:T(8,128)(2,1)S(1)}, u32[]{:S(2)}, u32[]{:S(2)}) collective-permute-start(bf16[256,256]{1,0:T(8,128)(2,1)S(1)} %get-tuple-element.32), channel_id=1, source_target_pairs={{0,3},{1,0},{2,1},{3,2},{4,7},{5,4},{6,5},{7,6},{8,11},{9,8},{10,9... | collective-permute-start | bytes 393224 | tf_op jit(solution)/shard_map/ppermute | solution.py:27

commit v10 on v9

--- a/solution.py
+++ b/solution.py
@@ -27,6 +27,13 @@
     return lax.ppermute(value, axis, [(i, (i + by) % size) for i in range(size)])
 
 
+def shifts(values, axis):
+    size = len(values)
+    order = sorted(range(size), key=lambda d: -min(d, size - d))
+    moved = {d: shift(values[d], axis, d) for d in order}
+    return [moved[d] for d in range(size)]
+
+
 def hits(positive, place, shape):
     return lax.broadcasted_iota(i32, shape, 0) + place == positive
 
@@ -39,12 +46,23 @@
         rest = rest - piece.astype(f32)
 
 
+def indices(codes, own_rows):
+    rows, lanes = codes.shape
+    first, second = (lax.broadcasted_iota(i32, (lanes, rows), k) for k in (0, 1))
+    spread = (lax.rem(second, own_rows) == first).astype(f32).astype(bf16)
+    spread = jnp.dot(codes, spread, preferred_element_type=f32)
+    first, second = (lax.broadcasted_iota(i32, (rows, rows), k) for k in (0, 1))
+    begin = second - lax.rem(second, own_rows)
+    return [
+        jnp.sum(jnp.where(first == begin + kind, spread, 0.0), axis=0, keepdims=True).astype(i32) for kind in range(3)
+    ]
+
+
 def score_kernel(places, query, passages, passages_other, teacher, teacher_other, values, positives, stats):
     depth = passages.shape[1]
     rows = query.shape[0]
-    codes = query[:, depth:].astype(f32).T
-    row_index = codes[0:1].astype(i32)
-    positive = codes[1:2].astype(i32) + 256 * codes[2:3].astype(i32)
+    row_index, low, high = indices(query[:, depth:], rows // stats.shape[0])
+    positive = low + 256 * high
     positives[...] = positive
     pick = (lax.broadcasted_iota(i32, (teacher.shape[2], rows), 0) == row_index).astype(f32).astype(bf16)
     parts = []
@@ -68,17 +86,11 @@
     stats[...] = jnp.broadcast_to(whole[None], stats.shape)
 
 
-def pack_kernel(places, query, grads, *outs):
-    rows = query.shape[0]
-    width = outs[0].shape[1]
-    tall = outs[0].shape[0] - rows
-    for d, out in enumerate(outs):
-        out[:rows] = query[:, pl.ds(pl.multiple_of(lax.rem(places[2] + d, len(outs)) * width, width), width)]
-        for k in range(width // rows):
-            out[rows:, k * rows : (k + 1) * rows] = grads[k * tall : (k + 1) * tall]
-
-
-def grad_kernel(places, logits, positives, stats, rows_first, grads, losses):
+def grad_kernel(places, query, logits, positives, stats, rows_first, losses, *packed):
+    rows, width = query.shape[0], packed[0].shape[1]
+    for d, out in enumerate(packed):
+        out[:rows] = query[:, pl.ds(pl.multiple_of(lax.rem(places[2] + d, len(packed)) * width, width), width)]
+    tall = packed[0].shape[0] - rows
     tops_s, tops_t, sums_s, sums_t, cross, hit = (stats[:, i, :] for i in range(6))
     top_s, top_t = jnp.max(tops_s, axis=0, keepdims=True), jnp.max(tops_t, axis=0, keepdims=True)
     lower_s, lower_t = tops_s - top_s, tops_t - top_t
@@ -99,7 +111,12 @@
             - jnp.where(hot, inv_temp, 0.0)
         )
         rows_first[half] = values.T.astype(bf16)
-        grads[half * block_rows : (half + 1) * block_rows] = values.astype(bf16)
+        values = values.astype(bf16)
+        steps = block_rows // tall
+        for k in range(steps):
+            lane = (half * steps + k) * rows
+            for out in packed:
+                out[rows:, lane : lane + rows] = values[k * tall : (k + 1) * tall]
 
 
 def query_kernel(grads, passages, passages_other, after, out):
@@ -152,12 +169,9 @@
         [(chip * CORES + core) * block_rows, (chip * CORES + 1 - core) * block_rows, x, yh]
     ).astype(i32)
 
-    indices = jnp.stack(
-        [teacher_rows[0], positives[0] % 256, positives[0] // 256], axis=1
-    ).astype(bf16)
-    sent = jnp.concatenate(
-        [queries[0], jnp.pad(indices, ((0, 0), (0, LANES - indices.shape[1])))], axis=1
-    )
+    codes = jnp.concatenate([teacher_rows, positives & 255, lax.shift_right_logical(positives, 8)], axis=0)
+    codes = jnp.pad(codes, ((0, own_rows - codes.shape[0]), (0, LANES - own_rows)))
+    sent = jnp.concatenate([queries[0], codes.astype(bf16)], axis=1)
     passages_other = shift(passages, "core", 1)
     query = lax.all_to_all(
         jnp.broadcast_to(sent[None], (chips,) + sent.shape), CHIPS, 0, 0, tiled=True
@@ -184,28 +198,21 @@
         compiler_params=PARAMS,
     )(places, query, passages, passages_other, table, table_other)
     stats = lax.all_to_all(stats, CHIPS, 0, 0, tiled=True)
-    rows_first, grads, losses = pl.pallas_call(
+    width = depth // x_size
+    rows_first, losses, *packed = pl.pallas_call(
         grad_kernel,
         out_shape=(
             jax.ShapeDtypeStruct((CORES, rows, block_rows), bf16),
-            jax.ShapeDtypeStruct((wide, rows), bf16),
             jax.ShapeDtypeStruct((1, rows), f32),
-        ),
-        in_specs=[SMEM] + [VMEM] * 3,
-        out_specs=(VMEM,) * 3,
-        compiler_params=PARAMS,
-    )(places, logits, positive, stats)
+        )
+        + (jax.ShapeDtypeStruct((rows + wide * rows // width, width), bf16),) * x_size,
+        in_specs=[SMEM] + [VMEM] * 4,
+        out_specs=(VMEM,) * (2 + x_size),
+        compiler_params=PARAMS,
+    )(places, query, logits, positive, stats)
     loss = lax.dynamic_slice_in_dim(losses[0], chip * own_rows, own_rows)
 
     width = depth // x_size
-    packed_shape = jax.ShapeDtypeStruct((rows + wide * rows // width, width), bf16)
-    packed = pl.pallas_call(
-        pack_kernel,
-        out_shape=(packed_shape,) * x_size,
-        in_specs=[SMEM, VMEM, VMEM],
-        out_specs=(VMEM,) * x_size,
-        compiler_params=PARAMS,
-    )(places, query, grads)
     query_part = pl.pallas_call(
         query_kernel,
         out_shape=jax.ShapeDtypeStruct((rows, depth), bf16),
@@ -214,7 +221,7 @@
         compiler_params=PARAMS,
     )(rows_first, passages, passages_other, packed[0])
     query_parts = lax.all_to_all(query_part.reshape(chips, own_rows, depth), CHIPS, 0, 0, tiled=True)
-    packed = [shift(value, "x", d) for d, value in enumerate(packed)]
+    packed = shifts(packed, "x")
     part_other = pl.pallas_call(
         functools.partial(other_kernel, rows),
         out_shape=jax.ShapeDtypeStruct((block_rows, width), bf16),
@@ -231,7 +238,7 @@
         scratch_shapes=[pltpu.VMEM((block_rows, width), bf16)],
         compiler_params=PARAMS,
     )(places, *packed, shift(part_other, "core", 1))
-    parts = [shift(part, "yh", d) for d, part in enumerate(parts)]
+    parts = shifts(parts, "yh")
     query_total, passage_total = pl.pallas_call(
         sum_kernel,
         out_shape=(

time: 117 us -> 117 us (level)
    pallas_call x1 -> x0, Pallas kernels: 1.72 us -> none  [per_device(): pl.pallas_call(pack_kernel, out_shape=(packed_shape,) * x_size, in_specs=...]
where the time goes in v10:
time: 117 us; the launch traced here: 116 us
  starting transfers between devices  48.9 us (42%)
  waiting for transfers between devices  35.4 us (30%)
  blocking collectives  14.4 us (12%)
  Pallas kernels  12.3 us (11%)
  other arithmetic  2.41 us (2%)
  local copies, waits for them, and re-layouts  1.66 us (1%)
    ppermute x9, starting transfers between devices, shift(): lax.ppermute(value, axis, [(i, (i + by) % size) for i in range(size)])  33.1 us
    all_to_all x1, waiting for transfers between devices, per_device(): lax.all_to_all(jnp.broadcast_to(sent[None], (chips,) + sent.shape), CHIPS...  18.3 us
    ppermute x9, waiting for transfers between devices, shift(): lax.ppermute(value, axis, [(i, (i + by) % size) for i in range(size)])  17 us
    all_to_all x1, blocking collectives, per_device(): stats = lax.all_to_all(stats, CHIPS, 0, 0, tiled=True)  14.4 us
    all_to_all x1, starting transfers between devices, per_device(): lax.all_to_all(jnp.broadcast_to(sent[None], (chips,) + sent.shape), CHIPS...  12 us
    all_to_all x1, starting transfers between devices, per_device(): lax.all_to_all(query_part.reshape(chips, own_rows, depth), CHIPS, 0, 0, t...  3.78 us
    pallas_call x1, Pallas kernels, per_device(): pl.pallas_call(score_kernel, out_shape=(jax.ShapeDtypeStruct((2 * CORES,...  3.46 us
    pallas_call x1, Pallas kernels, per_device(): pl.pallas_call(query_kernel, out_shape=jax.ShapeDtypeStruct((rows, depth)...  3.29 us
  transfers between devices with their start and end apart: 11, of which 7 were waited for; matrix products, arithmetic and copies ran while one was open for 1% of the time, Pallas kernels for 5%

profile of v10, /device:TPU:1, one launch (start us, length us, event | category | flops | bytes accessed | tf_op | source)
XLA Modules:
  0.0 115.8 jit_solution(4485005164343346061)
XLA Ops:
  0.6 0.0 copy-start
  0.6 0.0 copy-start.3
  0.7 0.8 convert.11
  1.5 0.7 and_convert_fusion
  2.1 0.8 pad_maximum_fusion
  3.0 1.1 broadcast_in_dim.4
  4.0 12.0 %all-to-all-start = ((bf16[16,8,4224]{2,1,0:T(8,128)(2,1)}), bf16[16,8,4224]{2,1,0:T(8,128)(2,1)S(1)}, u32[]{:S(2)}, u32[]{:S(2)}) async-start(bf16[16,8,4224]{2,1,0:T(8,128)(2,1)} %broadcast_in_dim.4), calls=%async_computation | async-start | bytes 2162688 | tf_op jit(solution)/shard_map/all_to_all | solution.py:176
  16.0 0.0 copy-done
  16.0 2.9 %collective-permute-start = (bf16[256,4096]{1,0:T(8,128)(2,1)S(1)}, bf16[256,4096]{1,0:T(8,128)(2,1)}, u32[]{:S(2)}, u32[]{:S(2)}) collective-permute-start(bf16[256,4096]{1,0:T(8,128)(2,1)S(1)} %copy-done), channel_id=1, source_target_pairs={{0,16},{16,0},{1,17},{17,1},{2,18},{18,2},{3,19},{19,3},{4,20},{20... | collective-permute-start | bytes 6291464 | tf_op jit(solution)/shard_map/ppermute | solution.py:27
  18.9 0.0 copy-done.3
  18.9 0.9 shard_map.76.teacher
  19.8 1.9 %collective-permute-start.1 = (bf16[3,256,256]{2,1,0:T(8,128)(2,1)}, bf16[3,256,256]{2,1,0:T(8,128)(2,1)}, u32[]{:S(2)}, u32[]{:S(2)}) collective-permute-start(bf16[3,256,256]{2,1,0:T(8,128)(2,1)} %shard_map.76.teacher), channel_id=1, source_target_pairs={{0,16},{16,0},{1,17},{17,1},{2,18},{18,2},{3,19},{19,3},{4,20},{20... | collective-permute-start | bytes 1179656 | tf_op jit(solution)/shard_map/ppermute | solution.py:27
  21.7 0.1 pad_add_fusion.places
  21.8 1.9 %collective-permute-done.1.teacher_other = bf16[3,256,256]{2,1,0:T(8,128)(2,1)} collective-permute-done((bf16[3,256,256]{2,1,0:T(8,128)(2,1)}, bf16[3,256,256]{2,1,0:T(8,128)(2,1)}, u32[]{:S(2)}, u32[]{:S(2)}) %collective-permute-start.1) | collective-permute-done | bytes 393248 | tf_op jit(solution)/shard_map/ppermute | solution.py:27
  23.8 18.3 %all-to-all-done = bf16[16,8,4224]{2,1,0:T(8,128)(2,1)S(1)} async-done(((bf16[16,8,4224]{2,1,0:T(8,128)(2,1)}), bf16[16,8,4224]{2,1,0:T(8,128)(2,1)S(1)}, u32[]{:S(2)}, u32[]{:S(2)}) %all-to-all-start) | async-done | bytes 1081376 | tf_op jit(solution)/shard_map/all_to_all | solution.py:176
  42.1 0.0 collective-permute-done.passages_other
  42.1 3.5 %shard_map.77 = (f32[4,256,128]{2,1,0:T(8,128)S(1)}, s32[1,128]{1,0:T(1,128)S(1)}, f32[16,8,128]{2,1,0:T(8,128)S(1)}) custom-call(s32[4]{0:T(128)S(1)} %pad_add_fusion.places, bf16[128,4224]{1,0:T(8,128)(2,1)S(1)} %bitcast.9, bf16[256,4096]{1,0:T(8,128)(2,1)S(1)} %copy-done, bf16[256,4096]{1,0:T(8,128)(2,1)} %collective-permute-done.passages_other, ...), custom_call_target="tpu_custom_call" | custom-call | tf_op jit(solution)/shard_map/pallas_call | solution.py:189
  45.6 14.4 %all_to_all.15.stats = f32[16,8,128]{2,1,0:T(8,128)S(1)} all-to-all(f32[16,8,128]{2,1,0:T(8,128)S(1)} %get-tuple-element.20), channel_id=1, replica_groups=mesh['yl'=2,'z'=8,'core'=2,'x'=4,'yh'=4] {'yl','z'}, dimensions={0} | all-to-all | bytes 131072 | tf_op jit(solution)/shard_map/all_to_all | solution.py:200
  60.0 1.8 %shard_map.78 = (bf16[2,128,256]{2,1,0:T(8,128)(2,1)S(1)}, f32[1,128]{1,0:T(1,128)S(1)}, bf16[192,1024]{1,0:T(8,128)(2,1)S(1)}, bf16[192,1024]{1,0:T(8,128)(2,1)...) custom-call(s32[4]{0:T(128)S(1)} %pad_add_fusion.places, bf16[128,4224]{1,0:T(8,128)(2,1)S(1)} %bitcast.10, ...), custom_call_target="tpu_custom_call" | custom-call | tf_op jit(solution)/shard_map/pallas_call | solution.py:202
  61.8 0.0 copy-start.1
  61.8 3.1 %collective-permute-start.2 = (bf16[192,1024]{1,0:T(8,128)(2,1)}, bf16[192,1024]{1,0:T(8,128)(2,1)S(1)}, u32[]{:S(2)}, u32[]{:S(2)}) collective-permute-start(bf16[192,1024]{1,0:T(8,128)(2,1)} %get-tuple-element.24), channel_id=1, source_target_pairs={{0,4},{4,8},{8,12},{12,0},{1,5},{5,9},{9,13},{13,1},{2,6},{6,10},{... | collective-permute-start | bytes 1179656 | tf_op jit(solution)/shard_map/ppermute | solution.py:27
  64.9 4.4 %collective-permute-start.3 = (bf16[192,1024]{1,0:T(8,128)(2,1)}, bf16[192,1024]{1,0:T(8,128)(2,1)S(1)}, u32[]{:S(2)}, u32[]{:S(2)}) collective-permute-start(bf16[192,1024]{1,0:T(8,128)(2,1)} %get-tuple-element.25), channel_id=1, source_target_pairs={{0,8},{4,12},{8,0},{12,4},{1,9},{5,13},{9,1},{13,5},{2,10},{6,14},... | collective-permute-start | bytes 1179656 | tf_op jit(solution)/shard_map/ppermute | solution.py:27
  69.2 3.1 %collective-permute-start.4 = (bf16[192,1024]{1,0:T(8,128)(2,1)}, bf16[192,1024]{1,0:T(8,128)(2,1)S(1)}, u32[]{:S(2)}, u32[]{:S(2)}) collective-permute-start(bf16[192,1024]{1,0:T(8,128)(2,1)} %get-tuple-element.26), channel_id=1, source_target_pairs={{0,12},{4,0},{8,4},{12,8},{1,13},{5,1},{9,5},{13,9},{2,14},{6,2},{... | collective-permute-start | bytes 1179656 | tf_op jit(solution)/shard_map/ppermute | solution.py:27
  72.3 3.3 %shard_map.79 = bf16[128,4096]{1,0:T(8,128)(2,1)} custom-call(bf16[2,128,256]{2,1,0:T(8,128)(2,1)S(1)} %get-tuple-element.22.grads, bf16[256,4096]{1,0:T(8,128)(2,1)S(1)} %copy-done, bf16[256,4096]{1,0:T(8,128)(2,1)} %collective-permute-done.passages_other, bf16[192,1024]{1,0:T(8,128)(2,1)S(1)} %get-tuple-element.23.after.refs_0_), custom_call_target="tpu_custom_call" | custom-call | tf_op jit(solution)/shard_map/pallas_call | solution.py:216
  75.6 0.0 copy-done.1
  75.6 0.0 copy-start.2
  75.6 3.8 %all-to-all-start.2 = ((bf16[16,8,4096]{2,1,0:T(8,128)(2,1)}), bf16[16,8,4096]{2,1,0:T(8,128)(2,1)S(1)}, u32[]{:S(2)}, u32[]{:S(2)}) async-start(bf16[16,8,4096]{2,1,0:T(8,128)(2,1)} %bitcast.7), calls=%async_computation.2 | async-start | bytes 2097152 | tf_op jit(solution)/shard_map/all_to_all | solution.py:223
  79.4 0.0 collective-permute-done.2.refs_1_
  79.4 3.8 %collective-permute-done.3.refs_2_ = bf16[192,1024]{1,0:T(8,128)(2,1)S(1)} collective-permute-done((bf16[192,1024]{1,0:T(8,128)(2,1)}, bf16[192,1024]{1,0:T(8,128)(2,1)S(1)}, u32[]{:S(2)}, u32[]{:S(2)}) %collective-permute-start.3) | collective-permute-done | bytes 393248 | tf_op jit(solution)/shard_map/ppermute | solution.py:27
  83.2 2.5 %collective-permute-done.4.refs_3_ = bf16[192,1024]{1,0:T(8,128)(2,1)S(1)} collective-permute-done((bf16[192,1024]{1,0:T(8,128)(2,1)}, bf16[192,1024]{1,0:T(8,128)(2,1)S(1)}, u32[]{:S(2)}, u32[]{:S(2)}) %collective-permute-start.4) | collective-permute-done | bytes 393248 | tf_op jit(solution)/shard_map/ppermute | solution.py:27
  85.6 0.0 copy-done.2
  85.6 0.7 shard_map.80
  86.3 3.8 %collective-permute-start.5 = (bf16[256,1024]{1,0:T(8,128)(2,1)S(1)}, bf16[256,1024]{1,0:T(8,128)(2,1)S(1)}, u32[]{:S(2)}, u32[]{:S(2)}) collective-permute-start(bf16[256,1024]{1,0:T(8,128)(2,1)S(1)} %shard_map.80), channel_id=1, source_target_pairs={{0,16},{16,0},{1,17},{17,1},{2,18},{18,2},{3,19},{19,3},{4,20},{20... | collective-permute-start | bytes 1572872 | tf_op jit(solution)/shard_map/ppermute | solution.py:27
  90.2 1.5 %collective-permute-done.5.refs_4_ = bf16[256,1024]{1,0:T(8,128)(2,1)S(1)} collective-permute-done((bf16[256,1024]{1,0:T(8,128)(2,1)S(1)}, bf16[256,1024]{1,0:T(8,128)(2,1)S(1)}, u32[]{:S(2)}, u32[]{:S(2)}) %collective-permute-start.5) | collective-permute-done | bytes 524320 | tf_op jit(solution)/shard_map/ppermute | solution.py:27
  91.7 1.3 %shard_map.81 = (bf16[256,256]{1,0:T(8,128)(2,1)S(1)}, bf16[256,256]{1,0:T(8,128)(2,1)S(1)}, bf16[256,256]{1,0:T(8,128)(2,1)S(1)}, bf16[256,256]{1,0:T(8,128)(2,1)S(1)}) custom-call(s32[4]{0:T(128)S(1)} %pad_add_fusion.places, bf16[192,1024]{1,0:T(8,128)(2,1)S(1)} %copy-done.2, bf16[192,1024]{1,0:T(8,128)(2,1)S(1)} %collective-permute-done.2.refs_1_, ...), custom_call_target="tpu_custom_call" | custom-call | tf_op jit(solution)/shard_map/pallas_call | solution.py:233
  93.0 4.2 %collective-permute-start.6 = (bf16[256,256]{1,0:T(8,128)(2,1)S(1)}, bf16[256,256]{1,0:T(8,128)(2,1)S(1)}, u32[]{:S(2)}, u32[]{:S(2)}) collective-permute-start(bf16[256,256]{1,0:T(8,128)(2,1)S(1)} %get-tuple-element.28), channel_id=1, source_target_pairs={{0,1},{1,2},{2,3},{3,0},{4,5},{5,6},{6,7},{7,4},{8,9},{9,10},{10,1... | collective-permute-start | bytes 393224 | tf_op jit(solution)/shard_map/ppermute | solution.py:27
  97.2 4.7 %collective-permute-start.7 = (bf16[256,256]{1,0:T(8,128)(2,1)S(1)}, bf16[256,256]{1,0:T(8,128)(2,1)S(1)}, u32[]{:S(2)}, u32[]{:S(2)}) collective-permute-start(bf16[256,256]{1,0:T(8,128)(2,1)S(1)} %get-tuple-element.29), channel_id=1, source_target_pairs={{0,2},{1,3},{2,0},{3,1},{4,6},{5,7},{6,4},{7,5},{8,10},{9,11},{10,... | collective-permute-start | bytes 393224 | tf_op jit(solution)/shard_map/ppermute | solution.py:27
  102.0 5.0 %collective-permute-start.8 = (bf16[256,256]{1,0:T(8,128)(2,1)S(1)}, bf16[256,256]{1,0:T(8,128)(2,1)S(1)}, u32[]{:S(2)}, u32[]{:S(2)}) collective-permute-start(bf16[256,256]{1,0:T(8,128)(2,1)S(1)} %get-tuple-element.30), channel_id=1, source_target_pairs={{0,3},{1,0},{2,1},{3,2},{4,7},{5,4},{6,5},{7,6},{8,11},{9,8},{10,9... | collective-permute-start | bytes 393224 | tf_op jit(solution)/shard_map/ppermute | solution.py:27
  107.0 0.6 constant_dynamic-slice_fusion
  107.6 0.0 collective-permute-done.6.refs_1_
  107.6 2.4 %collective-permute-done.7.refs_2_ = bf16[256,256]{1,0:T(8,128)(2,1)S(1)} collective-permute-done((bf16[256,256]{1,0:T(8,128)(2,1)S(1)}, bf16[256,256]{1,0:T(8,128)(2,1)S(1)}, u32[]{:S(2)}, u32[]{:S(2)}) %collective-permute-start.7) | collective-permute-done | bytes 131104 | tf_op jit(solution)/shard_map/ppermute | solution.py:27
  110.0 5.0 %collective-permute-done.8.refs_3_ = bf16[256,256]{1,0:T(8,128)(2,1)S(1)} collective-permute-done((bf16[256,256]{1,0:T(8,128)(2,1)S(1)}, bf16[256,256]{1,0:T(8,128)(2,1)S(1)}, u32[]{:S(2)}, u32[]{:S(2)}) %collective-permute-start.8) | collective-permute-done | bytes 131104 | tf_op jit(solution)/shard_map/ppermute | solution.py:27
  114.9 0.0 all-to-all-done.2.query_parts
  114.9 0.9 shard_map.82
  (1 shorter events, 0.0 us)
Async XLA Ops:
  0.6 15.4 %copy-start = (bf16[256,4096]{1,0:T(8,128)(2,1)S(1)}, bf16[256,4096]{1,0:T(8,128)(2,1)}, u32[]{:S(2)}) copy-start(bf16[256,4096]{1,0:T(8,128)(2,1)} %passages.3) | copy-start | bytes 6291460
  0.6 18.3 %copy-start.3 = (f32[1,256,256]{2,1,0:T(8,128)S(1)}, f32[1,256,256]{2,1,0:T(8,128)}, u32[]{:S(2)}) copy-start(f32[1,256,256]{2,1,0:T(8,128)} %param.7) | copy-start | bytes 786436
  4.0 38.0 %all-to-all-start = ((bf16[16,8,4224]{2,1,0:T(8,128)(2,1)}), bf16[16,8,4224]{2,1,0:T(8,128)(2,1)S(1)}, u32[]{:S(2)}, u32[]{:S(2)}) async-start(bf16[16,8,4224]{2,1,0:T(8,128)(2,1)} %broadcast_in_dim.4), calls=%async_computation | async-start | bytes 2162688 | tf_op jit(solution)/shard_map/all_to_all | solution.py:176
  16.0 26.0 %collective-permute-start = (bf16[256,4096]{1,0:T(8,128)(2,1)S(1)}, bf16[256,4096]{1,0:T(8,128)(2,1)}, u32[]{:S(2)}, u32[]{:S(2)}) collective-permute-start(bf16[256,4096]{1,0:T(8,128)(2,1)S(1)} %copy-done), channel_id=1, source_target_pairs={{0,16},{16,0},{1,17},{17,1},{2,18},{18,2},{3,19},{19,3},{4,20},{20... | collective-permute-start | bytes 6291464 | tf_op jit(solution)/shard_map/ppermute | solution.py:27
  19.8 3.9 %collective-permute-start.1 = (bf16[3,256,256]{2,1,0:T(8,128)(2,1)}, bf16[3,256,256]{2,1,0:T(8,128)(2,1)}, u32[]{:S(2)}, u32[]{:S(2)}) collective-permute-start(bf16[3,256,256]{2,1,0:T(8,128)(2,1)} %shard_map.76.teacher), channel_id=1, source_target_pairs={{0,16},{16,0},{1,17},{17,1},{2,18},{18,2},{3,19},{19,3},{4,20},{20... | collective-permute-start | bytes 1179656 | tf_op jit(solution)/shard_map/ppermute | solution.py:27
  61.8 13.8 %copy-start.1 = (bf16[192,1024]{1,0:T(8,128)(2,1)}, bf16[192,1024]{1,0:T(8,128)(2,1)S(1)}, u32[]{:S(2)}) copy-start(bf16[192,1024]{1,0:T(8,128)(2,1)S(1)} %get-tuple-element.23.after.refs_0_) | copy-start | bytes 1179652
  61.8 17.6 %collective-permute-start.2 = (bf16[192,1024]{1,0:T(8,128)(2,1)}, bf16[192,1024]{1,0:T(8,128)(2,1)S(1)}, u32[]{:S(2)}, u32[]{:S(2)}) collective-permute-start(bf16[192,1024]{1,0:T(8,128)(2,1)} %get-tuple-element.24), channel_id=1, source_target_pairs={{0,4},{4,8},{8,12},{12,0},{1,5},{5,9},{9,13},{13,1},{2,6},{6,10},{... | collective-permute-start | bytes 1179656 | tf_op jit(solution)/shard_map/ppermute | solution.py:27
  64.9 18.3 %collective-permute-start.3 = (bf16[192,1024]{1,0:T(8,128)(2,1)}, bf16[192,1024]{1,0:T(8,128)(2,1)S(1)}, u32[]{:S(2)}, u32[]{:S(2)}) collective-permute-start(bf16[192,1024]{1,0:T(8,128)(2,1)} %get-tuple-element.25), channel_id=1, source_target_pairs={{0,8},{4,12},{8,0},{12,4},{1,9},{5,13},{9,1},{13,5},{2,10},{6,14},... | collective-permute-start | bytes 1179656 | tf_op jit(solution)/shard_map/ppermute | solution.py:27
  69.2 16.4 %collective-permute-start.4 = (bf16[192,1024]{1,0:T(8,128)(2,1)}, bf16[192,1024]{1,0:T(8,128)(2,1)S(1)}, u32[]{:S(2)}, u32[]{:S(2)}) collective-permute-start(bf16[192,1024]{1,0:T(8,128)(2,1)} %get-tuple-element.26), channel_id=1, source_target_pairs={{0,12},{4,0},{8,4},{12,8},{1,13},{5,1},{9,5},{13,9},{2,14},{6,2},{... | collective-permute-start | bytes 1179656 | tf_op jit(solution)/shard_map/ppermute | solution.py:27
  75.6 10.0 %copy-start.2 = (bf16[192,1024]{1,0:T(8,128)(2,1)S(1)}, bf16[192,1024]{1,0:T(8,128)(2,1)}, u32[]{:S(2)}) copy-start(bf16[192,1024]{1,0:T(8,128)(2,1)} %copy-done.1) | copy-start | bytes 1179652
  75.6 39.3 %all-to-all-start.2 = ((bf16[16,8,4096]{2,1,0:T(8,128)(2,1)}), bf16[16,8,4096]{2,1,0:T(8,128)(2,1)S(1)}, u32[]{:S(2)}, u32[]{:S(2)}) async-start(bf16[16,8,4096]{2,1,0:T(8,128)(2,1)} %bitcast.7), calls=%async_computation.2 | async-start | bytes 2097152 | tf_op jit(solution)/shard_map/all_to_all | solution.py:223
  86.3 5.4 %collective-permute-start.5 = (bf16[256,1024]{1,0:T(8,128)(2,1)S(1)}, bf16[256,1024]{1,0:T(8,128)(2,1)S(1)}, u32[]{:S(2)}, u32[]{:S(2)}) collective-permute-start(bf16[256,1024]{1,0:T(8,128)(2,1)S(1)} %shard_map.80), channel_id=1, source_target_pairs={{0,16},{16,0},{1,17},{17,1},{2,18},{18,2},{3,19},{19,3},{4,20},{20... | collective-permute-start | bytes 1572872 | tf_op jit(solution)/shard_map/ppermute | solution.py:27
  93.0 14.6 %collective-permute-start.6 = (bf16[256,256]{1,0:T(8,128)(2,1)S(1)}, bf16[256,256]{1,0:T(8,128)(2,1)S(1)}, u32[]{:S(2)}, u32[]{:S(2)}) collective-permute-start(bf16[256,256]{1,0:T(8,128)(2,1)S(1)} %get-tuple-element.28), channel_id=1, source_target_pairs={{0,1},{1,2},{2,3},{3,0},{4,5},{5,6},{6,7},{7,4},{8,9},{9,10},{10,1... | collective-permute-start | bytes 393224 | tf_op jit(solution)/shard_map/ppermute | solution.py:27
  97.2 12.7 %collective-permute-start.7 = (bf16[256,256]{1,0:T(8,128)(2,1)S(1)}, bf16[256,256]{1,0:T(8,128)(2,1)S(1)}, u32[]{:S(2)}, u32[]{:S(2)}) collective-permute-start(bf16[256,256]{1,0:T(8,128)(2,1)S(1)} %get-tuple-element.29), channel_id=1, source_target_pairs={{0,2},{1,3},{2,0},{3,1},{4,6},{5,7},{6,4},{7,5},{8,10},{9,11},{10,... | collective-permute-start | bytes 393224 | tf_op jit(solution)/shard_map/ppermute | solution.py:27
  102.0 12.9 %collective-permute-start.8 = (bf16[256,256]{1,0:T(8,128)(2,1)S(1)}, bf16[256,256]{1,0:T(8,128)(2,1)S(1)}, u32[]{:S(2)}, u32[]{:S(2)}) collective-permute-start(bf16[256,256]{1,0:T(8,128)(2,1)S(1)} %get-tuple-element.30), channel_id=1, source_target_pairs={{0,3},{1,0},{2,1},{3,2},{4,7},{5,4},{6,5},{7,6},{8,11},{9,8},{10,9... | collective-permute-start | bytes 393224 | tf_op jit(solution)/shard_map/ppermute | solution.py:27

commit v11 on v10

--- a/solution.py
+++ b/solution.py
@@ -8,11 +8,12 @@
 from jax.sharding import Mesh, PartitionSpec as P
 
 inv_temp = 50.0
-YL, CORES, X = 2, 2, 4
+YL, ZL, CORES, X = 2, 2, 2, 4
 LANES = 128
 STATS = 8
 PIECES = 3
-CHIPS = ("yl", "z")
+NEAR, FAR = ("yl", "zl"), ("zh",)
+CHIPS = NEAR + FAR
 f32, bf16, i32 = jnp.float32, jnp.bfloat16, jnp.int32
 VMEM = pl.BlockSpec(memory_space=pltpu.VMEM)
 ANY = pl.BlockSpec(memory_space=pl.ANY)
@@ -32,6 +33,14 @@
     order = sorted(range(size), key=lambda d: -min(d, size - d))
     moved = {d: shift(values[d], axis, d) for d in order}
     return [moved[d] for d in range(size)]
+
+
+def spread(value, axes):
+    size = 1
+    for axis in axes:
+        size *= lax.axis_size(axis)
+    copies = jnp.broadcast_to(value[None], (size,) + value.shape)
+    return lax.all_to_all(copies, axes, 0, 0, tiled=True).reshape(size * value.shape[0], value.shape[1])
 
 
 def hits(positive, place, shape):
@@ -138,17 +147,16 @@
     return total
 
 
-def other_kernel(rows, *refs):
+def product_kernel(half, rows, *refs):
     out = refs[-1]
-    out[...] = products(refs[:-1], 1, out.shape[0], rows).astype(bf16)
-
-
-def own_kernel(groups, rows, places, *refs):
-    packed, back, outs, total = refs[:groups], refs[groups], refs[groups + 1 : -1], refs[-1]
+    out[...] = products(refs[:-1], half, out.shape[0], rows).astype(out.dtype)
+
+
+def add_kernel(places, part, back, *outs):
     width = outs[0].shape[1]
-    total[...] = (products(packed, 0, back.shape[0], rows) + back[...].astype(f32)).astype(bf16)
     for d, out in enumerate(outs):
-        out[...] = total[:, pl.ds(pl.multiple_of(lax.rem(places[3] + d, len(outs)) * width, width), width)]
+        columns = pl.ds(pl.multiple_of(lax.rem(places[3] + d, len(outs)) * width, width), width)
+        out[...] = (part[:, columns] + back[:, columns].astype(f32)).astype(bf16)
 
 
 def sum_kernel(query_parts, *refs):
@@ -160,22 +168,22 @@
 def per_device(queries, passages, teacher, teacher_rows, positives):
     own_rows, depth = queries.shape[1:]
     block_rows = passages.shape[0]
-    chips = lax.axis_size("yl") * lax.axis_size("z")
+    yl, zh, zl = (lax.axis_index(axis) for axis in ("yl", "zh", "zl"))
+    far, near = lax.axis_size("zh"), lax.axis_size("zl")
+    chips = lax.axis_size("yl") * near * far
     x_size, yh_size = lax.axis_size("x"), lax.axis_size("yh")
     rows, wide = chips * own_rows, CORES * block_rows
-    chip = lax.axis_index("yl") * lax.axis_size("z") + lax.axis_index("z")
+    chip, block = (yl * near + zl) * far + zh, (yl * far + zh) * near + zl
     core, x, yh = lax.axis_index("core"), lax.axis_index("x"), lax.axis_index("yh")
     places = jnp.stack(
-        [(chip * CORES + core) * block_rows, (chip * CORES + 1 - core) * block_rows, x, yh]
+        [(block * CORES + core) * block_rows, (block * CORES + 1 - core) * block_rows, x, yh]
     ).astype(i32)
 
     codes = jnp.concatenate([teacher_rows, positives & 255, lax.shift_right_logical(positives, 8)], axis=0)
     codes = jnp.pad(codes, ((0, own_rows - codes.shape[0]), (0, LANES - own_rows)))
     sent = jnp.concatenate([queries[0], codes.astype(bf16)], axis=1)
     passages_other = shift(passages, "core", 1)
-    query = lax.all_to_all(
-        jnp.broadcast_to(sent[None], (chips,) + sent.shape), CHIPS, 0, 0, tiled=True
-    ).reshape(rows, depth + LANES)
+    query = spread(spread(sent, FAR), NEAR)
 
     table = pl.pallas_call(
         teacher_kernel,
@@ -222,22 +230,24 @@
     )(rows_first, passages, passages_other, packed[0])
     query_parts = lax.all_to_all(query_part.reshape(chips, own_rows, depth), CHIPS, 0, 0, tiled=True)
     packed = shifts(packed, "x")
-    part_other = pl.pallas_call(
-        functools.partial(other_kernel, rows),
-        out_shape=jax.ShapeDtypeStruct((block_rows, width), bf16),
-        in_specs=[VMEM] * x_size,
-        out_specs=VMEM,
-        compiler_params=PARAMS,
-        cost_estimate=pl.CostEstimate(flops=10**11, bytes_accessed=2**21, transcendentals=0),
-    )(*packed)
+    part, part_other = (
+        pl.pallas_call(
+            functools.partial(product_kernel, half, rows),
+            out_shape=jax.ShapeDtypeStruct((block_rows, width), dtype),
+            in_specs=[VMEM] * x_size,
+            out_specs=VMEM,
+            compiler_params=PARAMS,
+            cost_estimate=pl.CostEstimate(flops=10**11, bytes_accessed=2**21, transcendentals=0),
+        )(*packed)
+        for half, dtype in enumerate((f32, bf16))
+    )
     parts = pl.pallas_call(
-        functools.partial(own_kernel, x_size, rows),
+        add_kernel,
         out_shape=(jax.ShapeDtypeStruct((block_rows, width // yh_size), bf16),) * yh_size,
-        in_specs=[SMEM] + [VMEM] * (x_size + 1),
+        in_specs=[SMEM] + [VMEM] * 2,
         out_specs=(VMEM,) * yh_size,
-        scratch_shapes=[pltpu.VMEM((block_rows, width), bf16)],
-        compiler_params=PARAMS,
-    )(places, *packed, shift(part_other, "core", 1))
+        compiler_params=PARAMS,
+    )(places, part, shift(part_other, "core", 1))
     parts = shifts(parts, "yh")
     query_total, passage_total = pl.pallas_call(
         sum_kernel,
@@ -255,10 +265,10 @@
 def solution(mesh):
     blk, qgroup = mesh.devices.shape
     split = Mesh(
-        mesh.devices.reshape(YL, blk // (YL * CORES), CORES, X, qgroup // X),
-        ("yl", "z", "core", "x", "yh"),
+        mesh.devices.reshape(YL, blk // (YL * ZL * CORES), ZL, CORES, X, qgroup // X),
+        ("yl", "zh", "zl", "core", "x", "yh"),
     )
-    blk, qgroup = ("yl", "z", "core"), ("x", "yh")
+    blk, qgroup = ("yl", "zh", "zl", "core"), ("x", "yh")
     in_specs = (
         P(qgroup, blk, None),
         P(blk, None),

time: 117 us -> 118 us (level)
  waiting for transfers between devices: 35.4 us -> 26.6 us
  starting transfers between devices: 48.9 us -> 57 us
  Pallas kernels: 12.3 us -> 15.8 us
  blocking collectives: 14.4 us -> 12 us
    all_to_all x1 -> x2, waiting for transfers between devices: 18.3 us -> 12.4 us  [spread(): lax.all_to_all(copies, axes, 0, 0, tiled=True)]
    all_to_all x1 -> x2, starting transfers between devices: 12 us -> 16.5 us  [spread(): lax.all_to_all(copies, axes, 0, 0, tiled=True)]
    ppermute x9, starting transfers between devices: 33.1 us -> 36 us  [shift(): lax.ppermute(value, axis, [(i, (i + by) % size) for i in range(size)])]
    ppermute x9, waiting for transfers between devices: 17 us -> 14.2 us  [shift(): lax.ppermute(value, axis, [(i, (i + by) % size) for i in range(size)])]
    all_to_all x1, blocking collectives: 14.4 us -> 12 us  [per_device(): stats = lax.all_to_all(stats, CHIPS, 0, 0, tiled=True)]
    pallas_call x2 -> x3, Pallas kernels: 1.98 us -> 4.29 us  [the longest x2 3.59 us: per_device(): pl.pallas_call(functools.partial(product_kernel, half, rows), out_shape=j...]
    pallas_call x1, Pallas kernels: 0.86 us -> 2.08 us  [per_device(): pl.pallas_call(sum_kernel, out_shape=(jax.ShapeDtypeStruct((own_rows, dep...]
  transfers between devices with their start and end apart: 11 -> 12, of which waited for: 7 -> 7; matrix products, arithmetic and copies ran while one was open for 1% -> 1% of each run, Pallas kernels for 5% -> 7%
where the time goes in v11:
time: 118 us; the launch traced here: 117 us
  starting transfers between devices  57 us (48%)
  waiting for transfers between devices  26.6 us (23%)
  Pallas kernels  15.8 us (13%)
  blocking collectives  12 us (10%)
  local copies, waits for them, and re-layouts  2.39 us (2%)
  other arithmetic  2.26 us (2%)
    ppermute x9, starting transfers between devices, shift(): lax.ppermute(value, axis, [(i, (i + by) % size) for i in range(size)])  36 us
    all_to_all x2, starting transfers between devices, spread(): lax.all_to_all(copies, axes, 0, 0, tiled=True)  16.5 us
    ppermute x9, waiting for transfers between devices, shift(): lax.ppermute(value, axis, [(i, (i + by) % size) for i in range(size)])  14.2 us
    all_to_all x2, waiting for transfers between devices, spread(): lax.all_to_all(copies, axes, 0, 0, tiled=True)  12.4 us
    all_to_all x1, blocking collectives, per_device(): stats = lax.all_to_all(stats, CHIPS, 0, 0, tiled=True)  12 us
    all_to_all x1, starting transfers between devices, per_device(): lax.all_to_all(query_part.reshape(chips, own_rows, depth), CHIPS, 0, 0, t...  4.47 us
    pallas_call x2, Pallas kernels, per_device(): pl.pallas_call(functools.partial(product_kernel, half, rows), out_shape=j...  3.59 us
    pallas_call x1, Pallas kernels, per_device(): pl.pallas_call(score_kernel, out_shape=(jax.ShapeDtypeStruct((2 * CORES,...  3.46 us
  transfers between devices with their start and end apart: 12, of which 7 were waited for; matrix products, arithmetic and copies ran while one was open for 1% of the time, Pallas kernels for 7%

profile of v11, /device:TPU:1, one launch (start us, length us, event | category | flops | bytes accessed | tf_op | source)
XLA Modules:
  0.0 116.8 jit_solution(2095742150008356576)
XLA Ops:
  0.6 0.7 convert.11
  1.3 0.7 and_convert_fusion
  2.0 0.8 pad_maximum_fusion
  2.8 0.7 broadcast_in_dim.8
  3.5 0.0 copy-start.3
  3.5 11.0 %all-to-all-start = ((bf16[4,8,4224]{2,1,0:T(8,128)(2,1)}), bf16[4,8,4224]{2,1,0:T(8,128)(2,1)S(1)}, u32[]{:S(2)}, u32[]{:S(2)}) async-start(bf16[4,8,4224]{2,1,0:T(8,128)(2,1)} %broadcast_in_dim.8), calls=%async_computation | async-start | bytes 540672 | tf_op jit(solution)/shard_map/all_to_all | solution.py:43
  14.5 2.9 %collective-permute-start = (bf16[256,4096]{1,0:T(8,128)(2,1)}, bf16[256,4096]{1,0:T(8,128)(2,1)}, u32[]{:S(2)}, u32[]{:S(2)}) collective-permute-start(bf16[256,4096]{1,0:T(8,128)(2,1)} %passages.3), channel_id=1, source_target_pairs={{0,16},{16,0},{1,17},{17,1},{2,18},{18,2},{3,19},{19,3},{4,20},{20... | collective-permute-start | bytes 6291464 | tf_op jit(solution)/shard_map/ppermute | solution.py:28
  17.4 5.4 %all-to-all-done = bf16[4,8,4224]{2,1,0:T(8,128)(2,1)S(1)} async-done(((bf16[4,8,4224]{2,1,0:T(8,128)(2,1)}), bf16[4,8,4224]{2,1,0:T(8,128)(2,1)S(1)}, u32[]{:S(2)}, u32[]{:S(2)}) %all-to-all-start) | async-done | bytes 270368 | tf_op jit(solution)/shard_map/all_to_all | solution.py:43
  22.8 1.1 broadcast_in_dim.19
  23.8 5.5 %all-to-all-start.1 = ((bf16[4,32,4224]{2,1,0:T(8,128)(2,1)}), bf16[4,32,4224]{2,1,0:T(8,128)(2,1)S(1)}, u32[]{:S(2)}, u32[]{:S(2)}) async-start(bf16[4,32,4224]{2,1,0:T(8,128)(2,1)} %broadcast_in_dim.19), calls=%async_computation.1 | async-start | bytes 2162688 | tf_op jit(solution)/shard_map/all_to_all | solution.py:43
  29.4 0.0 copy-done.3
  29.4 0.0 copy-start
  29.4 0.9 shard_map.76.teacher
  30.3 3.9 %collective-permute-start.1 = (bf16[3,256,256]{2,1,0:T(8,128)(2,1)}, bf16[3,256,256]{2,1,0:T(8,128)(2,1)}, u32[]{:S(2)}, u32[]{:S(2)}) collective-permute-start(bf16[3,256,256]{2,1,0:T(8,128)(2,1)} %shard_map.76.teacher), channel_id=1, source_target_pairs={{0,16},{16,0},{1,17},{17,1},{2,18},{18,2},{3,19},{19,3},{4,20},{20... | collective-permute-start | bytes 1179656 | tf_op jit(solution)/shard_map/ppermute | solution.py:28
  34.2 0.1 pad_add_fusion.places
  34.3 1.6 %collective-permute-done.1.teacher_other = bf16[3,256,256]{2,1,0:T(8,128)(2,1)} collective-permute-done((bf16[3,256,256]{2,1,0:T(8,128)(2,1)}, bf16[3,256,256]{2,1,0:T(8,128)(2,1)}, u32[]{:S(2)}, u32[]{:S(2)}) %collective-permute-start.1) | collective-permute-done | bytes 393248 | tf_op jit(solution)/shard_map/ppermute | solution.py:28
  35.9 7.0 %all-to-all-done.1 = bf16[4,32,4224]{2,1,0:T(8,128)(2,1)S(1)} async-done(((bf16[4,32,4224]{2,1,0:T(8,128)(2,1)}), bf16[4,32,4224]{2,1,0:T(8,128)(2,1)S(1)}, u32[]{:S(2)}, u32[]{:S(2)}) %all-to-all-start.1) | async-done | bytes 1081376 | tf_op jit(solution)/shard_map/all_to_all | solution.py:43
  42.8 0.0 collective-permute-done.passages_other
  42.8 0.0 copy-done
  42.8 3.5 %shard_map.77 = (f32[4,256,128]{2,1,0:T(8,128)S(1)}, s32[1,128]{1,0:T(1,128)S(1)}, f32[16,8,128]{2,1,0:T(8,128)S(1)}) custom-call(s32[4]{0:T(128)S(1)} %pad_add_fusion.places, bf16[128,4224]{1,0:T(8,128)(2,1)S(1)} %bitcast.10, bf16[256,4096]{1,0:T(8,128)(2,1)S(1)} %copy-done, bf16[256,4096]{1,0:T(8,128)(2,1)} %collective-permute-done.passages_other, ...), custom_call_target="tpu_custom_call" | custom-call | tf_op jit(solution)/shard_map/pallas_call | solution.py:197
  46.3 12.0 %all_to_all.20.stats = f32[16,8,128]{2,1,0:T(8,128)S(1)} all-to-all(f32[16,8,128]{2,1,0:T(8,128)S(1)} %get-tuple-element.20), channel_id=1, replica_groups=mesh['yl'=2,'zh'=4,'zl'=2,'core'=2,'x'=4,'yh'=4] {'yl','zl','zh'}, dimensions={0} | all-to-all | bytes 131072 | tf_op jit(solution)/shard_map/all_to_all | solution.py:208
  58.3 1.7 %shard_map.78 = (bf16[2,128,256]{2,1,0:T(8,128)(2,1)S(1)}, f32[1,128]{1,0:T(1,128)S(1)}, bf16[192,1024]{1,0:T(8,128)(2,1)S(1)}, bf16[192,1024]{1,0:T(8,128)(2,1)...) custom-call(s32[4]{0:T(128)S(1)} %pad_add_fusion.places, bf16[128,4224]{1,0:T(8,128)(2,1)S(1)} %bitcast.11, ...), custom_call_target="tpu_custom_call" | custom-call | tf_op jit(solution)/shard_map/pallas_call | solution.py:210
  60.1 0.0 copy-start.1
  60.1 3.1 %collective-permute-start.2 = (bf16[192,1024]{1,0:T(8,128)(2,1)}, bf16[192,1024]{1,0:T(8,128)(2,1)S(1)}, u32[]{:S(2)}, u32[]{:S(2)}) collective-permute-start(bf16[192,1024]{1,0:T(8,128)(2,1)} %get-tuple-element.24), channel_id=1, source_target_pairs={{0,4},{4,8},{8,12},{12,0},{1,5},{5,9},{9,13},{13,1},{2,6},{6,10},{... | collective-permute-start | bytes 1179656 | tf_op jit(solution)/shard_map/ppermute | solution.py:28
  63.2 4.4 %collective-permute-start.3 = (bf16[192,1024]{1,0:T(8,128)(2,1)}, bf16[192,1024]{1,0:T(8,128)(2,1)}, u32[]{:S(2)}, u32[]{:S(2)}) collective-permute-start(bf16[192,1024]{1,0:T(8,128)(2,1)} %get-tuple-element.25), channel_id=1, source_target_pairs={{0,8},{4,12},{8,0},{12,4},{1,9},{5,13},{9,1},{13,5},{2,10},{6,14},... | collective-permute-start | bytes 1179656 | tf_op jit(solution)/shard_map/ppermute | solution.py:28
  67.5 3.1 %collective-permute-start.4 = (bf16[192,1024]{1,0:T(8,128)(2,1)}, bf16[192,1024]{1,0:T(8,128)(2,1)}, u32[]{:S(2)}, u32[]{:S(2)}) collective-permute-start(bf16[192,1024]{1,0:T(8,128)(2,1)} %get-tuple-element.26), channel_id=1, source_target_pairs={{0,12},{4,0},{8,4},{12,8},{1,13},{5,1},{9,5},{13,9},{2,14},{6,2},{... | collective-permute-start | bytes 1179656 | tf_op jit(solution)/shard_map/ppermute | solution.py:28
  70.6 3.3 %shard_map.79 = bf16[128,4096]{1,0:T(8,128)(2,1)} custom-call(bf16[2,128,256]{2,1,0:T(8,128)(2,1)S(1)} %get-tuple-element.22.grads, bf16[256,4096]{1,0:T(8,128)(2,1)S(1)} %copy-done, bf16[256,4096]{1,0:T(8,128)(2,1)} %collective-permute-done.passages_other, bf16[192,1024]{1,0:T(8,128)(2,1)S(1)} %get-tuple-element.23.after.refs_0_), custom_call_target="tpu_custom_call" | custom-call | tf_op jit(solution)/shard_map/pallas_call | solution.py:224
  73.9 0.0 copy-done.1
  73.9 0.0 copy-start.2
  73.9 4.5 %all-to-all-start.3 = ((bf16[16,8,4096]{2,1,0:T(8,128)(2,1)}), bf16[16,8,4096]{2,1,0:T(8,128)(2,1)}, u32[]{:S(2)}, u32[]{:S(2)}) async-start(bf16[16,8,4096]{2,1,0:T(8,128)(2,1)} %bitcast.8), calls=%async_computation.3 | async-start | bytes 2097152 | tf_op jit(solution)/shard_map/all_to_all | solution.py:231
  78.4 0.0 collective-permute-done.2.refs_1_
  78.4 3.1 %collective-permute-done.3.refs_2_ = bf16[192,1024]{1,0:T(8,128)(2,1)} collective-permute-done((bf16[192,1024]{1,0:T(8,128)(2,1)}, bf16[192,1024]{1,0:T(8,128)(2,1)}, u32[]{:S(2)}, u32[]{:S(2)}) %collective-permute-start.3) | collective-permute-done | bytes 393248 | tf_op jit(solution)/shard_map/ppermute | solution.py:28
  81.6 2.4 %collective-permute-done.4.refs_3_ = bf16[192,1024]{1,0:T(8,128)(2,1)} collective-permute-done((bf16[192,1024]{1,0:T(8,128)(2,1)}, bf16[192,1024]{1,0:T(8,128)(2,1)}, u32[]{:S(2)}, u32[]{:S(2)}) %collective-permute-start.4) | collective-permute-done | bytes 393248 | tf_op jit(solution)/shard_map/ppermute | solution.py:28
  83.9 0.0 copy-done.2
  83.9 1.8 %shard_map.81 = bf16[256,1024]{1,0:T(8,128)(2,1)S(1)} custom-call(bf16[192,1024]{1,0:T(8,128)(2,1)S(1)} %copy-done.2, bf16[192,1024]{1,0:T(8,128)(2,1)S(1)} %collective-permute-done.2.refs_1_, bf16[192,1024]{1,0:T(8,128)(2,1)} %collective-permute-done.3.refs_2_, bf16[192,1024]{1,0:T(8,128)(2,1)} %collective-permute-done.4.refs_3_), custom_call_target="tpu_custom_call" | custom-call | flops 99999997952 | bytes 2097152 | tf_op jit(solution)/shard_map/pallas_call | solution.py:234
  85.7 4.0 %collective-permute-start.5 = (bf16[256,1024]{1,0:T(8,128)(2,1)S(1)}, bf16[256,1024]{1,0:T(8,128)(2,1)S(1)}, u32[]{:S(2)}, u32[]{:S(2)}) collective-permute-start(bf16[256,1024]{1,0:T(8,128)(2,1)S(1)} %shard_map.81), channel_id=1, source_target_pairs={{0,16},{16,0},{1,17},{17,1},{2,18},{18,2},{3,19},{19,3},{4,20},{20... | collective-permute-start | bytes 1572872 | tf_op jit(solution)/shard_map/ppermute | solution.py:28
  89.7 1.8 %shard_map.80.part = f32[256,1024]{1,0:T(8,128)S(1)} custom-call(bf16[192,1024]{1,0:T(8,128)(2,1)S(1)} %copy-done.2, bf16[192,1024]{1,0:T(8,128)(2,1)S(1)} %collective-permute-done.2.refs_1_, bf16[192,1024]{1,0:T(8,128)(2,1)} %collective-permute-done.3.refs_2_, bf16[192,1024]{1,0:T(8,128)(2,1)} %collective-permute-done.4.refs_3_), custom_call_target="tpu_custom_call" | custom-call | flops 99999997952 | bytes 2097152 | tf_op jit(solution)/shard_map/pallas_call | solution.py:234
  91.5 0.0 collective-permute-done.5.back
  91.5 0.7 shard_map.82
  92.2 4.2 %collective-permute-start.6 = (bf16[256,256]{1,0:T(8,128)(2,1)S(1)}, bf16[256,256]{1,0:T(8,128)(2,1)S(1)}, u32[]{:S(2)}, u32[]{:S(2)}) collective-permute-start(bf16[256,256]{1,0:T(8,128)(2,1)S(1)} %get-tuple-element.28), channel_id=1, source_target_pairs={{0,1},{1,2},{2,3},{3,0},{4,5},{5,6},{6,7},{7,4},{8,9},{9,10},{10,1... | collective-permute-start | bytes 393224 | tf_op jit(solution)/shard_map/ppermute | solution.py:28
  96.4 5.6 %collective-permute-start.7 = (bf16[256,256]{1,0:T(8,128)(2,1)S(1)}, bf16[256,256]{1,0:T(8,128)(2,1)S(1)}, u32[]{:S(2)}, u32[]{:S(2)}) collective-permute-start(bf16[256,256]{1,0:T(8,128)(2,1)S(1)} %get-tuple-element.29), channel_id=1, source_target_pairs={{0,2},{1,3},{2,0},{3,1},{4,6},{5,7},{6,4},{7,5},{8,10},{9,11},{10,... | collective-permute-start | bytes 393224 | tf_op jit(solution)/shard_map/ppermute | solution.py:28
  102.0 5.0 %collective-permute-start.8 = (bf16[256,256]{1,0:T(8,128)(2,1)S(1)}, bf16[256,256]{1,0:T(8,128)(2,1)S(1)}, u32[]{:S(2)}, u32[]{:S(2)}) collective-permute-start(bf16[256,256]{1,0:T(8,128)(2,1)S(1)} %get-tuple-element.30), channel_id=1, source_target_pairs={{0,3},{1,0},{2,1},{3,2},{4,7},{5,4},{6,5},{7,6},{8,11},{9,8},{10,9... | collective-permute-start | bytes 393224 | tf_op jit(solution)/shard_map/ppermute | solution.py:28
  107.0 0.6 constant_dynamic-slice_fusion
  107.6 0.0 collective-permute-done.6.refs_1_
  107.6 1.6 %collective-permute-done.7.refs_2_ = bf16[256,256]{1,0:T(8,128)(2,1)S(1)} collective-permute-done((bf16[256,256]{1,0:T(8,128)(2,1)S(1)}, bf16[256,256]{1,0:T(8,128)(2,1)S(1)}, u32[]{:S(2)}, u32[]{:S(2)}) %collective-permute-start.7) | collective-permute-done | bytes 131104 | tf_op jit(solution)/shard_map/ppermute | solution.py:28
  109.2 5.5 %collective-permute-done.8.refs_3_ = bf16[256,256]{1,0:T(8,128)(2,1)S(1)} collective-permute-done((bf16[256,256]{1,0:T(8,128)(2,1)S(1)}, bf16[256,256]{1,0:T(8,128)(2,1)S(1)}, u32[]{:S(2)}, u32[]{:S(2)}) %collective-permute-start.8) | collective-permute-done | bytes 131104 | tf_op jit(solution)/shard_map/ppermute | solution.py:28
  114.8 0.0 all-to-all-done.3.query_parts
  114.8 2.1 %shard_map.83 = (bf16[8,4096]{1,0:T(8,128)(2,1)}, bf16[256,256]{1,0:T(8,128)(2,1)}) custom-call(bf16[16,8,4096]{2,1,0:T(8,128)(2,1)} %all-to-all-done.3.query_parts, bf16[256,256]{1,0:T(8,128)(2,1)S(1)} %get-tuple-element.27.refs_0_, bf16[256,256]{1,0:T(8,128)(2,1)S(1)} %collective-permute-done.6.refs_1_, ...), custom_call_target="tpu_custom_call" | custom-call | tf_op jit(solution)/shard_map/pallas_call | solution.py:252
  (1 shorter events, 0.0 us)
Async XLA Ops:
  3.5 25.8 %copy-start.3 = (f32[1,256,256]{2,1,0:T(8,128)S(1)}, f32[1,256,256]{2,1,0:T(8,128)}, u32[]{:S(2)}) copy-start(f32[1,256,256]{2,1,0:T(8,128)} %param.7) | copy-start | bytes 786436
  3.5 19.2 %all-to-all-start = ((bf16[4,8,4224]{2,1,0:T(8,128)(2,1)}), bf16[4,8,4224]{2,1,0:T(8,128)(2,1)S(1)}, u32[]{:S(2)}, u32[]{:S(2)}) async-start(bf16[4,8,4224]{2,1,0:T(8,128)(2,1)} %broadcast_in_dim.8), calls=%async_computation | async-start | bytes 540672 | tf_op jit(solution)/shard_map/all_to_all | solution.py:43
  14.5 28.3 %collective-permute-start = (bf16[256,4096]{1,0:T(8,128)(2,1)}, bf16[256,4096]{1,0:T(8,128)(2,1)}, u32[]{:S(2)}, u32[]{:S(2)}) collective-permute-start(bf16[256,4096]{1,0:T(8,128)(2,1)} %passages.3), channel_id=1, source_target_pairs={{0,16},{16,0},{1,17},{17,1},{2,18},{18,2},{3,19},{19,3},{4,20},{20... | collective-permute-start | bytes 6291464 | tf_op jit(solution)/shard_map/ppermute | solution.py:28
  23.8 19.0 %all-to-all-start.1 = ((bf16[4,32,4224]{2,1,0:T(8,128)(2,1)}), bf16[4,32,4224]{2,1,0:T(8,128)(2,1)S(1)}, u32[]{:S(2)}, u32[]{:S(2)}) async-start(bf16[4,32,4224]{2,1,0:T(8,128)(2,1)} %broadcast_in_dim.19), calls=%async_computation.1 | async-start | bytes 2162688 | tf_op jit(solution)/shard_map/all_to_all | solution.py:43
  29.4 13.4 %copy-start = (bf16[256,4096]{1,0:T(8,128)(2,1)S(1)}, bf16[256,4096]{1,0:T(8,128)(2,1)}, u32[]{:S(2)}) copy-start(bf16[256,4096]{1,0:T(8,128)(2,1)} %passages.3) | copy-start | bytes 6291460
  30.3 5.6 %collective-permute-start.1 = (bf16[3,256,256]{2,1,0:T(8,128)(2,1)}, bf16[3,256,256]{2,1,0:T(8,128)(2,1)}, u32[]{:S(2)}, u32[]{:S(2)}) collective-permute-start(bf16[3,256,256]{2,1,0:T(8,128)(2,1)} %shard_map.76.teacher), channel_id=1, source_target_pairs={{0,16},{16,0},{1,17},{17,1},{2,18},{18,2},{3,19},{19,3},{4,20},{20... | collective-permute-start | bytes 1179656 | tf_op jit(solution)/shard_map/ppermute | solution.py:28
  60.1 13.9 %copy-start.1 = (bf16[192,1024]{1,0:T(8,128)(2,1)}, bf16[192,1024]{1,0:T(8,128)(2,1)S(1)}, u32[]{:S(2)}) copy-start(bf16[192,1024]{1,0:T(8,128)(2,1)S(1)} %get-tuple-element.23.after.refs_0_) | copy-start | bytes 1179652
  60.1 18.4 %collective-permute-start.2 = (bf16[192,1024]{1,0:T(8,128)(2,1)}, bf16[192,1024]{1,0:T(8,128)(2,1)S(1)}, u32[]{:S(2)}, u32[]{:S(2)}) collective-permute-start(bf16[192,1024]{1,0:T(8,128)(2,1)} %get-tuple-element.24), channel_id=1, source_target_pairs={{0,4},{4,8},{8,12},{12,0},{1,5},{5,9},{9,13},{13,1},{2,6},{6,10},{... | collective-permute-start | bytes 1179656 | tf_op jit(solution)/shard_map/ppermute | solution.py:28
  63.2 18.4 %collective-permute-start.3 = (bf16[192,1024]{1,0:T(8,128)(2,1)}, bf16[192,1024]{1,0:T(8,128)(2,1)}, u32[]{:S(2)}, u32[]{:S(2)}) collective-permute-start(bf16[192,1024]{1,0:T(8,128)(2,1)} %get-tuple-element.25), channel_id=1, source_target_pairs={{0,8},{4,12},{8,0},{12,4},{1,9},{5,13},{9,1},{13,5},{2,10},{6,14},... | collective-permute-start | bytes 1179656 | tf_op jit(solution)/shard_map/ppermute | solution.py:28
  67.5 16.4 %collective-permute-start.4 = (bf16[192,1024]{1,0:T(8,128)(2,1)}, bf16[192,1024]{1,0:T(8,128)(2,1)}, u32[]{:S(2)}, u32[]{:S(2)}) collective-permute-start(bf16[192,1024]{1,0:T(8,128)(2,1)} %get-tuple-element.26), channel_id=1, source_target_pairs={{0,12},{4,0},{8,4},{12,8},{1,13},{5,1},{9,5},{13,9},{2,14},{6,2},{... | collective-permute-start | bytes 1179656 | tf_op jit(solution)/shard_map/ppermute | solution.py:28
  73.9 10.0 %copy-start.2 = (bf16[192,1024]{1,0:T(8,128)(2,1)S(1)}, bf16[192,1024]{1,0:T(8,128)(2,1)}, u32[]{:S(2)}) copy-start(bf16[192,1024]{1,0:T(8,128)(2,1)} %copy-done.1) | copy-start | bytes 1179652
  73.9 40.8 %all-to-all-start.3 = ((bf16[16,8,4096]{2,1,0:T(8,128)(2,1)}), bf16[16,8,4096]{2,1,0:T(8,128)(2,1)}, u32[]{:S(2)}, u32[]{:S(2)}) async-start(bf16[16,8,4096]{2,1,0:T(8,128)(2,1)} %bitcast.8), calls=%async_computation.3 | async-start | bytes 2097152 | tf_op jit(solution)/shard_map/all_to_all | solution.py:231
  85.7 5.8 %collective-permute-start.5 = (bf16[256,1024]{1,0:T(8,128)(2,1)S(1)}, bf16[256,1024]{1,0:T(8,128)(2,1)S(1)}, u32[]{:S(2)}, u32[]{:S(2)}) collective-permute-start(bf16[256,1024]{1,0:T(8,128)(2,1)S(1)} %shard_map.81), channel_id=1, source_target_pairs={{0,16},{16,0},{1,17},{17,1},{2,18},{18,2},{3,19},{19,3},{4,20},{20... | collective-permute-start | bytes 1572872 | tf_op jit(solution)/shard_map/ppermute | solution.py:28
  92.2 15.4 %collective-permute-start.6 = (bf16[256,256]{1,0:T(8,128)(2,1)S(1)}, bf16[256,256]{1,0:T(8,128)(2,1)S(1)}, u32[]{:S(2)}, u32[]{:S(2)}) collective-permute-start(bf16[256,256]{1,0:T(8,128)(2,1)S(1)} %get-tuple-element.28), channel_id=1, source_target_pairs={{0,1},{1,2},{2,3},{3,0},{4,5},{5,6},{6,7},{7,4},{8,9},{9,10},{10,1... | collective-permute-start | bytes 393224 | tf_op jit(solution)/shard_map/ppermute | solution.py:28
  96.4 12.8 %collective-permute-start.7 = (bf16[256,256]{1,0:T(8,128)(2,1)S(1)}, bf16[256,256]{1,0:T(8,128)(2,1)S(1)}, u32[]{:S(2)}, u32[]{:S(2)}) collective-permute-start(bf16[256,256]{1,0:T(8,128)(2,1)S(1)} %get-tuple-element.29), channel_id=1, source_target_pairs={{0,2},{1,3},{2,0},{3,1},{4,6},{5,7},{6,4},{7,5},{8,10},{9,11},{10,... | collective-permute-start | bytes 393224 | tf_op jit(solution)/shard_map/ppermute | solution.py:28
  102.0 12.7 %collective-permute-start.8 = (bf16[256,256]{1,0:T(8,128)(2,1)S(1)}, bf16[256,256]{1,0:T(8,128)(2,1)S(1)}, u32[]{:S(2)}, u32[]{:S(2)}) collective-permute-start(bf16[256,256]{1,0:T(8,128)(2,1)S(1)} %get-tuple-element.30), channel_id=1, source_target_pairs={{0,3},{1,0},{2,1},{3,2},{4,7},{5,4},{6,5},{7,6},{8,11},{9,8},{10,9... | collective-permute-start | bytes 393224 | tf_op jit(solution)/shard_map/ppermute | solution.py:28

commit v12 on v10

--- a/solution.py
+++ b/solution.py
@@ -86,11 +86,25 @@
     stats[...] = jnp.broadcast_to(whole[None], stats.shape)
 
 
-def grad_kernel(places, query, logits, positives, stats, rows_first, losses, *packed):
-    rows, width = query.shape[0], packed[0].shape[1]
-    for d, out in enumerate(packed):
-        out[:rows] = query[:, pl.ds(pl.multiple_of(lax.rem(places[2] + d, len(packed)) * width, width), width)]
-    tall = packed[0].shape[0] - rows
+def slice_kernel(places, query, out):
+    width = out.shape[1]
+    count = (query.shape[1] - LANES) // width
+    out[...] = query[:, pl.ds(pl.multiple_of(lax.rem(places[2] + count // 2, count) * width, width), width)]
+
+
+def pack_kernel(places, query, grads, after, *outs):
+    del after
+    rows = query.shape[0]
+    tall, width = outs[len(outs) // 2].shape
+    for d, out in enumerate(outs):
+        if d != len(outs) // 2:
+            out[:rows] = query[:, pl.ds(pl.multiple_of(lax.rem(places[2] + d, len(outs)) * width, width), width)]
+        for k in range(width // rows):
+            out[out.shape[0] - tall :, k * rows : (k + 1) * rows] = grads[k * tall : (k + 1) * tall]
+
+
+def grad_kernel(places, logits, positives, stats, after, rows_first, grads, losses):
+    del after
     tops_s, tops_t, sums_s, sums_t, cross, hit = (stats[:, i, :] for i in range(6))
     top_s, top_t = jnp.max(tops_s, axis=0, keepdims=True), jnp.max(tops_t, axis=0, keepdims=True)
     lower_s, lower_t = tops_s - top_s, tops_t - top_t
@@ -111,42 +125,37 @@
             - jnp.where(hot, inv_temp, 0.0)
         )
         rows_first[half] = values.T.astype(bf16)
-        values = values.astype(bf16)
-        steps = block_rows // tall
-        for k in range(steps):
-            lane = (half * steps + k) * rows
-            for out in packed:
-                out[rows:, lane : lane + rows] = values[k * tall : (k + 1) * tall]
-
-
-def query_kernel(grads, passages, passages_other, after, out):
-    del after
+        grads[half * block_rows : (half + 1) * block_rows] = values.astype(bf16)
+
+
+def query_kernel(grads, passages, passages_other, out):
     total = jnp.dot(grads[0], passages[...], preferred_element_type=f32)
     total += jnp.dot(grads[1], passages_other[...], preferred_element_type=f32)
     out[...] = total.astype(bf16)
 
 
-def products(packed, half, block_rows, rows):
-    tall = packed[0].shape[0] - rows
+def products(packed, columns, half, block_rows, rows):
+    tall = packed[len(packed) // 2].shape[0]
     total = 0.0
-    for ref in packed:
+    for d, ref in enumerate(packed):
+        begin = ref.shape[0] - tall
         steps = block_rows // tall
         grads = jnp.concatenate(
-            [ref[rows:, k * rows : (k + 1) * rows] for k in range(half * steps, (half + 1) * steps)], axis=0
+            [ref[begin:, k * rows : (k + 1) * rows] for k in range(half * steps, (half + 1) * steps)], axis=0
         )
-        total += jnp.dot(grads, ref[:rows], preferred_element_type=f32)
+        total += jnp.dot(grads, ref[:rows] if begin else columns[...], preferred_element_type=f32)
     return total
 
 
 def other_kernel(rows, *refs):
-    out = refs[-1]
-    out[...] = products(refs[:-1], 1, out.shape[0], rows).astype(bf16)
+    *packed, columns, out = refs
+    out[...] = products(packed, columns, 1, out.shape[0], rows).astype(bf16)
 
 
 def own_kernel(groups, rows, places, *refs):
-    packed, back, outs, total = refs[:groups], refs[groups], refs[groups + 1 : -1], refs[-1]
+    packed, columns, back, outs, total = refs[:groups], refs[groups], refs[groups + 1], refs[groups + 2 : -1], refs[-1]
     width = outs[0].shape[1]
-    total[...] = (products(packed, 0, back.shape[0], rows) + back[...].astype(f32)).astype(bf16)
+    total[...] = (products(packed, columns, 0, back.shape[0], rows) + back[...].astype(f32)).astype(bf16)
     for d, out in enumerate(outs):
         out[...] = total[:, pl.ds(pl.multiple_of(lax.rem(places[3] + d, len(outs)) * width, width), width)]
 
@@ -197,47 +206,64 @@
         out_specs=(VMEM,) * 3,
         compiler_params=PARAMS,
     )(places, query, passages, passages_other, table, table_other)
+    width = depth // x_size
+    columns = pl.pallas_call(
+        slice_kernel,
+        out_shape=jax.ShapeDtypeStruct((rows, width), bf16),
+        in_specs=[SMEM, VMEM],
+        out_specs=VMEM,
+        compiler_params=PARAMS,
+    )(places, query)
+    columns = shift(columns, "x", x_size // 2)
     stats = lax.all_to_all(stats, CHIPS, 0, 0, tiled=True)
-    width = depth // x_size
-    rows_first, losses, *packed = pl.pallas_call(
+    rows_first, grads, losses = pl.pallas_call(
         grad_kernel,
         out_shape=(
             jax.ShapeDtypeStruct((CORES, rows, block_rows), bf16),
+            jax.ShapeDtypeStruct((wide, rows), bf16),
             jax.ShapeDtypeStruct((1, rows), f32),
-        )
-        + (jax.ShapeDtypeStruct((rows + wide * rows // width, width), bf16),) * x_size,
-        in_specs=[SMEM] + [VMEM] * 4,
-        out_specs=(VMEM,) * (2 + x_size),
-        compiler_params=PARAMS,
-    )(places, query, logits, positive, stats)
+        ),
+        in_specs=[SMEM] + [VMEM] * 3 + [ANY],
+        out_specs=(VMEM,) * 3,
+        compiler_params=PARAMS,
+    )(places, logits, positive, stats, columns)
     loss = lax.dynamic_slice_in_dim(losses[0], chip * own_rows, own_rows)
 
-    width = depth // x_size
     query_part = pl.pallas_call(
         query_kernel,
         out_shape=jax.ShapeDtypeStruct((rows, depth), bf16),
-        in_specs=[VMEM] * 3 + [ANY],
-        out_specs=VMEM,
-        compiler_params=PARAMS,
-    )(rows_first, passages, passages_other, packed[0])
+        in_specs=[VMEM] * 3,
+        out_specs=VMEM,
+        compiler_params=PARAMS,
+    )(rows_first, passages, passages_other)
     query_parts = lax.all_to_all(query_part.reshape(chips, own_rows, depth), CHIPS, 0, 0, tiled=True)
+
+    tall = wide * rows // width
+    packed = pl.pallas_call(
+        pack_kernel,
+        out_shape=tuple(
+            jax.ShapeDtypeStruct((tall if d == x_size // 2 else rows + tall, width), bf16) for d in range(x_size)
+        ),
+        in_specs=[SMEM, VMEM, VMEM, ANY],
+        out_specs=(VMEM,) * x_size,
+        compiler_params=PARAMS,
+    )(places, query, grads, query_part)
     packed = shifts(packed, "x")
     part_other = pl.pallas_call(
         functools.partial(other_kernel, rows),
         out_shape=jax.ShapeDtypeStruct((block_rows, width), bf16),
-        in_specs=[VMEM] * x_size,
-        out_specs=VMEM,
-        compiler_params=PARAMS,
-        cost_estimate=pl.CostEstimate(flops=10**11, bytes_accessed=2**21, transcendentals=0),
-    )(*packed)
+        in_specs=[VMEM] * (x_size + 1),
+        out_specs=VMEM,
+        compiler_params=PARAMS,
+    )(*packed, columns)
     parts = pl.pallas_call(
         functools.partial(own_kernel, x_size, rows),
         out_shape=(jax.ShapeDtypeStruct((block_rows, width // yh_size), bf16),) * yh_size,
-        in_specs=[SMEM] + [VMEM] * (x_size + 1),
+        in_specs=[SMEM] + [VMEM] * (x_size + 2),
         out_specs=(VMEM,) * yh_size,
         scratch_shapes=[pltpu.VMEM((block_rows, width), bf16)],
         compiler_params=PARAMS,
-    )(places, *packed, shift(part_other, "core", 1))
+    )(places, *packed, columns, shift(part_other, "core", 1))
     parts = shifts(parts, "yh")
     query_total, passage_total = pl.pallas_call(
         sum_kernel,

time: 117 us -> 123 us (1.051)
  starting transfers between devices: 48.9 us -> 53.1 us
  waiting for transfers between devices: 35.4 us -> 36.7 us
    ppermute x9 -> x10, starting transfers between devices: 33.1 us -> 37.3 us  [shift(): lax.ppermute(value, axis, [(i, (i + by) % size) for i in range(size)])]
    all_to_all x1, waiting for transfers between devices: 18.3 us -> 20.3 us  [per_device(): lax.all_to_all(jnp.broadcast_to(sent[None], (chips,) + sent.shape), CHIPS...]
    pallas_call x0 -> x2, Pallas kernels: none -> 1.26 us  [the longest x1 0.7 us: per_device(): pl.pallas_call(pack_kernel, out_shape=tuple((jax.ShapeDtypeStruct((tall i...]
    ppermute x9 -> x10, waiting for transfers between devices: 17 us -> 16.5 us  [shift(): lax.ppermute(value, axis, [(i, (i + by) % size) for i in range(size)])]
  transfers between devices with their start and end apart: 11 -> 12, of which waited for: 7 -> 5; matrix products, arithmetic and copies ran while one was open for 1% -> 1% of each run, Pallas kernels for 5% -> 6%
where the time goes in v12:
time: 123 us; the launch traced here: 122 us
  starting transfers between devices  53.1 us (43%)
  waiting for transfers between devices  36.7 us (30%)
  blocking collectives  14.5 us (12%)
  Pallas kernels  12.6 us (10%)
  other arithmetic  2.41 us (2%)
  local copies, waits for them, and re-layouts  1.67 us (1%)
    ppermute x10, starting transfers between devices, shift(): lax.ppermute(value, axis, [(i, (i + by) % size) for i in range(size)])  37.3 us
    all_to_all x1, waiting for transfers between devices, per_device(): lax.all_to_all(jnp.broadcast_to(sent[None], (chips,) + sent.shape), CHIPS...  20.3 us
    ppermute x10, waiting for transfers between devices, shift(): lax.ppermute(value, axis, [(i, (i + by) % size) for i in range(size)])  16.5 us
    all_to_all x1, blocking collectives, per_device(): stats = lax.all_to_all(stats, CHIPS, 0, 0, tiled=True)  14.5 us
    all_to_all x1, starting transfers between devices, per_device(): lax.all_to_all(jnp.broadcast_to(sent[None], (chips,) + sent.shape), CHIPS...  12 us
    all_to_all x1, starting transfers between devices, per_device(): lax.all_to_all(query_part.reshape(chips, own_rows, depth), CHIPS, 0, 0, t...  3.78 us
    pallas_call x1, Pallas kernels, per_device(): pl.pallas_call(score_kernel, out_shape=(jax.ShapeDtypeStruct((2 * CORES,...  3.47 us
    pallas_call x1, Pallas kernels, per_device(): pl.pallas_call(query_kernel, out_shape=jax.ShapeDtypeStruct((rows, depth)...  3.35 us
  transfers between devices with their start and end apart: 12, of which 5 were waited for; matrix products, arithmetic and copies ran while one was open for 1% of the time, Pallas kernels for 6%

profile of v12, /device:TPU:1, one launch (start us, length us, event | category | flops | bytes accessed | tf_op | source)
XLA Modules:
  0.0 121.8 jit_solution(6585676712526719985)
XLA Ops:
  0.6 0.0 copy-start
  0.6 0.0 copy-start.3
  0.7 0.8 and_convert_fusion
  1.5 0.7 convert.11
  2.1 0.8 pad_maximum_fusion
  3.0 1.1 broadcast_in_dim.4
  4.1 12.0 %all-to-all-start = ((bf16[16,8,4224]{2,1,0:T(8,128)(2,1)}), bf16[16,8,4224]{2,1,0:T(8,128)(2,1)S(1)}, u32[]{:S(2)}, u32[]{:S(2)}) async-start(bf16[16,8,4224]{2,1,0:T(8,128)(2,1)} %broadcast_in_dim.4), calls=%async_computation | async-start | bytes 2162688 | tf_op jit(solution)/shard_map/all_to_all | solution.py:185
  16.0 0.0 copy-done
  16.1 2.9 %collective-permute-start = (bf16[256,4096]{1,0:T(8,128)(2,1)S(1)}, bf16[256,4096]{1,0:T(8,128)(2,1)}, u32[]{:S(2)}, u32[]{:S(2)}) collective-permute-start(bf16[256,4096]{1,0:T(8,128)(2,1)S(1)} %copy-done), channel_id=1, source_target_pairs={{0,16},{16,0},{1,17},{17,1},{2,18},{18,2},{3,19},{19,3},{4,20},{20... | collective-permute-start | bytes 6291464 | tf_op jit(solution)/shard_map/ppermute | solution.py:27
  18.9 0.0 copy-done.3
  18.9 0.9 shard_map.76.teacher
  19.8 1.9 %collective-permute-start.1 = (bf16[3,256,256]{2,1,0:T(8,128)(2,1)}, bf16[3,256,256]{2,1,0:T(8,128)(2,1)}, u32[]{:S(2)}, u32[]{:S(2)}) collective-permute-start(bf16[3,256,256]{2,1,0:T(8,128)(2,1)} %shard_map.76.teacher), channel_id=1, source_target_pairs={{0,16},{16,0},{1,17},{17,1},{2,18},{18,2},{3,19},{19,3},{4,20},{20... | collective-permute-start | bytes 1179656 | tf_op jit(solution)/shard_map/ppermute | solution.py:27
  21.7 0.1 pad_add_fusion.places
  21.8 20.3 %all-to-all-done = bf16[16,8,4224]{2,1,0:T(8,128)(2,1)S(1)} async-done(((bf16[16,8,4224]{2,1,0:T(8,128)(2,1)}), bf16[16,8,4224]{2,1,0:T(8,128)(2,1)S(1)}, u32[]{:S(2)}, u32[]{:S(2)}) %all-to-all-start) | async-done | bytes 1081376 | tf_op jit(solution)/shard_map/all_to_all | solution.py:185
  42.1 0.6 shard_map.78
  42.7 4.7 %collective-permute-start.2 = (bf16[128,1024]{1,0:T(8,128)(2,1)S(1)}, bf16[128,1024]{1,0:T(8,128)(2,1)S(1)}, u32[]{:S(2)}, u32[]{:S(2)}) collective-permute-start(bf16[128,1024]{1,0:T(8,128)(2,1)S(1)} %shard_map.78), channel_id=1, source_target_pairs={{0,8},{4,12},{8,0},{12,4},{1,9},{5,13},{9,1},{13,5},{2,10},{6,14},... | collective-permute-start | bytes 786440 | tf_op jit(solution)/shard_map/ppermute | solution.py:27
  47.3 0.0 collective-permute-done.1.teacher_other
  47.3 0.0 collective-permute-done.passages_other
  47.3 3.5 %shard_map.77 = (f32[4,256,128]{2,1,0:T(8,128)S(1)}, s32[1,128]{1,0:T(1,128)S(1)}, f32[16,8,128]{2,1,0:T(8,128)S(1)}) custom-call(s32[4]{0:T(128)S(1)} %pad_add_fusion.places, bf16[128,4224]{1,0:T(8,128)(2,1)S(1)} %bitcast.10, bf16[256,4096]{1,0:T(8,128)(2,1)S(1)} %copy-done, bf16[256,4096]{1,0:T(8,128)(2,1)} %collective-permute-done.passages_other, ...), custom_call_target="tpu_custom_call" | custom-call | tf_op jit(solution)/shard_map/pallas_call | solution.py:198
  50.8 14.5 %all_to_all.15.stats = f32[16,8,128]{2,1,0:T(8,128)S(1)} all-to-all(f32[16,8,128]{2,1,0:T(8,128)S(1)} %get-tuple-element.21), channel_id=1, replica_groups=mesh['yl'=2,'z'=8,'core'=2,'x'=4,'yh'=4] {'yl','z'}, dimensions={0} | all-to-all | bytes 131072 | tf_op jit(solution)/shard_map/all_to_all | solution.py:218
  65.3 0.0 collective-permute-done.2.after.refs_4_
  65.3 0.8 shard_map.79
  66.1 0.0 copy-start.1
  66.1 3.3 %shard_map.80.after = bf16[128,4096]{1,0:T(8,128)(2,1)} custom-call(bf16[2,128,256]{2,1,0:T(8,128)(2,1)S(1)} %get-tuple-element.23.grads, bf16[256,4096]{1,0:T(8,128)(2,1)S(1)} %copy-done, bf16[256,4096]{1,0:T(8,128)(2,1)} %collective-permute-done.passages_other), custom_call_target="tpu_custom_call" | custom-call | tf_op jit(solution)/shard_map/pallas_call | solution.py:232
  69.4 0.0 copy-done.1
  69.4 0.0 copy-start.2
  69.4 3.8 %all-to-all-start.2 = ((bf16[16,8,4096]{2,1,0:T(8,128)(2,1)}), bf16[16,8,4096]{2,1,0:T(8,128)(2,1)S(1)}, u32[]{:S(2)}, u32[]{:S(2)}) async-start(bf16[16,8,4096]{2,1,0:T(8,128)(2,1)} %bitcast.7), calls=%async_computation.2 | async-start | bytes 2097152 | tf_op jit(solution)/shard_map/all_to_all | solution.py:239
  73.2 0.0 copy-done.2
  73.2 0.7 shard_map.81
  74.0 2.2 %collective-permute-start.3 = (bf16[192,1024]{1,0:T(8,128)(2,1)S(1)}, bf16[192,1024]{1,0:T(8,128)(2,1)S(1)}, u32[]{:S(2)}, u32[]{:S(2)}) collective-permute-start(bf16[192,1024]{1,0:T(8,128)(2,1)S(1)} %get-tuple-element.26), channel_id=1, source_target_pairs={{0,4},{4,8},{8,12},{12,0},{1,5},{5,9},{9,13},{13,1},{2,6},{6,10},{... | collective-permute-start | bytes 1179656 | tf_op jit(solution)/shard_map/ppermute | solution.py:27
  76.2 4.3 %collective-permute-start.5 = (bf16[192,1024]{1,0:T(8,128)(2,1)S(1)}, bf16[192,1024]{1,0:T(8,128)(2,1)S(1)}, u32[]{:S(2)}, u32[]{:S(2)}) collective-permute-start(bf16[192,1024]{1,0:T(8,128)(2,1)S(1)} %get-tuple-element.28), channel_id=1, source_target_pairs={{0,12},{4,0},{8,4},{12,8},{1,13},{5,1},{9,5},{13,9},{2,14},{6,2},{... | collective-permute-start | bytes 1179656 | tf_op jit(solution)/shard_map/ppermute | solution.py:27
  80.5 1.9 %collective-permute-start.4 = (bf16[64,1024]{1,0:T(8,128)(2,1)S(1)}, bf16[64,1024]{1,0:T(8,128)(2,1)S(1)}, u32[]{:S(2)}, u32[]{:S(2)}) collective-permute-start(bf16[64,1024]{1,0:T(8,128)(2,1)S(1)} %get-tuple-element.27), channel_id=1, source_target_pairs={{0,8},{4,12},{8,0},{12,4},{1,9},{5,13},{9,1},{13,5},{2,10},{6,14},... | collective-permute-start | bytes 393224 | tf_op jit(solution)/shard_map/ppermute | solution.py:27
  82.4 6.6 %collective-permute-done.4.refs_2_ = bf16[64,1024]{1,0:T(8,128)(2,1)S(1)} collective-permute-done((bf16[64,1024]{1,0:T(8,128)(2,1)S(1)}, bf16[64,1024]{1,0:T(8,128)(2,1)S(1)}, u32[]{:S(2)}, u32[]{:S(2)}) %collective-permute-start.4) | collective-permute-done | bytes 131104 | tf_op jit(solution)/shard_map/ppermute | solution.py:27
  89.0 0.0 collective-permute-done.3.refs_1_
  89.0 0.0 collective-permute-done.5.refs_3_
  89.0 0.7 shard_map.82
  89.7 5.5 %collective-permute-start.6 = (bf16[256,1024]{1,0:T(8,128)(2,1)S(1)}, bf16[256,1024]{1,0:T(8,128)(2,1)S(1)}, u32[]{:S(2)}, u32[]{:S(2)}) collective-permute-start(bf16[256,1024]{1,0:T(8,128)(2,1)S(1)} %shard_map.82), channel_id=1, source_target_pairs={{0,16},{16,0},{1,17},{17,1},{2,18},{18,2},{3,19},{19,3},{4,20},{20... | collective-permute-start | bytes 1572872 | tf_op jit(solution)/shard_map/ppermute | solution.py:27
  95.2 1.5 %collective-permute-done.6.refs_5_ = bf16[256,1024]{1,0:T(8,128)(2,1)S(1)} collective-permute-done((bf16[256,1024]{1,0:T(8,128)(2,1)S(1)}, bf16[256,1024]{1,0:T(8,128)(2,1)S(1)}, u32[]{:S(2)}, u32[]{:S(2)}) %collective-permute-start.6) | collective-permute-done | bytes 524320 | tf_op jit(solution)/shard_map/ppermute | solution.py:27
  96.7 1.3 %shard_map.83 = (bf16[256,256]{1,0:T(8,128)(2,1)S(1)}, bf16[256,256]{1,0:T(8,128)(2,1)S(1)}, bf16[256,256]{1,0:T(8,128)(2,1)S(1)}, bf16[256,256]{1,0:T(8,128)(2,1)S(1)}) custom-call(s32[4]{0:T(128)S(1)} %pad_add_fusion.places, bf16[192,1024]{1,0:T(8,128)(2,1)S(1)} %get-tuple-element.25.refs_0_, bf16[192,1024]{1,0:T(8,128)(2,1)S(1)} %collective-permute-done.3.refs_1_, ...), custom_call_target="tpu_custom_call" | custom-call | tf_op jit(solution)/shard_map/pallas_call | solution.py:259
  98.1 4.2 %collective-permute-start.7 = (bf16[256,256]{1,0:T(8,128)(2,1)S(1)}, bf16[256,256]{1,0:T(8,128)(2,1)S(1)}, u32[]{:S(2)}, u32[]{:S(2)}) collective-permute-start(bf16[256,256]{1,0:T(8,128)(2,1)S(1)} %get-tuple-element.30), channel_id=1, source_target_pairs={{0,1},{1,2},{2,3},{3,0},{4,5},{5,6},{6,7},{7,4},{8,9},{9,10},{10,1... | collective-permute-start | bytes 393224 | tf_op jit(solution)/shard_map/ppermute | solution.py:27
  102.3 4.8 %collective-permute-start.8 = (bf16[256,256]{1,0:T(8,128)(2,1)S(1)}, bf16[256,256]{1,0:T(8,128)(2,1)S(1)}, u32[]{:S(2)}, u32[]{:S(2)}) collective-permute-start(bf16[256,256]{1,0:T(8,128)(2,1)S(1)} %get-tuple-element.31), channel_id=1, source_target_pairs={{0,2},{1,3},{2,0},{3,1},{4,6},{5,7},{6,4},{7,5},{8,10},{9,11},{10,... | collective-permute-start | bytes 393224 | tf_op jit(solution)/shard_map/ppermute | solution.py:27
  107.0 5.0 %collective-permute-start.9 = (bf16[256,256]{1,0:T(8,128)(2,1)S(1)}, bf16[256,256]{1,0:T(8,128)(2,1)S(1)}, u32[]{:S(2)}, u32[]{:S(2)}) collective-permute-start(bf16[256,256]{1,0:T(8,128)(2,1)S(1)} %get-tuple-element.32), channel_id=1, source_target_pairs={{0,3},{1,0},{2,1},{3,2},{4,7},{5,4},{6,5},{7,6},{8,11},{9,8},{10,9... | collective-permute-start | bytes 393224 | tf_op jit(solution)/shard_map/ppermute | solution.py:27
  112.0 0.6 constant_dynamic-slice_fusion
  112.6 0.0 collective-permute-done.7.refs_1_
  112.6 3.3 %collective-permute-done.8.refs_2_ = bf16[256,256]{1,0:T(8,128)(2,1)S(1)} collective-permute-done((bf16[256,256]{1,0:T(8,128)(2,1)S(1)}, bf16[256,256]{1,0:T(8,128)(2,1)S(1)}, u32[]{:S(2)}, u32[]{:S(2)}) %collective-permute-start.8) | collective-permute-done | bytes 131104 | tf_op jit(solution)/shard_map/ppermute | solution.py:27
  115.9 5.0 %collective-permute-done.9.refs_3_ = bf16[256,256]{1,0:T(8,128)(2,1)S(1)} collective-permute-done((bf16[256,256]{1,0:T(8,128)(2,1)S(1)}, bf16[256,256]{1,0:T(8,128)(2,1)S(1)}, u32[]{:S(2)}, u32[]{:S(2)}) %collective-permute-start.9) | collective-permute-done | bytes 131104 | tf_op jit(solution)/shard_map/ppermute | solution.py:27
  121.0 0.0 all-to-all-done.2.query_parts
  121.0 0.9 shard_map.84
  (1 shorter events, 0.0 us)
Async XLA Ops:
  0.6 15.4 %copy-start = (bf16[256,4096]{1,0:T(8,128)(2,1)S(1)}, bf16[256,4096]{1,0:T(8,128)(2,1)}, u32[]{:S(2)}) copy-start(bf16[256,4096]{1,0:T(8,128)(2,1)} %passages.3) | copy-start | bytes 6291460
  0.6 18.3 %copy-start.3 = (f32[1,256,256]{2,1,0:T(8,128)S(1)}, f32[1,256,256]{2,1,0:T(8,128)}, u32[]{:S(2)}) copy-start(f32[1,256,256]{2,1,0:T(8,128)} %param.7) | copy-start | bytes 786436
  4.1 38.0 %all-to-all-start = ((bf16[16,8,4224]{2,1,0:T(8,128)(2,1)}), bf16[16,8,4224]{2,1,0:T(8,128)(2,1)S(1)}, u32[]{:S(2)}, u32[]{:S(2)}) async-start(bf16[16,8,4224]{2,1,0:T(8,128)(2,1)} %broadcast_in_dim.4), calls=%async_computation | async-start | bytes 2162688 | tf_op jit(solution)/shard_map/all_to_all | solution.py:185
  16.1 31.3 %collective-permute-start = (bf16[256,4096]{1,0:T(8,128)(2,1)S(1)}, bf16[256,4096]{1,0:T(8,128)(2,1)}, u32[]{:S(2)}, u32[]{:S(2)}) collective-permute-start(bf16[256,4096]{1,0:T(8,128)(2,1)S(1)} %copy-done), channel_id=1, source_target_pairs={{0,16},{16,0},{1,17},{17,1},{2,18},{18,2},{3,19},{19,3},{4,20},{20... | collective-permute-start | bytes 6291464 | tf_op jit(solution)/shard_map/ppermute | solution.py:27
  19.8 27.5 %collective-permute-start.1 = (bf16[3,256,256]{2,1,0:T(8,128)(2,1)}, bf16[3,256,256]{2,1,0:T(8,128)(2,1)}, u32[]{:S(2)}, u32[]{:S(2)}) collective-permute-start(bf16[3,256,256]{2,1,0:T(8,128)(2,1)} %shard_map.76.teacher), channel_id=1, source_target_pairs={{0,16},{16,0},{1,17},{17,1},{2,18},{18,2},{3,19},{19,3},{4,20},{20... | collective-permute-start | bytes 1179656 | tf_op jit(solution)/shard_map/ppermute | solution.py:27
  42.7 22.6 %collective-permute-start.2 = (bf16[128,1024]{1,0:T(8,128)(2,1)S(1)}, bf16[128,1024]{1,0:T(8,128)(2,1)S(1)}, u32[]{:S(2)}, u32[]{:S(2)}) collective-permute-start(bf16[128,1024]{1,0:T(8,128)(2,1)S(1)} %shard_map.78), channel_id=1, source_target_pairs={{0,8},{4,12},{8,0},{12,4},{1,9},{5,13},{9,1},{13,5},{2,10},{6,14},... | collective-permute-start | bytes 786440 | tf_op jit(solution)/shard_map/ppermute | solution.py:27
  66.1 3.4 %copy-start.1 = (bf16[512,128]{1,0:T(8,128)(2,1)}, bf16[512,128]{1,0:T(8,128)(2,1)S(1)}, u32[]{:S(2)}) copy-start(bf16[512,128]{1,0:T(8,128)(2,1)S(1)} %get-tuple-element.24.grads) | copy-start | bytes 393220
  69.4 3.8 %copy-start.2 = (bf16[512,128]{1,0:T(8,128)(2,1)S(1)}, bf16[512,128]{1,0:T(8,128)(2,1)}, u32[]{:S(2)}) copy-start(bf16[512,128]{1,0:T(8,128)(2,1)} %copy-done.1) | copy-start | bytes 393220
  69.4 51.5 %all-to-all-start.2 = ((bf16[16,8,4096]{2,1,0:T(8,128)(2,1)}), bf16[16,8,4096]{2,1,0:T(8,128)(2,1)S(1)}, u32[]{:S(2)}, u32[]{:S(2)}) async-start(bf16[16,8,4096]{2,1,0:T(8,128)(2,1)} %bitcast.7), calls=%async_computation.2 | async-start | bytes 2097152 | tf_op jit(solution)/shard_map/all_to_all | solution.py:239
  74.0 15.0 %collective-permute-start.3 = (bf16[192,1024]{1,0:T(8,128)(2,1)S(1)}, bf16[192,1024]{1,0:T(8,128)(2,1)S(1)}, u32[]{:S(2)}, u32[]{:S(2)}) collective-permute-start(bf16[192,1024]{1,0:T(8,128)(2,1)S(1)} %get-tuple-element.26), channel_id=1, source_target_pairs={{0,4},{4,8},{8,12},{12,0},{1,5},{5,9},{9,13},{13,1},{2,6},{6,10},{... | collective-permute-start | bytes 1179656 | tf_op jit(solution)/shard_map/ppermute | solution.py:27
  76.2 12.8 %collective-permute-start.5 = (bf16[192,1024]{1,0:T(8,128)(2,1)S(1)}, bf16[192,1024]{1,0:T(8,128)(2,1)S(1)}, u32[]{:S(2)}, u32[]{:S(2)}) collective-permute-start(bf16[192,1024]{1,0:T(8,128)(2,1)S(1)} %get-tuple-element.28), channel_id=1, source_target_pairs={{0,12},{4,0},{8,4},{12,8},{1,13},{5,1},{9,5},{13,9},{2,14},{6,2},{... | collective-permute-start | bytes 1179656 | tf_op jit(solution)/shard_map/ppermute | solution.py:27
  80.5 8.5 %collective-permute-start.4 = (bf16[64,1024]{1,0:T(8,128)(2,1)S(1)}, bf16[64,1024]{1,0:T(8,128)(2,1)S(1)}, u32[]{:S(2)}, u32[]{:S(2)}) collective-permute-start(bf16[64,1024]{1,0:T(8,128)(2,1)S(1)} %get-tuple-element.27), channel_id=1, source_target_pairs={{0,8},{4,12},{8,0},{12,4},{1,9},{5,13},{9,1},{13,5},{2,10},{6,14},... | collective-permute-start | bytes 393224 | tf_op jit(solution)/shard_map/ppermute | solution.py:27
  89.7 7.1 %collective-permute-start.6 = (bf16[256,1024]{1,0:T(8,128)(2,1)S(1)}, bf16[256,1024]{1,0:T(8,128)(2,1)S(1)}, u32[]{:S(2)}, u32[]{:S(2)}) collective-permute-start(bf16[256,1024]{1,0:T(8,128)(2,1)S(1)} %shard_map.82), channel_id=1, source_target_pairs={{0,16},{16,0},{1,17},{17,1},{2,18},{18,2},{3,19},{19,3},{4,20},{20... | collective-permute-start | bytes 1572872 | tf_op jit(solution)/shard_map/ppermute | solution.py:27
  98.1 14.6 %collective-permute-start.7 = (bf16[256,256]{1,0:T(8,128)(2,1)S(1)}, bf16[256,256]{1,0:T(8,128)(2,1)S(1)}, u32[]{:S(2)}, u32[]{:S(2)}) collective-permute-start(bf16[256,256]{1,0:T(8,128)(2,1)S(1)} %get-tuple-element.30), channel_id=1, source_target_pairs={{0,1},{1,2},{2,3},{3,0},{4,5},{5,6},{6,7},{7,4},{8,9},{9,10},{10,1... | collective-permute-start | bytes 393224 | tf_op jit(solution)/shard_map/ppermute | solution.py:27
  102.3 13.7 %collective-permute-start.8 = (bf16[256,256]{1,0:T(8,128)(2,1)S(1)}, bf16[256,256]{1,0:T(8,128)(2,1)S(1)}, u32[]{:S(2)}, u32[]{:S(2)}) collective-permute-start(bf16[256,256]{1,0:T(8,128)(2,1)S(1)} %get-tuple-element.31), channel_id=1, source_target_pairs={{0,2},{1,3},{2,0},{3,1},{4,6},{5,7},{6,4},{7,5},{8,10},{9,11},{10,... | collective-permute-start | bytes 393224 | tf_op jit(solution)/shard_map/ppermute | solution.py:27
  107.0 13.9 %collective-permute-start.9 = (bf16[256,256]{1,0:T(8,128)(2,1)S(1)}, bf16[256,256]{1,0:T(8,128)(2,1)S(1)}, u32[]{:S(2)}, u32[]{:S(2)}) collective-permute-start(bf16[256,256]{1,0:T(8,128)(2,1)S(1)} %get-tuple-element.32), channel_id=1, source_target_pairs={{0,3},{1,0},{2,1},{3,2},{4,7},{5,4},{6,5},{7,6},{8,11},{9,8},{10,9... | collective-permute-start | bytes 393224 | tf_op jit(solution)/shard_map/ppermute | solution.py:27

commit v13 on v10

--- a/solution.py
+++ b/solution.py
@@ -8,11 +8,12 @@
 from jax.sharding import Mesh, PartitionSpec as P
 
 inv_temp = 50.0
-YL, CORES, X = 2, 2, 4
+YL, ZL, CORES, X = 2, 2, 2, 4
 LANES = 128
 STATS = 8
 PIECES = 3
-CHIPS = ("yl", "z")
+NEAR, FAR = ("yl", "zl"), ("zh",)
+CHIPS = NEAR + FAR
 f32, bf16, i32 = jnp.float32, jnp.bfloat16, jnp.int32
 VMEM = pl.BlockSpec(memory_space=pltpu.VMEM)
 ANY = pl.BlockSpec(memory_space=pl.ANY)
@@ -86,11 +87,11 @@
     stats[...] = jnp.broadcast_to(whole[None], stats.shape)
 
 
-def grad_kernel(places, query, logits, positives, stats, rows_first, losses, *packed):
-    rows, width = query.shape[0], packed[0].shape[1]
-    for d, out in enumerate(packed):
-        out[:rows] = query[:, pl.ds(pl.multiple_of(lax.rem(places[2] + d, len(packed)) * width, width), width)]
-    tall = packed[0].shape[0] - rows
+def grad_kernel(places, query, logits, positives, stats, rows_first, losses, packed):
+    rows, width = query.shape[0], packed.shape[2]
+    for x in range(packed.shape[0]):
+        packed[x, :rows] = query[:, x * width : (x + 1) * width]
+    tall = packed.shape[1] - rows
     tops_s, tops_t, sums_s, sums_t, cross, hit = (stats[:, i, :] for i in range(6))
     top_s, top_t = jnp.max(tops_s, axis=0, keepdims=True), jnp.max(tops_t, axis=0, keepdims=True)
     lower_s, lower_t = tops_s - top_s, tops_t - top_t
@@ -115,42 +116,48 @@
         steps = block_rows // tall
         for k in range(steps):
             lane = (half * steps + k) * rows
-            for out in packed:
-                out[rows:, lane : lane + rows] = values[k * tall : (k + 1) * tall]
-
-
-def query_kernel(grads, passages, passages_other, after, out):
-    del after
-    total = jnp.dot(grads[0], passages[...], preferred_element_type=f32)
-    total += jnp.dot(grads[1], passages_other[...], preferred_element_type=f32)
-    out[...] = total.astype(bf16)
+            for x in range(packed.shape[0]):
+                packed[x, rows:, lane : lane + rows] = values[k * tall : (k + 1) * tall]
+
+
+def query_kernel(places, grads, passages, passages_other, total, *outs):
+    result = jnp.dot(grads[0], passages[...], preferred_element_type=f32)
+    result += jnp.dot(grads[1], passages_other[...], preferred_element_type=f32)
+    total[...] = result.astype(bf16).reshape(total.shape)
+    for d, out in enumerate(outs):
+        out[...] = total[places[4] ^ d]
 
 
 def products(packed, half, block_rows, rows):
-    tall = packed[0].shape[0] - rows
+    tall = packed.shape[1] - rows
     total = 0.0
-    for ref in packed:
+    for x in range(packed.shape[0]):
         steps = block_rows // tall
         grads = jnp.concatenate(
-            [ref[rows:, k * rows : (k + 1) * rows] for k in range(half * steps, (half + 1) * steps)], axis=0
+            [packed[x, rows:, k * rows : (k + 1) * rows] for k in range(half * steps, (half + 1) * steps)], axis=0
         )
-        total += jnp.dot(grads, ref[:rows], preferred_element_type=f32)
+        total += jnp.dot(grads, packed[x, :rows], preferred_element_type=f32)
     return total
 
 
-def other_kernel(rows, *refs):
-    out = refs[-1]
-    out[...] = products(refs[:-1], 1, out.shape[0], rows).astype(bf16)
-
-
-def own_kernel(groups, rows, places, *refs):
-    packed, back, outs, total = refs[:groups], refs[groups], refs[groups + 1 : -1], refs[-1]
+def other_kernel(rows, packed, out):
+    out[...] = products(packed, 1, out.shape[0], rows).astype(bf16)
+
+
+def own_kernel(rows, places, packed, back, after, *refs):
+    del after
+    *outs, total = refs
     width = outs[0].shape[1]
     total[...] = (products(packed, 0, back.shape[0], rows) + back[...].astype(f32)).astype(bf16)
     for d, out in enumerate(outs):
         out[...] = total[:, pl.ds(pl.multiple_of(lax.rem(places[3] + d, len(outs)) * width, width), width)]
 
 
+def near_kernel(*refs):
+    *parts, out = refs
+    out[...] = sum(part[...].astype(f32) for part in parts).astype(bf16)
+
+
 def sum_kernel(query_parts, *refs):
     parts, query_total, total = refs[:-2], refs[-2], refs[-1]
     query_total[...] = sum(query_parts[i].astype(f32) for i in range(query_parts.shape[0])).astype(bf16)
@@ -160,13 +167,17 @@
 def per_device(queries, passages, teacher, teacher_rows, positives):
     own_rows, depth = queries.shape[1:]
     block_rows = passages.shape[0]
-    chips = lax.axis_size("yl") * lax.axis_size("z")
+    yl, zh, zl = (lax.axis_index(axis) for axis in ("yl", "zh", "zl"))
+    far_size, zl_size = lax.axis_size("zh"), lax.axis_size("zl")
+    near_size = lax.axis_size("yl") * zl_size
+    chips = near_size * far_size
     x_size, yh_size = lax.axis_size("x"), lax.axis_size("yh")
     rows, wide = chips * own_rows, CORES * block_rows
-    chip = lax.axis_index("yl") * lax.axis_size("z") + lax.axis_index("z")
+    near = yl * zl_size + zl
+    chip, block = near * far_size + zh, (yl * far_size + zh) * zl_size + zl
     core, x, yh = lax.axis_index("core"), lax.axis_index("x"), lax.axis_index("yh")
     places = jnp.stack(
-        [(chip * CORES + core) * block_rows, (chip * CORES + 1 - core) * block_rows, x, yh]
+        [(block * CORES + core) * block_rows, (block * CORES + 1 - core) * block_rows, x, yh, near]
     ).astype(i32)
 
     codes = jnp.concatenate([teacher_rows, positives & 255, lax.shift_right_logical(positives, 8)], axis=0)
@@ -199,45 +210,56 @@
     )(places, query, passages, passages_other, table, table_other)
     stats = lax.all_to_all(stats, CHIPS, 0, 0, tiled=True)
     width = depth // x_size
-    rows_first, losses, *packed = pl.pallas_call(
+    rows_first, losses, packed = pl.pallas_call(
         grad_kernel,
         out_shape=(
             jax.ShapeDtypeStruct((CORES, rows, block_rows), bf16),
             jax.ShapeDtypeStruct((1, rows), f32),
-        )
-        + (jax.ShapeDtypeStruct((rows + wide * rows // width, width), bf16),) * x_size,
+            jax.ShapeDtypeStruct((x_size, rows + wide * rows // width, width), bf16),
+        ),
         in_specs=[SMEM] + [VMEM] * 4,
-        out_specs=(VMEM,) * (2 + x_size),
+        out_specs=(VMEM,) * 3,
         compiler_params=PARAMS,
     )(places, query, logits, positive, stats)
     loss = lax.dynamic_slice_in_dim(losses[0], chip * own_rows, own_rows)
 
     width = depth // x_size
-    query_part = pl.pallas_call(
+    packed = lax.all_to_all(packed, "x", 0, 0, tiled=True)
+    _, *query_parts = pl.pallas_call(
         query_kernel,
-        out_shape=jax.ShapeDtypeStruct((rows, depth), bf16),
-        in_specs=[VMEM] * 3 + [ANY],
-        out_specs=VMEM,
-        compiler_params=PARAMS,
-    )(rows_first, passages, passages_other, packed[0])
-    query_parts = lax.all_to_all(query_part.reshape(chips, own_rows, depth), CHIPS, 0, 0, tiled=True)
-    packed = shifts(packed, "x")
+        out_shape=(jax.ShapeDtypeStruct((near_size, rows // near_size, depth), bf16),)
+        + (jax.ShapeDtypeStruct((rows // near_size, depth), bf16),) * near_size,
+        in_specs=[SMEM] + [VMEM] * 3,
+        out_specs=(VMEM,) * (1 + near_size),
+        compiler_params=PARAMS,
+    )(places, rows_first, passages, passages_other)
+    query_parts = [
+        lax.ppermute(part, NEAR, [(i, i ^ d) for i in range(near_size)]) if d else part
+        for d, part in enumerate(query_parts)
+    ]
     part_other = pl.pallas_call(
         functools.partial(other_kernel, rows),
         out_shape=jax.ShapeDtypeStruct((block_rows, width), bf16),
-        in_specs=[VMEM] * x_size,
+        in_specs=[VMEM],
         out_specs=VMEM,
         compiler_params=PARAMS,
-        cost_estimate=pl.CostEstimate(flops=10**11, bytes_accessed=2**21, transcendentals=0),
-    )(*packed)
+    )(packed)
+    query_part = pl.pallas_call(
+        near_kernel,
+        out_shape=jax.ShapeDtypeStruct((rows // near_size, depth), bf16),
+        in_specs=[VMEM] * near_size,
+        out_specs=VMEM,
+        compiler_params=PARAMS,
+    )(*query_parts)
+    query_parts = lax.all_to_all(query_part.reshape(far_size, own_rows, depth), FAR, 0, 0, tiled=True)
     parts = pl.pallas_call(
-        functools.partial(own_kernel, x_size, rows),
+        functools.partial(own_kernel, rows),
         out_shape=(jax.ShapeDtypeStruct((block_rows, width // yh_size), bf16),) * yh_size,
-        in_specs=[SMEM] + [VMEM] * (x_size + 1),
+        in_specs=[SMEM] + [VMEM] * 2 + [ANY],
         out_specs=(VMEM,) * yh_size,
         scratch_shapes=[pltpu.VMEM((block_rows, width), bf16)],
         compiler_params=PARAMS,
-    )(places, *packed, shift(part_other, "core", 1))
+    )(places, packed, shift(part_other, "core", 1), query_part)
     parts = shifts(parts, "yh")
     query_total, passage_total = pl.pallas_call(
         sum_kernel,
@@ -255,10 +277,10 @@
 def solution(mesh):
     blk, qgroup = mesh.devices.shape
     split = Mesh(
-        mesh.devices.reshape(YL, blk // (YL * CORES), CORES, X, qgroup // X),
-        ("yl", "z", "core", "x", "yh"),
+        mesh.devices.reshape(YL, blk // (YL * ZL * CORES), ZL, CORES, X, qgroup // X),
+        ("yl", "zh", "zl", "core", "x", "yh"),
     )
-    blk, qgroup = ("yl", "z", "core"), ("x", "yh")
+    blk, qgroup = ("yl", "zh", "zl", "core"), ("x", "yh")
     in_specs = (
         P(qgroup, blk, None),
         P(blk, None),

time: 117 us -> 120 us (1.026)
  starting transfers between devices: 48.9 us -> 52.5 us
  waiting for transfers between devices: 35.4 us -> 32.6 us
  Pallas kernels: 12.3 us -> 14.4 us
  local copies, waits for them, and re-layouts: 1.66 us -> 3.34 us
    ppermute x9 -> x6, starting transfers between devices: 33.1 us -> 24.6 us  [shift(): lax.ppermute(value, axis, [(i, (i + by) % size) for i in range(size)])]
    ppermute x0 -> x3, starting transfers between devices: none -> 8.36 us  [per_device(): lax.ppermute(part, NEAR, [(i, i ^ d) for i in range(near_size)])]
    ppermute x9 -> x6, waiting for transfers between devices: 17 us -> 9.67 us  [shift(): lax.ppermute(value, axis, [(i, (i + by) % size) for i in range(size)])]
    all_to_all x1 -> x2, waiting for transfers between devices: 0.01 us -> 4.12 us  [the longest x1 4.11 us: per_device(): packed = lax.all_to_all(packed, 'x', 0, 0, tiled=True)]
    all_to_all x1 -> x2, starting transfers between devices: 3.78 us -> 7.41 us  [the longest x1 4.01 us: per_device(): packed = lax.all_to_all(packed, 'x', 0, 0, tiled=True)]
    pallas_call x2 -> x3, Pallas kernels: 4.59 us -> 6.67 us  [the longest x1 3.58 us: per_device(): pl.pallas_call(query_kernel, out_shape=(jax.ShapeDtypeStruct((near_size,...]
    unnamed x8 -> x6, local copies, waits for them, and re-layouts: 0.02 us -> 1.6 us
  transfers between devices with their start and end apart: 11 -> 12, of which waited for: 7 -> 5; matrix products, arithmetic and copies ran while one was open for 1% -> 1% of each run, Pallas kernels for 5% -> 7%
where the time goes in v13:
time: 120 us; the launch traced here: 119 us
  starting transfers between devices  52.5 us (44%)
  waiting for transfers between devices  32.6 us (27%)
  Pallas kernels  14.4 us (12%)
  blocking collectives  13.3 us (11%)
  local copies, waits for them, and re-layouts  3.34 us (3%)
  other arithmetic  2.18 us (2%)
    ppermute x6, starting transfers between devices, shift(): lax.ppermute(value, axis, [(i, (i + by) % size) for i in range(size)])  24.6 us
    all_to_all x1, waiting for transfers between devices, per_device(): lax.all_to_all(jnp.broadcast_to(sent[None], (chips,) + sent.shape), CHIPS...  18.8 us
    all_to_all x1, blocking collectives, per_device(): stats = lax.all_to_all(stats, CHIPS, 0, 0, tiled=True)  13.3 us
    all_to_all x1, starting transfers between devices, per_device(): lax.all_to_all(jnp.broadcast_to(sent[None], (chips,) + sent.shape), CHIPS...  12.1 us
    ppermute x6, waiting for transfers between devices, shift(): lax.ppermute(value, axis, [(i, (i + by) % size) for i in range(size)])  9.67 us
    ppermute x3, starting transfers between devices, per_device(): lax.ppermute(part, NEAR, [(i, i ^ d) for i in range(near_size)])  8.36 us
    all_to_all x1, waiting for transfers between devices, per_device(): packed = lax.all_to_all(packed, 'x', 0, 0, tiled=True)  4.11 us
    all_to_all x1, starting transfers between devices, per_device(): packed = lax.all_to_all(packed, 'x', 0, 0, tiled=True)  4.01 us
  transfers between devices with their start and end apart: 12, of which 5 were waited for; matrix products, arithmetic and copies ran while one was open for 1% of the time, Pallas kernels for 7%

profile of v13, /device:TPU:1, one launch (start us, length us, event | category | flops | bytes accessed | tf_op | source)
XLA Modules:
  0.0 119.1 jit_solution(2501278487182311583)
XLA Ops:
  0.6 0.7 convert.11
  1.3 0.7 and_convert_fusion
  2.0 0.8 pad_maximum_fusion
  2.8 0.0 copy-start
  2.8 0.0 copy-start.2
  2.8 1.1 broadcast_in_dim.4
  3.9 12.1 %all-to-all-start = ((bf16[16,8,4224]{2,1,0:T(8,128)(2,1)}), bf16[16,8,4224]{2,1,0:T(8,128)(2,1)S(1)}, u32[]{:S(2)}, u32[]{:S(2)}) async-start(bf16[16,8,4224]{2,1,0:T(8,128)(2,1)} %broadcast_in_dim.4), calls=%async_computation | async-start | bytes 2162688 | tf_op jit(solution)/shard_map/all_to_all | solution.py:187
  16.0 0.0 copy-done
  16.0 2.9 %collective-permute-start = (bf16[256,4096]{1,0:T(8,128)(2,1)S(1)}, bf16[256,4096]{1,0:T(8,128)(2,1)}, u32[]{:S(2)}, u32[]{:S(2)}) collective-permute-start(bf16[256,4096]{1,0:T(8,128)(2,1)S(1)} %copy-done), channel_id=1, source_target_pairs={{0,16},{16,0},{1,17},{17,1},{2,18},{18,2},{3,19},{19,3},{4,20},{20... | collective-permute-start | bytes 6291464 | tf_op jit(solution)/shard_map/ppermute | solution.py:28
  18.9 0.0 copy-done.2
  18.9 0.9 shard_map.76.teacher
  19.8 1.9 %collective-permute-start.1 = (bf16[3,256,256]{2,1,0:T(8,128)(2,1)}, bf16[3,256,256]{2,1,0:T(8,128)(2,1)}, u32[]{:S(2)}, u32[]{:S(2)}) collective-permute-start(bf16[3,256,256]{2,1,0:T(8,128)(2,1)} %shard_map.76.teacher), channel_id=1, source_target_pairs={{0,16},{16,0},{1,17},{17,1},{2,18},{18,2},{3,19},{19,3},{4,20},{20... | collective-permute-start | bytes 1179656 | tf_op jit(solution)/shard_map/ppermute | solution.py:28
  21.7 0.1 stack.23.places
  21.8 1.9 %collective-permute-done.1.teacher_other = bf16[3,256,256]{2,1,0:T(8,128)(2,1)} collective-permute-done((bf16[3,256,256]{2,1,0:T(8,128)(2,1)}, bf16[3,256,256]{2,1,0:T(8,128)(2,1)}, u32[]{:S(2)}, u32[]{:S(2)}) %collective-permute-start.1) | collective-permute-done | bytes 393248 | tf_op jit(solution)/shard_map/ppermute | solution.py:28
  23.7 18.8 %all-to-all-done = bf16[16,8,4224]{2,1,0:T(8,128)(2,1)S(1)} async-done(((bf16[16,8,4224]{2,1,0:T(8,128)(2,1)}), bf16[16,8,4224]{2,1,0:T(8,128)(2,1)S(1)}, u32[]{:S(2)}, u32[]{:S(2)}) %all-to-all-start) | async-done | bytes 1081376 | tf_op jit(solution)/shard_map/all_to_all | solution.py:187
  42.5 0.0 collective-permute-done.passages_other
  42.5 3.5 %shard_map.77 = (f32[4,256,128]{2,1,0:T(8,128)S(1)}, s32[1,128]{1,0:T(1,128)S(1)}, f32[16,8,128]{2,1,0:T(8,128)S(1)}) custom-call(s32[5]{0:T(128)S(1)} %stack.23.places, bf16[128,4224]{1,0:T(8,128)(2,1)S(1)} %bitcast.10, bf16[256,4096]{1,0:T(8,128)(2,1)S(1)} %copy-done, bf16[256,4096]{1,0:T(8,128)(2,1)} %collective-permute-done.passages_other, ...), custom_call_target="tpu_custom_call" | custom-call | tf_op jit(solution)/shard_map/pallas_call | solution.py:200
  46.0 13.3 %all_to_all.20.stats = f32[16,8,128]{2,1,0:T(8,128)S(1)} all-to-all(f32[16,8,128]{2,1,0:T(8,128)S(1)} %get-tuple-element.21), channel_id=1, replica_groups=mesh['yl'=2,'zh'=4,'zl'=2,'core'=2,'x'=4,'yh'=4] {'yl','zl','zh'}, dimensions={0} | all-to-all | bytes 131072 | tf_op jit(solution)/shard_map/all_to_all | solution.py:211
  59.3 1.9 %shard_map.78 = (bf16[2,128,256]{2,1,0:T(8,128)(2,1)S(1)}, f32[1,128]{1,0:T(1,128)S(1)}, bf16[4,192,1024]{2,1,0:T(8,128)(2,1)}) custom-call(s32[5]{0:T(128)S(1)} %stack.23.places, bf16[128,4224]{1,0:T(8,128)(2,1)S(1)} %bitcast.11, f32[4,256,128]{2,1,0:T(8,128)S(1)} %get-tuple-element.19.logits, s32[1,128]{1,0:T(1,128)S(1)} %get-tuple-element.20.positives, ...), custom_call_target="tpu_custom_call" | custom-call | tf_op jit(solution)/shard_map/pallas_call | solution.py:213
  61.2 4.0 %all-to-all-start.3 = ((bf16[4,192,1024]{2,1,0:T(8,128)(2,1)}), bf16[4,192,1024]{2,1,0:T(8,128)(2,1)S(1)}, u32[]{:S(2)}, u32[]{:S(2)}) async-start(bf16[4,192,1024]{2,1,0:T(8,128)(2,1)} %get-tuple-element.28), calls=%async_computation.3 | async-start | bytes 3145728 | tf_op jit(solution)/shard_map/all_to_all | solution.py:227
  65.2 0.0 copy-start.1
  65.2 1.6 %copy-done.1 = bf16[256,4096]{1,0:T(8,128)(2,1)S(1)} copy-done((bf16[256,4096]{1,0:T(8,128)(2,1)S(1)}, bf16[256,4096]{1,0:T(8,128)(2,1)}, u32[]{:S(2)}) %copy-start.1) | copy-done | bytes 2097176
  66.8 3.6 %shard_map.79 = (bf16[4,32,4096]{2,1,0:T(8,128)(2,1)}, bf16[32,4096]{1,0:T(8,128)(2,1)S(1)}, bf16[32,4096]{1,0:T(8,128)(2,1)}, bf16[32,4096]{1,0:T(8,128)(2,1)}, bf16[32,4096]{1,0:T(8,128)(2,1)}) custom-call(s32[5]{0:T(128)S(1)} %stack.23.places, bf16[2,128,256]{2,1,0:T(8,128)(2,1)S(1)} %get-tuple-element.23.grads, bf16[256,4096]{1,0:T(8,128)(2,1)S(1)} %copy-done.1, ...), custom_call_target="tpu_custom_call" | custom-call | tf_op jit(solution)/shard_map/pallas_call | solution.py:228
  70.4 2.3 %collective-permute-start.2 = (bf16[32,4096]{1,0:T(8,128)(2,1)}, bf16[32,4096]{1,0:T(8,128)(2,1)S(1)}, u32[]{:S(2)}, u32[]{:S(2)}) collective-permute-start(bf16[32,4096]{1,0:T(8,128)(2,1)} %get-tuple-element.25), channel_id=1, source_target_pairs={{0,32},{32,0},{256,288},{288,256},{1,33},{33,1},{257,289},{289,257... | collective-permute-start | bytes 786440 | tf_op jit(solution)/shard_map/ppermute | solution.py:237
  72.7 2.6 %collective-permute-start.3 = (bf16[32,4096]{1,0:T(8,128)(2,1)}, bf16[32,4096]{1,0:T(8,128)(2,1)S(1)}, u32[]{:S(2)}, u32[]{:S(2)}) collective-permute-start(bf16[32,4096]{1,0:T(8,128)(2,1)} %get-tuple-element.26), channel_id=1, source_target_pairs={{0,256},{32,288},{256,0},{288,32},{1,257},{33,289},{257,1},{289,33... | collective-permute-start | bytes 786440 | tf_op jit(solution)/shard_map/ppermute | solution.py:237
  75.4 3.4 %collective-permute-start.4 = (bf16[32,4096]{1,0:T(8,128)(2,1)}, bf16[32,4096]{1,0:T(8,128)(2,1)}, u32[]{:S(2)}, u32[]{:S(2)}) collective-permute-start(bf16[32,4096]{1,0:T(8,128)(2,1)} %get-tuple-element.27), channel_id=1, source_target_pairs={{0,288},{32,256},{256,32},{288,0},{1,289},{33,257},{257,33},{289,1... | collective-permute-start | bytes 786440 | tf_op jit(solution)/shard_map/ppermute | solution.py:237
  78.8 4.1 %all-to-all-done.3.packed = bf16[4,192,1024]{2,1,0:T(8,128)(2,1)S(1)} async-done(((bf16[4,192,1024]{2,1,0:T(8,128)(2,1)}), bf16[4,192,1024]{2,1,0:T(8,128)(2,1)S(1)}, u32[]{:S(2)}, u32[]{:S(2)}) %all-to-all-start.3) | async-done | bytes 1572896 | tf_op jit(solution)/shard_map/all_to_all | solution.py:227
  82.9 0.7 shard_map.81
  83.6 5.9 %collective-permute-start.5 = (bf16[256,1024]{1,0:T(8,128)(2,1)S(1)}, bf16[256,1024]{1,0:T(8,128)(2,1)S(1)}, u32[]{:S(2)}, u32[]{:S(2)}) collective-permute-start(bf16[256,1024]{1,0:T(8,128)(2,1)S(1)} %shard_map.81), channel_id=1, source_target_pairs={{0,16},{16,0},{1,17},{17,1},{2,18},{18,2},{3,19},{19,3},{4,20},{20... | collective-permute-start | bytes 1572872 | tf_op jit(solution)/shard_map/ppermute | solution.py:28
  89.5 0.0 collective-permute-done.2.refs_1_
  89.5 0.0 collective-permute-done.3.refs_2_
  89.5 0.0 collective-permute-done.4.refs_3_
  89.5 1.8 %shard_map.80.after = bf16[32,4096]{1,0:T(8,128)(2,1)} custom-call(bf16[32,4096]{1,0:T(8,128)(2,1)S(1)} %get-tuple-element.24.refs_0_, bf16[32,4096]{1,0:T(8,128)(2,1)S(1)} %collective-permute-done.2.refs_1_, bf16[32,4096]{1,0:T(8,128)(2,1)S(1)} %collective-permute-done.3.refs_2_, bf16[32,4096]{1,0:T(8,128)(2,1)} %collective-permute-done.4.refs_3_), custom_call_target="tpu_custom_call" | custom-call | tf_op jit(solution)/shard_map/pallas_call | solution.py:247
  91.3 3.4 %all-to-all-start.2 = ((bf16[4,8,4096]{2,1,0:T(8,128)(2,1)}), bf16[4,8,4096]{2,1,0:T(8,128)(2,1)S(1)}, u32[]{:S(2)}, u32[]{:S(2)}) async-start(bf16[4,8,4096]{2,1,0:T(8,128)(2,1)} %bitcast.8), calls=%async_computation.2 | async-start | bytes 524288 | tf_op jit(solution)/shard_map/all_to_all | solution.py:254
  94.7 0.0 collective-permute-done.5.back
  94.7 1.3 %shard_map.82 = (bf16[256,256]{1,0:T(8,128)(2,1)S(1)}, bf16[256,256]{1,0:T(8,128)(2,1)S(1)}, bf16[256,256]{1,0:T(8,128)(2,1)S(1)}, bf16[256,256]{1,0:T(8,128)(2,1)S(1)}) custom-call(s32[5]{0:T(128)S(1)} %stack.23.places, bf16[4,192,1024]{2,1,0:T(8,128)(2,1)S(1)} %all-to-all-done.3.packed, bf16[256,1024]{1,0:T(8,128)(2,1)S(1)} %collective-permute-done.5.back, ...), custom_call_target="tpu_custom_call" | custom-call | tf_op jit(solution)/shard_map/pallas_call | solution.py:255
  96.1 4.2 %collective-permute-start.6 = (bf16[256,256]{1,0:T(8,128)(2,1)S(1)}, bf16[256,256]{1,0:T(8,128)(2,1)S(1)}, u32[]{:S(2)}, u32[]{:S(2)}) collective-permute-start(bf16[256,256]{1,0:T(8,128)(2,1)S(1)} %get-tuple-element.30), channel_id=1, source_target_pairs={{0,1},{1,2},{2,3},{3,0},{4,5},{5,6},{6,7},{7,4},{8,9},{9,10},{10,1... | collective-permute-start | bytes 393224 | tf_op jit(solution)/shard_map/ppermute | solution.py:28
  100.3 4.8 %collective-permute-start.7 = (bf16[256,256]{1,0:T(8,128)(2,1)S(1)}, bf16[256,256]{1,0:T(8,128)(2,1)S(1)}, u32[]{:S(2)}, u32[]{:S(2)}) collective-permute-start(bf16[256,256]{1,0:T(8,128)(2,1)S(1)} %get-tuple-element.31), channel_id=1, source_target_pairs={{0,2},{1,3},{2,0},{3,1},{4,6},{5,7},{6,4},{7,5},{8,10},{9,11},{10,... | collective-permute-start | bytes 393224 | tf_op jit(solution)/shard_map/ppermute | solution.py:28
  105.0 5.0 %collective-permute-start.8 = (bf16[256,256]{1,0:T(8,128)(2,1)S(1)}, bf16[256,256]{1,0:T(8,128)(2,1)S(1)}, u32[]{:S(2)}, u32[]{:S(2)}) collective-permute-start(bf16[256,256]{1,0:T(8,128)(2,1)S(1)} %get-tuple-element.32), channel_id=1, source_target_pairs={{0,3},{1,0},{2,1},{3,2},{4,7},{5,4},{6,5},{7,6},{8,11},{9,8},{10,9... | collective-permute-start | bytes 393224 | tf_op jit(solution)/shard_map/ppermute | solution.py:28
  110.0 0.6 constant_dynamic-slice_fusion
  110.6 0.0 all-to-all-done.2.query_parts
  110.6 0.0 collective-permute-done.6.refs_1_
  110.6 2.5 %collective-permute-done.7.refs_2_ = bf16[256,256]{1,0:T(8,128)(2,1)S(1)} collective-permute-done((bf16[256,256]{1,0:T(8,128)(2,1)S(1)}, bf16[256,256]{1,0:T(8,128)(2,1)S(1)}, u32[]{:S(2)}, u32[]{:S(2)}) %collective-permute-start.7) | collective-permute-done | bytes 131104 | tf_op jit(solution)/shard_map/ppermute | solution.py:28
  113.2 5.2 %collective-permute-done.8.refs_3_ = bf16[256,256]{1,0:T(8,128)(2,1)S(1)} collective-permute-done((bf16[256,256]{1,0:T(8,128)(2,1)S(1)}, bf16[256,256]{1,0:T(8,128)(2,1)S(1)}, u32[]{:S(2)}, u32[]{:S(2)}) %collective-permute-start.8) | collective-permute-done | bytes 131104 | tf_op jit(solution)/shard_map/ppermute | solution.py:28
  118.4 0.8 shard_map.83
  (1 shorter events, 0.0 us)
Async XLA Ops:
  2.8 13.2 %copy-start = (bf16[256,4096]{1,0:T(8,128)(2,1)S(1)}, bf16[256,4096]{1,0:T(8,128)(2,1)}, u32[]{:S(2)}) copy-start(bf16[256,4096]{1,0:T(8,128)(2,1)} %passages.3) | copy-start | bytes 6291460
  2.8 16.1 %copy-start.2 = (f32[1,256,256]{2,1,0:T(8,128)S(1)}, f32[1,256,256]{2,1,0:T(8,128)}, u32[]{:S(2)}) copy-start(f32[1,256,256]{2,1,0:T(8,128)} %param.7) | copy-start | bytes 786436
  3.9 38.6 %all-to-all-start = ((bf16[16,8,4224]{2,1,0:T(8,128)(2,1)}), bf16[16,8,4224]{2,1,0:T(8,128)(2,1)S(1)}, u32[]{:S(2)}, u32[]{:S(2)}) async-start(bf16[16,8,4224]{2,1,0:T(8,128)(2,1)} %broadcast_in_dim.4), calls=%async_computation | async-start | bytes 2162688 | tf_op jit(solution)/shard_map/all_to_all | solution.py:187
  16.0 26.5 %collective-permute-start = (bf16[256,4096]{1,0:T(8,128)(2,1)S(1)}, bf16[256,4096]{1,0:T(8,128)(2,1)}, u32[]{:S(2)}, u32[]{:S(2)}) collective-permute-start(bf16[256,4096]{1,0:T(8,128)(2,1)S(1)} %copy-done), channel_id=1, source_target_pairs={{0,16},{16,0},{1,17},{17,1},{2,18},{18,2},{3,19},{19,3},{4,20},{20... | collective-permute-start | bytes 6291464 | tf_op jit(solution)/shard_map/ppermute | solution.py:28
  19.8 3.9 %collective-permute-start.1 = (bf16[3,256,256]{2,1,0:T(8,128)(2,1)}, bf16[3,256,256]{2,1,0:T(8,128)(2,1)}, u32[]{:S(2)}, u32[]{:S(2)}) collective-permute-start(bf16[3,256,256]{2,1,0:T(8,128)(2,1)} %shard_map.76.teacher), channel_id=1, source_target_pairs={{0,16},{16,0},{1,17},{17,1},{2,18},{18,2},{3,19},{19,3},{4,20},{20... | collective-permute-start | bytes 1179656 | tf_op jit(solution)/shard_map/ppermute | solution.py:28
  61.2 21.7 %all-to-all-start.3 = ((bf16[4,192,1024]{2,1,0:T(8,128)(2,1)}), bf16[4,192,1024]{2,1,0:T(8,128)(2,1)S(1)}, u32[]{:S(2)}, u32[]{:S(2)}) async-start(bf16[4,192,1024]{2,1,0:T(8,128)(2,1)} %get-tuple-element.28), calls=%async_computation.3 | async-start | bytes 3145728 | tf_op jit(solution)/shard_map/all_to_all | solution.py:227
  65.2 1.6 %copy-start.1 = (bf16[256,4096]{1,0:T(8,128)(2,1)S(1)}, bf16[256,4096]{1,0:T(8,128)(2,1)}, u32[]{:S(2)}) copy-start(bf16[256,4096]{1,0:T(8,128)(2,1)} %passages.3) | copy-start | bytes 6291460
  70.4 19.1 %collective-permute-start.2 = (bf16[32,4096]{1,0:T(8,128)(2,1)}, bf16[32,4096]{1,0:T(8,128)(2,1)S(1)}, u32[]{:S(2)}, u32[]{:S(2)}) collective-permute-start(bf16[32,4096]{1,0:T(8,128)(2,1)} %get-tuple-element.25), channel_id=1, source_target_pairs={{0,32},{32,0},{256,288},{288,256},{1,33},{33,1},{257,289},{289,257... | collective-permute-start | bytes 786440 | tf_op jit(solution)/shard_map/ppermute | solution.py:237
  72.7 16.8 %collective-permute-start.3 = (bf16[32,4096]{1,0:T(8,128)(2,1)}, bf16[32,4096]{1,0:T(8,128)(2,1)S(1)}, u32[]{:S(2)}, u32[]{:S(2)}) collective-permute-start(bf16[32,4096]{1,0:T(8,128)(2,1)} %get-tuple-element.26), channel_id=1, source_target_pairs={{0,256},{32,288},{256,0},{288,32},{1,257},{33,289},{257,1},{289,33... | collective-permute-start | bytes 786440 | tf_op jit(solution)/shard_map/ppermute | solution.py:237
  75.4 14.2 %collective-permute-start.4 = (bf16[32,4096]{1,0:T(8,128)(2,1)}, bf16[32,4096]{1,0:T(8,128)(2,1)}, u32[]{:S(2)}, u32[]{:S(2)}) collective-permute-start(bf16[32,4096]{1,0:T(8,128)(2,1)} %get-tuple-element.27), channel_id=1, source_target_pairs={{0,288},{32,256},{256,32},{288,0},{1,289},{33,257},{257,33},{289,1... | collective-permute-start | bytes 786440 | tf_op jit(solution)/shard_map/ppermute | solution.py:237
  83.6 11.1 %collective-permute-start.5 = (bf16[256,1024]{1,0:T(8,128)(2,1)S(1)}, bf16[256,1024]{1,0:T(8,128)(2,1)S(1)}, u32[]{:S(2)}, u32[]{:S(2)}) collective-permute-start(bf16[256,1024]{1,0:T(8,128)(2,1)S(1)} %shard_map.81), channel_id=1, source_target_pairs={{0,16},{16,0},{1,17},{17,1},{2,18},{18,2},{3,19},{19,3},{4,20},{20... | collective-permute-start | bytes 1572872 | tf_op jit(solution)/shard_map/ppermute | solution.py:28
  91.3 19.3 %all-to-all-start.2 = ((bf16[4,8,4096]{2,1,0:T(8,128)(2,1)}), bf16[4,8,4096]{2,1,0:T(8,128)(2,1)S(1)}, u32[]{:S(2)}, u32[]{:S(2)}) async-start(bf16[4,8,4096]{2,1,0:T(8,128)(2,1)} %bitcast.8), calls=%async_computation.2 | async-start | bytes 524288 | tf_op jit(solution)/shard_map/all_to_all | solution.py:254
  96.1 14.6 %collective-permute-start.6 = (bf16[256,256]{1,0:T(8,128)(2,1)S(1)}, bf16[256,256]{1,0:T(8,128)(2,1)S(1)}, u32[]{:S(2)}, u32[]{:S(2)}) collective-permute-start(bf16[256,256]{1,0:T(8,128)(2,1)S(1)} %get-tuple-element.30), channel_id=1, source_target_pairs={{0,1},{1,2},{2,3},{3,0},{4,5},{5,6},{6,7},{7,4},{8,9},{9,10},{10,1... | collective-permute-start | bytes 393224 | tf_op jit(solution)/shard_map/ppermute | solution.py:28
  100.3 12.9 %collective-permute-start.7 = (bf16[256,256]{1,0:T(8,128)(2,1)S(1)}, bf16[256,256]{1,0:T(8,128)(2,1)S(1)}, u32[]{:S(2)}, u32[]{:S(2)}) collective-permute-start(bf16[256,256]{1,0:T(8,128)(2,1)S(1)} %get-tuple-element.31), channel_id=1, source_target_pairs={{0,2},{1,3},{2,0},{3,1},{4,6},{5,7},{6,4},{7,5},{8,10},{9,11},{10,... | collective-permute-start | bytes 393224 | tf_op jit(solution)/shard_map/ppermute | solution.py:28
  105.0 13.3 %collective-permute-start.8 = (bf16[256,256]{1,0:T(8,128)(2,1)S(1)}, bf16[256,256]{1,0:T(8,128)(2,1)S(1)}, u32[]{:S(2)}, u32[]{:S(2)}) collective-permute-start(bf16[256,256]{1,0:T(8,128)(2,1)S(1)} %get-tuple-element.32), channel_id=1, source_target_pairs={{0,3},{1,0},{2,1},{3,2},{4,7},{5,4},{6,5},{7,6},{8,11},{9,8},{10,9... | collective-permute-start | bytes 393224 | tf_op jit(solution)/shard_map/ppermute | solution.py:28

commit v14 on v10

--- a/solution.py
+++ b/solution.py
@@ -86,7 +86,7 @@
     stats[...] = jnp.broadcast_to(whole[None], stats.shape)
 
 
-def grad_kernel(places, query, logits, positives, stats, rows_first, losses, *packed):
+def grad_kernel(places, query, logits, positives, stats, grads, losses, *packed):
     rows, width = query.shape[0], packed[0].shape[1]
     for d, out in enumerate(packed):
         out[:rows] = query[:, pl.ds(pl.multiple_of(lax.rem(places[2] + d, len(packed)) * width, width), width)]
@@ -110,8 +110,8 @@
             - jnp.exp(logits[CORES + half] - top_t) * scale_t
             - jnp.where(hot, inv_temp, 0.0)
         )
-        rows_first[half] = values.T.astype(bf16)
         values = values.astype(bf16)
+        grads[half] = values
         steps = block_rows // tall
         for k in range(steps):
             lane = (half * steps + k) * rows
@@ -121,8 +121,9 @@
 
 def query_kernel(grads, passages, passages_other, after, out):
     del after
-    total = jnp.dot(grads[0], passages[...], preferred_element_type=f32)
-    total += jnp.dot(grads[1], passages_other[...], preferred_element_type=f32)
+    total = 0.0
+    for half, block in enumerate((passages, passages_other)):
+        total += lax.dot_general(grads[half], block[...], (((0,), (0,)), ((), ())), preferred_element_type=f32)
     out[...] = total.astype(bf16)
 
 
@@ -169,7 +170,7 @@
         [(chip * CORES + core) * block_rows, (chip * CORES + 1 - core) * block_rows, x, yh]
     ).astype(i32)
 
-    codes = jnp.concatenate([teacher_rows, positives & 255, lax.shift_right_logical(positives, 8)], axis=0)
+    codes = jnp.concatenate([teacher_rows & 255, positives & 255, lax.shift_right_logical(positives, 8) & 255], axis=0)
     codes = jnp.pad(codes, ((0, own_rows - codes.shape[0]), (0, LANES - own_rows)))
     sent = jnp.concatenate([queries[0], codes.astype(bf16)], axis=1)
     passages_other = shift(passages, "core", 1)
@@ -199,10 +200,10 @@
     )(places, query, passages, passages_other, table, table_other)
     stats = lax.all_to_all(stats, CHIPS, 0, 0, tiled=True)
     width = depth // x_size
-    rows_first, losses, *packed = pl.pallas_call(
+    grads, losses, *packed = pl.pallas_call(
         grad_kernel,
         out_shape=(
-            jax.ShapeDtypeStruct((CORES, rows, block_rows), bf16),
+            jax.ShapeDtypeStruct((CORES, block_rows, rows), bf16),
             jax.ShapeDtypeStruct((1, rows), f32),
         )
         + (jax.ShapeDtypeStruct((rows + wide * rows // width, width), bf16),) * x_size,
@@ -219,7 +220,7 @@
         in_specs=[VMEM] * 3 + [ANY],
         out_specs=VMEM,
         compiler_params=PARAMS,
-    )(rows_first, passages, passages_other, packed[0])
+    )(grads, passages, passages_other, packed[0])
     query_parts = lax.all_to_all(query_part.reshape(chips, own_rows, depth), CHIPS, 0, 0, tiled=True)
     packed = shifts(packed, "x")
     part_other = pl.pallas_call(

time: 117 us -> 116 us (level)
  no operation moved by 1% of the time
where the time goes in v14:
time: 116 us; the launch traced here: 115 us
  starting transfers between devices  48.8 us (42%)
  waiting for transfers between devices  35.4 us (31%)
  blocking collectives  14.4 us (12%)
  Pallas kernels  12.3 us (11%)
  other arithmetic  1.77 us (2%)
  local copies, waits for them, and re-layouts  1.66 us (1%)
    ppermute x9, starting transfers between devices, shift(): lax.ppermute(value, axis, [(i, (i + by) % size) for i in range(size)])  33.1 us
    all_to_all x1, waiting for transfers between devices, per_device(): lax.all_to_all(jnp.broadcast_to(sent[None], (chips,) + sent.shape), CHIPS...  18.3 us
    ppermute x9, waiting for transfers between devices, shift(): lax.ppermute(value, axis, [(i, (i + by) % size) for i in range(size)])  17 us
    all_to_all x1, blocking collectives, per_device(): stats = lax.all_to_all(stats, CHIPS, 0, 0, tiled=True)  14.4 us
    all_to_all x1, starting transfers between devices, per_device(): lax.all_to_all(jnp.broadcast_to(sent[None], (chips,) + sent.shape), CHIPS...  12 us
    all_to_all x1, starting transfers between devices, per_device(): lax.all_to_all(query_part.reshape(chips, own_rows, depth), CHIPS, 0, 0, t...  3.78 us
    pallas_call x1, Pallas kernels, per_device(): pl.pallas_call(score_kernel, out_shape=(jax.ShapeDtypeStruct((2 * CORES,...  3.46 us
    pallas_call x1, Pallas kernels, per_device(): pl.pallas_call(query_kernel, out_shape=jax.ShapeDtypeStruct((rows, depth)...  3.31 us
  transfers between devices with their start and end apart: 11, of which 7 were waited for; matrix products, arithmetic and copies ran while one was open for 1% of the time, Pallas kernels for 5%

profile of v14, /device:TPU:1, one launch (start us, length us, event | category | flops | bytes accessed | tf_op | source)
XLA Modules:
  0.0 115.2 jit_solution(8995779693132492935)
XLA Ops:
  0.6 0.0 copy-start
  0.6 0.0 copy-start.3
  0.7 0.8 and_convert_fusion.1
  1.5 0.8 pad_maximum_fusion
  2.3 1.1 broadcast_in_dim.4
  3.4 12.0 %all-to-all-start = ((bf16[16,8,4224]{2,1,0:T(8,128)(2,1)}), bf16[16,8,4224]{2,1,0:T(8,128)(2,1)S(1)}, u32[]{:S(2)}, u32[]{:S(2)}) async-start(bf16[16,8,4224]{2,1,0:T(8,128)(2,1)} %broadcast_in_dim.4), calls=%async_computation | async-start | bytes 2162688 | tf_op jit(solution)/shard_map/all_to_all | solution.py:177
  15.4 0.0 copy-done
  15.4 2.9 %collective-permute-start = (bf16[256,4096]{1,0:T(8,128)(2,1)S(1)}, bf16[256,4096]{1,0:T(8,128)(2,1)}, u32[]{:S(2)}, u32[]{:S(2)}) collective-permute-start(bf16[256,4096]{1,0:T(8,128)(2,1)S(1)} %copy-done), channel_id=1, source_target_pairs={{0,16},{16,0},{1,17},{17,1},{2,18},{18,2},{3,19},{19,3},{4,20},{20... | collective-permute-start | bytes 6291464 | tf_op jit(solution)/shard_map/ppermute | solution.py:27
  18.3 0.0 copy-done.3
  18.3 0.9 shard_map.76.teacher
  19.2 1.9 %collective-permute-start.1 = (bf16[3,256,256]{2,1,0:T(8,128)(2,1)}, bf16[3,256,256]{2,1,0:T(8,128)(2,1)}, u32[]{:S(2)}, u32[]{:S(2)}) collective-permute-start(bf16[3,256,256]{2,1,0:T(8,128)(2,1)} %shard_map.76.teacher), channel_id=1, source_target_pairs={{0,16},{16,0},{1,17},{17,1},{2,18},{18,2},{3,19},{19,3},{4,20},{20... | collective-permute-start | bytes 1179656 | tf_op jit(solution)/shard_map/ppermute | solution.py:27
  21.1 0.1 pad_add_fusion.places
  21.2 1.9 %collective-permute-done.1.teacher_other = bf16[3,256,256]{2,1,0:T(8,128)(2,1)} collective-permute-done((bf16[3,256,256]{2,1,0:T(8,128)(2,1)}, bf16[3,256,256]{2,1,0:T(8,128)(2,1)}, u32[]{:S(2)}, u32[]{:S(2)}) %collective-permute-start.1) | collective-permute-done | bytes 393248 | tf_op jit(solution)/shard_map/ppermute | solution.py:27
  23.1 18.3 %all-to-all-done = bf16[16,8,4224]{2,1,0:T(8,128)(2,1)S(1)} async-done(((bf16[16,8,4224]{2,1,0:T(8,128)(2,1)}), bf16[16,8,4224]{2,1,0:T(8,128)(2,1)S(1)}, u32[]{:S(2)}, u32[]{:S(2)}) %all-to-all-start) | async-done | bytes 1081376 | tf_op jit(solution)/shard_map/all_to_all | solution.py:177
  41.4 0.0 collective-permute-done.passages_other
  41.4 3.5 %shard_map.77 = (f32[4,256,128]{2,1,0:T(8,128)S(1)}, s32[1,128]{1,0:T(1,128)S(1)}, f32[16,8,128]{2,1,0:T(8,128)S(1)}) custom-call(s32[4]{0:T(128)S(1)} %pad_add_fusion.places, bf16[128,4224]{1,0:T(8,128)(2,1)S(1)} %bitcast.9, bf16[256,4096]{1,0:T(8,128)(2,1)S(1)} %copy-done, bf16[256,4096]{1,0:T(8,128)(2,1)} %collective-permute-done.passages_other, ...), custom_call_target="tpu_custom_call" | custom-call | tf_op jit(solution)/shard_map/pallas_call | solution.py:190
  44.9 14.4 %all_to_all.15.stats = f32[16,8,128]{2,1,0:T(8,128)S(1)} all-to-all(f32[16,8,128]{2,1,0:T(8,128)S(1)} %get-tuple-element.20), channel_id=1, replica_groups=mesh['yl'=2,'z'=8,'core'=2,'x'=4,'yh'=4] {'yl','z'}, dimensions={0} | all-to-all | bytes 131072 | tf_op jit(solution)/shard_map/all_to_all | solution.py:201
  59.4 1.8 %shard_map.78 = (bf16[2,256,128]{2,1,0:T(8,128)(2,1)S(1)}, f32[1,128]{1,0:T(1,128)S(1)}, bf16[192,1024]{1,0:T(8,128)(2,1)S(1)}, bf16[192,1024]{1,0:T(8,128)(2,1)...) custom-call(s32[4]{0:T(128)S(1)} %pad_add_fusion.places, bf16[128,4224]{1,0:T(8,128)(2,1)S(1)} %bitcast.10, ...), custom_call_target="tpu_custom_call" | custom-call | tf_op jit(solution)/shard_map/pallas_call | solution.py:203
  61.2 0.0 copy-start.1
  61.2 3.1 %collective-permute-start.2 = (bf16[192,1024]{1,0:T(8,128)(2,1)}, bf16[192,1024]{1,0:T(8,128)(2,1)S(1)}, u32[]{:S(2)}, u32[]{:S(2)}) collective-permute-start(bf16[192,1024]{1,0:T(8,128)(2,1)} %get-tuple-element.24), channel_id=1, source_target_pairs={{0,4},{4,8},{8,12},{12,0},{1,5},{5,9},{9,13},{13,1},{2,6},{6,10},{... | collective-permute-start | bytes 1179656 | tf_op jit(solution)/shard_map/ppermute | solution.py:27
  64.3 4.4 %collective-permute-start.3 = (bf16[192,1024]{1,0:T(8,128)(2,1)}, bf16[192,1024]{1,0:T(8,128)(2,1)S(1)}, u32[]{:S(2)}, u32[]{:S(2)}) collective-permute-start(bf16[192,1024]{1,0:T(8,128)(2,1)} %get-tuple-element.25), channel_id=1, source_target_pairs={{0,8},{4,12},{8,0},{12,4},{1,9},{5,13},{9,1},{13,5},{2,10},{6,14},... | collective-permute-start | bytes 1179656 | tf_op jit(solution)/shard_map/ppermute | solution.py:27
  68.7 3.1 %collective-permute-start.4 = (bf16[192,1024]{1,0:T(8,128)(2,1)}, bf16[192,1024]{1,0:T(8,128)(2,1)S(1)}, u32[]{:S(2)}, u32[]{:S(2)}) collective-permute-start(bf16[192,1024]{1,0:T(8,128)(2,1)} %get-tuple-element.26), channel_id=1, source_target_pairs={{0,12},{4,0},{8,4},{12,8},{1,13},{5,1},{9,5},{13,9},{2,14},{6,2},{... | collective-permute-start | bytes 1179656 | tf_op jit(solution)/shard_map/ppermute | solution.py:27
  71.7 3.3 %shard_map.79 = bf16[128,4096]{1,0:T(8,128)(2,1)} custom-call(bf16[2,256,128]{2,1,0:T(8,128)(2,1)S(1)} %get-tuple-element.22.grads, bf16[256,4096]{1,0:T(8,128)(2,1)S(1)} %copy-done, bf16[256,4096]{1,0:T(8,128)(2,1)} %collective-permute-done.passages_other, bf16[192,1024]{1,0:T(8,128)(2,1)S(1)} %get-tuple-element.23.after.refs_0_), custom_call_target="tpu_custom_call" | custom-call | tf_op jit(solution)/shard_map/pallas_call | solution.py:217
  75.1 0.0 copy-done.1
  75.1 0.0 copy-start.2
  75.1 3.8 %all-to-all-start.2 = ((bf16[16,8,4096]{2,1,0:T(8,128)(2,1)}), bf16[16,8,4096]{2,1,0:T(8,128)(2,1)S(1)}, u32[]{:S(2)}, u32[]{:S(2)}) async-start(bf16[16,8,4096]{2,1,0:T(8,128)(2,1)} %bitcast.7), calls=%async_computation.2 | async-start | bytes 2097152 | tf_op jit(solution)/shard_map/all_to_all | solution.py:224
  78.8 0.0 collective-permute-done.2.refs_1_
  78.9 3.7 %collective-permute-done.3.refs_2_ = bf16[192,1024]{1,0:T(8,128)(2,1)S(1)} collective-permute-done((bf16[192,1024]{1,0:T(8,128)(2,1)}, bf16[192,1024]{1,0:T(8,128)(2,1)S(1)}, u32[]{:S(2)}, u32[]{:S(2)}) %collective-permute-start.3) | collective-permute-done | bytes 393248 | tf_op jit(solution)/shard_map/ppermute | solution.py:27
  82.6 2.5 %collective-permute-done.4.refs_3_ = bf16[192,1024]{1,0:T(8,128)(2,1)S(1)} collective-permute-done((bf16[192,1024]{1,0:T(8,128)(2,1)}, bf16[192,1024]{1,0:T(8,128)(2,1)S(1)}, u32[]{:S(2)}, u32[]{:S(2)}) %collective-permute-start.4) | collective-permute-done | bytes 393248 | tf_op jit(solution)/shard_map/ppermute | solution.py:27
  85.0 0.0 copy-done.2
  85.1 0.7 shard_map.80
  85.7 3.8 %collective-permute-start.5 = (bf16[256,1024]{1,0:T(8,128)(2,1)S(1)}, bf16[256,1024]{1,0:T(8,128)(2,1)S(1)}, u32[]{:S(2)}, u32[]{:S(2)}) collective-permute-start(bf16[256,1024]{1,0:T(8,128)(2,1)S(1)} %shard_map.80), channel_id=1, source_target_pairs={{0,16},{16,0},{1,17},{17,1},{2,18},{18,2},{3,19},{19,3},{4,20},{20... | collective-permute-start | bytes 1572872 | tf_op jit(solution)/shard_map/ppermute | solution.py:27
  89.6 1.5 %collective-permute-done.5.refs_4_ = bf16[256,1024]{1,0:T(8,128)(2,1)S(1)} collective-permute-done((bf16[256,1024]{1,0:T(8,128)(2,1)S(1)}, bf16[256,1024]{1,0:T(8,128)(2,1)S(1)}, u32[]{:S(2)}, u32[]{:S(2)}) %collective-permute-start.5) | collective-permute-done | bytes 524320 | tf_op jit(solution)/shard_map/ppermute | solution.py:27
  91.1 1.3 %shard_map.81 = (bf16[256,256]{1,0:T(8,128)(2,1)S(1)}, bf16[256,256]{1,0:T(8,128)(2,1)S(1)}, bf16[256,256]{1,0:T(8,128)(2,1)S(1)}, bf16[256,256]{1,0:T(8,128)(2,1)S(1)}) custom-call(s32[4]{0:T(128)S(1)} %pad_add_fusion.places, bf16[192,1024]{1,0:T(8,128)(2,1)S(1)} %copy-done.2, bf16[192,1024]{1,0:T(8,128)(2,1)S(1)} %collective-permute-done.2.refs_1_, ...), custom_call_target="tpu_custom_call" | custom-call | tf_op jit(solution)/shard_map/pallas_call | solution.py:234
  92.4 4.2 %collective-permute-start.6 = (bf16[256,256]{1,0:T(8,128)(2,1)S(1)}, bf16[256,256]{1,0:T(8,128)(2,1)S(1)}, u32[]{:S(2)}, u32[]{:S(2)}) collective-permute-start(bf16[256,256]{1,0:T(8,128)(2,1)S(1)} %get-tuple-element.28), channel_id=1, source_target_pairs={{0,1},{1,2},{2,3},{3,0},{4,5},{5,6},{6,7},{7,4},{8,9},{9,10},{10,1... | collective-permute-start | bytes 393224 | tf_op jit(solution)/shard_map/ppermute | solution.py:27
  96.7 4.7 %collective-permute-start.7 = (bf16[256,256]{1,0:T(8,128)(2,1)S(1)}, bf16[256,256]{1,0:T(8,128)(2,1)S(1)}, u32[]{:S(2)}, u32[]{:S(2)}) collective-permute-start(bf16[256,256]{1,0:T(8,128)(2,1)S(1)} %get-tuple-element.29), channel_id=1, source_target_pairs={{0,2},{1,3},{2,0},{3,1},{4,6},{5,7},{6,4},{7,5},{8,10},{9,11},{10,... | collective-permute-start | bytes 393224 | tf_op jit(solution)/shard_map/ppermute | solution.py:27
  101.4 5.0 %collective-permute-start.8 = (bf16[256,256]{1,0:T(8,128)(2,1)S(1)}, bf16[256,256]{1,0:T(8,128)(2,1)S(1)}, u32[]{:S(2)}, u32[]{:S(2)}) collective-permute-start(bf16[256,256]{1,0:T(8,128)(2,1)S(1)} %get-tuple-element.30), channel_id=1, source_target_pairs={{0,3},{1,0},{2,1},{3,2},{4,7},{5,4},{6,5},{7,6},{8,11},{9,8},{10,9... | collective-permute-start | bytes 393224 | tf_op jit(solution)/shard_map/ppermute | solution.py:27
  106.4 0.6 constant_dynamic-slice_fusion
  107.0 0.0 collective-permute-done.6.refs_1_
  107.0 2.4 %collective-permute-done.7.refs_2_ = bf16[256,256]{1,0:T(8,128)(2,1)S(1)} collective-permute-done((bf16[256,256]{1,0:T(8,128)(2,1)S(1)}, bf16[256,256]{1,0:T(8,128)(2,1)S(1)}, u32[]{:S(2)}, u32[]{:S(2)}) %collective-permute-start.7) | collective-permute-done | bytes 131104 | tf_op jit(solution)/shard_map/ppermute | solution.py:27
  109.4 5.0 %collective-permute-done.8.refs_3_ = bf16[256,256]{1,0:T(8,128)(2,1)S(1)} collective-permute-done((bf16[256,256]{1,0:T(8,128)(2,1)S(1)}, bf16[256,256]{1,0:T(8,128)(2,1)S(1)}, u32[]{:S(2)}, u32[]{:S(2)}) %collective-permute-start.8) | collective-permute-done | bytes 131104 | tf_op jit(solution)/shard_map/ppermute | solution.py:27
  114.4 0.0 all-to-all-done.2.query_parts
  114.4 0.9 shard_map.82
  (1 shorter events, 0.0 us)
Async XLA Ops:
  0.6 14.8 %copy-start = (bf16[256,4096]{1,0:T(8,128)(2,1)S(1)}, bf16[256,4096]{1,0:T(8,128)(2,1)}, u32[]{:S(2)}) copy-start(bf16[256,4096]{1,0:T(8,128)(2,1)} %passages.3) | copy-start | bytes 6291460
  0.6 17.6 %copy-start.3 = (f32[1,256,256]{2,1,0:T(8,128)S(1)}, f32[1,256,256]{2,1,0:T(8,128)}, u32[]{:S(2)}) copy-start(f32[1,256,256]{2,1,0:T(8,128)} %param.7) | copy-start | bytes 786436
  3.4 38.0 %all-to-all-start = ((bf16[16,8,4224]{2,1,0:T(8,128)(2,1)}), bf16[16,8,4224]{2,1,0:T(8,128)(2,1)S(1)}, u32[]{:S(2)}, u32[]{:S(2)}) async-start(bf16[16,8,4224]{2,1,0:T(8,128)(2,1)} %broadcast_in_dim.4), calls=%async_computation | async-start | bytes 2162688 | tf_op jit(solution)/shard_map/all_to_all | solution.py:177
  15.4 26.0 %collective-permute-start = (bf16[256,4096]{1,0:T(8,128)(2,1)S(1)}, bf16[256,4096]{1,0:T(8,128)(2,1)}, u32[]{:S(2)}, u32[]{:S(2)}) collective-permute-start(bf16[256,4096]{1,0:T(8,128)(2,1)S(1)} %copy-done), channel_id=1, source_target_pairs={{0,16},{16,0},{1,17},{17,1},{2,18},{18,2},{3,19},{19,3},{4,20},{20... | collective-permute-start | bytes 6291464 | tf_op jit(solution)/shard_map/ppermute | solution.py:27
  19.2 3.9 %collective-permute-start.1 = (bf16[3,256,256]{2,1,0:T(8,128)(2,1)}, bf16[3,256,256]{2,1,0:T(8,128)(2,1)}, u32[]{:S(2)}, u32[]{:S(2)}) collective-permute-start(bf16[3,256,256]{2,1,0:T(8,128)(2,1)} %shard_map.76.teacher), channel_id=1, source_target_pairs={{0,16},{16,0},{1,17},{17,1},{2,18},{18,2},{3,19},{19,3},{4,20},{20... | collective-permute-start | bytes 1179656 | tf_op jit(solution)/shard_map/ppermute | solution.py:27
  61.2 13.9 %copy-start.1 = (bf16[192,1024]{1,0:T(8,128)(2,1)}, bf16[192,1024]{1,0:T(8,128)(2,1)S(1)}, u32[]{:S(2)}) copy-start(bf16[192,1024]{1,0:T(8,128)(2,1)S(1)} %get-tuple-element.23.after.refs_0_) | copy-start | bytes 1179652
  61.2 17.7 %collective-permute-start.2 = (bf16[192,1024]{1,0:T(8,128)(2,1)}, bf16[192,1024]{1,0:T(8,128)(2,1)S(1)}, u32[]{:S(2)}, u32[]{:S(2)}) collective-permute-start(bf16[192,1024]{1,0:T(8,128)(2,1)} %get-tuple-element.24), channel_id=1, source_target_pairs={{0,4},{4,8},{8,12},{12,0},{1,5},{5,9},{9,13},{13,1},{2,6},{6,10},{... | collective-permute-start | bytes 1179656 | tf_op jit(solution)/shard_map/ppermute | solution.py:27
  64.3 18.3 %collective-permute-start.3 = (bf16[192,1024]{1,0:T(8,128)(2,1)}, bf16[192,1024]{1,0:T(8,128)(2,1)S(1)}, u32[]{:S(2)}, u32[]{:S(2)}) collective-permute-start(bf16[192,1024]{1,0:T(8,128)(2,1)} %get-tuple-element.25), channel_id=1, source_target_pairs={{0,8},{4,12},{8,0},{12,4},{1,9},{5,13},{9,1},{13,5},{2,10},{6,14},... | collective-permute-start | bytes 1179656 | tf_op jit(solution)/shard_map/ppermute | solution.py:27
  68.7 16.4 %collective-permute-start.4 = (bf16[192,1024]{1,0:T(8,128)(2,1)}, bf16[192,1024]{1,0:T(8,128)(2,1)S(1)}, u32[]{:S(2)}, u32[]{:S(2)}) collective-permute-start(bf16[192,1024]{1,0:T(8,128)(2,1)} %get-tuple-element.26), channel_id=1, source_target_pairs={{0,12},{4,0},{8,4},{12,8},{1,13},{5,1},{9,5},{13,9},{2,14},{6,2},{... | collective-permute-start | bytes 1179656 | tf_op jit(solution)/shard_map/ppermute | solution.py:27
  75.1 10.0 %copy-start.2 = (bf16[192,1024]{1,0:T(8,128)(2,1)S(1)}, bf16[192,1024]{1,0:T(8,128)(2,1)}, u32[]{:S(2)}) copy-start(bf16[192,1024]{1,0:T(8,128)(2,1)} %copy-done.1) | copy-start | bytes 1179652
  75.1 39.3 %all-to-all-start.2 = ((bf16[16,8,4096]{2,1,0:T(8,128)(2,1)}), bf16[16,8,4096]{2,1,0:T(8,128)(2,1)S(1)}, u32[]{:S(2)}, u32[]{:S(2)}) async-start(bf16[16,8,4096]{2,1,0:T(8,128)(2,1)} %bitcast.7), calls=%async_computation.2 | async-start | bytes 2097152 | tf_op jit(solution)/shard_map/all_to_all | solution.py:224
  85.7 5.4 %collective-permute-start.5 = (bf16[256,1024]{1,0:T(8,128)(2,1)S(1)}, bf16[256,1024]{1,0:T(8,128)(2,1)S(1)}, u32[]{:S(2)}, u32[]{:S(2)}) collective-permute-start(bf16[256,1024]{1,0:T(8,128)(2,1)S(1)} %shard_map.80), channel_id=1, source_target_pairs={{0,16},{16,0},{1,17},{17,1},{2,18},{18,2},{3,19},{19,3},{4,20},{20... | collective-permute-start | bytes 1572872 | tf_op jit(solution)/shard_map/ppermute | solution.py:27
  92.4 14.6 %collective-permute-start.6 = (bf16[256,256]{1,0:T(8,128)(2,1)S(1)}, bf16[256,256]{1,0:T(8,128)(2,1)S(1)}, u32[]{:S(2)}, u32[]{:S(2)}) collective-permute-start(bf16[256,256]{1,0:T(8,128)(2,1)S(1)} %get-tuple-element.28), channel_id=1, source_target_pairs={{0,1},{1,2},{2,3},{3,0},{4,5},{5,6},{6,7},{7,4},{8,9},{9,10},{10,1... | collective-permute-start | bytes 393224 | tf_op jit(solution)/shard_map/ppermute | solution.py:27
  96.7 12.7 %collective-permute-start.7 = (bf16[256,256]{1,0:T(8,128)(2,1)S(1)}, bf16[256,256]{1,0:T(8,128)(2,1)S(1)}, u32[]{:S(2)}, u32[]{:S(2)}) collective-permute-start(bf16[256,256]{1,0:T(8,128)(2,1)S(1)} %get-tuple-element.29), channel_id=1, source_target_pairs={{0,2},{1,3},{2,0},{3,1},{4,6},{5,7},{6,4},{7,5},{8,10},{9,11},{10,... | collective-permute-start | bytes 393224 | tf_op jit(solution)/shard_map/ppermute | solution.py:27
  101.4 12.9 %collective-permute-start.8 = (bf16[256,256]{1,0:T(8,128)(2,1)S(1)}, bf16[256,256]{1,0:T(8,128)(2,1)S(1)}, u32[]{:S(2)}, u32[]{:S(2)}) collective-permute-start(bf16[256,256]{1,0:T(8,128)(2,1)S(1)} %get-tuple-element.30), channel_id=1, source_target_pairs={{0,3},{1,0},{2,1},{3,2},{4,7},{5,4},{6,5},{7,6},{8,11},{9,8},{10,9... | collective-permute-start | bytes 393224 | tf_op jit(solution)/shard_map/ppermute | solution.py:27

commit v15 on v14

--- a/solution.py
+++ b/solution.py
@@ -29,9 +29,8 @@
 
 def shifts(values, axis):
     size = len(values)
-    order = sorted(range(size), key=lambda d: -min(d, size - d))
-    moved = {d: shift(values[d], axis, d) for d in order}
-    return [moved[d] for d in range(size)]
+    order = sorted(range(size), key=lambda d: (-min(d, size - d), -d))
+    return [shift(values[d], axis, d) for d in order]
 
 
 def hits(positive, place, shape):

time: 116 us -> 112 us (0.966)
  waiting for transfers between devices: 35.4 us -> 33.1 us
  starting transfers between devices: 48.8 us -> 47 us
    ppermute x9, waiting for transfers between devices: 17 us -> 14.8 us  [shift(): lax.ppermute(value, axis, [(i, (i + by) % size) for i in range(size)])]
    ppermute x9, starting transfers between devices: 33.1 us -> 31.2 us  [shift(): lax.ppermute(value, axis, [(i, (i + by) % size) for i in range(size)])]
  transfers between devices with their start and end apart: 11 -> 11, of which waited for: 7 -> 5; matrix products, arithmetic and copies ran while one was open for 1% -> 1% of each run, Pallas kernels for 5% -> 6%
where the time goes in v15:
time: 112 us; the launch traced here: 111 us
  starting transfers between devices  47 us (42%)
  waiting for transfers between devices  33.1 us (30%)
  blocking collectives  14.4 us (13%)
  Pallas kernels  12.3 us (11%)
  other arithmetic  1.77 us (2%)
  local copies, waits for them, and re-layouts  1.66 us (1%)
    ppermute x9, starting transfers between devices, shift(): lax.ppermute(value, axis, [(i, (i + by) % size) for i in range(size)])  31.2 us
    all_to_all x1, waiting for transfers between devices, per_device(): lax.all_to_all(jnp.broadcast_to(sent[None], (chips,) + sent.shape), CHIPS...  18.3 us
    ppermute x9, waiting for transfers between devices, shift(): lax.ppermute(value, axis, [(i, (i + by) % size) for i in range(size)])  14.8 us
    all_to_all x1, blocking collectives, per_device(): stats = lax.all_to_all(stats, CHIPS, 0, 0, tiled=True)  14.4 us
    all_to_all x1, starting transfers between devices, per_device(): lax.all_to_all(jnp.broadcast_to(sent[None], (chips,) + sent.shape), CHIPS...  12 us
    all_to_all x1, starting transfers between devices, per_device(): lax.all_to_all(query_part.reshape(chips, own_rows, depth), CHIPS, 0, 0, t...  3.78 us
    pallas_call x1, Pallas kernels, per_device(): pl.pallas_call(score_kernel, out_shape=(jax.ShapeDtypeStruct((2 * CORES,...  3.46 us
    pallas_call x1, Pallas kernels, per_device(): pl.pallas_call(query_kernel, out_shape=jax.ShapeDtypeStruct((rows, depth)...  3.3 us
  transfers between devices with their start and end apart: 11, of which 5 were waited for; matrix products, arithmetic and copies ran while one was open for 1% of the time, Pallas kernels for 6%

profile of v15, /device:TPU:1, one launch (start us, length us, event | category | flops | bytes accessed | tf_op | source)
XLA Modules:
  0.0 111.1 jit_solution(9978805265743527925)
XLA Ops:
  0.6 0.0 copy-start
  0.6 0.0 copy-start.3
  0.7 0.8 and_convert_fusion.1
  1.5 0.8 pad_maximum_fusion
  2.3 1.1 broadcast_in_dim.4
  3.4 12.0 %all-to-all-start = ((bf16[16,8,4224]{2,1,0:T(8,128)(2,1)}), bf16[16,8,4224]{2,1,0:T(8,128)(2,1)S(1)}, u32[]{:S(2)}, u32[]{:S(2)}) async-start(bf16[16,8,4224]{2,1,0:T(8,128)(2,1)} %broadcast_in_dim.4), calls=%async_computation | async-start | bytes 2162688 | tf_op jit(solution)/shard_map/all_to_all | solution.py:176
  15.4 0.0 copy-done
  15.4 2.9 %collective-permute-start = (bf16[256,4096]{1,0:T(8,128)(2,1)S(1)}, bf16[256,4096]{1,0:T(8,128)(2,1)}, u32[]{:S(2)}, u32[]{:S(2)}) collective-permute-start(bf16[256,4096]{1,0:T(8,128)(2,1)S(1)} %copy-done), channel_id=1, source_target_pairs={{0,16},{16,0},{1,17},{17,1},{2,18},{18,2},{3,19},{19,3},{4,20},{20... | collective-permute-start | bytes 6291464 | tf_op jit(solution)/shard_map/ppermute | solution.py:27
  18.3 0.0 copy-done.3
  18.3 0.9 shard_map.76.teacher
  19.2 1.9 %collective-permute-start.1 = (bf16[3,256,256]{2,1,0:T(8,128)(2,1)}, bf16[3,256,256]{2,1,0:T(8,128)(2,1)}, u32[]{:S(2)}, u32[]{:S(2)}) collective-permute-start(bf16[3,256,256]{2,1,0:T(8,128)(2,1)} %shard_map.76.teacher), channel_id=1, source_target_pairs={{0,16},{16,0},{1,17},{17,1},{2,18},{18,2},{3,19},{19,3},{4,20},{20... | collective-permute-start | bytes 1179656 | tf_op jit(solution)/shard_map/ppermute | solution.py:27
  21.1 0.1 pad_add_fusion.places
  21.2 1.9 %collective-permute-done.1.teacher_other = bf16[3,256,256]{2,1,0:T(8,128)(2,1)} collective-permute-done((bf16[3,256,256]{2,1,0:T(8,128)(2,1)}, bf16[3,256,256]{2,1,0:T(8,128)(2,1)}, u32[]{:S(2)}, u32[]{:S(2)}) %collective-permute-start.1) | collective-permute-done | bytes 393248 | tf_op jit(solution)/shard_map/ppermute | solution.py:27
  23.1 18.3 %all-to-all-done = bf16[16,8,4224]{2,1,0:T(8,128)(2,1)S(1)} async-done(((bf16[16,8,4224]{2,1,0:T(8,128)(2,1)}), bf16[16,8,4224]{2,1,0:T(8,128)(2,1)S(1)}, u32[]{:S(2)}, u32[]{:S(2)}) %all-to-all-start) | async-done | bytes 1081376 | tf_op jit(solution)/shard_map/all_to_all | solution.py:176
  41.4 0.0 collective-permute-done.passages_other
  41.4 3.5 %shard_map.77 = (f32[4,256,128]{2,1,0:T(8,128)S(1)}, s32[1,128]{1,0:T(1,128)S(1)}, f32[16,8,128]{2,1,0:T(8,128)S(1)}) custom-call(s32[4]{0:T(128)S(1)} %pad_add_fusion.places, bf16[128,4224]{1,0:T(8,128)(2,1)S(1)} %bitcast.9, bf16[256,4096]{1,0:T(8,128)(2,1)S(1)} %copy-done, bf16[256,4096]{1,0:T(8,128)(2,1)} %collective-permute-done.passages_other, ...), custom_call_target="tpu_custom_call" | custom-call | tf_op jit(solution)/shard_map/pallas_call | solution.py:189
  44.9 14.4 %all_to_all.15.stats = f32[16,8,128]{2,1,0:T(8,128)S(1)} all-to-all(f32[16,8,128]{2,1,0:T(8,128)S(1)} %get-tuple-element.20), channel_id=1, replica_groups=mesh['yl'=2,'z'=8,'core'=2,'x'=4,'yh'=4] {'yl','z'}, dimensions={0} | all-to-all | bytes 131072 | tf_op jit(solution)/shard_map/all_to_all | solution.py:200
  59.4 1.8 %shard_map.78 = (bf16[2,256,128]{2,1,0:T(8,128)(2,1)S(1)}, f32[1,128]{1,0:T(1,128)S(1)}, bf16[192,1024]{1,0:T(8,128)(2,1)S(1)}, bf16[192,1024]{1,0:T(8,128)(2,1)...) custom-call(s32[4]{0:T(128)S(1)} %pad_add_fusion.places, bf16[128,4224]{1,0:T(8,128)(2,1)S(1)} %bitcast.10, ...), custom_call_target="tpu_custom_call" | custom-call | tf_op jit(solution)/shard_map/pallas_call | solution.py:202
  61.2 0.0 copy-start.1
  61.2 4.6 %collective-permute-start.2 = (bf16[192,1024]{1,0:T(8,128)(2,1)}, bf16[192,1024]{1,0:T(8,128)(2,1)S(1)}, u32[]{:S(2)}, u32[]{:S(2)}) collective-permute-start(bf16[192,1024]{1,0:T(8,128)(2,1)} %get-tuple-element.24), channel_id=1, source_target_pairs={{0,8},{4,12},{8,0},{12,4},{1,9},{5,13},{9,1},{13,5},{2,10},{6,14},... | collective-permute-start | bytes 1179656 | tf_op jit(solution)/shard_map/ppermute | solution.py:27
  65.8 2.8 %collective-permute-start.3 = (bf16[192,1024]{1,0:T(8,128)(2,1)}, bf16[192,1024]{1,0:T(8,128)(2,1)S(1)}, u32[]{:S(2)}, u32[]{:S(2)}) collective-permute-start(bf16[192,1024]{1,0:T(8,128)(2,1)} %get-tuple-element.25), channel_id=1, source_target_pairs={{0,12},{4,0},{8,4},{12,8},{1,13},{5,1},{9,5},{13,9},{2,14},{6,2},{... | collective-permute-start | bytes 1179656 | tf_op jit(solution)/shard_map/ppermute | solution.py:27
  68.6 2.5 %collective-permute-start.4 = (bf16[192,1024]{1,0:T(8,128)(2,1)}, bf16[192,1024]{1,0:T(8,128)(2,1)S(1)}, u32[]{:S(2)}, u32[]{:S(2)}) collective-permute-start(bf16[192,1024]{1,0:T(8,128)(2,1)} %get-tuple-element.26), channel_id=1, source_target_pairs={{0,4},{4,8},{8,12},{12,0},{1,5},{5,9},{9,13},{13,1},{2,6},{6,10},{... | collective-permute-start | bytes 1179656 | tf_op jit(solution)/shard_map/ppermute | solution.py:27
  71.1 3.3 %shard_map.79 = bf16[128,4096]{1,0:T(8,128)(2,1)} custom-call(bf16[2,256,128]{2,1,0:T(8,128)(2,1)S(1)} %get-tuple-element.22.grads, bf16[256,4096]{1,0:T(8,128)(2,1)S(1)} %copy-done, bf16[256,4096]{1,0:T(8,128)(2,1)} %collective-permute-done.passages_other, bf16[192,1024]{1,0:T(8,128)(2,1)S(1)} %get-tuple-element.23.after.refs_3_), custom_call_target="tpu_custom_call" | custom-call | tf_op jit(solution)/shard_map/pallas_call | solution.py:216
  74.4 0.0 copy-done.1
  74.4 0.0 copy-start.2
  74.4 3.8 %all-to-all-start.2 = ((bf16[16,8,4096]{2,1,0:T(8,128)(2,1)}), bf16[16,8,4096]{2,1,0:T(8,128)(2,1)S(1)}, u32[]{:S(2)}, u32[]{:S(2)}) async-start(bf16[16,8,4096]{2,1,0:T(8,128)(2,1)} %bitcast.7), calls=%async_computation.2 | async-start | bytes 2097152 | tf_op jit(solution)/shard_map/all_to_all | solution.py:223
  78.2 0.0 collective-permute-done.2.refs_0_
  78.2 5.2 %collective-permute-done.3.refs_1_ = bf16[192,1024]{1,0:T(8,128)(2,1)S(1)} collective-permute-done((bf16[192,1024]{1,0:T(8,128)(2,1)}, bf16[192,1024]{1,0:T(8,128)(2,1)S(1)}, u32[]{:S(2)}, u32[]{:S(2)}) %collective-permute-start.3) | collective-permute-done | bytes 393248 | tf_op jit(solution)/shard_map/ppermute | solution.py:27
  83.4 0.0 collective-permute-done.4.refs_2_
  83.4 0.0 copy-done.2
  83.4 0.7 shard_map.80
  84.1 3.8 %collective-permute-start.5 = (bf16[256,1024]{1,0:T(8,128)(2,1)S(1)}, bf16[256,1024]{1,0:T(8,128)(2,1)S(1)}, u32[]{:S(2)}, u32[]{:S(2)}) collective-permute-start(bf16[256,1024]{1,0:T(8,128)(2,1)S(1)} %shard_map.80), channel_id=1, source_target_pairs={{0,16},{16,0},{1,17},{17,1},{2,18},{18,2},{3,19},{19,3},{4,20},{20... | collective-permute-start | bytes 1572872 | tf_op jit(solution)/shard_map/ppermute | solution.py:27
  87.9 1.5 %collective-permute-done.5.refs_4_ = bf16[256,1024]{1,0:T(8,128)(2,1)S(1)} collective-permute-done((bf16[256,1024]{1,0:T(8,128)(2,1)S(1)}, bf16[256,1024]{1,0:T(8,128)(2,1)S(1)}, u32[]{:S(2)}, u32[]{:S(2)}) %collective-permute-start.5) | collective-permute-done | bytes 524320 | tf_op jit(solution)/shard_map/ppermute | solution.py:27
  89.4 1.3 %shard_map.81 = (bf16[256,256]{1,0:T(8,128)(2,1)S(1)}, bf16[256,256]{1,0:T(8,128)(2,1)S(1)}, bf16[256,256]{1,0:T(8,128)(2,1)S(1)}, bf16[256,256]{1,0:T(8,128)(2,1)S(1)}) custom-call(s32[4]{0:T(128)S(1)} %pad_add_fusion.places, bf16[192,1024]{1,0:T(8,128)(2,1)S(1)} %collective-permute-done.2.refs_0_, bf16[192,1024]{1,0:T(8,128)(2,1)S(1)} %collective-permute-done.3.refs_1_, ...), custom_call_target="tpu_custom_call" | custom-call | tf_op jit(solution)/shard_map/pallas_call | solution.py:233
  90.8 6.6 %collective-permute-start.6 = (bf16[256,256]{1,0:T(8,128)(2,1)S(1)}, bf16[256,256]{1,0:T(8,128)(2,1)S(1)}, u32[]{:S(2)}, u32[]{:S(2)}) collective-permute-start(bf16[256,256]{1,0:T(8,128)(2,1)S(1)} %get-tuple-element.27), channel_id=1, source_target_pairs={{0,2},{1,3},{2,0},{3,1},{4,6},{5,7},{6,4},{7,5},{8,10},{9,11},{10,... | collective-permute-start | bytes 393224 | tf_op jit(solution)/shard_map/ppermute | solution.py:27
  97.3 2.9 %collective-permute-start.7 = (bf16[256,256]{1,0:T(8,128)(2,1)S(1)}, bf16[256,256]{1,0:T(8,128)(2,1)S(1)}, u32[]{:S(2)}, u32[]{:S(2)}) collective-permute-start(bf16[256,256]{1,0:T(8,128)(2,1)S(1)} %get-tuple-element.28), channel_id=1, source_target_pairs={{0,3},{1,0},{2,1},{3,2},{4,7},{5,4},{6,5},{7,6},{8,11},{9,8},{10,9... | collective-permute-start | bytes 393224 | tf_op jit(solution)/shard_map/ppermute | solution.py:27
  100.2 3.3 %collective-permute-start.8 = (bf16[256,256]{1,0:T(8,128)(2,1)S(1)}, bf16[256,256]{1,0:T(8,128)(2,1)S(1)}, u32[]{:S(2)}, u32[]{:S(2)}) collective-permute-start(bf16[256,256]{1,0:T(8,128)(2,1)S(1)} %get-tuple-element.29), channel_id=1, source_target_pairs={{0,1},{1,2},{2,3},{3,0},{4,5},{5,6},{6,7},{7,4},{8,9},{9,10},{10,1... | collective-permute-start | bytes 393224 | tf_op jit(solution)/shard_map/ppermute | solution.py:27
  103.5 0.6 constant_dynamic-slice_fusion
  104.1 0.0 collective-permute-done.6.refs_0_
  104.1 6.2 %collective-permute-done.7.refs_1_ = bf16[256,256]{1,0:T(8,128)(2,1)S(1)} collective-permute-done((bf16[256,256]{1,0:T(8,128)(2,1)S(1)}, bf16[256,256]{1,0:T(8,128)(2,1)S(1)}, u32[]{:S(2)}, u32[]{:S(2)}) %collective-permute-start.7) | collective-permute-done | bytes 131104 | tf_op jit(solution)/shard_map/ppermute | solution.py:27
  110.3 0.0 collective-permute-done.8.refs_2_
  110.3 0.0 all-to-all-done.2.query_parts
  110.3 0.9 shard_map.82
  (1 shorter events, 0.0 us)
Async XLA Ops:
  0.6 14.8 %copy-start = (bf16[256,4096]{1,0:T(8,128)(2,1)S(1)}, bf16[256,4096]{1,0:T(8,128)(2,1)}, u32[]{:S(2)}) copy-start(bf16[256,4096]{1,0:T(8,128)(2,1)} %passages.3) | copy-start | bytes 6291460
  0.6 17.6 %copy-start.3 = (f32[1,256,256]{2,1,0:T(8,128)S(1)}, f32[1,256,256]{2,1,0:T(8,128)}, u32[]{:S(2)}) copy-start(f32[1,256,256]{2,1,0:T(8,128)} %param.7) | copy-start | bytes 786436
  3.4 38.0 %all-to-all-start = ((bf16[16,8,4224]{2,1,0:T(8,128)(2,1)}), bf16[16,8,4224]{2,1,0:T(8,128)(2,1)S(1)}, u32[]{:S(2)}, u32[]{:S(2)}) async-start(bf16[16,8,4224]{2,1,0:T(8,128)(2,1)} %broadcast_in_dim.4), calls=%async_computation | async-start | bytes 2162688 | tf_op jit(solution)/shard_map/all_to_all | solution.py:176
  15.4 26.0 %collective-permute-start = (bf16[256,4096]{1,0:T(8,128)(2,1)S(1)}, bf16[256,4096]{1,0:T(8,128)(2,1)}, u32[]{:S(2)}, u32[]{:S(2)}) collective-permute-start(bf16[256,4096]{1,0:T(8,128)(2,1)S(1)} %copy-done), channel_id=1, source_target_pairs={{0,16},{16,0},{1,17},{17,1},{2,18},{18,2},{3,19},{19,3},{4,20},{20... | collective-permute-start | bytes 6291464 | tf_op jit(solution)/shard_map/ppermute | solution.py:27
  19.2 3.9 %collective-permute-start.1 = (bf16[3,256,256]{2,1,0:T(8,128)(2,1)}, bf16[3,256,256]{2,1,0:T(8,128)(2,1)}, u32[]{:S(2)}, u32[]{:S(2)}) collective-permute-start(bf16[3,256,256]{2,1,0:T(8,128)(2,1)} %shard_map.76.teacher), channel_id=1, source_target_pairs={{0,16},{16,0},{1,17},{17,1},{2,18},{18,2},{3,19},{19,3},{4,20},{20... | collective-permute-start | bytes 1179656 | tf_op jit(solution)/shard_map/ppermute | solution.py:27
  61.2 13.2 %copy-start.1 = (bf16[192,1024]{1,0:T(8,128)(2,1)}, bf16[192,1024]{1,0:T(8,128)(2,1)S(1)}, u32[]{:S(2)}) copy-start(bf16[192,1024]{1,0:T(8,128)(2,1)S(1)} %get-tuple-element.23.after.refs_3_) | copy-start | bytes 1179652
  61.2 17.0 %collective-permute-start.2 = (bf16[192,1024]{1,0:T(8,128)(2,1)}, bf16[192,1024]{1,0:T(8,128)(2,1)S(1)}, u32[]{:S(2)}, u32[]{:S(2)}) collective-permute-start(bf16[192,1024]{1,0:T(8,128)(2,1)} %get-tuple-element.24), channel_id=1, source_target_pairs={{0,8},{4,12},{8,0},{12,4},{1,9},{5,13},{9,1},{13,5},{2,10},{6,14},... | collective-permute-start | bytes 1179656 | tf_op jit(solution)/shard_map/ppermute | solution.py:27
  65.8 17.6 %collective-permute-start.3 = (bf16[192,1024]{1,0:T(8,128)(2,1)}, bf16[192,1024]{1,0:T(8,128)(2,1)S(1)}, u32[]{:S(2)}, u32[]{:S(2)}) collective-permute-start(bf16[192,1024]{1,0:T(8,128)(2,1)} %get-tuple-element.25), channel_id=1, source_target_pairs={{0,12},{4,0},{8,4},{12,8},{1,13},{5,1},{9,5},{13,9},{2,14},{6,2},{... | collective-permute-start | bytes 1179656 | tf_op jit(solution)/shard_map/ppermute | solution.py:27
  68.6 14.8 %collective-permute-start.4 = (bf16[192,1024]{1,0:T(8,128)(2,1)}, bf16[192,1024]{1,0:T(8,128)(2,1)S(1)}, u32[]{:S(2)}, u32[]{:S(2)}) collective-permute-start(bf16[192,1024]{1,0:T(8,128)(2,1)} %get-tuple-element.26), channel_id=1, source_target_pairs={{0,4},{4,8},{8,12},{12,0},{1,5},{5,9},{9,13},{13,1},{2,6},{6,10},{... | collective-permute-start | bytes 1179656 | tf_op jit(solution)/shard_map/ppermute | solution.py:27
  74.4 9.0 %copy-start.2 = (bf16[192,1024]{1,0:T(8,128)(2,1)S(1)}, bf16[192,1024]{1,0:T(8,128)(2,1)}, u32[]{:S(2)}) copy-start(bf16[192,1024]{1,0:T(8,128)(2,1)} %copy-done.1) | copy-start | bytes 1179652
  74.4 35.8 %all-to-all-start.2 = ((bf16[16,8,4096]{2,1,0:T(8,128)(2,1)}), bf16[16,8,4096]{2,1,0:T(8,128)(2,1)S(1)}, u32[]{:S(2)}, u32[]{:S(2)}) async-start(bf16[16,8,4096]{2,1,0:T(8,128)(2,1)} %bitcast.7), calls=%async_computation.2 | async-start | bytes 2097152 | tf_op jit(solution)/shard_map/all_to_all | solution.py:223
  84.1 5.3 %collective-permute-start.5 = (bf16[256,1024]{1,0:T(8,128)(2,1)S(1)}, bf16[256,1024]{1,0:T(8,128)(2,1)S(1)}, u32[]{:S(2)}, u32[]{:S(2)}) collective-permute-start(bf16[256,1024]{1,0:T(8,128)(2,1)S(1)} %shard_map.80), channel_id=1, source_target_pairs={{0,16},{16,0},{1,17},{17,1},{2,18},{18,2},{3,19},{19,3},{4,20},{20... | collective-permute-start | bytes 1572872 | tf_op jit(solution)/shard_map/ppermute | solution.py:27
  90.8 13.4 %collective-permute-start.6 = (bf16[256,256]{1,0:T(8,128)(2,1)S(1)}, bf16[256,256]{1,0:T(8,128)(2,1)S(1)}, u32[]{:S(2)}, u32[]{:S(2)}) collective-permute-start(bf16[256,256]{1,0:T(8,128)(2,1)S(1)} %get-tuple-element.27), channel_id=1, source_target_pairs={{0,2},{1,3},{2,0},{3,1},{4,6},{5,7},{6,4},{7,5},{8,10},{9,11},{10,... | collective-permute-start | bytes 393224 | tf_op jit(solution)/shard_map/ppermute | solution.py:27
  97.3 13.0 %collective-permute-start.7 = (bf16[256,256]{1,0:T(8,128)(2,1)S(1)}, bf16[256,256]{1,0:T(8,128)(2,1)S(1)}, u32[]{:S(2)}, u32[]{:S(2)}) collective-permute-start(bf16[256,256]{1,0:T(8,128)(2,1)S(1)} %get-tuple-element.28), channel_id=1, source_target_pairs={{0,3},{1,0},{2,1},{3,2},{4,7},{5,4},{6,5},{7,6},{8,11},{9,8},{10,9... | collective-permute-start | bytes 393224 | tf_op jit(solution)/shard_map/ppermute | solution.py:27
  100.2 10.1 %collective-permute-start.8 = (bf16[256,256]{1,0:T(8,128)(2,1)S(1)}, bf16[256,256]{1,0:T(8,128)(2,1)S(1)}, u32[]{:S(2)}, u32[]{:S(2)}) collective-permute-start(bf16[256,256]{1,0:T(8,128)(2,1)S(1)} %get-tuple-element.29), channel_id=1, source_target_pairs={{0,1},{1,2},{2,3},{3,0},{4,5},{5,6},{6,7},{7,4},{8,9},{9,10},{10,1... | collective-permute-start | bytes 393224 | tf_op jit(solution)/shard_map/ppermute | solution.py:27

commit v16 on v15

--- a/solution.py
+++ b/solution.py
@@ -29,7 +29,7 @@
 
 def shifts(values, axis):
     size = len(values)
-    order = sorted(range(size), key=lambda d: (-min(d, size - d), -d))
+    order = list(reversed(range(size)))
     return [shift(values[d], axis, d) for d in order]
 
 

time: 112 us -> 117 us (1.045); the launches traced: 111 us -> 115 us
  waiting for transfers between devices: 33.1 us -> 38.9 us
  starting transfers between devices: 47 us -> 45 us
    ppermute x9, waiting for transfers between devices: 14.8 us -> 20.5 us  [shift(): lax.ppermute(value, axis, [(i, (i + by) % size) for i in range(size)])]
    ppermute x9, starting transfers between devices: 31.2 us -> 29.2 us  [shift(): lax.ppermute(value, axis, [(i, (i + by) % size) for i in range(size)])]
  transfers between devices with their start and end apart: 11 -> 11, of which waited for: 5 -> 6; matrix products, arithmetic and copies ran while one was open for 1% -> 1% of each run, Pallas kernels for 6% -> 5%
where the time goes in v16:
time: 117 us; the launch traced here: 115 us
  starting transfers between devices  45 us (38%)
  waiting for transfers between devices  38.9 us (33%)
  blocking collectives  14.4 us (12%)
  Pallas kernels  12.3 us (11%)
  other arithmetic  1.77 us (2%)
  local copies, waits for them, and re-layouts  1.66 us (1%)
    ppermute x9, starting transfers between devices, shift(): lax.ppermute(value, axis, [(i, (i + by) % size) for i in range(size)])  29.2 us
    ppermute x9, waiting for transfers between devices, shift(): lax.ppermute(value, axis, [(i, (i + by) % size) for i in range(size)])  20.5 us
    all_to_all x1, waiting for transfers between devices, per_device(): lax.all_to_all(jnp.broadcast_to(sent[None], (chips,) + sent.shape), CHIPS...  18.3 us
    all_to_all x1, blocking collectives, per_device(): stats = lax.all_to_all(stats, CHIPS, 0, 0, tiled=True)  14.4 us
    all_to_all x1, starting transfers between devices, per_device(): lax.all_to_all(jnp.broadcast_to(sent[None], (chips,) + sent.shape), CHIPS...  12 us
    all_to_all x1, starting transfers between devices, per_device(): lax.all_to_all(query_part.reshape(chips, own_rows, depth), CHIPS, 0, 0, t...  3.78 us
    pallas_call x1, Pallas kernels, per_device(): pl.pallas_call(score_kernel, out_shape=(jax.ShapeDtypeStruct((2 * CORES,...  3.46 us
    pallas_call x1, Pallas kernels, per_device(): pl.pallas_call(query_kernel, out_shape=jax.ShapeDtypeStruct((rows, depth)...  3.31 us
  transfers between devices with their start and end apart: 11, of which 6 were waited for; matrix products, arithmetic and copies ran while one was open for 1% of the time, Pallas kernels for 5%

profile of v16, /device:TPU:1, one launch (start us, length us, event | category | flops | bytes accessed | tf_op | source)
XLA Modules:
  0.0 114.9 jit_solution(9749726463800075004)
XLA Ops:
  0.6 0.0 copy-start
  0.6 0.0 copy-start.3
  0.7 0.8 and_convert_fusion.1
  1.5 0.8 pad_maximum_fusion
  2.3 1.1 broadcast_in_dim.4
  3.4 12.0 %all-to-all-start = ((bf16[16,8,4224]{2,1,0:T(8,128)(2,1)}), bf16[16,8,4224]{2,1,0:T(8,128)(2,1)S(1)}, u32[]{:S(2)}, u32[]{:S(2)}) async-start(bf16[16,8,4224]{2,1,0:T(8,128)(2,1)} %broadcast_in_dim.4), calls=%async_computation | async-start | bytes 2162688 | tf_op jit(solution)/shard_map/all_to_all | solution.py:176
  15.4 0.0 copy-done
  15.4 2.9 %collective-permute-start = (bf16[256,4096]{1,0:T(8,128)(2,1)S(1)}, bf16[256,4096]{1,0:T(8,128)(2,1)}, u32[]{:S(2)}, u32[]{:S(2)}) collective-permute-start(bf16[256,4096]{1,0:T(8,128)(2,1)S(1)} %copy-done), channel_id=1, source_target_pairs={{0,16},{16,0},{1,17},{17,1},{2,18},{18,2},{3,19},{19,3},{4,20},{20... | collective-permute-start | bytes 6291464 | tf_op jit(solution)/shard_map/ppermute | solution.py:27
  18.3 0.0 copy-done.3
  18.3 0.9 shard_map.76.teacher
  19.2 1.9 %collective-permute-start.1 = (bf16[3,256,256]{2,1,0:T(8,128)(2,1)}, bf16[3,256,256]{2,1,0:T(8,128)(2,1)}, u32[]{:S(2)}, u32[]{:S(2)}) collective-permute-start(bf16[3,256,256]{2,1,0:T(8,128)(2,1)} %shard_map.76.teacher), channel_id=1, source_target_pairs={{0,16},{16,0},{1,17},{17,1},{2,18},{18,2},{3,19},{19,3},{4,20},{20... | collective-permute-start | bytes 1179656 | tf_op jit(solution)/shard_map/ppermute | solution.py:27
  21.1 0.1 pad_add_fusion.places
  21.2 1.9 %collective-permute-done.1.teacher_other = bf16[3,256,256]{2,1,0:T(8,128)(2,1)} collective-permute-done((bf16[3,256,256]{2,1,0:T(8,128)(2,1)}, bf16[3,256,256]{2,1,0:T(8,128)(2,1)}, u32[]{:S(2)}, u32[]{:S(2)}) %collective-permute-start.1) | collective-permute-done | bytes 393248 | tf_op jit(solution)/shard_map/ppermute | solution.py:27
  23.1 18.3 %all-to-all-done = bf16[16,8,4224]{2,1,0:T(8,128)(2,1)S(1)} async-done(((bf16[16,8,4224]{2,1,0:T(8,128)(2,1)}), bf16[16,8,4224]{2,1,0:T(8,128)(2,1)S(1)}, u32[]{:S(2)}, u32[]{:S(2)}) %all-to-all-start) | async-done | bytes 1081376 | tf_op jit(solution)/shard_map/all_to_all | solution.py:176
  41.4 0.0 collective-permute-done.passages_other
  41.4 3.5 %shard_map.77 = (f32[4,256,128]{2,1,0:T(8,128)S(1)}, s32[1,128]{1,0:T(1,128)S(1)}, f32[16,8,128]{2,1,0:T(8,128)S(1)}) custom-call(s32[4]{0:T(128)S(1)} %pad_add_fusion.places, bf16[128,4224]{1,0:T(8,128)(2,1)S(1)} %bitcast.9, bf16[256,4096]{1,0:T(8,128)(2,1)S(1)} %copy-done, bf16[256,4096]{1,0:T(8,128)(2,1)} %collective-permute-done.passages_other, ...), custom_call_target="tpu_custom_call" | custom-call | tf_op jit(solution)/shard_map/pallas_call | solution.py:189
  44.9 14.4 %all_to_all.15.stats = f32[16,8,128]{2,1,0:T(8,128)S(1)} all-to-all(f32[16,8,128]{2,1,0:T(8,128)S(1)} %get-tuple-element.20), channel_id=1, replica_groups=mesh['yl'=2,'z'=8,'core'=2,'x'=4,'yh'=4] {'yl','z'}, dimensions={0} | all-to-all | bytes 131072 | tf_op jit(solution)/shard_map/all_to_all | solution.py:200
  59.4 1.8 %shard_map.78 = (bf16[2,256,128]{2,1,0:T(8,128)(2,1)S(1)}, f32[1,128]{1,0:T(1,128)S(1)}, bf16[192,1024]{1,0:T(8,128)(2,1)S(1)}, bf16[192,1024]{1,0:T(8,128)(2,1)...) custom-call(s32[4]{0:T(128)S(1)} %pad_add_fusion.places, bf16[128,4224]{1,0:T(8,128)(2,1)S(1)} %bitcast.10, ...), custom_call_target="tpu_custom_call" | custom-call | tf_op jit(solution)/shard_map/pallas_call | solution.py:202
  61.2 0.0 copy-start.1
  61.2 4.4 %collective-permute-start.2 = (bf16[192,1024]{1,0:T(8,128)(2,1)}, bf16[192,1024]{1,0:T(8,128)(2,1)S(1)}, u32[]{:S(2)}, u32[]{:S(2)}) collective-permute-start(bf16[192,1024]{1,0:T(8,128)(2,1)} %get-tuple-element.24), channel_id=1, source_target_pairs={{0,12},{4,0},{8,4},{12,8},{1,13},{5,1},{9,5},{13,9},{2,14},{6,2},{... | collective-permute-start | bytes 1179656 | tf_op jit(solution)/shard_map/ppermute | solution.py:27
  65.6 2.4 %collective-permute-start.3 = (bf16[192,1024]{1,0:T(8,128)(2,1)}, bf16[192,1024]{1,0:T(8,128)(2,1)S(1)}, u32[]{:S(2)}, u32[]{:S(2)}) collective-permute-start(bf16[192,1024]{1,0:T(8,128)(2,1)} %get-tuple-element.25), channel_id=1, source_target_pairs={{0,8},{4,12},{8,0},{12,4},{1,9},{5,13},{9,1},{13,5},{2,10},{6,14},... | collective-permute-start | bytes 1179656 | tf_op jit(solution)/shard_map/ppermute | solution.py:27
  68.0 2.5 %collective-permute-start.4 = (bf16[192,1024]{1,0:T(8,128)(2,1)}, bf16[192,1024]{1,0:T(8,128)(2,1)S(1)}, u32[]{:S(2)}, u32[]{:S(2)}) collective-permute-start(bf16[192,1024]{1,0:T(8,128)(2,1)} %get-tuple-element.26), channel_id=1, source_target_pairs={{0,4},{4,8},{8,12},{12,0},{1,5},{5,9},{9,13},{13,1},{2,6},{6,10},{... | collective-permute-start | bytes 1179656 | tf_op jit(solution)/shard_map/ppermute | solution.py:27
  70.5 3.3 %shard_map.79 = bf16[128,4096]{1,0:T(8,128)(2,1)} custom-call(bf16[2,256,128]{2,1,0:T(8,128)(2,1)S(1)} %get-tuple-element.22.grads, bf16[256,4096]{1,0:T(8,128)(2,1)S(1)} %copy-done, bf16[256,4096]{1,0:T(8,128)(2,1)} %collective-permute-done.passages_other, bf16[192,1024]{1,0:T(8,128)(2,1)S(1)} %get-tuple-element.23.after.refs_3_), custom_call_target="tpu_custom_call" | custom-call | tf_op jit(solution)/shard_map/pallas_call | solution.py:216
  73.8 0.0 copy-done.1
  73.8 0.0 copy-start.2
  73.8 3.8 %all-to-all-start.2 = ((bf16[16,8,4096]{2,1,0:T(8,128)(2,1)}), bf16[16,8,4096]{2,1,0:T(8,128)(2,1)S(1)}, u32[]{:S(2)}, u32[]{:S(2)}) async-start(bf16[16,8,4096]{2,1,0:T(8,128)(2,1)} %bitcast.7), calls=%async_computation.2 | async-start | bytes 2097152 | tf_op jit(solution)/shard_map/all_to_all | solution.py:223
  77.6 0.0 collective-permute-done.2.refs_0_
  77.6 0.0 collective-permute-done.3.refs_1_
  77.7 11.0 %collective-permute-done.4.refs_2_ = bf16[192,1024]{1,0:T(8,128)(2,1)S(1)} collective-permute-done((bf16[192,1024]{1,0:T(8,128)(2,1)}, bf16[192,1024]{1,0:T(8,128)(2,1)S(1)}, u32[]{:S(2)}, u32[]{:S(2)}) %collective-permute-start.4) | collective-permute-done | bytes 393248 | tf_op jit(solution)/shard_map/ppermute | solution.py:27
  88.6 0.0 copy-done.2
  88.7 0.7 shard_map.80
  89.3 2.4 %collective-permute-start.5 = (bf16[256,1024]{1,0:T(8,128)(2,1)S(1)}, bf16[256,1024]{1,0:T(8,128)(2,1)S(1)}, u32[]{:S(2)}, u32[]{:S(2)}) collective-permute-start(bf16[256,1024]{1,0:T(8,128)(2,1)S(1)} %shard_map.80), channel_id=1, source_target_pairs={{0,16},{16,0},{1,17},{17,1},{2,18},{18,2},{3,19},{19,3},{4,20},{20... | collective-permute-start | bytes 1572872 | tf_op jit(solution)/shard_map/ppermute | solution.py:27
  91.7 1.5 %collective-permute-done.5.refs_4_ = bf16[256,1024]{1,0:T(8,128)(2,1)S(1)} collective-permute-done((bf16[256,1024]{1,0:T(8,128)(2,1)S(1)}, bf16[256,1024]{1,0:T(8,128)(2,1)S(1)}, u32[]{:S(2)}, u32[]{:S(2)}) %collective-permute-start.5) | collective-permute-done | bytes 524320 | tf_op jit(solution)/shard_map/ppermute | solution.py:27
  93.3 1.3 %shard_map.81 = (bf16[256,256]{1,0:T(8,128)(2,1)S(1)}, bf16[256,256]{1,0:T(8,128)(2,1)S(1)}, bf16[256,256]{1,0:T(8,128)(2,1)S(1)}, bf16[256,256]{1,0:T(8,128)(2,1)S(1)}) custom-call(s32[4]{0:T(128)S(1)} %pad_add_fusion.places, bf16[192,1024]{1,0:T(8,128)(2,1)S(1)} %collective-permute-done.2.refs_0_, bf16[192,1024]{1,0:T(8,128)(2,1)S(1)} %collective-permute-done.3.refs_1_, ...), custom_call_target="tpu_custom_call" | custom-call | tf_op jit(solution)/shard_map/pallas_call | solution.py:233
  94.6 5.0 %collective-permute-start.6 = (bf16[256,256]{1,0:T(8,128)(2,1)S(1)}, bf16[256,256]{1,0:T(8,128)(2,1)S(1)}, u32[]{:S(2)}, u32[]{:S(2)}) collective-permute-start(bf16[256,256]{1,0:T(8,128)(2,1)S(1)} %get-tuple-element.27), channel_id=1, source_target_pairs={{0,3},{1,0},{2,1},{3,2},{4,7},{5,4},{6,5},{7,6},{8,11},{9,8},{10,9... | collective-permute-start | bytes 393224 | tf_op jit(solution)/shard_map/ppermute | solution.py:27
  99.6 4.5 %collective-permute-start.7 = (bf16[256,256]{1,0:T(8,128)(2,1)S(1)}, bf16[256,256]{1,0:T(8,128)(2,1)S(1)}, u32[]{:S(2)}, u32[]{:S(2)}) collective-permute-start(bf16[256,256]{1,0:T(8,128)(2,1)S(1)} %get-tuple-element.28), channel_id=1, source_target_pairs={{0,2},{1,3},{2,0},{3,1},{4,6},{5,7},{6,4},{7,5},{8,10},{9,11},{10,... | collective-permute-start | bytes 393224 | tf_op jit(solution)/shard_map/ppermute | solution.py:27
  104.0 3.3 %collective-permute-start.8 = (bf16[256,256]{1,0:T(8,128)(2,1)S(1)}, bf16[256,256]{1,0:T(8,128)(2,1)S(1)}, u32[]{:S(2)}, u32[]{:S(2)}) collective-permute-start(bf16[256,256]{1,0:T(8,128)(2,1)S(1)} %get-tuple-element.29), channel_id=1, source_target_pairs={{0,1},{1,2},{2,3},{3,0},{4,5},{5,6},{6,7},{7,4},{8,9},{9,10},{10,1... | collective-permute-start | bytes 393224 | tf_op jit(solution)/shard_map/ppermute | solution.py:27
  107.3 0.6 constant_dynamic-slice_fusion
  107.9 0.0 collective-permute-done.6.refs_0_
  107.9 2.9 %collective-permute-done.7.refs_1_ = bf16[256,256]{1,0:T(8,128)(2,1)S(1)} collective-permute-done((bf16[256,256]{1,0:T(8,128)(2,1)S(1)}, bf16[256,256]{1,0:T(8,128)(2,1)S(1)}, u32[]{:S(2)}, u32[]{:S(2)}) %collective-permute-start.7) | collective-permute-done | bytes 131104 | tf_op jit(solution)/shard_map/ppermute | solution.py:27
  110.8 3.2 %collective-permute-done.8.refs_2_ = bf16[256,256]{1,0:T(8,128)(2,1)S(1)} collective-permute-done((bf16[256,256]{1,0:T(8,128)(2,1)S(1)}, bf16[256,256]{1,0:T(8,128)(2,1)S(1)}, u32[]{:S(2)}, u32[]{:S(2)}) %collective-permute-start.8) | collective-permute-done | bytes 131104 | tf_op jit(solution)/shard_map/ppermute | solution.py:27
  114.0 0.0 all-to-all-done.2.query_parts
  114.0 0.9 shard_map.82
  (1 shorter events, 0.0 us)
Async XLA Ops:
  0.6 14.8 %copy-start = (bf16[256,4096]{1,0:T(8,128)(2,1)S(1)}, bf16[256,4096]{1,0:T(8,128)(2,1)}, u32[]{:S(2)}) copy-start(bf16[256,4096]{1,0:T(8,128)(2,1)} %passages.3) | copy-start | bytes 6291460
  0.6 17.6 %copy-start.3 = (f32[1,256,256]{2,1,0:T(8,128)S(1)}, f32[1,256,256]{2,1,0:T(8,128)}, u32[]{:S(2)}) copy-start(f32[1,256,256]{2,1,0:T(8,128)} %param.7) | copy-start | bytes 786436
  3.4 38.0 %all-to-all-start = ((bf16[16,8,4224]{2,1,0:T(8,128)(2,1)}), bf16[16,8,4224]{2,1,0:T(8,128)(2,1)S(1)}, u32[]{:S(2)}, u32[]{:S(2)}) async-start(bf16[16,8,4224]{2,1,0:T(8,128)(2,1)} %broadcast_in_dim.4), calls=%async_computation | async-start | bytes 2162688 | tf_op jit(solution)/shard_map/all_to_all | solution.py:176
  15.4 26.0 %collective-permute-start = (bf16[256,4096]{1,0:T(8,128)(2,1)S(1)}, bf16[256,4096]{1,0:T(8,128)(2,1)}, u32[]{:S(2)}, u32[]{:S(2)}) collective-permute-start(bf16[256,4096]{1,0:T(8,128)(2,1)S(1)} %copy-done), channel_id=1, source_target_pairs={{0,16},{16,0},{1,17},{17,1},{2,18},{18,2},{3,19},{19,3},{4,20},{20... | collective-permute-start | bytes 6291464 | tf_op jit(solution)/shard_map/ppermute | solution.py:27
  19.2 3.9 %collective-permute-start.1 = (bf16[3,256,256]{2,1,0:T(8,128)(2,1)}, bf16[3,256,256]{2,1,0:T(8,128)(2,1)}, u32[]{:S(2)}, u32[]{:S(2)}) collective-permute-start(bf16[3,256,256]{2,1,0:T(8,128)(2,1)} %shard_map.76.teacher), channel_id=1, source_target_pairs={{0,16},{16,0},{1,17},{17,1},{2,18},{18,2},{3,19},{19,3},{4,20},{20... | collective-permute-start | bytes 1179656 | tf_op jit(solution)/shard_map/ppermute | solution.py:27
  61.2 12.7 %copy-start.1 = (bf16[192,1024]{1,0:T(8,128)(2,1)}, bf16[192,1024]{1,0:T(8,128)(2,1)S(1)}, u32[]{:S(2)}) copy-start(bf16[192,1024]{1,0:T(8,128)(2,1)S(1)} %get-tuple-element.23.after.refs_3_) | copy-start | bytes 1179652
  61.2 16.4 %collective-permute-start.2 = (bf16[192,1024]{1,0:T(8,128)(2,1)}, bf16[192,1024]{1,0:T(8,128)(2,1)S(1)}, u32[]{:S(2)}, u32[]{:S(2)}) collective-permute-start(bf16[192,1024]{1,0:T(8,128)(2,1)} %get-tuple-element.24), channel_id=1, source_target_pairs={{0,12},{4,0},{8,4},{12,8},{1,13},{5,1},{9,5},{13,9},{2,14},{6,2},{... | collective-permute-start | bytes 1179656 | tf_op jit(solution)/shard_map/ppermute | solution.py:27
  65.6 12.1 %collective-permute-start.3 = (bf16[192,1024]{1,0:T(8,128)(2,1)}, bf16[192,1024]{1,0:T(8,128)(2,1)S(1)}, u32[]{:S(2)}, u32[]{:S(2)}) collective-permute-start(bf16[192,1024]{1,0:T(8,128)(2,1)} %get-tuple-element.25), channel_id=1, source_target_pairs={{0,8},{4,12},{8,0},{12,4},{1,9},{5,13},{9,1},{13,5},{2,10},{6,14},... | collective-permute-start | bytes 1179656 | tf_op jit(solution)/shard_map/ppermute | solution.py:27
  68.0 20.6 %collective-permute-start.4 = (bf16[192,1024]{1,0:T(8,128)(2,1)}, bf16[192,1024]{1,0:T(8,128)(2,1)S(1)}, u32[]{:S(2)}, u32[]{:S(2)}) collective-permute-start(bf16[192,1024]{1,0:T(8,128)(2,1)} %get-tuple-element.26), channel_id=1, source_target_pairs={{0,4},{4,8},{8,12},{12,0},{1,5},{5,9},{9,13},{13,1},{2,6},{6,10},{... | collective-permute-start | bytes 1179656 | tf_op jit(solution)/shard_map/ppermute | solution.py:27
  73.8 14.8 %copy-start.2 = (bf16[192,1024]{1,0:T(8,128)(2,1)S(1)}, bf16[192,1024]{1,0:T(8,128)(2,1)}, u32[]{:S(2)}) copy-start(bf16[192,1024]{1,0:T(8,128)(2,1)} %copy-done.1) | copy-start | bytes 1179652
  73.8 40.2 %all-to-all-start.2 = ((bf16[16,8,4096]{2,1,0:T(8,128)(2,1)}), bf16[16,8,4096]{2,1,0:T(8,128)(2,1)S(1)}, u32[]{:S(2)}, u32[]{:S(2)}) async-start(bf16[16,8,4096]{2,1,0:T(8,128)(2,1)} %bitcast.7), calls=%async_computation.2 | async-start | bytes 2097152 | tf_op jit(solution)/shard_map/all_to_all | solution.py:223
  89.3 3.9 %collective-permute-start.5 = (bf16[256,1024]{1,0:T(8,128)(2,1)S(1)}, bf16[256,1024]{1,0:T(8,128)(2,1)S(1)}, u32[]{:S(2)}, u32[]{:S(2)}) collective-permute-start(bf16[256,1024]{1,0:T(8,128)(2,1)S(1)} %shard_map.80), channel_id=1, source_target_pairs={{0,16},{16,0},{1,17},{17,1},{2,18},{18,2},{3,19},{19,3},{4,20},{20... | collective-permute-start | bytes 1572872 | tf_op jit(solution)/shard_map/ppermute | solution.py:27
  94.6 13.4 %collective-permute-start.6 = (bf16[256,256]{1,0:T(8,128)(2,1)S(1)}, bf16[256,256]{1,0:T(8,128)(2,1)S(1)}, u32[]{:S(2)}, u32[]{:S(2)}) collective-permute-start(bf16[256,256]{1,0:T(8,128)(2,1)S(1)} %get-tuple-element.27), channel_id=1, source_target_pairs={{0,3},{1,0},{2,1},{3,2},{4,7},{5,4},{6,5},{7,6},{8,11},{9,8},{10,9... | collective-permute-start | bytes 393224 | tf_op jit(solution)/shard_map/ppermute | solution.py:27
  99.6 11.2 %collective-permute-start.7 = (bf16[256,256]{1,0:T(8,128)(2,1)S(1)}, bf16[256,256]{1,0:T(8,128)(2,1)S(1)}, u32[]{:S(2)}, u32[]{:S(2)}) collective-permute-start(bf16[256,256]{1,0:T(8,128)(2,1)S(1)} %get-tuple-element.28), channel_id=1, source_target_pairs={{0,2},{1,3},{2,0},{3,1},{4,6},{5,7},{6,4},{7,5},{8,10},{9,11},{10,... | collective-permute-start | bytes 393224 | tf_op jit(solution)/shard_map/ppermute | solution.py:27
  104.0 10.0 %collective-permute-start.8 = (bf16[256,256]{1,0:T(8,128)(2,1)S(1)}, bf16[256,256]{1,0:T(8,128)(2,1)S(1)}, u32[]{:S(2)}, u32[]{:S(2)}) collective-permute-start(bf16[256,256]{1,0:T(8,128)(2,1)S(1)} %get-tuple-element.29), channel_id=1, source_target_pairs={{0,1},{1,2},{2,3},{3,0},{4,5},{5,6},{6,7},{7,4},{8,9},{9,10},{10,1... | collective-permute-start | bytes 393224 | tf_op jit(solution)/shard_map/ppermute | solution.py:27

commit v17 on v16

--- a/solution.py
+++ b/solution.py
@@ -29,7 +29,7 @@
 
 def shifts(values, axis):
     size = len(values)
-    order = list(reversed(range(size)))
+    order = sorted(range(size), key=lambda d: (-min(d, size - d), d))
     return [shift(values[d], axis, d) for d in order]
 
 

time: 117 us -> 112 us (0.957); the launches traced: 115 us -> 112 us
  waiting for transfers between devices: 38.9 us -> 32 us
  starting transfers between devices: 45 us -> 48.6 us
    ppermute x9, waiting for transfers between devices: 20.5 us -> 13.6 us  [shift(): lax.ppermute(value, axis, [(i, (i + by) % size) for i in range(size)])]
    ppermute x9, starting transfers between devices: 29.2 us -> 32.8 us  [shift(): lax.ppermute(value, axis, [(i, (i + by) % size) for i in range(size)])]
  transfers between devices with their start and end apart: 11 -> 11, of which waited for: 6 -> 6; matrix products, arithmetic and copies ran while one was open for 1% -> 1% of each run, Pallas kernels for 5% -> 6%
where the time goes in v17:
time: 112 us
  starting transfers between devices  48.6 us (43%)
  waiting for transfers between devices  32 us (29%)
  blocking collectives  14.4 us (13%)
  Pallas kernels  12.3 us (11%)
  other arithmetic  1.77 us (2%)
  local copies, waits for them, and re-layouts  1.66 us (1%)
    ppermute x9, starting transfers between devices, shift(): lax.ppermute(value, axis, [(i, (i + by) % size) for i in range(size)])  32.8 us
    all_to_all x1, waiting for transfers between devices, per_device(): lax.all_to_all(jnp.broadcast_to(sent[None], (chips,) + sent.shape), CHIPS...  18.3 us
    all_to_all x1, blocking collectives, per_device(): stats = lax.all_to_all(stats, CHIPS, 0, 0, tiled=True)  14.4 us
    ppermute x9, waiting for transfers between devices, shift(): lax.ppermute(value, axis, [(i, (i + by) % size) for i in range(size)])  13.6 us
    all_to_all x1, starting transfers between devices, per_device(): lax.all_to_all(jnp.broadcast_to(sent[None], (chips,) + sent.shape), CHIPS...  12 us
    all_to_all x1, starting transfers between devices, per_device(): lax.all_to_all(query_part.reshape(chips, own_rows, depth), CHIPS, 0, 0, t...  3.78 us
    pallas_call x1, Pallas kernels, per_device(): pl.pallas_call(score_kernel, out_shape=(jax.ShapeDtypeStruct((2 * CORES,...  3.46 us
    pallas_call x1, Pallas kernels, per_device(): pl.pallas_call(query_kernel, out_shape=jax.ShapeDtypeStruct((rows, depth)...  3.3 us
  transfers between devices with their start and end apart: 11, of which 6 were waited for; matrix products, arithmetic and copies ran while one was open for 1% of the time, Pallas kernels for 6%

profile of v17, /device:TPU:1, one launch (start us, length us, event | category | flops | bytes accessed | tf_op | source)
XLA Modules:
  0.0 111.6 jit_solution(2083645524575683927)
XLA Ops:
  0.6 0.0 copy-start
  0.6 0.0 copy-start.3
  0.7 0.8 and_convert_fusion.1
  1.5 0.8 pad_maximum_fusion
  2.3 1.1 broadcast_in_dim.4
  3.4 12.0 %all-to-all-start = ((bf16[16,8,4224]{2,1,0:T(8,128)(2,1)}), bf16[16,8,4224]{2,1,0:T(8,128)(2,1)S(1)}, u32[]{:S(2)}, u32[]{:S(2)}) async-start(bf16[16,8,4224]{2,1,0:T(8,128)(2,1)} %broadcast_in_dim.4), calls=%async_computation | async-start | bytes 2162688 | tf_op jit(solution)/shard_map/all_to_all | solution.py:176
  15.4 0.0 copy-done
  15.4 2.9 %collective-permute-start = (bf16[256,4096]{1,0:T(8,128)(2,1)S(1)}, bf16[256,4096]{1,0:T(8,128)(2,1)}, u32[]{:S(2)}, u32[]{:S(2)}) collective-permute-start(bf16[256,4096]{1,0:T(8,128)(2,1)S(1)} %copy-done), channel_id=1, source_target_pairs={{0,16},{16,0},{1,17},{17,1},{2,18},{18,2},{3,19},{19,3},{4,20},{20... | collective-permute-start | bytes 6291464 | tf_op jit(solution)/shard_map/ppermute | solution.py:27
  18.3 0.0 copy-done.3
  18.3 0.9 shard_map.76.teacher
  19.2 1.9 %collective-permute-start.1 = (bf16[3,256,256]{2,1,0:T(8,128)(2,1)}, bf16[3,256,256]{2,1,0:T(8,128)(2,1)}, u32[]{:S(2)}, u32[]{:S(2)}) collective-permute-start(bf16[3,256,256]{2,1,0:T(8,128)(2,1)} %shard_map.76.teacher), channel_id=1, source_target_pairs={{0,16},{16,0},{1,17},{17,1},{2,18},{18,2},{3,19},{19,3},{4,20},{20... | collective-permute-start | bytes 1179656 | tf_op jit(solution)/shard_map/ppermute | solution.py:27
  21.1 0.1 pad_add_fusion.places
  21.2 1.9 %collective-permute-done.1.teacher_other = bf16[3,256,256]{2,1,0:T(8,128)(2,1)} collective-permute-done((bf16[3,256,256]{2,1,0:T(8,128)(2,1)}, bf16[3,256,256]{2,1,0:T(8,128)(2,1)}, u32[]{:S(2)}, u32[]{:S(2)}) %collective-permute-start.1) | collective-permute-done | bytes 393248 | tf_op jit(solution)/shard_map/ppermute | solution.py:27
  23.1 18.3 %all-to-all-done = bf16[16,8,4224]{2,1,0:T(8,128)(2,1)S(1)} async-done(((bf16[16,8,4224]{2,1,0:T(8,128)(2,1)}), bf16[16,8,4224]{2,1,0:T(8,128)(2,1)S(1)}, u32[]{:S(2)}, u32[]{:S(2)}) %all-to-all-start) | async-done | bytes 1081376 | tf_op jit(solution)/shard_map/all_to_all | solution.py:176
  41.4 0.0 collective-permute-done.passages_other
  41.4 3.5 %shard_map.77 = (f32[4,256,128]{2,1,0:T(8,128)S(1)}, s32[1,128]{1,0:T(1,128)S(1)}, f32[16,8,128]{2,1,0:T(8,128)S(1)}) custom-call(s32[4]{0:T(128)S(1)} %pad_add_fusion.places, bf16[128,4224]{1,0:T(8,128)(2,1)S(1)} %bitcast.9, bf16[256,4096]{1,0:T(8,128)(2,1)S(1)} %copy-done, bf16[256,4096]{1,0:T(8,128)(2,1)} %collective-permute-done.passages_other, ...), custom_call_target="tpu_custom_call" | custom-call | tf_op jit(solution)/shard_map/pallas_call | solution.py:189
  44.9 14.4 %all_to_all.15.stats = f32[16,8,128]{2,1,0:T(8,128)S(1)} all-to-all(f32[16,8,128]{2,1,0:T(8,128)S(1)} %get-tuple-element.20), channel_id=1, replica_groups=mesh['yl'=2,'z'=8,'core'=2,'x'=4,'yh'=4] {'yl','z'}, dimensions={0} | all-to-all | bytes 131072 | tf_op jit(solution)/shard_map/all_to_all | solution.py:200
  59.4 1.8 %shard_map.78 = (bf16[2,256,128]{2,1,0:T(8,128)(2,1)S(1)}, f32[1,128]{1,0:T(1,128)S(1)}, bf16[192,1024]{1,0:T(8,128)(2,1)S(1)}, bf16[192,1024]{1,0:T(8,128)(2,1)...) custom-call(s32[4]{0:T(128)S(1)} %pad_add_fusion.places, bf16[128,4224]{1,0:T(8,128)(2,1)S(1)} %bitcast.10, ...), custom_call_target="tpu_custom_call" | custom-call | tf_op jit(solution)/shard_map/pallas_call | solution.py:202
  61.2 0.0 copy-start.1
  61.2 4.6 %collective-permute-start.2 = (bf16[192,1024]{1,0:T(8,128)(2,1)}, bf16[192,1024]{1,0:T(8,128)(2,1)S(1)}, u32[]{:S(2)}, u32[]{:S(2)}) collective-permute-start(bf16[192,1024]{1,0:T(8,128)(2,1)} %get-tuple-element.24), channel_id=1, source_target_pairs={{0,8},{4,12},{8,0},{12,4},{1,9},{5,13},{9,1},{13,5},{2,10},{6,14},... | collective-permute-start | bytes 1179656 | tf_op jit(solution)/shard_map/ppermute | solution.py:27
  65.8 2.2 %collective-permute-start.3 = (bf16[192,1024]{1,0:T(8,128)(2,1)}, bf16[192,1024]{1,0:T(8,128)(2,1)S(1)}, u32[]{:S(2)}, u32[]{:S(2)}) collective-permute-start(bf16[192,1024]{1,0:T(8,128)(2,1)} %get-tuple-element.25), channel_id=1, source_target_pairs={{0,4},{4,8},{8,12},{12,0},{1,5},{5,9},{9,13},{13,1},{2,6},{6,10},{... | collective-permute-start | bytes 1179656 | tf_op jit(solution)/shard_map/ppermute | solution.py:27
  68.1 4.3 %collective-permute-start.4 = (bf16[192,1024]{1,0:T(8,128)(2,1)}, bf16[192,1024]{1,0:T(8,128)(2,1)S(1)}, u32[]{:S(2)}, u32[]{:S(2)}) collective-permute-start(bf16[192,1024]{1,0:T(8,128)(2,1)} %get-tuple-element.26), channel_id=1, source_target_pairs={{0,12},{4,0},{8,4},{12,8},{1,13},{5,1},{9,5},{13,9},{2,14},{6,2},{... | collective-permute-start | bytes 1179656 | tf_op jit(solution)/shard_map/ppermute | solution.py:27
  72.3 3.3 %shard_map.79 = bf16[128,4096]{1,0:T(8,128)(2,1)} custom-call(bf16[2,256,128]{2,1,0:T(8,128)(2,1)S(1)} %get-tuple-element.22.grads, bf16[256,4096]{1,0:T(8,128)(2,1)S(1)} %copy-done, bf16[256,4096]{1,0:T(8,128)(2,1)} %collective-permute-done.passages_other, bf16[192,1024]{1,0:T(8,128)(2,1)S(1)} %get-tuple-element.23.after.refs_3_), custom_call_target="tpu_custom_call" | custom-call | tf_op jit(solution)/shard_map/pallas_call | solution.py:216
  75.6 0.0 copy-done.1
  75.7 0.0 copy-start.2
  75.7 3.8 %all-to-all-start.2 = ((bf16[16,8,4096]{2,1,0:T(8,128)(2,1)}), bf16[16,8,4096]{2,1,0:T(8,128)(2,1)S(1)}, u32[]{:S(2)}, u32[]{:S(2)}) async-start(bf16[16,8,4096]{2,1,0:T(8,128)(2,1)} %bitcast.7), calls=%async_computation.2 | async-start | bytes 2097152 | tf_op jit(solution)/shard_map/all_to_all | solution.py:223
  79.4 0.0 collective-permute-done.2.refs_0_
  79.5 4.3 %collective-permute-done.3.refs_1_ = bf16[192,1024]{1,0:T(8,128)(2,1)S(1)} collective-permute-done((bf16[192,1024]{1,0:T(8,128)(2,1)}, bf16[192,1024]{1,0:T(8,128)(2,1)S(1)}, u32[]{:S(2)}, u32[]{:S(2)}) %collective-permute-start.3) | collective-permute-done | bytes 393248 | tf_op jit(solution)/shard_map/ppermute | solution.py:27
  83.8 0.0 collective-permute-done.4.refs_2_
  83.8 0.0 copy-done.2
  83.8 0.7 shard_map.80
  84.4 3.0 %collective-permute-start.5 = (bf16[256,1024]{1,0:T(8,128)(2,1)S(1)}, bf16[256,1024]{1,0:T(8,128)(2,1)S(1)}, u32[]{:S(2)}, u32[]{:S(2)}) collective-permute-start(bf16[256,1024]{1,0:T(8,128)(2,1)S(1)} %shard_map.80), channel_id=1, source_target_pairs={{0,16},{16,0},{1,17},{17,1},{2,18},{18,2},{3,19},{19,3},{4,20},{20... | collective-permute-start | bytes 1572872 | tf_op jit(solution)/shard_map/ppermute | solution.py:27
  87.4 1.5 %collective-permute-done.5.refs_4_ = bf16[256,1024]{1,0:T(8,128)(2,1)S(1)} collective-permute-done((bf16[256,1024]{1,0:T(8,128)(2,1)S(1)}, bf16[256,1024]{1,0:T(8,128)(2,1)S(1)}, u32[]{:S(2)}, u32[]{:S(2)}) %collective-permute-start.5) | collective-permute-done | bytes 524320 | tf_op jit(solution)/shard_map/ppermute | solution.py:27
  89.0 1.3 %shard_map.81 = (bf16[256,256]{1,0:T(8,128)(2,1)S(1)}, bf16[256,256]{1,0:T(8,128)(2,1)S(1)}, bf16[256,256]{1,0:T(8,128)(2,1)S(1)}, bf16[256,256]{1,0:T(8,128)(2,1)S(1)}) custom-call(s32[4]{0:T(128)S(1)} %pad_add_fusion.places, bf16[192,1024]{1,0:T(8,128)(2,1)S(1)} %collective-permute-done.2.refs_0_, bf16[192,1024]{1,0:T(8,128)(2,1)S(1)} %collective-permute-done.3.refs_1_, ...), custom_call_target="tpu_custom_call" | custom-call | tf_op jit(solution)/shard_map/pallas_call | solution.py:233
  90.3 6.6 %collective-permute-start.6 = (bf16[256,256]{1,0:T(8,128)(2,1)S(1)}, bf16[256,256]{1,0:T(8,128)(2,1)S(1)}, u32[]{:S(2)}, u32[]{:S(2)}) collective-permute-start(bf16[256,256]{1,0:T(8,128)(2,1)S(1)} %get-tuple-element.27), channel_id=1, source_target_pairs={{0,2},{1,3},{2,0},{3,1},{4,6},{5,7},{6,4},{7,5},{8,10},{9,11},{10,... | collective-permute-start | bytes 393224 | tf_op jit(solution)/shard_map/ppermute | solution.py:27
  96.8 2.4 %collective-permute-start.7 = (bf16[256,256]{1,0:T(8,128)(2,1)S(1)}, bf16[256,256]{1,0:T(8,128)(2,1)S(1)}, u32[]{:S(2)}, u32[]{:S(2)}) collective-permute-start(bf16[256,256]{1,0:T(8,128)(2,1)S(1)} %get-tuple-element.28), channel_id=1, source_target_pairs={{0,1},{1,2},{2,3},{3,0},{4,5},{5,6},{6,7},{7,4},{8,9},{9,10},{10,1... | collective-permute-start | bytes 393224 | tf_op jit(solution)/shard_map/ppermute | solution.py:27
  99.3 5.0 %collective-permute-start.8 = (bf16[256,256]{1,0:T(8,128)(2,1)S(1)}, bf16[256,256]{1,0:T(8,128)(2,1)S(1)}, u32[]{:S(2)}, u32[]{:S(2)}) collective-permute-start(bf16[256,256]{1,0:T(8,128)(2,1)S(1)} %get-tuple-element.29), channel_id=1, source_target_pairs={{0,3},{1,0},{2,1},{3,2},{4,7},{5,4},{6,5},{7,6},{8,11},{9,8},{10,9... | collective-permute-start | bytes 393224 | tf_op jit(solution)/shard_map/ppermute | solution.py:27
  104.2 0.6 constant_dynamic-slice_fusion
  104.8 0.0 collective-permute-done.6.refs_0_
  104.8 2.8 %collective-permute-done.7.refs_1_ = bf16[256,256]{1,0:T(8,128)(2,1)S(1)} collective-permute-done((bf16[256,256]{1,0:T(8,128)(2,1)S(1)}, bf16[256,256]{1,0:T(8,128)(2,1)S(1)}, u32[]{:S(2)}, u32[]{:S(2)}) %collective-permute-start.7) | collective-permute-done | bytes 131104 | tf_op jit(solution)/shard_map/ppermute | solution.py:27
  107.6 3.1 %collective-permute-done.8.refs_2_ = bf16[256,256]{1,0:T(8,128)(2,1)S(1)} collective-permute-done((bf16[256,256]{1,0:T(8,128)(2,1)S(1)}, bf16[256,256]{1,0:T(8,128)(2,1)S(1)}, u32[]{:S(2)}, u32[]{:S(2)}) %collective-permute-start.8) | collective-permute-done | bytes 131104 | tf_op jit(solution)/shard_map/ppermute | solution.py:27
  110.7 0.0 all-to-all-done.2.query_parts
  110.7 0.9 shard_map.82
  (1 shorter events, 0.0 us)
Async XLA Ops:
  0.6 14.8 %copy-start = (bf16[256,4096]{1,0:T(8,128)(2,1)S(1)}, bf16[256,4096]{1,0:T(8,128)(2,1)}, u32[]{:S(2)}) copy-start(bf16[256,4096]{1,0:T(8,128)(2,1)} %passages.3) | copy-start | bytes 6291460
  0.6 17.6 %copy-start.3 = (f32[1,256,256]{2,1,0:T(8,128)S(1)}, f32[1,256,256]{2,1,0:T(8,128)}, u32[]{:S(2)}) copy-start(f32[1,256,256]{2,1,0:T(8,128)} %param.7) | copy-start | bytes 786436
  3.4 38.0 %all-to-all-start = ((bf16[16,8,4224]{2,1,0:T(8,128)(2,1)}), bf16[16,8,4224]{2,1,0:T(8,128)(2,1)S(1)}, u32[]{:S(2)}, u32[]{:S(2)}) async-start(bf16[16,8,4224]{2,1,0:T(8,128)(2,1)} %broadcast_in_dim.4), calls=%async_computation | async-start | bytes 2162688 | tf_op jit(solution)/shard_map/all_to_all | solution.py:176
  15.4 26.0 %collective-permute-start = (bf16[256,4096]{1,0:T(8,128)(2,1)S(1)}, bf16[256,4096]{1,0:T(8,128)(2,1)}, u32[]{:S(2)}, u32[]{:S(2)}) collective-permute-start(bf16[256,4096]{1,0:T(8,128)(2,1)S(1)} %copy-done), channel_id=1, source_target_pairs={{0,16},{16,0},{1,17},{17,1},{2,18},{18,2},{3,19},{19,3},{4,20},{20... | collective-permute-start | bytes 6291464 | tf_op jit(solution)/shard_map/ppermute | solution.py:27
  19.2 3.9 %collective-permute-start.1 = (bf16[3,256,256]{2,1,0:T(8,128)(2,1)}, bf16[3,256,256]{2,1,0:T(8,128)(2,1)}, u32[]{:S(2)}, u32[]{:S(2)}) collective-permute-start(bf16[3,256,256]{2,1,0:T(8,128)(2,1)} %shard_map.76.teacher), channel_id=1, source_target_pairs={{0,16},{16,0},{1,17},{17,1},{2,18},{18,2},{3,19},{19,3},{4,20},{20... | collective-permute-start | bytes 1179656 | tf_op jit(solution)/shard_map/ppermute | solution.py:27
  61.2 14.5 %copy-start.1 = (bf16[192,1024]{1,0:T(8,128)(2,1)}, bf16[192,1024]{1,0:T(8,128)(2,1)S(1)}, u32[]{:S(2)}) copy-start(bf16[192,1024]{1,0:T(8,128)(2,1)S(1)} %get-tuple-element.23.after.refs_3_) | copy-start | bytes 1179652
  61.2 18.3 %collective-permute-start.2 = (bf16[192,1024]{1,0:T(8,128)(2,1)}, bf16[192,1024]{1,0:T(8,128)(2,1)S(1)}, u32[]{:S(2)}, u32[]{:S(2)}) collective-permute-start(bf16[192,1024]{1,0:T(8,128)(2,1)} %get-tuple-element.24), channel_id=1, source_target_pairs={{0,8},{4,12},{8,0},{12,4},{1,9},{5,13},{9,1},{13,5},{2,10},{6,14},... | collective-permute-start | bytes 1179656 | tf_op jit(solution)/shard_map/ppermute | solution.py:27
  65.8 17.9 %collective-permute-start.3 = (bf16[192,1024]{1,0:T(8,128)(2,1)}, bf16[192,1024]{1,0:T(8,128)(2,1)S(1)}, u32[]{:S(2)}, u32[]{:S(2)}) collective-permute-start(bf16[192,1024]{1,0:T(8,128)(2,1)} %get-tuple-element.25), channel_id=1, source_target_pairs={{0,4},{4,8},{8,12},{12,0},{1,5},{5,9},{9,13},{13,1},{2,6},{6,10},{... | collective-permute-start | bytes 1179656 | tf_op jit(solution)/shard_map/ppermute | solution.py:27
  68.1 15.7 %collective-permute-start.4 = (bf16[192,1024]{1,0:T(8,128)(2,1)}, bf16[192,1024]{1,0:T(8,128)(2,1)S(1)}, u32[]{:S(2)}, u32[]{:S(2)}) collective-permute-start(bf16[192,1024]{1,0:T(8,128)(2,1)} %get-tuple-element.26), channel_id=1, source_target_pairs={{0,12},{4,0},{8,4},{12,8},{1,13},{5,1},{9,5},{13,9},{2,14},{6,2},{... | collective-permute-start | bytes 1179656 | tf_op jit(solution)/shard_map/ppermute | solution.py:27
  75.7 8.1 %copy-start.2 = (bf16[192,1024]{1,0:T(8,128)(2,1)S(1)}, bf16[192,1024]{1,0:T(8,128)(2,1)}, u32[]{:S(2)}) copy-start(bf16[192,1024]{1,0:T(8,128)(2,1)} %copy-done.1) | copy-start | bytes 1179652
  75.7 35.0 %all-to-all-start.2 = ((bf16[16,8,4096]{2,1,0:T(8,128)(2,1)}), bf16[16,8,4096]{2,1,0:T(8,128)(2,1)S(1)}, u32[]{:S(2)}, u32[]{:S(2)}) async-start(bf16[16,8,4096]{2,1,0:T(8,128)(2,1)} %bitcast.7), calls=%async_computation.2 | async-start | bytes 2097152 | tf_op jit(solution)/shard_map/all_to_all | solution.py:223
  84.4 4.5 %collective-permute-start.5 = (bf16[256,1024]{1,0:T(8,128)(2,1)S(1)}, bf16[256,1024]{1,0:T(8,128)(2,1)S(1)}, u32[]{:S(2)}, u32[]{:S(2)}) collective-permute-start(bf16[256,1024]{1,0:T(8,128)(2,1)S(1)} %shard_map.80), channel_id=1, source_target_pairs={{0,16},{16,0},{1,17},{17,1},{2,18},{18,2},{3,19},{19,3},{4,20},{20... | collective-permute-start | bytes 1572872 | tf_op jit(solution)/shard_map/ppermute | solution.py:27
  90.3 14.6 %collective-permute-start.6 = (bf16[256,256]{1,0:T(8,128)(2,1)S(1)}, bf16[256,256]{1,0:T(8,128)(2,1)S(1)}, u32[]{:S(2)}, u32[]{:S(2)}) collective-permute-start(bf16[256,256]{1,0:T(8,128)(2,1)S(1)} %get-tuple-element.27), channel_id=1, source_target_pairs={{0,2},{1,3},{2,0},{3,1},{4,6},{5,7},{6,4},{7,5},{8,10},{9,11},{10,... | collective-permute-start | bytes 393224 | tf_op jit(solution)/shard_map/ppermute | solution.py:27
  96.8 10.8 %collective-permute-start.7 = (bf16[256,256]{1,0:T(8,128)(2,1)S(1)}, bf16[256,256]{1,0:T(8,128)(2,1)S(1)}, u32[]{:S(2)}, u32[]{:S(2)}) collective-permute-start(bf16[256,256]{1,0:T(8,128)(2,1)S(1)} %get-tuple-element.28), channel_id=1, source_target_pairs={{0,1},{1,2},{2,3},{3,0},{4,5},{5,6},{6,7},{7,4},{8,9},{9,10},{10,1... | collective-permute-start | bytes 393224 | tf_op jit(solution)/shard_map/ppermute | solution.py:27
  99.3 11.4 %collective-permute-start.8 = (bf16[256,256]{1,0:T(8,128)(2,1)S(1)}, bf16[256,256]{1,0:T(8,128)(2,1)S(1)}, u32[]{:S(2)}, u32[]{:S(2)}) collective-permute-start(bf16[256,256]{1,0:T(8,128)(2,1)S(1)} %get-tuple-element.29), channel_id=1, source_target_pairs={{0,3},{1,0},{2,1},{3,2},{4,7},{5,4},{6,5},{7,6},{8,11},{9,8},{10,9... | collective-permute-start | bytes 393224 | tf_op jit(solution)/shard_map/ppermute | solution.py:27

commit v18 on v15

--- a/solution.py
+++ b/solution.py
@@ -138,17 +138,16 @@
     return total
 
 
-def other_kernel(rows, *refs):
+def product_kernel(half, rows, *refs):
     out = refs[-1]
-    out[...] = products(refs[:-1], 1, out.shape[0], rows).astype(bf16)
-
-
-def own_kernel(groups, rows, places, *refs):
-    packed, back, outs, total = refs[:groups], refs[groups], refs[groups + 1 : -1], refs[-1]
+    out[...] = products(refs[:-1], half, out.shape[0], rows).astype(out.dtype)
+
+
+def add_kernel(places, part, back, *outs):
     width = outs[0].shape[1]
-    total[...] = (products(packed, 0, back.shape[0], rows) + back[...].astype(f32)).astype(bf16)
     for d, out in enumerate(outs):
-        out[...] = total[:, pl.ds(pl.multiple_of(lax.rem(places[3] + d, len(outs)) * width, width), width)]
+        columns = pl.ds(pl.multiple_of(lax.rem(places[3] + d, len(outs)) * width, width), width)
+        out[...] = (part[:, columns] + back[:, columns].astype(f32)).astype(bf16)
 
 
 def sum_kernel(query_parts, *refs):
@@ -222,22 +221,24 @@
     )(grads, passages, passages_other, packed[0])
     query_parts = lax.all_to_all(query_part.reshape(chips, own_rows, depth), CHIPS, 0, 0, tiled=True)
     packed = shifts(packed, "x")
-    part_other = pl.pallas_call(
-        functools.partial(other_kernel, rows),
-        out_shape=jax.ShapeDtypeStruct((block_rows, width), bf16),
-        in_specs=[VMEM] * x_size,
-        out_specs=VMEM,
-        compiler_params=PARAMS,
-        cost_estimate=pl.CostEstimate(flops=10**11, bytes_accessed=2**21, transcendentals=0),
-    )(*packed)
+    part, part_other = (
+        pl.pallas_call(
+            functools.partial(product_kernel, half, rows),
+            out_shape=jax.ShapeDtypeStruct((block_rows, width), dtype),
+            in_specs=[VMEM] * x_size,
+            out_specs=VMEM,
+            compiler_params=PARAMS,
+            cost_estimate=pl.CostEstimate(flops=10 ** (11 if half else 9), bytes_accessed=2**21, transcendentals=0),
+        )(*packed)
+        for half, dtype in enumerate((f32, bf16))
+    )
     parts = pl.pallas_call(
-        functools.partial(own_kernel, x_size, rows),
+        add_kernel,
         out_shape=(jax.ShapeDtypeStruct((block_rows, width // yh_size), bf16),) * yh_size,
-        in_specs=[SMEM] + [VMEM] * (x_size + 1),
+        in_specs=[SMEM] + [VMEM] * 2,
         out_specs=(VMEM,) * yh_size,
-        scratch_shapes=[pltpu.VMEM((block_rows, width), bf16)],
-        compiler_params=PARAMS,
-    )(places, *packed, shift(part_other, "core", 1))
+        compiler_params=PARAMS,
+    )(places, part, shift(part_other, "core", 1))
     parts = shifts(parts, "yh")
     query_total, passage_total = pl.pallas_call(
         sum_kernel,

time: 112 us -> 113 us (level)
  Pallas kernels: 12.3 us -> 14.4 us
  waiting for transfers between devices: 33.1 us -> 31.7 us
    pallas_call x2 -> x3, Pallas kernels: 1.98 us -> 4.05 us  [the longest x2 3.36 us: per_device(): pl.pallas_call(functools.partial(product_kernel, half, rows), out_shape=j...]
    ppermute x9, waiting for transfers between devices: 14.8 us -> 13.4 us  [shift(): lax.ppermute(value, axis, [(i, (i + by) % size) for i in range(size)])]
  transfers between devices with their start and end apart: 11 -> 11, of which waited for: 5 -> 5; matrix products, arithmetic and copies ran while one was open for 1% -> 1% of each run, Pallas kernels for 6% -> 7%
where the time goes in v18:
time: 113 us; the launch traced here: 112 us
  starting transfers between devices  47 us (42%)
  waiting for transfers between devices  31.7 us (28%)
  Pallas kernels  14.4 us (13%)
  blocking collectives  14.4 us (13%)
  other arithmetic  1.77 us (2%)
  local copies, waits for them, and re-layouts  1.66 us (1%)
    ppermute x9, starting transfers between devices, shift(): lax.ppermute(value, axis, [(i, (i + by) % size) for i in range(size)])  31.3 us
    all_to_all x1, waiting for transfers between devices, per_device(): lax.all_to_all(jnp.broadcast_to(sent[None], (chips,) + sent.shape), CHIPS...  18.3 us
    all_to_all x1, blocking collectives, per_device(): stats = lax.all_to_all(stats, CHIPS, 0, 0, tiled=True)  14.4 us
    ppermute x9, waiting for transfers between devices, shift(): lax.ppermute(value, axis, [(i, (i + by) % size) for i in range(size)])  13.4 us
    all_to_all x1, starting transfers between devices, per_device(): lax.all_to_all(jnp.broadcast_to(sent[None], (chips,) + sent.shape), CHIPS...  12 us
    all_to_all x1, starting transfers between devices, per_device(): lax.all_to_all(query_part.reshape(chips, own_rows, depth), CHIPS, 0, 0, t...  3.78 us
    pallas_call x1, Pallas kernels, per_device(): pl.pallas_call(score_kernel, out_shape=(jax.ShapeDtypeStruct((2 * CORES,...  3.46 us
    pallas_call x2, Pallas kernels, per_device(): pl.pallas_call(functools.partial(product_kernel, half, rows), out_shape=j...  3.36 us
  transfers between devices with their start and end apart: 11, of which 5 were waited for; matrix products, arithmetic and copies ran while one was open for 1% of the time, Pallas kernels for 7%

profile of v18, /device:TPU:1, one launch (start us, length us, event | category | flops | bytes accessed | tf_op | source)
XLA Modules:
  0.0 111.8 jit_solution(15068317133607789833)
XLA Ops:
  0.6 0.0 copy-start
  0.6 0.0 copy-start.3
  0.7 0.8 and_convert_fusion.1
  1.5 0.8 pad_maximum_fusion
  2.3 1.1 broadcast_in_dim.4
  3.4 12.0 %all-to-all-start = ((bf16[16,8,4224]{2,1,0:T(8,128)(2,1)}), bf16[16,8,4224]{2,1,0:T(8,128)(2,1)S(1)}, u32[]{:S(2)}, u32[]{:S(2)}) async-start(bf16[16,8,4224]{2,1,0:T(8,128)(2,1)} %broadcast_in_dim.4), calls=%async_computation | async-start | bytes 2162688 | tf_op jit(solution)/shard_map/all_to_all | solution.py:175
  15.4 0.0 copy-done
  15.4 2.9 %collective-permute-start = (bf16[256,4096]{1,0:T(8,128)(2,1)S(1)}, bf16[256,4096]{1,0:T(8,128)(2,1)}, u32[]{:S(2)}, u32[]{:S(2)}) collective-permute-start(bf16[256,4096]{1,0:T(8,128)(2,1)S(1)} %copy-done), channel_id=1, source_target_pairs={{0,16},{16,0},{1,17},{17,1},{2,18},{18,2},{3,19},{19,3},{4,20},{20... | collective-permute-start | bytes 6291464 | tf_op jit(solution)/shard_map/ppermute | solution.py:27
  18.3 0.0 copy-done.3
  18.3 0.9 shard_map.76.teacher
  19.2 1.9 %collective-permute-start.1 = (bf16[3,256,256]{2,1,0:T(8,128)(2,1)}, bf16[3,256,256]{2,1,0:T(8,128)(2,1)}, u32[]{:S(2)}, u32[]{:S(2)}) collective-permute-start(bf16[3,256,256]{2,1,0:T(8,128)(2,1)} %shard_map.76.teacher), channel_id=1, source_target_pairs={{0,16},{16,0},{1,17},{17,1},{2,18},{18,2},{3,19},{19,3},{4,20},{20... | collective-permute-start | bytes 1179656 | tf_op jit(solution)/shard_map/ppermute | solution.py:27
  21.1 0.1 pad_add_fusion.places
  21.2 1.9 %collective-permute-done.1.teacher_other = bf16[3,256,256]{2,1,0:T(8,128)(2,1)} collective-permute-done((bf16[3,256,256]{2,1,0:T(8,128)(2,1)}, bf16[3,256,256]{2,1,0:T(8,128)(2,1)}, u32[]{:S(2)}, u32[]{:S(2)}) %collective-permute-start.1) | collective-permute-done | bytes 393248 | tf_op jit(solution)/shard_map/ppermute | solution.py:27
  23.1 18.3 %all-to-all-done = bf16[16,8,4224]{2,1,0:T(8,128)(2,1)S(1)} async-done(((bf16[16,8,4224]{2,1,0:T(8,128)(2,1)}), bf16[16,8,4224]{2,1,0:T(8,128)(2,1)S(1)}, u32[]{:S(2)}, u32[]{:S(2)}) %all-to-all-start) | async-done | bytes 1081376 | tf_op jit(solution)/shard_map/all_to_all | solution.py:175
  41.4 0.0 collective-permute-done.passages_other
  41.4 3.5 %shard_map.77 = (f32[4,256,128]{2,1,0:T(8,128)S(1)}, s32[1,128]{1,0:T(1,128)S(1)}, f32[16,8,128]{2,1,0:T(8,128)S(1)}) custom-call(s32[4]{0:T(128)S(1)} %pad_add_fusion.places, bf16[128,4224]{1,0:T(8,128)(2,1)S(1)} %bitcast.9, bf16[256,4096]{1,0:T(8,128)(2,1)S(1)} %copy-done, bf16[256,4096]{1,0:T(8,128)(2,1)} %collective-permute-done.passages_other, ...), custom_call_target="tpu_custom_call" | custom-call | tf_op jit(solution)/shard_map/pallas_call | solution.py:188
  44.9 14.4 %all_to_all.15.stats = f32[16,8,128]{2,1,0:T(8,128)S(1)} all-to-all(f32[16,8,128]{2,1,0:T(8,128)S(1)} %get-tuple-element.20), channel_id=1, replica_groups=mesh['yl'=2,'z'=8,'core'=2,'x'=4,'yh'=4] {'yl','z'}, dimensions={0} | all-to-all | bytes 131072 | tf_op jit(solution)/shard_map/all_to_all | solution.py:199
  59.4 1.8 %shard_map.78 = (bf16[2,256,128]{2,1,0:T(8,128)(2,1)S(1)}, f32[1,128]{1,0:T(1,128)S(1)}, bf16[192,1024]{1,0:T(8,128)(2,1)S(1)}, bf16[192,1024]{1,0:T(8,128)(2,1)...) custom-call(s32[4]{0:T(128)S(1)} %pad_add_fusion.places, bf16[128,4224]{1,0:T(8,128)(2,1)S(1)} %bitcast.10, ...), custom_call_target="tpu_custom_call" | custom-call | tf_op jit(solution)/shard_map/pallas_call | solution.py:201
  61.2 0.0 copy-start.1
  61.2 4.6 %collective-permute-start.2 = (bf16[192,1024]{1,0:T(8,128)(2,1)}, bf16[192,1024]{1,0:T(8,128)(2,1)S(1)}, u32[]{:S(2)}, u32[]{:S(2)}) collective-permute-start(bf16[192,1024]{1,0:T(8,128)(2,1)} %get-tuple-element.24), channel_id=1, source_target_pairs={{0,8},{4,12},{8,0},{12,4},{1,9},{5,13},{9,1},{13,5},{2,10},{6,14},... | collective-permute-start | bytes 1179656 | tf_op jit(solution)/shard_map/ppermute | solution.py:27
  65.8 2.8 %collective-permute-start.3 = (bf16[192,1024]{1,0:T(8,128)(2,1)}, bf16[192,1024]{1,0:T(8,128)(2,1)S(1)}, u32[]{:S(2)}, u32[]{:S(2)}) collective-permute-start(bf16[192,1024]{1,0:T(8,128)(2,1)} %get-tuple-element.25), channel_id=1, source_target_pairs={{0,12},{4,0},{8,4},{12,8},{1,13},{5,1},{9,5},{13,9},{2,14},{6,2},{... | collective-permute-start | bytes 1179656 | tf_op jit(solution)/shard_map/ppermute | solution.py:27
  68.6 2.5 %collective-permute-start.4 = (bf16[192,1024]{1,0:T(8,128)(2,1)}, bf16[192,1024]{1,0:T(8,128)(2,1)}, u32[]{:S(2)}, u32[]{:S(2)}) collective-permute-start(bf16[192,1024]{1,0:T(8,128)(2,1)} %get-tuple-element.26), channel_id=1, source_target_pairs={{0,4},{4,8},{8,12},{12,0},{1,5},{5,9},{9,13},{13,1},{2,6},{6,10},{... | collective-permute-start | bytes 1179656 | tf_op jit(solution)/shard_map/ppermute | solution.py:27
  71.1 3.3 %shard_map.79 = bf16[128,4096]{1,0:T(8,128)(2,1)} custom-call(bf16[2,256,128]{2,1,0:T(8,128)(2,1)S(1)} %get-tuple-element.22.grads, bf16[256,4096]{1,0:T(8,128)(2,1)S(1)} %copy-done, bf16[256,4096]{1,0:T(8,128)(2,1)} %collective-permute-done.passages_other, bf16[192,1024]{1,0:T(8,128)(2,1)S(1)} %get-tuple-element.23.after.refs_3_), custom_call_target="tpu_custom_call" | custom-call | tf_op jit(solution)/shard_map/pallas_call | solution.py:215
  74.4 0.0 copy-done.1
  74.4 0.0 copy-start.2
  74.4 3.8 %all-to-all-start.2 = ((bf16[16,8,4096]{2,1,0:T(8,128)(2,1)}), bf16[16,8,4096]{2,1,0:T(8,128)(2,1)S(1)}, u32[]{:S(2)}, u32[]{:S(2)}) async-start(bf16[16,8,4096]{2,1,0:T(8,128)(2,1)} %bitcast.7), calls=%async_computation.2 | async-start | bytes 2097152 | tf_op jit(solution)/shard_map/all_to_all | solution.py:222
  78.2 0.0 collective-permute-done.2.refs_0_
  78.2 5.2 %collective-permute-done.3.refs_1_ = bf16[192,1024]{1,0:T(8,128)(2,1)S(1)} collective-permute-done((bf16[192,1024]{1,0:T(8,128)(2,1)}, bf16[192,1024]{1,0:T(8,128)(2,1)S(1)}, u32[]{:S(2)}, u32[]{:S(2)}) %collective-permute-start.3) | collective-permute-done | bytes 393248 | tf_op jit(solution)/shard_map/ppermute | solution.py:27
  83.4 0.1 collective-permute-done.4.refs_2_
  83.5 0.0 copy-done.2
  83.5 1.7 %shard_map.81 = bf16[256,1024]{1,0:T(8,128)(2,1)S(1)} custom-call(bf16[192,1024]{1,0:T(8,128)(2,1)S(1)} %collective-permute-done.2.refs_0_, bf16[192,1024]{1,0:T(8,128)(2,1)S(1)} %collective-permute-done.3.refs_1_, bf16[192,1024]{1,0:T(8,128)(2,1)} %collective-permute-done.4.refs_2_, bf16[192,1024]{1,0:T(8,128)(2,1)S(1)} %copy-done.2), custom_call_target="tpu_custom_call" | custom-call | flops 99999997952 | bytes 2097152 | tf_op jit(solution)/shard_map/pallas_call | solution.py:225
  85.2 3.8 %collective-permute-start.5 = (bf16[256,1024]{1,0:T(8,128)(2,1)S(1)}, bf16[256,1024]{1,0:T(8,128)(2,1)S(1)}, u32[]{:S(2)}, u32[]{:S(2)}) collective-permute-start(bf16[256,1024]{1,0:T(8,128)(2,1)S(1)} %shard_map.81), channel_id=1, source_target_pairs={{0,16},{16,0},{1,17},{17,1},{2,18},{18,2},{3,19},{19,3},{4,20},{20... | collective-permute-start | bytes 1572872 | tf_op jit(solution)/shard_map/ppermute | solution.py:27
  89.0 1.7 %shard_map.80.part = f32[256,1024]{1,0:T(8,128)S(1)} custom-call(bf16[192,1024]{1,0:T(8,128)(2,1)S(1)} %collective-permute-done.2.refs_0_, bf16[192,1024]{1,0:T(8,128)(2,1)S(1)} %collective-permute-done.3.refs_1_, bf16[192,1024]{1,0:T(8,128)(2,1)} %collective-permute-done.4.refs_2_, bf16[192,1024]{1,0:T(8,128)(2,1)S(1)} %copy-done.2), custom_call_target="tpu_custom_call" | custom-call | flops 1000000000 | bytes 2097152 | tf_op jit(solution)/shard_map/pallas_call | solution.py:225
  90.7 0.0 collective-permute-done.5.back
  90.7 0.7 shard_map.82
  91.4 6.6 %collective-permute-start.6 = (bf16[256,256]{1,0:T(8,128)(2,1)S(1)}, bf16[256,256]{1,0:T(8,128)(2,1)S(1)}, u32[]{:S(2)}, u32[]{:S(2)}) collective-permute-start(bf16[256,256]{1,0:T(8,128)(2,1)S(1)} %get-tuple-element.27), channel_id=1, source_target_pairs={{0,2},{1,3},{2,0},{3,1},{4,6},{5,7},{6,4},{7,5},{8,10},{9,11},{10,... | collective-permute-start | bytes 393224 | tf_op jit(solution)/shard_map/ppermute | solution.py:27
  98.0 2.9 %collective-permute-start.7 = (bf16[256,256]{1,0:T(8,128)(2,1)S(1)}, bf16[256,256]{1,0:T(8,128)(2,1)S(1)}, u32[]{:S(2)}, u32[]{:S(2)}) collective-permute-start(bf16[256,256]{1,0:T(8,128)(2,1)S(1)} %get-tuple-element.28), channel_id=1, source_target_pairs={{0,3},{1,0},{2,1},{3,2},{4,7},{5,4},{6,5},{7,6},{8,11},{9,8},{10,9... | collective-permute-start | bytes 393224 | tf_op jit(solution)/shard_map/ppermute | solution.py:27
  100.9 3.3 %collective-permute-start.8 = (bf16[256,256]{1,0:T(8,128)(2,1)S(1)}, bf16[256,256]{1,0:T(8,128)(2,1)S(1)}, u32[]{:S(2)}, u32[]{:S(2)}) collective-permute-start(bf16[256,256]{1,0:T(8,128)(2,1)S(1)} %get-tuple-element.29), channel_id=1, source_target_pairs={{0,1},{1,2},{2,3},{3,0},{4,5},{5,6},{6,7},{7,4},{8,9},{9,10},{10,1... | collective-permute-start | bytes 393224 | tf_op jit(solution)/shard_map/ppermute | solution.py:27
  104.2 0.6 constant_dynamic-slice_fusion
  104.8 0.0 collective-permute-done.6.refs_0_
  104.8 6.2 %collective-permute-done.7.refs_1_ = bf16[256,256]{1,0:T(8,128)(2,1)S(1)} collective-permute-done((bf16[256,256]{1,0:T(8,128)(2,1)S(1)}, bf16[256,256]{1,0:T(8,128)(2,1)S(1)}, u32[]{:S(2)}, u32[]{:S(2)}) %collective-permute-start.7) | collective-permute-done | bytes 131104 | tf_op jit(solution)/shard_map/ppermute | solution.py:27
  111.0 0.0 collective-permute-done.8.refs_2_
  111.0 0.0 all-to-all-done.2.query_parts
  111.0 0.9 shard_map.83
  (1 shorter events, 0.0 us)
Async XLA Ops:
  0.6 14.8 %copy-start = (bf16[256,4096]{1,0:T(8,128)(2,1)S(1)}, bf16[256,4096]{1,0:T(8,128)(2,1)}, u32[]{:S(2)}) copy-start(bf16[256,4096]{1,0:T(8,128)(2,1)} %passages.3) | copy-start | bytes 6291460
  0.6 17.6 %copy-start.3 = (f32[1,256,256]{2,1,0:T(8,128)S(1)}, f32[1,256,256]{2,1,0:T(8,128)}, u32[]{:S(2)}) copy-start(f32[1,256,256]{2,1,0:T(8,128)} %param.7) | copy-start | bytes 786436
  3.4 38.0 %all-to-all-start = ((bf16[16,8,4224]{2,1,0:T(8,128)(2,1)}), bf16[16,8,4224]{2,1,0:T(8,128)(2,1)S(1)}, u32[]{:S(2)}, u32[]{:S(2)}) async-start(bf16[16,8,4224]{2,1,0:T(8,128)(2,1)} %broadcast_in_dim.4), calls=%async_computation | async-start | bytes 2162688 | tf_op jit(solution)/shard_map/all_to_all | solution.py:175
  15.4 26.0 %collective-permute-start = (bf16[256,4096]{1,0:T(8,128)(2,1)S(1)}, bf16[256,4096]{1,0:T(8,128)(2,1)}, u32[]{:S(2)}, u32[]{:S(2)}) collective-permute-start(bf16[256,4096]{1,0:T(8,128)(2,1)S(1)} %copy-done), channel_id=1, source_target_pairs={{0,16},{16,0},{1,17},{17,1},{2,18},{18,2},{3,19},{19,3},{4,20},{20... | collective-permute-start | bytes 6291464 | tf_op jit(solution)/shard_map/ppermute | solution.py:27
  19.2 3.9 %collective-permute-start.1 = (bf16[3,256,256]{2,1,0:T(8,128)(2,1)}, bf16[3,256,256]{2,1,0:T(8,128)(2,1)}, u32[]{:S(2)}, u32[]{:S(2)}) collective-permute-start(bf16[3,256,256]{2,1,0:T(8,128)(2,1)} %shard_map.76.teacher), channel_id=1, source_target_pairs={{0,16},{16,0},{1,17},{17,1},{2,18},{18,2},{3,19},{19,3},{4,20},{20... | collective-permute-start | bytes 1179656 | tf_op jit(solution)/shard_map/ppermute | solution.py:27
  61.2 13.3 %copy-start.1 = (bf16[192,1024]{1,0:T(8,128)(2,1)}, bf16[192,1024]{1,0:T(8,128)(2,1)S(1)}, u32[]{:S(2)}) copy-start(bf16[192,1024]{1,0:T(8,128)(2,1)S(1)} %get-tuple-element.23.after.refs_3_) | copy-start | bytes 1179652
  61.2 17.0 %collective-permute-start.2 = (bf16[192,1024]{1,0:T(8,128)(2,1)}, bf16[192,1024]{1,0:T(8,128)(2,1)S(1)}, u32[]{:S(2)}, u32[]{:S(2)}) collective-permute-start(bf16[192,1024]{1,0:T(8,128)(2,1)} %get-tuple-element.24), channel_id=1, source_target_pairs={{0,8},{4,12},{8,0},{12,4},{1,9},{5,13},{9,1},{13,5},{2,10},{6,14},... | collective-permute-start | bytes 1179656 | tf_op jit(solution)/shard_map/ppermute | solution.py:27
  65.8 17.6 %collective-permute-start.3 = (bf16[192,1024]{1,0:T(8,128)(2,1)}, bf16[192,1024]{1,0:T(8,128)(2,1)S(1)}, u32[]{:S(2)}, u32[]{:S(2)}) collective-permute-start(bf16[192,1024]{1,0:T(8,128)(2,1)} %get-tuple-element.25), channel_id=1, source_target_pairs={{0,12},{4,0},{8,4},{12,8},{1,13},{5,1},{9,5},{13,9},{2,14},{6,2},{... | collective-permute-start | bytes 1179656 | tf_op jit(solution)/shard_map/ppermute | solution.py:27
  68.6 14.9 %collective-permute-start.4 = (bf16[192,1024]{1,0:T(8,128)(2,1)}, bf16[192,1024]{1,0:T(8,128)(2,1)}, u32[]{:S(2)}, u32[]{:S(2)}) collective-permute-start(bf16[192,1024]{1,0:T(8,128)(2,1)} %get-tuple-element.26), channel_id=1, source_target_pairs={{0,4},{4,8},{8,12},{12,0},{1,5},{5,9},{9,13},{13,1},{2,6},{6,10},{... | collective-permute-start | bytes 1179656 | tf_op jit(solution)/shard_map/ppermute | solution.py:27
  74.4 9.1 %copy-start.2 = (bf16[192,1024]{1,0:T(8,128)(2,1)S(1)}, bf16[192,1024]{1,0:T(8,128)(2,1)}, u32[]{:S(2)}) copy-start(bf16[192,1024]{1,0:T(8,128)(2,1)} %copy-done.1) | copy-start | bytes 1179652
  74.4 36.5 %all-to-all-start.2 = ((bf16[16,8,4096]{2,1,0:T(8,128)(2,1)}), bf16[16,8,4096]{2,1,0:T(8,128)(2,1)S(1)}, u32[]{:S(2)}, u32[]{:S(2)}) async-start(bf16[16,8,4096]{2,1,0:T(8,128)(2,1)} %bitcast.7), calls=%async_computation.2 | async-start | bytes 2097152 | tf_op jit(solution)/shard_map/all_to_all | solution.py:222
  85.2 5.5 %collective-permute-start.5 = (bf16[256,1024]{1,0:T(8,128)(2,1)S(1)}, bf16[256,1024]{1,0:T(8,128)(2,1)S(1)}, u32[]{:S(2)}, u32[]{:S(2)}) collective-permute-start(bf16[256,1024]{1,0:T(8,128)(2,1)S(1)} %shard_map.81), channel_id=1, source_target_pairs={{0,16},{16,0},{1,17},{17,1},{2,18},{18,2},{3,19},{19,3},{4,20},{20... | collective-permute-start | bytes 1572872 | tf_op jit(solution)/shard_map/ppermute | solution.py:27
  91.4 13.4 %collective-permute-start.6 = (bf16[256,256]{1,0:T(8,128)(2,1)S(1)}, bf16[256,256]{1,0:T(8,128)(2,1)S(1)}, u32[]{:S(2)}, u32[]{:S(2)}) collective-permute-start(bf16[256,256]{1,0:T(8,128)(2,1)S(1)} %get-tuple-element.27), channel_id=1, source_target_pairs={{0,2},{1,3},{2,0},{3,1},{4,6},{5,7},{6,4},{7,5},{8,10},{9,11},{10,... | collective-permute-start | bytes 393224 | tf_op jit(solution)/shard_map/ppermute | solution.py:27
  98.0 13.0 %collective-permute-start.7 = (bf16[256,256]{1,0:T(8,128)(2,1)S(1)}, bf16[256,256]{1,0:T(8,128)(2,1)S(1)}, u32[]{:S(2)}, u32[]{:S(2)}) collective-permute-start(bf16[256,256]{1,0:T(8,128)(2,1)S(1)} %get-tuple-element.28), channel_id=1, source_target_pairs={{0,3},{1,0},{2,1},{3,2},{4,7},{5,4},{6,5},{7,6},{8,11},{9,8},{10,9... | collective-permute-start | bytes 393224 | tf_op jit(solution)/shard_map/ppermute | solution.py:27
  100.9 10.1 %collective-permute-start.8 = (bf16[256,256]{1,0:T(8,128)(2,1)S(1)}, bf16[256,256]{1,0:T(8,128)(2,1)S(1)}, u32[]{:S(2)}, u32[]{:S(2)}) collective-permute-start(bf16[256,256]{1,0:T(8,128)(2,1)S(1)} %get-tuple-element.29), channel_id=1, source_target_pairs={{0,1},{1,2},{2,3},{3,0},{4,5},{5,6},{6,7},{7,4},{8,9},{9,10},{10,1... | collective-permute-start | bytes 393224 | tf_op jit(solution)/shard_map/ppermute | solution.py:27
